TPU v7x, 512 devices: a whole 4x4x16 slice. The times are simulated.
512 devices in a mesh: dom: 16 (over y, x_lo, core), feat: 32 (over x_hi, z).
Axes of the slice: x: 4 (x_hi: 2, x_lo: 2; x = x_hi * 2 + x_lo), y: 4, z: 16, core: 2. Of those that a mesh axis runs over, the one named last changes fastest.
Arguments:
- x0: bfloat16 [6144, 32768], P('dom', 'feat'), may hold values from -6 to 6
- cotangent: bfloat16 [6144, 32768], P('dom', 'feat'), may hold values from -6 to 6
- domain_ids: int32 [6144], P('dom'), may hold values from 0 to 8, as said below
- expert_u: bfloat16 [32768, 4096], P('feat', 'dom'), may hold values from -0.25 to 0.25
- expert_v: bfloat16 [32768, 4096], P('feat', 'dom'), may hold values from -0.03125 to 0.03125
- shared_u: bfloat16 [32768, 512], P(('feat', 'dom')), may hold values from -0.25 to 0.25
- shared_v: bfloat16 [32768, 512], P(('feat', 'dom')), may hold values from -0.03125 to 0.03125
- bias: float32 [2, 32768], P(None, 'feat'), may hold values from -4 to 4
Outputs:
- grad_x0: bfloat16 [6144, 32768], P('dom', 'feat')
- grad_expert_u: bfloat16 [32768, 4096], P('feat', 'dom')
- grad_expert_v: bfloat16 [32768, 4096], P('feat', 'dom')
- grad_shared_u: bfloat16 [32768, 512], P(('feat', 'dom'))
- grad_shared_v: bfloat16 [32768, 512], P(('feat', 'dom'))
- grad_bias: float32 [2, 32768], P(None, 'feat')
Inputs may be any that keep to these rules, and one draw needn't show every extreme that they name: `domain_ids`: block k of 384 slots holds first the live examples of domain k // 2, then padding slots marked 8; every block has at least 128 live examples, and block 0 has no padding.
All inputs are finite; a program needn't handle non-finite values.
Results may differ from a plain program's by a relative error of at most 0.009.
Values may be sent and summed in bfloat16 or wider, within the bound.
No kernel may reach another device: no remote copies, remote signals or barrier semaphores. Data moves between devices by JAX's collectives and lax.ppermute only.
A program may use at most 64 MiB of HBM per device.

v0:
```python
import jax
import jax.numpy as jnp
from jax import lax
from jax.sharding import PartitionSpec as P


def swapped(value, axis, bit):
    mask = 2**bit
    pairs = [(source, source ^ mask) for source in range(lax.axis_size(axis))]
    return lax.ppermute(value, axis, pairs)


def transposed_dot(left_side, right_side):
    return lax.dot_general(
        left_side, right_side, (((0,), (0,)), ((), ())), preferred_element_type=jnp.float32
    )


def cross_dot(left_side, right_side):
    return lax.dot_general(
        left_side, right_side, (((1,), (1,)), ((), ())), preferred_element_type=jnp.float32
    )


def local(x0, cotangent, domain_ids, expert_u, expert_v, shared_u, shared_v, bias):
    position = lax.axis_index("dom")
    domain = position // 2
    parity = position % 2
    half_rank = expert_u.shape[1]
    other_u, other_v = swapped((expert_u, expert_v), "dom", 0)
    is_first = parity == 0
    full_u = jnp.where(
        is_first, jnp.concatenate([expert_u, other_u], 1), jnp.concatenate([other_u, expert_u], 1)
    )
    full_v = jnp.where(
        is_first, jnp.concatenate([expert_v, other_v], 1), jnp.concatenate([other_v, expert_v], 1)
    )
    whole_su, whole_sv = (
        lax.all_gather(shared_u, "dom", axis=0, tiled=True),
        lax.all_gather(shared_v, "dom", axis=0, tiled=True),
    )
    live_rows = (domain_ids == domain)[:, None]
    masked = jnp.where(live_rows, cotangent, jnp.zeros_like(cotangent))
    inputs = x0.astype(jnp.float32)
    first_sum = lax.psum(jnp.dot(x0, full_v, preferred_element_type=jnp.float32), "feat")
    first_rank = first_sum.astype(jnp.bfloat16)
    first_gate = cross_dot(first_rank, full_u) + bias[0][None, :]
    layer_one = (inputs * first_gate + inputs).astype(jnp.bfloat16)
    second_sum = lax.psum(jnp.dot(layer_one, whole_sv, preferred_element_type=jnp.float32), "feat")
    second_rank = second_sum.astype(jnp.bfloat16)
    second_gate = cross_dot(second_rank, whole_su) + bias[1][None, :]
    masked_wide = masked.astype(jnp.float32)
    second_adj = (masked_wide * inputs).astype(jnp.bfloat16)
    back_two_sum = lax.psum(
        jnp.dot(second_adj, whole_su, preferred_element_type=jnp.float32), "feat"
    )
    back_two = back_two_sum.astype(jnp.bfloat16)
    layer_grad = masked_wide + cross_dot(back_two, whole_sv)
    first_adj = (layer_grad * inputs).astype(jnp.bfloat16)
    back_one_sum = lax.psum(jnp.dot(first_adj, full_u, preferred_element_type=jnp.float32), "feat")
    back_one = back_one_sum.astype(jnp.bfloat16)
    grad_inputs = (
        masked_wide * second_gate
        + layer_grad * first_gate
        + layer_grad
        + cross_dot(back_one, full_v)
    )
    term_su = transposed_dot(second_adj, second_rank)
    term_sv = transposed_dot(layer_one, back_two)
    sum_su, sum_sv = (
        lax.psum_scatter(term_su, "dom", scatter_dimension=0, tiled=True),
        lax.psum_scatter(term_sv, "dom", scatter_dimension=0, tiled=True),
    )
    bias_terms = jnp.stack(
        [
            jnp.sum(first_adj.astype(jnp.float32), axis=0),
            jnp.sum(second_adj.astype(jnp.float32), axis=0),
        ]
    )
    grad_bias = lax.psum(bias_terms, "dom")
    own_start = parity * half_rank
    their_start = (1 - parity) * half_rank
    own_rank = lax.dynamic_slice_in_dim(first_rank, own_start, half_rank, 1)
    own_back = lax.dynamic_slice_in_dim(back_one, own_start, half_rank, 1)
    give_rank = lax.dynamic_slice_in_dim(first_rank, their_start, half_rank, 1)
    give_back = lax.dynamic_slice_in_dim(back_one, their_start, half_rank, 1)
    recv_adj, recv_inputs, recv_rank, recv_back = swapped(
        (first_adj, x0, give_rank, give_back), "dom", 0
    )
    mine_gu = transposed_dot(first_adj, own_rank)
    peer_gu = transposed_dot(recv_adj, recv_rank)
    mine_gv = transposed_dot(x0, own_back)
    peer_gv = transposed_dot(recv_inputs, recv_back)
    grad_eu = (mine_gu + peer_gu).astype(jnp.bfloat16)
    grad_ev = (mine_gv + peer_gv).astype(jnp.bfloat16)
    return (
        grad_inputs.astype(jnp.bfloat16),
        grad_eu,
        grad_ev,
        sum_su.astype(jnp.bfloat16),
        sum_sv.astype(jnp.bfloat16),
        grad_bias,
    )


def solution(mesh):
    placed = (
        P("dom", "feat"),
        P("dom", "feat"),
        P("dom"),
        P("feat", "dom"),
        P("feat", "dom"),
        P(("feat", "dom"), None),
        P(("feat", "dom"), None),
        P(None, "feat"),
    )
    return jax.shard_map(
        local,
        mesh=mesh,
        in_specs=placed,
        out_specs=(
            P("dom", "feat"),
            P("feat", "dom"),
            P("feat", "dom"),
            P(("feat", "dom"), None),
            P(("feat", "dom"), None),
            P(None, "feat"),
        ),
        check_vma=False,
    )
```

profile of v0, /device:TPU:1, one launch (start us, length us, event | category | flops | bytes accessed | tf_op | source)
XLA Modules:
  0.0 539.6 jit_solution(12566012812103963593)
XLA Ops:
  8.0 8.8 %collective-permute-start = (bf16[1024,256]{1,0:T(8,128)(2,1)}, bf16[1024,256]{1,0:T(8,128)(2,1)}, u32[]{:S(2)}, u32[]{:S(2)}) collective-permute-start(bf16[1024,256]{1,0:T(8,128)(2,1)} %param.12), channel_id=1, source_target_pairs={{0,32},{32,0},{64,96},{96,64},{128,160},{160,128},{192,224},{224,1... | collective-permute-start | bytes 1572872 | tf_op jit(solution)/shard_map/ppermute | solution.py:10
  16.8 1.9 collective-permute-start.1
  20.3 1.7 convert_reduce_fusion
  22.0 2.0 convolution_bitcast_fusion
  24.0 32.0 %all-gather.5.cloned.1.call-done = bf16[1024,512]{1,0:T(8,128)(2,1)} async-done(((bf16[64,512]{1,0:T(8,128)(2,1)}), bf16[1024,512]{1,0:T(8,128)(2,1)}) %all-gather.5.cloned.1.call-update) | async-done | bytes 1048592 | tf_op jit(solution)/shard_map/all_gather | solution.py:39
  56.0 1.8 fusion.34
  57.8 139.9 %all-reduce.4 = (bf16[384,512]{1,0:T(8,128)(2,1)S(1)}, bf16[384,512]{0,1:T(8,128)(2,1)}) all-reduce(f32[384,512]{1,0:T(8,128)S(1)} %fusion.34, f32[384,512]{0,1:T(8,128)S(1)} %convolution_bitcast_fusion), channel_id=1, replica_groups=mesh['dom'=16,'feat'=32] {'feat'}, use_global_device_ids=true, to_apply=%region_2.3 | all-reduce | flops 393216 | bytes 2359296 | tf_op jit(solution)/shard_map/psum | solution.py:54
  197.7 2.3 convolution_add_fusion
  200.0 2.8 fusion.29
  202.8 1.9 convert_reduce_fusion.1
  205.6 2.7 fusion.21
  208.3 134.2 %all-reduce.5 = (bf16[384,512]{1,0:T(8,128)(2,1)}, bf16[384,512]{1,0:T(8,128)(2,1)}) all-reduce(f32[384,512]{1,0:T(8,128)} %fusion.29, f32[384,512]{1,0:T(8,128)} %fusion.21), channel_id=1, replica_groups=mesh['dom'=16,'feat'=32] {'feat'}, use_global_device_ids=true, to_apply=%region_1.2 | all-reduce | flops 393216 | bytes 2359296 | tf_op jit(solution)/shard_map/psum | solution.py:49
  342.5 3.1 fusion.35
  345.7 2.1 fusion.14
  347.8 56.3 %collective-permute-start.5 = (bf16[384,1024]{1,0:T(8,128)(2,1)S(1)}, bf16[384,1024]{1,0:T(8,128)(2,1)}, u32[]{:S(2)}, u32[]{:S(2)}) collective-permute-start(bf16[384,1024]{1,0:T(8,128)(2,1)S(1)} %copy-done), channel_id=1, source_target_pairs={{0,32},{32,0},{64,96},{96,64},{128,160},{160,128},{192,224},{224,1... | collective-permute-start | bytes 2359304 | tf_op jit(solution)/shard_map/ppermute | solution.py:10
  404.2 1.9 collective-permute-start.2
  407.7 2.4 collective-permute-start.3
  411.8 2.2 collective-permute-start.4
  415.7 3.1 fusion.3
  418.8 28.2 %psum.39 = f32[2,1024]{1,0:T(2,128)} all-reduce(f32[2,1024]{1,0:T(2,128)S(1)} %pad_maximum_fusion), channel_id=1, replica_groups=mesh['dom'=16,'feat'=32] {'dom'}, use_global_device_ids=true, to_apply=%region_8.9 | all-reduce | flops 2048 | bytes 16384 | tf_op jit(solution)/shard_map/psum | solution.py:80
  448.1 1.7 fusion.9
  450.8 2.4 fusion.7
  453.2 4.8 reduce-scatter.3.cloned.1.call-done
  459.5 71.9 %reduce-scatter.5.cloned.1.call-done = f32[64,512]{1,0:T(8,128)} async-done(((f32[1024,512]{1,0:T(8,128)}), f32[64,512]{1,0:T(8,128)}) %reduce-scatter.5.cloned.1.call-update) | async-done | bytes 131088 | tf_op jit(solution)/shard_map/reduce_scatter | solution.py:72
  (54 shorter events, 13.3 us)
Async XLA Ops:
  7.2 14.8 %copy-start.12 = (bf16[1024,256]{1,0:T(8,128)(2,1)S(1)}, bf16[1024,256]{1,0:T(8,128)(2,1)}, u32[]{:S(2)}) copy-start(bf16[1024,256]{1,0:T(8,128)(2,1)} %param.12) | copy-start | bytes 1572868
  7.2 14.8 %copy-start = (bf16[384,1024]{1,0:T(8,128)(2,1)S(1)}, bf16[384,1024]{1,0:T(8,128)(2,1)}, u32[]{:S(2)}) copy-start(bf16[384,1024]{1,0:T(8,128)(2,1)} %param.8) | copy-start | bytes 2359300
  7.2 48.8 %all-gather.5.cloned.1.call-start = ((), (), s32[]{:S(2)}) async-start(), calls=%async_computation.3 | async-start | bytes 1114112 | tf_op jit(solution)/shard_map/all_gather | solution.py:39
  7.9 192.1 %all-gather.3.cloned.1.call-start = ((), (), s32[]{:S(2)}) async-start(), calls=%async_computation.2 | async-start | bytes 1114112 | tf_op jit(solution)/shard_map/all_gather | solution.py:40
  8.0 14.0 %collective-permute-start = (bf16[1024,256]{1,0:T(8,128)(2,1)}, bf16[1024,256]{1,0:T(8,128)(2,1)}, u32[]{:S(2)}, u32[]{:S(2)}) collective-permute-start(bf16[1024,256]{1,0:T(8,128)(2,1)} %param.12), channel_id=1, source_target_pairs={{0,32},{32,0},{64,96},{96,64},{128,160},{160,128},{192,224},{224,1... | collective-permute-start | bytes 1572872 | tf_op jit(solution)/shard_map/ppermute | solution.py:10
  16.8 180.9 %collective-permute-start.1 = (bf16[1024,256]{1,0:T(8,128)(2,1)}, bf16[1024,256]{1,0:T(8,128)(2,1)}, u32[]{:S(2)}, u32[]{:S(2)}) collective-permute-start(bf16[1024,256]{1,0:T(8,128)(2,1)} %param.11), channel_id=1, source_target_pairs={{0,32},{32,0},{64,96},{96,64},{128,160},{160,128},{192,224},{224,1... | collective-permute-start | bytes 1572872 | tf_op jit(solution)/shard_map/ppermute | solution.py:10
  18.7 439.3 %reduce-scatter.3.cloned.1.call-start = ((), (), s32[]{:S(2)}) async-start(), calls=%async_computation.4 | async-start | bytes 2228224 | tf_op jit(solution)/shard_map/reduce_scatter | solution.py:71
  200.0 2.8 copy-start.2
  200.0 2.8 copy-start.5
  202.8 2.8 copy-start.11
  204.7 0.9 copy-start.3
  345.6 185.9 %reduce-scatter.5.cloned.1.call-start = ((), (), s32[]{:S(2)}) async-start(), calls=%async_computation.5 | async-start | bytes 2228224 | tf_op jit(solution)/shard_map/reduce_scatter | solution.py:72
  347.8 66.3 %copy-start.1 = (bf16[1024,512]{1,0:T(8,128)(2,1)S(1)}, bf16[1024,512]{1,0:T(8,128)(2,1)}, u32[]{:S(2)}) copy-start(bf16[1024,512]{1,0:T(8,128)(2,1)} %all-gather.5.cloned.1.call-done) | copy-start | bytes 3145732
  347.8 100.2 %collective-permute-start.5 = (bf16[384,1024]{1,0:T(8,128)(2,1)S(1)}, bf16[384,1024]{1,0:T(8,128)(2,1)}, u32[]{:S(2)}, u32[]{:S(2)}) collective-permute-start(bf16[384,1024]{1,0:T(8,128)(2,1)S(1)} %copy-done), channel_id=1, source_target_pairs={{0,32},{32,0},{64,96},{96,64},{128,160},{160,128},{192,224},{224,1... | collective-permute-start | bytes 2359304 | tf_op jit(solution)/shard_map/ppermute | solution.py:10
  404.2 46.6 %collective-permute-start.2 = (bf16[384,1024]{1,0:T(8,128)(2,1)}, bf16[384,1024]{1,0:T(8,128)(2,1)}, u32[]{:S(2)}, u32[]{:S(2)}) collective-permute-start(bf16[384,1024]{1,0:T(8,128)(2,1)} %copy-done.3), channel_id=1, source_target_pairs={{0,32},{32,0},{64,96},{96,64},{128,160},{160,128},{192,224},{224,1... | collective-permute-start | bytes 2359304 | tf_op jit(solution)/shard_map/ppermute | solution.py:10
  407.7 43.0 %collective-permute-start.3 = (bf16[384,256]{0,1:T(8,128)(2,1)}, bf16[384,256]{0,1:T(8,128)(2,1)}, u32[]{:S(2)}, u32[]{:S(2)}) collective-permute-start(bf16[384,256]{0,1:T(8,128)(2,1)} %constant_dynamic-slice_fusion.1), channel_id=1, source_target_pairs={{0,32},{32,0},{64,96},{96,64},{128,160},{160,128},{192,224},{224,1... | collective-permute-start | bytes 589832 | tf_op jit(solution)/shard_map/ppermute | solution.py:10
  410.1 5.5 %copy-start.13 = (bf16[1024,256]{1,0:T(8,128)(2,1)S(1)}, bf16[1024,256]{1,0:T(8,128)(2,1)}, u32[]{:S(2)}) copy-start(bf16[1024,256]{1,0:T(8,128)(2,1)} %param.12) | copy-start | bytes 1572868
  411.8 3.8 copy-start.6
  411.8 3.8 copy-start.7
  411.8 3.8 copy-start.9
  411.8 36.2 %collective-permute-start.4 = (bf16[384,256]{1,0:T(8,128)(2,1)}, bf16[384,256]{1,0:T(8,128)(2,1)}, u32[]{:S(2)}, u32[]{:S(2)}) collective-permute-start(bf16[384,256]{1,0:T(8,128)(2,1)} %constant_dynamic-slice_fusion), channel_id=1, source_target_pairs={{0,32},{32,0},{64,96},{96,64},{128,160},{160,128},{192,224},{224,1... | collective-permute-start | bytes 589832 | tf_op jit(solution)/shard_map/ppermute | solution.py:10
  415.7 31.4 %copy-start.4 = (bf16[384,1024]{1,0:T(8,128)(2,1)S(1)}, bf16[384,1024]{1,0:T(8,128)(2,1)}, u32[]{:S(2)}) copy-start(bf16[384,1024]{1,0:T(8,128)(2,1)} %copy-done.3) | copy-start | bytes 2359300
  415.7 31.4 %copy-start.8 = (bf16[384,512]{0,1:T(8,128)(2,1)S(1)}, bf16[384,512]{0,1:T(8,128)(2,1)}, u32[]{:S(2)}) copy-start(bf16[384,512]{0,1:T(8,128)(2,1)} %get-tuple-element.15) | copy-start | bytes 1179652
  418.8 28.8 %copy-start.10 = (bf16[384,512]{1,0:T(8,128)(2,1)S(1)}, bf16[384,512]{1,0:T(8,128)(2,1)}, u32[]{:S(2)}) copy-start(bf16[384,512]{1,0:T(8,128)(2,1)} %get-tuple-element.13) | copy-start | bytes 1179652
Sparse Core Ops, SparseCore 0:
  10.2 45.8 all-gather.4
  58.2 41.0 all-gather.2
  345.7 112.2 reduce-scatter.2
  460.7 70.7 reduce-scatter.4
where the time goes:
time: 542 us; the launch traced here: 540 us
  blocking collectives  302 us (56%)
  waiting for transfers between devices  110 us (20%)
  starting transfers between devices  73.7 us (14%)
  matrix products  28.4 us (5%)
  between operations  14.1 us (3%)
  local copies, waits for them, and re-layouts  6.04 us (1%)
  other arithmetic  5.51 us (1%)
    psum x1, blocking collectives, local(): lax.psum(jnp.dot(second_adj, whole_su, preferred_element_type=jnp.float32...  140 us
    psum x1, blocking collectives, local(): lax.psum(jnp.dot(layer_one, whole_sv, preferred_element_type=jnp.float32)...  134 us
    ppermute x6, starting transfers between devices, swapped(): return lax.ppermute(value, axis, pairs)  73.6 us
    reduce_scatter x1, waiting for transfers between devices, local(): lax.psum_scatter(term_sv, 'dom', scatter_dimension=0, tiled=True)  71.9 us
    all_gather x1, waiting for transfers between devices, local(): lax.all_gather(shared_u, 'dom', axis=0, tiled=True)  32 us
    psum x1, blocking collectives, local(): grad_bias = lax.psum(bias_terms, 'dom')  28.2 us
  transfers between devices with their start and end apart: 10, of which 3 were waited for; matrix products, arithmetic and copies ran while one was open for 5% of the time, Pallas kernels for 0%

commit v1 on v0

v1 whole, which is shorter than its diff:
```python
import jax
import jax.numpy as jnp
from jax import lax
from jax.sharding import PartitionSpec as P

FAR = 2


def partner_swap(value):
    pairs = [(source, source ^ 1) for source in range(lax.axis_size("dom"))]
    return lax.ppermute(value, "dom", pairs)


def near_groups():
    half = lax.axis_size("feat") // FAR
    return [[far * half + 2 * pair + bit for far in range(FAR) for bit in range(2)] for pair in range(half // 2)]


def ring_groups():
    half = lax.axis_size("feat") // FAR
    return [[far * half + 2 * step + bit for step in range(half // 2)] for far in range(FAR) for bit in range(2)]


def exchange(value, axis, groups=None):
    return lax.all_to_all(value, axis, 0, 0, axis_index_groups=groups, tiled=True)


def summed(value, axis, groups, members):
    rows = value.shape[0] // members
    pieces = exchange(value, axis, groups).reshape(members, rows, value.shape[1])
    return jnp.sum(pieces.astype(jnp.float32), axis=0).astype(jnp.bfloat16)


def gathered(value, axis, groups, members):
    repeated = jnp.broadcast_to(value[None], (members, *value.shape))
    return exchange(repeated.reshape(members * value.shape[0], value.shape[1]), axis, groups)


def feature_sum(value):
    near, ring = near_groups(), ring_groups()
    part = summed(value, "feat", near, len(near[0]))
    part = summed(part, "feat", ring, len(ring[0]))
    part = gathered(part, "feat", ring, len(ring[0]))
    return gathered(part, "feat", near, len(near[0]))


def dot(left_side, right_side):
    return jnp.dot(left_side, right_side, preferred_element_type=jnp.float32)


def transposed_dot(left_side, right_side):
    return lax.dot_general(
        left_side, right_side, (((0,), (0,)), ((), ())), preferred_element_type=jnp.float32
    )


def cross_dot(left_side, right_side):
    return lax.dot_general(
        left_side, right_side, (((1,), (1,)), ((), ())), preferred_element_type=jnp.float32
    )


def local(x0, cotangent, domain_ids, expert_u, expert_v, shared_u, shared_v, bias):
    low = jnp.bfloat16
    rows, width = x0.shape
    half_rank = expert_u.shape[1]
    rank = 2 * half_rank
    members = lax.axis_size("dom")
    domain = lax.axis_index("dom") // 2
    other_v = partner_swap(expert_v)
    other_u = partner_swap(expert_u)
    full_v = jnp.concatenate([expert_v, other_v], 1)
    full_u = jnp.concatenate([expert_u, other_u], 1)
    whole_sv = lax.all_gather(shared_v, "dom", axis=0, tiled=True)
    whole_su = gathered(shared_u, "dom", None, members)
    live_rows = (domain_ids == domain)[:, None]
    masked = jnp.where(live_rows, cotangent, jnp.zeros_like(cotangent))
    masked_wide = masked.astype(jnp.float32)
    inputs = x0.astype(jnp.float32)
    second_adj = (masked_wide * inputs).astype(low)
    first_part = dot(x0, full_v).astype(low)
    back_two_part = dot(second_adj, whole_su).astype(low)
    sums = feature_sum(jnp.concatenate([first_part, back_two_part], 0))
    first_rank, back_two = sums[:rows], sums[rows:]
    first_gate = cross_dot(first_rank, full_u) + bias[0][None, :]
    layer_one = (inputs * first_gate + inputs).astype(low)
    layer_grad = masked_wide + cross_dot(back_two, whole_sv)
    first_adj = (layer_grad * inputs).astype(low)
    second_part = dot(layer_one, whole_sv).astype(low)
    back_one_part = dot(first_adj, full_u).astype(low)
    partial_gu = transposed_dot(first_adj, first_rank)
    peer_gu = partner_swap(partial_gu[:, half_rank:].astype(low))
    grad_eu = (partial_gu[:, :half_rank] + peer_gu.astype(jnp.float32)).astype(low)
    term_sv = transposed_dot(layer_one, back_two)
    sum_sv = lax.psum_scatter(term_sv, "dom", scatter_dimension=0, tiled=True)
    sums = feature_sum(jnp.concatenate([second_part, back_one_part], 0))
    second_rank, back_one = sums[:rows], sums[rows:]
    partial_gv = transposed_dot(x0, back_one)
    peer_gv = partner_swap(partial_gv[:, half_rank:].astype(low))
    grad_ev = (partial_gv[:, :half_rank] + peer_gv.astype(jnp.float32)).astype(low)
    second_gate = cross_dot(second_rank, whole_su) + bias[1][None, :]
    grad_inputs = (
        masked_wide * second_gate
        + layer_grad * first_gate
        + layer_grad
        + cross_dot(back_one, full_v)
    ).astype(low)
    bias_terms = jnp.stack(
        [
            jnp.sum(first_adj.astype(jnp.float32), axis=0),
            jnp.sum(second_adj.astype(jnp.float32), axis=0),
        ]
    )
    bias_high = bias_terms.astype(low)
    bias_rest = (bias_terms - bias_high.astype(jnp.float32)).astype(low)
    bias_lines = jnp.stack([bias_high, bias_rest]).reshape(4 * width // rank, rank)
    term_su = transposed_dot(second_adj, second_rank).astype(low).reshape(members, width // members, rank)
    lines = bias_lines.shape[0]
    sent = jnp.concatenate([term_su, jnp.broadcast_to(bias_lines[None], (members, lines, rank))], 1)
    taken = exchange(sent, "dom").astype(jnp.float32).sum(0)
    sum_su = taken[: width // members]
    bias_sum = taken[width // members :].reshape(2, 2, width)
    grad_bias = bias_sum[0] + bias_sum[1]
    return (
        grad_inputs,
        grad_eu,
        grad_ev,
        sum_su.astype(low),
        sum_sv.astype(low),
        grad_bias,
    )


def solution(mesh):
    placed = (
        P("dom", "feat"),
        P("dom", "feat"),
        P("dom"),
        P("feat", "dom"),
        P("feat", "dom"),
        P(("feat", "dom"), None),
        P(("feat", "dom"), None),
        P(None, "feat"),
    )
    return jax.shard_map(
        local,
        mesh=mesh,
        in_specs=placed,
        out_specs=(
            P("dom", "feat"),
            P("feat", "dom"),
            P("feat", "dom"),
            P(("feat", "dom"), None),
            P(("feat", "dom"), None),
            P(None, "feat"),
        ),
        check_vma=False,
    )
```

time: 542 us -> 278 us (0.51)
  blocking collectives: 302 us -> 108 us
  waiting for transfers between devices: 110 us -> 63 us
  starting transfers between devices: 73.7 us -> 45.8 us
  local copies, waits for them, and re-layouts: 6.04 us -> 18.1 us
  matrix products: 28.4 us -> 17.3 us
    psum x3 -> x0, blocking collectives: 302 us -> none  [the longest x1 140 us: local(): lax.psum(jnp.dot(second_adj, whole_su, preferred_element_type=jnp.float32...]
    all_to_all x0 -> x5, blocking collectives: none -> 108 us  [exchange(): lax.all_to_all(value, axis, 0, 0, axis_index_groups=groups, tiled=True)]
    reduce_scatter x2 -> x1, waiting for transfers between devices: 76.7 us -> 0.01 us  [local(): sum_sv = lax.psum_scatter(term_sv, 'dom', scatter_dimension=0, tiled=True)]
    ppermute x6 -> x4, starting transfers between devices: 73.6 us -> 24.4 us  [partner_swap(): return lax.ppermute(value, 'dom', pairs)]
    all_to_all x0 -> x5, waiting for transfers between devices: none -> 31 us  [exchange(): lax.all_to_all(value, axis, 0, 0, axis_index_groups=groups, tiled=True)]
    all_to_all x0 -> x5, starting transfers between devices: none -> 21.4 us  [exchange(): lax.all_to_all(value, axis, 0, 0, axis_index_groups=groups, tiled=True)]
    all_gather x2 -> x1, waiting for transfers between devices: 32.1 us -> 28.9 us  [local(): whole_sv = lax.all_gather(shared_v, 'dom', axis=0, tiled=True)]
  transfers between devices with their start and end apart: 10 -> 11, of which waited for: 3 -> 6; matrix products, arithmetic and copies ran while one was open for 5% -> 9% of each run, Pallas kernels for 0% -> 0%
where the time goes in v1:
time: 278 us; the launch traced here: 277 us
  blocking collectives  108 us (39%)
  waiting for transfers between devices  63 us (23%)
  starting transfers between devices  45.8 us (16%)
  local copies, waits for them, and re-layouts  18.1 us (7%)
  matrix products  17.3 us (6%)
  between operations  14.5 us (5%)
  other arithmetic  10 us (4%)
    all_to_all x5, blocking collectives, exchange(): lax.all_to_all(value, axis, 0, 0, axis_index_groups=groups, tiled=True)  108 us
    all_to_all x5, waiting for transfers between devices, exchange(): lax.all_to_all(value, axis, 0, 0, axis_index_groups=groups, tiled=True)  31 us
    all_gather x1, waiting for transfers between devices, local(): whole_sv = lax.all_gather(shared_v, 'dom', axis=0, tiled=True)  28.9 us
    ppermute x4, starting transfers between devices, partner_swap(): return lax.ppermute(value, 'dom', pairs)  24.4 us
    all_to_all x5, starting transfers between devices, exchange(): lax.all_to_all(value, axis, 0, 0, axis_index_groups=groups, tiled=True)  21.4 us
    unnamed x53, local copies, waits for them, and re-layouts  7.27 us
    dot_general x4, matrix products, cross_dot(): lax.dot_general(left_side, right_side, (((1,), (1,)), ((), ())), preferre...  7.24 us
  transfers between devices with their start and end apart: 11, of which 6 were waited for; matrix products, arithmetic and copies ran while one was open for 9% of the time, Pallas kernels for 0%

profile of v1, /device:TPU:1, one launch (start us, length us, event | category | flops | bytes accessed | tf_op | source)
XLA Modules:
  0.0 276.6 jit_solution(6882785451450030662)
XLA Ops:
  7.2 8.9 %collective-permute-start = (bf16[1024,256]{1,0:T(8,128)(2,1)}, bf16[1024,256]{1,0:T(8,128)(2,1)}, u32[]{:S(2)}, u32[]{:S(2)}) collective-permute-start(bf16[1024,256]{1,0:T(8,128)(2,1)} %param.12), channel_id=1, source_target_pairs={{0,32},{32,0},{64,96},{96,64},{128,160},{160,128},{192,224},{224,1... | collective-permute-start | bytes 1572872 | tf_op jit(solution)/shard_map/ppermute | solution.py:11
  16.1 2.0 broadcast_in_dim.30
  18.1 3.7 %all-to-all-start = ((bf16[16,64,512]{2,1,0:T(8,128)(2,1)}), bf16[16,64,512]{2,1,0:T(8,128)(2,1)S(1)}, u32[]{:S(2)}, u32[]{:S(2)}) async-start(bf16[16,64,512]{2,1,0:T(8,128)(2,1)} %broadcast_in_dim.30), calls=%async_computation | async-start | bytes 2097152 | tf_op jit(solution)/shard_map/all_to_all | solution.py:25
  27.3 10.3 %all-to-all-done = bf16[16,64,512]{2,1,0:T(8,128)(2,1)S(1)} async-done(((bf16[16,64,512]{2,1,0:T(8,128)(2,1)}), bf16[16,64,512]{2,1,0:T(8,128)(2,1)S(1)}, u32[]{:S(2)}, u32[]{:S(2)}) %all-to-all-start) | async-done | bytes 1048608 | tf_op jit(solution)/shard_map/all_to_all | solution.py:25
  38.9 14.0 %all_to_all.74 = bf16[4,192,512]{2,1,0:T(8,128)(2,1)S(1)} all-to-all(bf16[4,192,512]{2,1,0:T(8,128)(2,1)S(1)} %bitcast.51), channel_id=1, replica_groups={{0,1,16,17},{2,3,18,19},{4,5,20,21},{6,7,22,23},{8,9,24,25},{10,11,26,2..., dimensions={0} | all-to-all | bytes 1572864 | tf_op jit(solution)/shard_map/all_to_all | solution.py:25
  53.1 27.3 %all_to_all.75 = bf16[8,24,512]{2,1,0:T(8,128)(2,1)S(1)} all-to-all(bf16[8,24,512]{2,1,0:T(8,128)(2,1)S(1)} %bitcast.55), channel_id=1, replica_groups={{0,2,4,6,8,10,12,14},{1,3,5,7,9,11,13,15},{16,18,20,22,24,26,28,30},{17..., dimensions={0} | all-to-all | bytes 393216 | tf_op jit(solution)/shard_map/all_to_all | solution.py:25
  80.5 19.0 %all_to_all.76 = bf16[8,24,512]{2,1,0:T(8,128)(2,1)S(1)} all-to-all(bf16[8,24,512]{2,1,0:T(8,128)(2,1)S(1)} %broadcast_in_dim.56), channel_id=1, replica_groups={{0,2,4,6,8,10,12,14},{1,3,5,7,9,11,13,15},{16,18,20,22,24,26,28,30},{17..., dimensions={0} | all-to-all | bytes 393216 | tf_op jit(solution)/shard_map/all_to_all | solution.py:25
  100.4 4.3 %all-to-all-start.4 = ((bf16[4,192,512]{2,1,0:T(8,128)(2,1)}), bf16[4,192,512]{2,1,0:T(8,128)(2,1)S(1)}, u32[]{:S(2)}, u32[]{:S(2)}) async-start(bf16[4,192,512]{2,1,0:T(8,128)(2,1)} %broadcast_in_dim.58), calls=%async_computation.4 | async-start | bytes 1572864 | tf_op jit(solution)/shard_map/all_to_all | solution.py:25
  105.4 6.4 %collective-permute-start.1 = (bf16[1024,256]{1,0:T(8,128)(2,1)S(1)}, bf16[1024,256]{1,0:T(8,128)(2,1)S(1)}, u32[]{:S(2)}, u32[]{:S(2)}) collective-permute-start(bf16[1024,256]{1,0:T(8,128)(2,1)S(1)} %copy-done.18), channel_id=1, source_target_pairs={{0,32},{32,0},{64,96},{96,64},{128,160},{160,128},{192,224},{224,1... | collective-permute-start | bytes 1572872 | tf_op jit(solution)/shard_map/ppermute | solution.py:11
  115.1 28.9 %all-gather.2.cloned.1.call-done = bf16[1024,512]{1,0:T(8,128)(2,1)} async-done(((bf16[64,512]{1,0:T(8,128)(2,1)}), bf16[1024,512]{1,0:T(8,128)(2,1)}) %all-gather.2.cloned.1.call-update) | async-done | bytes 1048592 | tf_op jit(solution)/shard_map/all_gather | solution.py:74
  144.0 3.1 %convert_reduce_fusion.2 = (f32[1024]{0:T(1024)S(1)}, bf16[384,1024]{1,0:T(8,128)(2,1)S(1)}, f32[384,1024]{1,0:T(8,128)}) fusion(bf16[384,1024]{1,0:T(8,128)(2,1)S(1)} %copy-done, bf16[384,512]{1,0:T(8,128)(2,1)S(1)} %bitcast.46, bf16[1024,512]{1,0:T(8,128)(2,1)} %all-gather.2.cloned.1.call-done, bf16[384,1024]{1,0:T(8,128)(2,1)S(1)} %copy-done.1, ...), kind=kOutput, calls=%fused_computation.16 | convolution fusion | flops 405797888 | bytes 5378432 | tf_op jit(solution)/shard_map/dot_general | solution.py:58
  147.0 2.1 convolution_convert_fusion.2
  149.2 1.9 convolution_add_fusion
  152.6 4.7 %all-to-all-start.5 = ((bf16[4,192,512]{2,1,0:T(8,128)(2,1)}), bf16[4,192,512]{2,1,0:T(8,128)(2,1)}, u32[]{:S(2)}, u32[]{:S(2)}) async-start(bf16[4,192,512]{2,1,0:T(8,128)(2,1)} %bitcast.50), calls=%async_computation.5 | async-start | bytes 1572864 | tf_op jit(solution)/shard_map/all_to_all | solution.py:25
  157.3 2.1 fusion.11
  159.5 9.8 %all-to-all-done.5 = bf16[4,192,512]{2,1,0:T(8,128)(2,1)} async-done(((bf16[4,192,512]{2,1,0:T(8,128)(2,1)}), bf16[4,192,512]{2,1,0:T(8,128)(2,1)}, u32[]{:S(2)}, u32[]{:S(2)}) %all-to-all-start.5) | async-done | bytes 786464 | tf_op jit(solution)/shard_map/all_to_all | solution.py:25
  170.6 26.8 %all_to_all.77 = bf16[8,24,512]{2,1,0:T(8,128)(2,1)S(1)} all-to-all(bf16[8,24,512]{2,1,0:T(8,128)(2,1)S(1)} %bitcast.56), channel_id=1, replica_groups={{0,2,4,6,8,10,12,14},{1,3,5,7,9,11,13,15},{16,18,20,22,24,26,28,30},{17..., dimensions={0} | all-to-all | bytes 393216 | tf_op jit(solution)/shard_map/all_to_all | solution.py:25
  198.8 20.8 %all_to_all.78 = bf16[8,24,512]{2,1,0:T(8,128)(2,1)S(1)} all-to-all(bf16[8,24,512]{2,1,0:T(8,128)(2,1)S(1)} %broadcast_in_dim.59), channel_id=1, replica_groups={{0,2,4,6,8,10,12,14},{1,3,5,7,9,11,13,15},{16,18,20,22,24,26,28,30},{17..., dimensions={0} | all-to-all | bytes 393216 | tf_op jit(solution)/shard_map/all_to_all | solution.py:25
  220.5 4.2 %all-to-all-start.8 = ((bf16[4,192,512]{2,1,0:T(8,128)(2,1)}), bf16[4,192,512]{2,1,0:T(8,128)(2,1)}, u32[]{:S(2)}, u32[]{:S(2)}) async-start(bf16[4,192,512]{2,1,0:T(8,128)(2,1)} %broadcast_in_dim.61), calls=%async_computation.8 | async-start | bytes 1572864 | tf_op jit(solution)/shard_map/all_to_all | solution.py:25
  228.8 6.7 %collective-permute-start.2 = (bf16[1024,256]{1,0:T(8,128)(2,1)}, bf16[1024,256]{1,0:T(8,128)(2,1)}, u32[]{:S(2)}, u32[]{:S(2)}) collective-permute-start(bf16[1024,256]{1,0:T(8,128)(2,1)} %slice.99), channel_id=1, source_target_pairs={{0,32},{32,0},{64,96},{96,64},{128,160},{160,128},{192,224},{224,1... | collective-permute-start | bytes 1572872 | tf_op jit(solution)/shard_map/ppermute | solution.py:11
  237.4 2.3 fusion.9
  245.1 4.5 %all-to-all-start.9 = ((bf16[16,72,512]{2,1,0:T(8,128)(2,1)}), bf16[16,72,512]{2,1,0:T(8,128)(2,1)}, u32[]{:S(2)}, u32[]{:S(2)}) async-start(bf16[16,72,512]{2,1,0:T(8,128)(2,1)} %pad_maximum_fusion), calls=%async_computation.9 | async-start | bytes 2359296 | tf_op jit(solution)/shard_map/all_to_all | solution.py:25
  250.5 2.3 collective-permute-start.3
  256.2 10.8 %all-to-all-done.9 = bf16[16,72,512]{2,1,0:T(8,128)(2,1)} async-done(((bf16[16,72,512]{2,1,0:T(8,128)(2,1)}), bf16[16,72,512]{2,1,0:T(8,128)(2,1)}, u32[]{:S(2)}, u32[]{:S(2)}) %all-to-all-start.9) | async-done | bytes 1179680 | tf_op jit(solution)/shard_map/all_to_all | solution.py:25
  (103 shorter events, 35.1 us)
Async XLA Ops:
  7.2 14.6 %copy-start.17 = (bf16[1024,256]{1,0:T(8,128)(2,1)S(1)}, bf16[1024,256]{1,0:T(8,128)(2,1)}, u32[]{:S(2)}) copy-start(bf16[1024,256]{1,0:T(8,128)(2,1)} %param.12) | copy-start | bytes 1572868
  7.2 15.9 %collective-permute-start = (bf16[1024,256]{1,0:T(8,128)(2,1)}, bf16[1024,256]{1,0:T(8,128)(2,1)}, u32[]{:S(2)}, u32[]{:S(2)}) collective-permute-start(bf16[1024,256]{1,0:T(8,128)(2,1)} %param.12), channel_id=1, source_target_pairs={{0,32},{32,0},{64,96},{96,64},{128,160},{160,128},{192,224},{224,1... | collective-permute-start | bytes 1572872 | tf_op jit(solution)/shard_map/ppermute | solution.py:11
  18.1 4.6 %copy-start.24 = (s32[384]{0:T(512)S(1)}, s32[384]{0:T(512)}, u32[]{:S(2)}) copy-start(s32[384]{0:T(512)} %param.10) | copy-start | bytes 4612
  18.1 4.6 %copy-start = (bf16[384,1024]{1,0:T(8,128)(2,1)S(1)}, bf16[384,1024]{1,0:T(8,128)(2,1)}, u32[]{:S(2)}) copy-start(bf16[384,1024]{1,0:T(8,128)(2,1)} %param.8) | copy-start | bytes 2359300
  18.1 4.6 %copy-start.1 = (bf16[384,1024]{1,0:T(8,128)(2,1)S(1)}, bf16[384,1024]{1,0:T(8,128)(2,1)}, u32[]{:S(2)}) copy-start(bf16[384,1024]{1,0:T(8,128)(2,1)} %param.9) | copy-start | bytes 2359300
  18.1 19.5 %all-to-all-start = ((bf16[16,64,512]{2,1,0:T(8,128)(2,1)}), bf16[16,64,512]{2,1,0:T(8,128)(2,1)S(1)}, u32[]{:S(2)}, u32[]{:S(2)}) async-start(bf16[16,64,512]{2,1,0:T(8,128)(2,1)} %broadcast_in_dim.30), calls=%async_computation | async-start | bytes 2097152 | tf_op jit(solution)/shard_map/all_to_all | solution.py:25
  23.0 14.5 %copy-start.15 = (bf16[384,1024]{1,0:T(8,128)(2,1)}, bf16[384,1024]{1,0:T(8,128)(2,1)S(1)}, u32[]{:S(2)}) copy-start(bf16[384,1024]{1,0:T(8,128)(2,1)S(1)} %get-tuple-element.21) | copy-start | bytes 2359300
  80.4 25.0 %copy-start.18 = (bf16[1024,256]{1,0:T(8,128)(2,1)S(1)}, bf16[1024,256]{1,0:T(8,128)(2,1)}, u32[]{:S(2)}) copy-start(bf16[1024,256]{1,0:T(8,128)(2,1)} %param.11) | copy-start | bytes 1572868
  100.4 12.3 %copy-start.20 = (f32[2,1024]{1,0:T(2,128)S(1)}, f32[2,1024]{1,0:T(2,128)}, u32[]{:S(2)}) copy-start(f32[2,1024]{1,0:T(2,128)} %param.15) | copy-start | bytes 24580
  100.4 13.8 %all-to-all-start.4 = ((bf16[4,192,512]{2,1,0:T(8,128)(2,1)}), bf16[4,192,512]{2,1,0:T(8,128)(2,1)S(1)}, u32[]{:S(2)}, u32[]{:S(2)}) async-start(bf16[4,192,512]{2,1,0:T(8,128)(2,1)} %broadcast_in_dim.58), calls=%async_computation.4 | async-start | bytes 1572864 | tf_op jit(solution)/shard_map/all_to_all | solution.py:25
  104.7 39.2 %all-gather.2.cloned.1.call-start = ((), (), s32[]{:S(2)}) async-start(), calls=%async_computation.11 | async-start | bytes 1114112 | tf_op jit(solution)/shard_map/all_gather | solution.py:74
  105.4 7.9 %collective-permute-start.1 = (bf16[1024,256]{1,0:T(8,128)(2,1)S(1)}, bf16[1024,256]{1,0:T(8,128)(2,1)S(1)}, u32[]{:S(2)}, u32[]{:S(2)}) collective-permute-start(bf16[1024,256]{1,0:T(8,128)(2,1)S(1)} %copy-done.18), channel_id=1, source_target_pairs={{0,32},{32,0},{64,96},{96,64},{128,160},{160,128},{192,224},{224,1... | collective-permute-start | bytes 1572872 | tf_op jit(solution)/shard_map/ppermute | solution.py:11
  112.7 31.2 %copy-start.22 = (pred[384]{0:T(512)(128)(4,1)S(1)}, pred[384]{0:T(512)(128)(4,1)}, u32[]{:S(2)}) copy-start(pred[384]{0:T(512)(128)(4,1)} %copy-done.21) | copy-start | bytes 1156
  147.0 4.1 %copy-start.9 = (bf16[384,1024]{1,0:T(8,128)(2,1)}, bf16[384,1024]{1,0:T(8,128)(2,1)S(1)}, u32[]{:S(2)}) copy-start(bf16[384,1024]{1,0:T(8,128)(2,1)S(1)} %get-tuple-element.19) | copy-start | bytes 2359300
  152.6 16.7 %all-to-all-start.5 = ((bf16[4,192,512]{2,1,0:T(8,128)(2,1)}), bf16[4,192,512]{2,1,0:T(8,128)(2,1)}, u32[]{:S(2)}, u32[]{:S(2)}) async-start(bf16[4,192,512]{2,1,0:T(8,128)(2,1)} %bitcast.50), calls=%async_computation.5 | async-start | bytes 1572864 | tf_op jit(solution)/shard_map/all_to_all | solution.py:25
  157.3 82.3 %reduce-scatter.2.cloned.1.call-start = ((), (), s32[]{:S(2)}) async-start(), calls=%async_computation.12 | async-start | bytes 2228224 | tf_op jit(solution)/shard_map/reduce_scatter | solution.py:95
  198.0 26.7 %copy-start.8 = (bf16[2,192,512]{2,1,0:T(8,128)(2,1)S(1)}, bf16[2,192,512]{2,1,0:T(8,128)(2,1)}, u32[]{:S(2)}) copy-start(bf16[2,192,512]{2,1,0:T(8,128)(2,1)} %get-tuple-element.24) | copy-start | bytes 1179652
  220.5 20.7 %all-to-all-start.8 = ((bf16[4,192,512]{2,1,0:T(8,128)(2,1)}), bf16[4,192,512]{2,1,0:T(8,128)(2,1)}, u32[]{:S(2)}, u32[]{:S(2)}) async-start(bf16[4,192,512]{2,1,0:T(8,128)(2,1)} %broadcast_in_dim.61), calls=%async_computation.8 | async-start | bytes 1572864 | tf_op jit(solution)/shard_map/all_to_all | solution.py:25
  228.8 8.6 %collective-permute-start.2 = (bf16[1024,256]{1,0:T(8,128)(2,1)}, bf16[1024,256]{1,0:T(8,128)(2,1)}, u32[]{:S(2)}, u32[]{:S(2)}) collective-permute-start(bf16[1024,256]{1,0:T(8,128)(2,1)} %slice.99), channel_id=1, source_target_pairs={{0,32},{32,0},{64,96},{96,64},{128,160},{160,128},{192,224},{224,1... | collective-permute-start | bytes 1572872 | tf_op jit(solution)/shard_map/ppermute | solution.py:11
  245.1 22.0 %all-to-all-start.9 = ((bf16[16,72,512]{2,1,0:T(8,128)(2,1)}), bf16[16,72,512]{2,1,0:T(8,128)(2,1)}, u32[]{:S(2)}, u32[]{:S(2)}) async-start(bf16[16,72,512]{2,1,0:T(8,128)(2,1)} %pad_maximum_fusion), calls=%async_computation.9 | async-start | bytes 2359296 | tf_op jit(solution)/shard_map/all_to_all | solution.py:25
  249.6 3.2 %copy-start.5 = (bf16[16,64,512]{2,1,0:T(8,128)(2,1)S(1)}, bf16[16,64,512]{2,1,0:T(8,128)(2,1)}, u32[]{:S(2)}) copy-start(bf16[16,64,512]{2,1,0:T(8,128)(2,1)} %copy-done.4) | copy-start | bytes 3145732
  249.6 3.2 %copy-start.14 = (bf16[2,192,512]{2,1,0:T(8,128)(2,1)S(1)}, bf16[2,192,512]{2,1,0:T(8,128)(2,1)}, u32[]{:S(2)}) copy-start(bf16[2,192,512]{2,1,0:T(8,128)(2,1)} %copy-done.13) | copy-start | bytes 1179652
  250.4 3.0 %copy-start.3 = (f32[384,1024]{1,0:T(8,128)S(1)}, f32[384,1024]{1,0:T(8,128)}, u32[]{:S(2)}) copy-start(f32[384,1024]{1,0:T(8,128)} %get-tuple-element.28) | copy-start | bytes 4718596
  250.5 4.6 %collective-permute-start.3 = (bf16[1024,256]{0,1:T(8,128)(2,1)S(1)}, bf16[1024,256]{0,1:T(8,128)(2,1)S(1)}, u32[]{:S(2)}, u32[]{:S(2)}) collective-permute-start(bf16[1024,256]{0,1:T(8,128)(2,1)S(1)} %slice.98), channel_id=1, source_target_pairs={{0,32},{32,0},{64,96},{96,64},{128,160},{160,128},{192,224},{224,1... | collective-permute-start | bytes 1572872 | tf_op jit(solution)/shard_map/ppermute | solution.py:11
  (12 other events, 21.2 us)
Sparse Core Ops, SparseCore 0:
  107.7 36.2 all-gather.1
  161.0 71.0 reduce-scatter.1

commit v2 on v1

--- a/solution.py
+++ b/solution.py
@@ -19,6 +19,10 @@
 def ring_groups():
     half = lax.axis_size("feat") // FAR
     return [[far * half + 2 * step + bit for step in range(half // 2)] for far in range(FAR) for bit in range(2)]
+
+
+def chip_groups():
+    return [list(range(core, lax.axis_size("dom"), 2)) for core in range(2)]
 
 
 def exchange(value, axis, groups=None):
@@ -71,8 +75,17 @@
     other_u = partner_swap(expert_u)
     full_v = jnp.concatenate([expert_v, other_v], 1)
     full_u = jnp.concatenate([expert_u, other_u], 1)
-    whole_sv = lax.all_gather(shared_v, "dom", axis=0, tiled=True)
-    whole_su = gathered(shared_u, "dom", None, members)
+    lines = shared_u.shape[0]
+    own_maps = gathered(jnp.concatenate([shared_u, shared_v], 0), "dom", chip_groups(), members // 2)
+    own_maps = own_maps.reshape(members // 2, 2, lines, rank)
+    is_first = lax.axis_index("dom") % 2 == 0
+
+    def whole(own):
+        other = partner_swap(own)
+        pair = [jnp.where(is_first, own, other), jnp.where(is_first, other, own)]
+        return jnp.stack(pair, 1).reshape(width, rank)
+
+    whole_su, whole_sv = whole(own_maps[:, 0]), whole(own_maps[:, 1])
     live_rows = (domain_ids == domain)[:, None]
     masked = jnp.where(live_rows, cotangent, jnp.zeros_like(cotangent))
     masked_wide = masked.astype(jnp.float32)

time: 278 us -> 243 us (0.87)
  waiting for transfers between devices: 63 us -> 29.1 us
  starting transfers between devices: 45.8 us -> 57.9 us
  blocking collectives: 108 us -> 101 us
  matrix products: 17.3 us -> 12.4 us
    all_gather x1 -> x0, waiting for transfers between devices: 28.9 us -> none  [local(): whole_sv = lax.all_gather(shared_v, 'dom', axis=0, tiled=True)]
    all_to_all x5, waiting for transfers between devices: 31 us -> 21.2 us  [exchange(): lax.all_to_all(value, axis, 0, 0, axis_index_groups=groups, tiled=True)]
    ppermute x4 -> x6, starting transfers between devices: 24.4 us -> 32.3 us  [partner_swap(): return lax.ppermute(value, 'dom', pairs)]
    all_to_all x5, blocking collectives: 108 us -> 101 us  [exchange(): lax.all_to_all(value, axis, 0, 0, axis_index_groups=groups, tiled=True)]
    reduce_scatter x1, waiting for transfers between devices: 0.01 us -> 4.66 us  [local(): sum_sv = lax.psum_scatter(term_sv, 'dom', scatter_dimension=0, tiled=True)]
    all_to_all x5, starting transfers between devices: 21.4 us -> 25.7 us  [exchange(): lax.all_to_all(value, axis, 0, 0, axis_index_groups=groups, tiled=True)]
    unnamed x53 -> x55, local copies, waits for them, and re-layouts: 7.27 us -> 7.23 us
  transfers between devices with their start and end apart: 11 -> 12, of which waited for: 6 -> 6; matrix products, arithmetic and copies ran while one was open for 9% -> 8% of each run, Pallas kernels for 0% -> 0%
where the time goes in v2:
time: 243 us; the launch traced here: 242 us
  blocking collectives  101 us (42%)
  starting transfers between devices  57.9 us (24%)
  waiting for transfers between devices  29.1 us (12%)
  local copies, waits for them, and re-layouts  17.8 us (7%)
  between operations  14.7 us (6%)
  matrix products  12.4 us (5%)
  other arithmetic  8.8 us (4%)
    all_to_all x5, blocking collectives, exchange(): lax.all_to_all(value, axis, 0, 0, axis_index_groups=groups, tiled=True)  101 us
    ppermute x6, starting transfers between devices, partner_swap(): return lax.ppermute(value, 'dom', pairs)  32.3 us
    all_to_all x5, starting transfers between devices, exchange(): lax.all_to_all(value, axis, 0, 0, axis_index_groups=groups, tiled=True)  25.7 us
    all_to_all x5, waiting for transfers between devices, exchange(): lax.all_to_all(value, axis, 0, 0, axis_index_groups=groups, tiled=True)  21.2 us
    unnamed x55, local copies, waits for them, and re-layouts  7.23 us
    dot_general x4, matrix products, transposed_dot(): lax.dot_general(left_side, right_side, (((0,), (0,)), ((), ())), preferre...  5.41 us
  transfers between devices with their start and end apart: 12, of which 6 were waited for; matrix products, arithmetic and copies ran while one was open for 8% of the time, Pallas kernels for 0%

profile of v2, /device:TPU:1, one launch (start us, length us, event | category | flops | bytes accessed | tf_op | source)
XLA Modules:
  0.0 241.8 jit_solution(5904376305257976619)
XLA Ops:
  9.2 5.9 %all-to-all-start = ((bf16[8,128,512]{2,1,0:T(8,128)(2,1)}), bf16[8,128,512]{2,1,0:T(8,128)(2,1)S(1)}, u32[]{:S(2)}, u32[]{:S(2)}) async-start(bf16[8,128,512]{2,1,0:T(8,128)(2,1)} %broadcast_in_dim.30), calls=%async_computation | async-start | bytes 2097152 | tf_op jit(solution)/shard_map/all_to_all | solution.py:29
  15.1 6.4 %collective-permute-start = (bf16[1024,256]{1,0:T(8,128)(2,1)}, bf16[1024,256]{1,0:T(8,128)(2,1)}, u32[]{:S(2)}, u32[]{:S(2)}) collective-permute-start(bf16[1024,256]{1,0:T(8,128)(2,1)} %param.12), channel_id=1, source_target_pairs={{0,32},{32,0},{64,96},{96,64},{128,160},{160,128},{192,224},{224,1... | collective-permute-start | bytes 1572872 | tf_op jit(solution)/shard_map/ppermute | solution.py:11
  22.0 4.2 %all-to-all-done = bf16[8,128,512]{2,1,0:T(8,128)(2,1)S(1)} async-done(((bf16[8,128,512]{2,1,0:T(8,128)(2,1)}), bf16[8,128,512]{2,1,0:T(8,128)(2,1)S(1)}, u32[]{:S(2)}, u32[]{:S(2)}) %all-to-all-start) | async-done | bytes 1048608 | tf_op jit(solution)/shard_map/all_to_all | solution.py:29
  26.3 7.6 %collective-permute-start.3 = (bf16[8,64,512]{2,1,0:T(8,128)(2,1)S(1)}, bf16[8,64,512]{2,1,0:T(8,128)(2,1)S(1)}, u32[]{:S(2)}, u32[]{:S(2)}) collective-permute-start(bf16[8,64,512]{2,1,0:T(8,128)(2,1)S(1)} %get-tuple-element.34), channel_id=1, source_target_pairs={{0,32},{32,0},{64,96},{96,64},{128,160},{160,128},{192,224},{224,1... | collective-permute-start | bytes 1572872 | tf_op jit(solution)/shard_map/ppermute | solution.py:11
  33.9 1.9 collective-permute-start.1
  41.0 16.3 %all_to_all.71 = bf16[4,192,512]{2,1,0:T(8,128)(2,1)S(1)} all-to-all(bf16[4,192,512]{2,1,0:T(8,128)(2,1)S(1)} %bitcast.79), channel_id=1, replica_groups={{0,1,16,17},{2,3,18,19},{4,5,20,21},{6,7,22,23},{8,9,24,25},{10,11,26,2..., dimensions={0} | all-to-all | bytes 1572864 | tf_op jit(solution)/shard_map/all_to_all | solution.py:29
  57.4 28.1 %all_to_all.72 = bf16[8,24,512]{2,1,0:T(8,128)(2,1)S(1)} all-to-all(bf16[8,24,512]{2,1,0:T(8,128)(2,1)S(1)} %bitcast.83), channel_id=1, replica_groups={{0,2,4,6,8,10,12,14},{1,3,5,7,9,11,13,15},{16,18,20,22,24,26,28,30},{17..., dimensions={0} | all-to-all | bytes 393216 | tf_op jit(solution)/shard_map/all_to_all | solution.py:29
  85.6 18.7 %all_to_all.73 = bf16[8,24,512]{2,1,0:T(8,128)(2,1)S(1)} all-to-all(bf16[8,24,512]{2,1,0:T(8,128)(2,1)S(1)} %broadcast_in_dim.56), channel_id=1, replica_groups={{0,2,4,6,8,10,12,14},{1,3,5,7,9,11,13,15},{16,18,20,22,24,26,28,30},{17..., dimensions={0} | all-to-all | bytes 393216 | tf_op jit(solution)/shard_map/all_to_all | solution.py:29
  105.2 4.2 %all-to-all-start.4 = ((bf16[4,192,512]{2,1,0:T(8,128)(2,1)}), bf16[4,192,512]{2,1,0:T(8,128)(2,1)}, u32[]{:S(2)}, u32[]{:S(2)}) async-start(bf16[4,192,512]{2,1,0:T(8,128)(2,1)} %broadcast_in_dim.58), calls=%async_computation.4 | async-start | bytes 1572864 | tf_op jit(solution)/shard_map/all_to_all | solution.py:29
  109.4 7.8 %collective-permute-start.2 = (bf16[1024,256]{1,0:T(8,128)(2,1)S(1)}, bf16[1024,256]{1,0:T(8,128)(2,1)S(1)}, u32[]{:S(2)}, u32[]{:S(2)}) collective-permute-start(bf16[1024,256]{1,0:T(8,128)(2,1)S(1)} %copy-done.23), channel_id=1, source_target_pairs={{0,32},{32,0},{64,96},{96,64},{128,160},{160,128},{192,224},{224,1... | collective-permute-start | bytes 1572872 | tf_op jit(solution)/shard_map/ppermute | solution.py:11
  123.1 1.9 convert_reduce_fusion.2
  126.5 5.4 %all-to-all-start.5 = ((bf16[4,192,512]{2,1,0:T(8,128)(2,1)}), bf16[4,192,512]{2,1,0:T(8,128)(2,1)S(1)}, u32[]{:S(2)}, u32[]{:S(2)}) async-start(bf16[4,192,512]{2,1,0:T(8,128)(2,1)} %bitcast.78), calls=%async_computation.5 | async-start | bytes 1572864 | tf_op jit(solution)/shard_map/all_to_all | solution.py:29
  131.9 2.1 fusion.11
  134.0 7.4 %all-to-all-done.5 = bf16[4,192,512]{2,1,0:T(8,128)(2,1)S(1)} async-done(((bf16[4,192,512]{2,1,0:T(8,128)(2,1)}), bf16[4,192,512]{2,1,0:T(8,128)(2,1)S(1)}, u32[]{:S(2)}, u32[]{:S(2)}) %all-to-all-start.5) | async-done | bytes 786464 | tf_op jit(solution)/shard_map/all_to_all | solution.py:29
  141.6 19.5 %all_to_all.74 = bf16[8,24,512]{2,1,0:T(8,128)(2,1)S(1)} all-to-all(bf16[8,24,512]{2,1,0:T(8,128)(2,1)S(1)} %bitcast.84), channel_id=1, replica_groups={{0,2,4,6,8,10,12,14},{1,3,5,7,9,11,13,15},{16,18,20,22,24,26,28,30},{17..., dimensions={0} | all-to-all | bytes 393216 | tf_op jit(solution)/shard_map/all_to_all | solution.py:29
  162.5 18.5 %all_to_all.75 = bf16[8,24,512]{2,1,0:T(8,128)(2,1)S(1)} all-to-all(bf16[8,24,512]{2,1,0:T(8,128)(2,1)S(1)} %broadcast_in_dim.59), channel_id=1, replica_groups={{0,2,4,6,8,10,12,14},{1,3,5,7,9,11,13,15},{16,18,20,22,24,26,28,30},{17..., dimensions={0} | all-to-all | bytes 393216 | tf_op jit(solution)/shard_map/all_to_all | solution.py:29
  182.0 4.2 %all-to-all-start.8 = ((bf16[4,192,512]{2,1,0:T(8,128)(2,1)}), bf16[4,192,512]{2,1,0:T(8,128)(2,1)}, u32[]{:S(2)}, u32[]{:S(2)}) async-start(bf16[4,192,512]{2,1,0:T(8,128)(2,1)} %broadcast_in_dim.61), calls=%async_computation.8 | async-start | bytes 1572864 | tf_op jit(solution)/shard_map/all_to_all | solution.py:29
  189.1 6.3 %collective-permute-start.4 = (bf16[1024,256]{1,0:T(8,128)(2,1)}, bf16[1024,256]{1,0:T(8,128)(2,1)}, u32[]{:S(2)}, u32[]{:S(2)}) collective-permute-start(bf16[1024,256]{1,0:T(8,128)(2,1)} %slice.119), channel_id=1, source_target_pairs={{0,32},{32,0},{64,96},{96,64},{128,160},{160,128},{192,224},{224,1... | collective-permute-start | bytes 1572872 | tf_op jit(solution)/shard_map/ppermute | solution.py:11
  197.3 2.3 fusion.9
  199.6 4.7 %reduce-scatter.2.cloned.1.call-done = f32[64,512]{1,0:T(8,128)} async-done(((f32[1024,512]{1,0:T(8,128)}), f32[64,512]{1,0:T(8,128)}) %reduce-scatter.2.cloned.1.call-update) | async-done | bytes 131088 | tf_op jit(solution)/shard_map/reduce_scatter | solution.py:108
  205.8 1.9 fusion.16
  210.3 6.0 %all-to-all-start.9 = ((bf16[16,72,512]{2,1,0:T(8,128)(2,1)}), bf16[16,72,512]{2,1,0:T(8,128)(2,1)S(1)}, u32[]{:S(2)}, u32[]{:S(2)}) async-start(bf16[16,72,512]{2,1,0:T(8,128)(2,1)} %pad_maximum_fusion), calls=%async_computation.9 | async-start | bytes 2359296 | tf_op jit(solution)/shard_map/all_to_all | solution.py:29
  218.2 2.3 collective-permute-start.5
  224.0 9.5 %all-to-all-done.9 = bf16[16,72,512]{2,1,0:T(8,128)(2,1)S(1)} async-done(((bf16[16,72,512]{2,1,0:T(8,128)(2,1)}), bf16[16,72,512]{2,1,0:T(8,128)(2,1)S(1)}, u32[]{:S(2)}, u32[]{:S(2)}) %all-to-all-start.9) | async-done | bytes 1179680 | tf_op jit(solution)/shard_map/all_to_all | solution.py:29
  (112 shorter events, 34.1 us)
Async XLA Ops:
  8.1 13.5 %copy-start.25 = (s32[384]{0:T(512)S(1)}, s32[384]{0:T(512)}, u32[]{:S(2)}) copy-start(s32[384]{0:T(512)} %param.10) | copy-start | bytes 4612
  8.1 13.5 %copy-start = (bf16[384,1024]{1,0:T(8,128)(2,1)S(1)}, bf16[384,1024]{1,0:T(8,128)(2,1)}, u32[]{:S(2)}) copy-start(bf16[384,1024]{1,0:T(8,128)(2,1)} %param.8) | copy-start | bytes 2359300
  8.1 13.5 %copy-start.1 = (bf16[384,1024]{1,0:T(8,128)(2,1)S(1)}, bf16[384,1024]{1,0:T(8,128)(2,1)}, u32[]{:S(2)}) copy-start(bf16[384,1024]{1,0:T(8,128)(2,1)} %param.9) | copy-start | bytes 2359300
  9.2 17.0 %all-to-all-start = ((bf16[8,128,512]{2,1,0:T(8,128)(2,1)}), bf16[8,128,512]{2,1,0:T(8,128)(2,1)S(1)}, u32[]{:S(2)}, u32[]{:S(2)}) async-start(bf16[8,128,512]{2,1,0:T(8,128)(2,1)} %broadcast_in_dim.30), calls=%async_computation | async-start | bytes 2097152 | tf_op jit(solution)/shard_map/all_to_all | solution.py:29
  15.1 21.8 %collective-permute-start = (bf16[1024,256]{1,0:T(8,128)(2,1)}, bf16[1024,256]{1,0:T(8,128)(2,1)}, u32[]{:S(2)}, u32[]{:S(2)}) collective-permute-start(bf16[1024,256]{1,0:T(8,128)(2,1)} %param.12), channel_id=1, source_target_pairs={{0,32},{32,0},{64,96},{96,64},{128,160},{160,128},{192,224},{224,1... | collective-permute-start | bytes 1572872 | tf_op jit(solution)/shard_map/ppermute | solution.py:11
  22.0 18.1 %copy-start.21 = (bf16[384,1024]{1,0:T(8,128)(2,1)}, bf16[384,1024]{1,0:T(8,128)(2,1)S(1)}, u32[]{:S(2)}) copy-start(bf16[384,1024]{1,0:T(8,128)(2,1)S(1)} %get-tuple-element.27) | copy-start | bytes 2359300
  26.3 13.2 %collective-permute-start.3 = (bf16[8,64,512]{2,1,0:T(8,128)(2,1)S(1)}, bf16[8,64,512]{2,1,0:T(8,128)(2,1)S(1)}, u32[]{:S(2)}, u32[]{:S(2)}) collective-permute-start(bf16[8,64,512]{2,1,0:T(8,128)(2,1)S(1)} %get-tuple-element.34), channel_id=1, source_target_pairs={{0,32},{32,0},{64,96},{96,64},{128,160},{160,128},{192,224},{224,1... | collective-permute-start | bytes 1572872 | tf_op jit(solution)/shard_map/ppermute | solution.py:11
  33.9 5.7 %collective-permute-start.1 = (bf16[8,64,512]{2,1,0:T(8,128)(2,1)S(1)}, bf16[8,64,512]{2,1,0:T(8,128)(2,1)S(1)}, u32[]{:S(2)}, u32[]{:S(2)}) collective-permute-start(bf16[8,64,512]{2,1,0:T(8,128)(2,1)S(1)} %get-tuple-element.35), channel_id=1, source_target_pairs={{0,32},{32,0},{64,96},{96,64},{128,160},{160,128},{192,224},{224,1... | collective-permute-start | bytes 1572872 | tf_op jit(solution)/shard_map/ppermute | solution.py:11
  85.5 23.8 %copy-start.23 = (bf16[1024,256]{1,0:T(8,128)(2,1)S(1)}, bf16[1024,256]{1,0:T(8,128)(2,1)}, u32[]{:S(2)}) copy-start(bf16[1024,256]{1,0:T(8,128)(2,1)} %param.11) | copy-start | bytes 1572868
  104.3 13.1 %copy-start.24 = (f32[2,1024]{1,0:T(2,128)S(1)}, f32[2,1024]{1,0:T(2,128)}, u32[]{:S(2)}) copy-start(f32[2,1024]{1,0:T(2,128)} %param.15) | copy-start | bytes 24580
  105.2 14.7 %all-to-all-start.4 = ((bf16[4,192,512]{2,1,0:T(8,128)(2,1)}), bf16[4,192,512]{2,1,0:T(8,128)(2,1)}, u32[]{:S(2)}, u32[]{:S(2)}) async-start(bf16[4,192,512]{2,1,0:T(8,128)(2,1)} %broadcast_in_dim.58), calls=%async_computation.4 | async-start | bytes 1572864 | tf_op jit(solution)/shard_map/all_to_all | solution.py:29
  109.4 9.4 %collective-permute-start.2 = (bf16[1024,256]{1,0:T(8,128)(2,1)S(1)}, bf16[1024,256]{1,0:T(8,128)(2,1)S(1)}, u32[]{:S(2)}, u32[]{:S(2)}) collective-permute-start(bf16[1024,256]{1,0:T(8,128)(2,1)S(1)} %copy-done.23), channel_id=1, source_target_pairs={{0,32},{32,0},{64,96},{96,64},{128,160},{160,128},{192,224},{224,1... | collective-permute-start | bytes 1572872 | tf_op jit(solution)/shard_map/ppermute | solution.py:11
  125.6 6.3 %copy-start.10 = (bf16[2,192,512]{2,1,0:T(8,128)(2,1)S(1)}, bf16[2,192,512]{2,1,0:T(8,128)(2,1)}, u32[]{:S(2)}) copy-start(bf16[2,192,512]{2,1,0:T(8,128)(2,1)} %copy-done.9) | copy-start | bytes 1179652
  126.5 14.9 %all-to-all-start.5 = ((bf16[4,192,512]{2,1,0:T(8,128)(2,1)}), bf16[4,192,512]{2,1,0:T(8,128)(2,1)S(1)}, u32[]{:S(2)}, u32[]{:S(2)}) async-start(bf16[4,192,512]{2,1,0:T(8,128)(2,1)} %bitcast.78), calls=%async_computation.5 | async-start | bytes 1572864 | tf_op jit(solution)/shard_map/all_to_all | solution.py:29
  131.9 72.3 %reduce-scatter.2.cloned.1.call-start = ((), (), s32[]{:S(2)}) async-start(), calls=%async_computation.11 | async-start | bytes 2228224 | tf_op jit(solution)/shard_map/reduce_scatter | solution.py:108
  161.7 24.5 %copy-start.12 = (bf16[2,192,512]{2,1,0:T(8,128)(2,1)S(1)}, bf16[2,192,512]{2,1,0:T(8,128)(2,1)}, u32[]{:S(2)}) copy-start(bf16[2,192,512]{2,1,0:T(8,128)(2,1)} %copy-done.11) | copy-start | bytes 1179652
  161.7 24.5 %copy-start.14 = (bf16[384,1024]{1,0:T(8,128)(2,1)S(1)}, bf16[384,1024]{1,0:T(8,128)(2,1)}, u32[]{:S(2)}) copy-start(bf16[384,1024]{1,0:T(8,128)(2,1)} %copy-done.13) | copy-start | bytes 2359300
  182.0 23.8 %all-to-all-start.8 = ((bf16[4,192,512]{2,1,0:T(8,128)(2,1)}), bf16[4,192,512]{2,1,0:T(8,128)(2,1)}, u32[]{:S(2)}, u32[]{:S(2)}) async-start(bf16[4,192,512]{2,1,0:T(8,128)(2,1)} %broadcast_in_dim.61), calls=%async_computation.8 | async-start | bytes 1572864 | tf_op jit(solution)/shard_map/all_to_all | solution.py:29
  189.1 8.2 %collective-permute-start.4 = (bf16[1024,256]{1,0:T(8,128)(2,1)}, bf16[1024,256]{1,0:T(8,128)(2,1)}, u32[]{:S(2)}, u32[]{:S(2)}) collective-permute-start(bf16[1024,256]{1,0:T(8,128)(2,1)} %slice.119), channel_id=1, source_target_pairs={{0,32},{32,0},{64,96},{96,64},{128,160},{160,128},{192,224},{224,1... | collective-permute-start | bytes 1572872 | tf_op jit(solution)/shard_map/ppermute | solution.py:11
  195.5 12.9 %copy-start.22 = (bf16[384,1024]{1,0:T(8,128)(2,1)S(1)}, bf16[384,1024]{1,0:T(8,128)(2,1)}, u32[]{:S(2)}) copy-start(bf16[384,1024]{1,0:T(8,128)(2,1)} %copy-done.21) | copy-start | bytes 2359300
  210.3 23.2 %all-to-all-start.9 = ((bf16[16,72,512]{2,1,0:T(8,128)(2,1)}), bf16[16,72,512]{2,1,0:T(8,128)(2,1)S(1)}, u32[]{:S(2)}, u32[]{:S(2)}) async-start(bf16[16,72,512]{2,1,0:T(8,128)(2,1)} %pad_maximum_fusion), calls=%async_computation.9 | async-start | bytes 2359296 | tf_op jit(solution)/shard_map/all_to_all | solution.py:29
  216.3 4.3 %copy-start.7 = (bf16[8,2,64,512]{3,2,1,0:T(8,128)(2,1)S(1)}, bf16[8,2,64,512]{3,2,1,0:T(8,128)(2,1)}, u32[]{:S(2)}) copy-start(bf16[8,2,64,512]{3,2,1,0:T(8,128)(2,1)} %copy-done.6) | copy-start | bytes 3145732
  216.3 4.3 %copy-start.20 = (bf16[2,192,512]{2,1,0:T(8,128)(2,1)S(1)}, bf16[2,192,512]{2,1,0:T(8,128)(2,1)}, u32[]{:S(2)}) copy-start(bf16[2,192,512]{2,1,0:T(8,128)(2,1)} %copy-done.19) | copy-start | bytes 1179652
  218.2 4.6 %collective-permute-start.5 = (bf16[1024,256]{0,1:T(8,128)(2,1)S(1)}, bf16[1024,256]{0,1:T(8,128)(2,1)S(1)}, u32[]{:S(2)}, u32[]{:S(2)}) collective-permute-start(bf16[1024,256]{0,1:T(8,128)(2,1)S(1)} %slice.118), channel_id=1, source_target_pairs={{0,32},{32,0},{64,96},{96,64},{128,160},{160,128},{192,224},{224,1... | collective-permute-start | bytes 1572872 | tf_op jit(solution)/shard_map/ppermute | solution.py:11
  (14 other events, 23.9 us)
Sparse Core Ops, SparseCore 0:
  135.5 68.6 reduce-scatter.1

commit v3 on v1

v3 whole, which is shorter than its diff:
```python
import jax
import jax.numpy as jnp
from jax import lax
from jax.sharding import PartitionSpec as P

FAR = 2


def core_swap(value):
    pairs = [(source, source ^ 1) for source in range(lax.axis_size("dom"))]
    return lax.ppermute(value, "dom", pairs)


def far_swap(value):
    count = lax.axis_size("feat")
    return lax.ppermute(value, "feat", [(source, (source + count // FAR) % count) for source in range(count)])


def line_groups():
    length = lax.axis_size("feat") // FAR
    return [list(range(far * length, (far + 1) * length)) for far in range(FAR)]


def chip_groups():
    return [list(range(core, lax.axis_size("dom"), 2)) for core in range(2)]


def exchange(value, axis, groups):
    return lax.all_to_all(value, axis, 0, 0, axis_index_groups=groups, tiled=True)


def gathered(value, axis, groups):
    members = len(groups[0])
    repeated = jnp.broadcast_to(value[None], (members, *value.shape))
    return exchange(repeated.reshape(members * value.shape[0], value.shape[1]), axis, groups)


def line_sum(value):
    groups = line_groups()
    members = len(groups[0])
    pieces = exchange(value, "feat", groups).reshape(members, -1, value.shape[1])
    part = jnp.sum(pieces.astype(jnp.float32), axis=0).astype(jnp.bfloat16)
    return gathered(part, "feat", groups)


def dot(left_side, right_side):
    return jnp.dot(left_side, right_side, preferred_element_type=jnp.float32)


def transposed_dot(left_side, right_side):
    return lax.dot_general(
        left_side, right_side, (((0,), (0,)), ((), ())), preferred_element_type=jnp.float32
    )


def cross_dot(left_side, right_side):
    return lax.dot_general(
        left_side, right_side, (((1,), (1,)), ((), ())), preferred_element_type=jnp.float32
    )


def local(x0, cotangent, domain_ids, expert_u, expert_v, shared_u, shared_v, bias):
    low = jnp.bfloat16
    wide = jnp.float32
    rows, width = x0.shape
    half_rows = rows // 2
    half_rank = expert_u.shape[1]
    rank = 2 * half_rank
    chips = lax.axis_size("dom") // 2
    lines = shared_u.shape[0]
    domain = lax.axis_index("dom") // 2
    core = lax.axis_index("dom") % 2
    far = lax.axis_index("feat") // (lax.axis_size("feat") // FAR)

    def halves(value):
        return [
            lax.dynamic_slice_in_dim(value, place * half_rows, half_rows, 0) for place in (far, 1 - far)
        ]

    own_maps = gathered(jnp.concatenate([shared_u, shared_v], 0), "dom", chip_groups())
    own_maps = own_maps.reshape(chips, 2, lines, rank)
    other_v = core_swap(expert_v)
    other_u = core_swap(expert_u)
    full_v = jnp.concatenate([expert_v, other_v], 1)
    full_u = jnp.concatenate([expert_u, other_u], 1)

    def whole(own, other):
        pair = [jnp.where(core == 0, own, other), jnp.where(core == 0, other, own)]
        return jnp.stack(pair, 1).reshape(width, rank)

    x_halves = halves(x0)
    inputs = [x.astype(wide) for x in x_halves]
    live = [(ids == domain)[:, None] for ids in halves(domain_ids)]
    masked = [jnp.where(on, cot, jnp.zeros_like(cot)).astype(wide) for on, cot in zip(live, halves(cotangent))]
    second_adj = [(m * x).astype(low) for m, x in zip(masked, inputs)]

    first_away = far_swap(dot(x_halves[1], full_v).astype(low))
    first_half = dot(x_halves[0], full_v) + first_away.astype(wide)
    whole_su = whole(own_maps[:, 0], core_swap(own_maps[:, 0]))
    back_away = far_swap(dot(second_adj[1], whole_su).astype(low))
    back_half = dot(second_adj[0], whole_su) + back_away.astype(wide)
    own_sums = jnp.concatenate([first_half.astype(low), back_half.astype(low)], 0)
    own_sv, own_sums = lax.optimization_barrier((own_maps[:, 1], own_sums))
    whole_sv = whole(own_sv, core_swap(own_sv))
    own_sums = line_sum(own_sums)
    sums = [own_sums, far_swap(own_sums)]
    first_rank = [s[:half_rows] for s in sums]
    back_two = [s[half_rows:] for s in sums]

    def middle(i):
        first_gate = cross_dot(first_rank[i], full_u) + bias[0][None, :]
        layer_one = (inputs[i] * first_gate + inputs[i]).astype(low)
        layer_grad = masked[i] + cross_dot(back_two[i], whole_sv)
        first_adj = (layer_grad * inputs[i]).astype(low)
        parts = [dot(layer_one, whole_sv), dot(first_adj, full_u)]
        return first_gate, layer_one, layer_grad, first_adj, parts

    first_gate, layer_one, layer_grad, first_adj, parts = zip(middle(0), middle(1))
    away = far_swap(jnp.concatenate([p.astype(low) for p in parts[1]], 0)).astype(wide)
    own_sums = jnp.concatenate(
        [
            (parts[0][0] + away[:half_rows]).astype(low),
            (parts[0][1] + away[half_rows:]).astype(low),
        ],
        0,
    )
    own_sums = line_sum(own_sums)

    def row_sum(left_side, right_side):
        return sum(transposed_dot(a, b) for a, b in zip(left_side, right_side))

    def with_partner(partial):
        peer = core_swap(partial[:, half_rank:].astype(low))
        return (partial[:, :half_rank] + peer.astype(wide)).astype(low)

    def chip_part(term):
        blocks = term.reshape(chips, 2, lines, rank)
        keep, give = [
            lax.dynamic_index_in_dim(blocks, place, 1, keepdims=False) for place in (core, 1 - core)
        ]
        return (keep + core_swap(give.astype(low)).astype(wide)).astype(low)

    grad_eu = with_partner(row_sum(first_adj, first_rank))
    part_sv = chip_part(row_sum(layer_one, back_two))
    bias_terms = jnp.stack(
        [sum(jnp.sum(a.astype(wide), axis=0) for a in adj) for adj in (first_adj, second_adj)]
    )
    bias_terms = bias_terms + core_swap(bias_terms)
    bias_high = bias_terms.astype(low)
    bias_rest = (bias_terms - bias_high.astype(wide)).astype(low)
    bias_lines = jnp.stack([bias_high, bias_rest]).reshape(4 * width // rank, rank)
    bias_lines = jnp.broadcast_to(bias_lines[None], (chips, *bias_lines.shape))

    sums = [own_sums, far_swap(own_sums)]
    second_rank = [s[:half_rows] for s in sums]
    back_one = [s[half_rows:] for s in sums]
    part_su = chip_part(row_sum(second_adj, second_rank))
    sent = jnp.concatenate([part_su, part_sv, bias_lines], 1)
    taken = exchange(sent.reshape(-1, rank), "dom", chip_groups()).reshape(sent.shape)
    taken = jnp.sum(taken.astype(wide), axis=0)
    bias_sum = taken[2 * lines :].reshape(2, 2, width)
    grad_ev = with_partner(row_sum(x_halves, back_one))
    grad_inputs = jnp.zeros((rows, width), low)
    for i, place in enumerate((far, 1 - far)):
        second_gate = cross_dot(second_rank[i], whole_su) + bias[1][None, :]
        grad_half = (
            masked[i] * second_gate
            + layer_grad[i] * first_gate[i]
            + layer_grad[i]
            + cross_dot(back_one[i], full_v)
        ).astype(low)
        grad_inputs = lax.dynamic_update_slice_in_dim(grad_inputs, grad_half, place * half_rows, 0)
    return (
        grad_inputs,
        grad_eu,
        grad_ev,
        taken[:lines].astype(low),
        taken[lines : 2 * lines].astype(low),
        bias_sum[0] + bias_sum[1],
    )


def solution(mesh):
    placed = (
        P("dom", "feat"),
        P("dom", "feat"),
        P("dom"),
        P("feat", "dom"),
        P("feat", "dom"),
        P(("feat", "dom"), None),
        P(("feat", "dom"), None),
        P(None, "feat"),
    )
    return jax.shard_map(
        local,
        mesh=mesh,
        in_specs=placed,
        out_specs=(
            P("dom", "feat"),
            P("feat", "dom"),
            P("feat", "dom"),
            P(("feat", "dom"), None),
            P(("feat", "dom"), None),
            P(None, "feat"),
        ),
        check_vma=False,
    )
```

time: 278 us -> 251 us (0.903)
  blocking collectives: 108 us -> 32.4 us
  starting transfers between devices: 45.8 us -> 110 us
  between operations: 14.5 us -> 1.83 us
  waiting for transfers between devices: 63 us -> 57.7 us
  other arithmetic: 10 us -> 13.2 us
    all_to_all x5 -> x1, blocking collectives: 108 us -> 32.4 us  [exchange(): lax.all_to_all(value, axis, 0, 0, axis_index_groups=groups, tiled=True)]
    ppermute x4 -> x14, starting transfers between devices: 24.4 us -> 57.4 us  [the longest x9 43 us: core_swap(): return lax.ppermute(value, 'dom', pairs)]
    all_to_all x5, starting transfers between devices: 21.4 us -> 52.6 us  [exchange(): lax.all_to_all(value, axis, 0, 0, axis_index_groups=groups, tiled=True)]
    all_gather x1 -> x0, waiting for transfers between devices: 28.9 us -> none  [local(): whole_sv = lax.all_gather(shared_v, 'dom', axis=0, tiled=True)]
    ppermute x4 -> x14, waiting for transfers between devices: 2.43 us -> 23.9 us  [the longest x5 23.9 us: far_swap(): lax.ppermute(value, 'feat', [(source, (source + count // FAR) % count) fo...]
    dot_general x4 -> x8, matrix products: 5.43 us -> 8.75 us  [transposed_dot(): lax.dot_general(left_side, right_side, (((0,), (0,)), ((), ())), preferre...]
    all_to_all x5, waiting for transfers between devices: 31 us -> 33.8 us  [exchange(): lax.all_to_all(value, axis, 0, 0, axis_index_groups=groups, tiled=True)]
    unnamed x53 -> x96, local copies, waits for them, and re-layouts: 7.27 us -> 5.98 us
  transfers between devices with their start and end apart: 11 -> 19, of which waited for: 6 -> 10; matrix products, arithmetic and copies ran while one was open for 9% -> 13% of each run, Pallas kernels for 0% -> 0%
where the time goes in v3:
time: 251 us; the launch traced here: 250 us
  starting transfers between devices  110 us (44%)
  waiting for transfers between devices  57.7 us (23%)
  blocking collectives  32.4 us (13%)
  matrix products  18.7 us (7%)
  local copies, waits for them, and re-layouts  16.1 us (6%)
  other arithmetic  13.2 us (5%)
    all_to_all x5, starting transfers between devices, exchange(): lax.all_to_all(value, axis, 0, 0, axis_index_groups=groups, tiled=True)  52.6 us
    ppermute x9, starting transfers between devices, core_swap(): return lax.ppermute(value, 'dom', pairs)  43 us
    all_to_all x5, waiting for transfers between devices, exchange(): lax.all_to_all(value, axis, 0, 0, axis_index_groups=groups, tiled=True)  33.8 us
    all_to_all x1, blocking collectives, exchange(): lax.all_to_all(value, axis, 0, 0, axis_index_groups=groups, tiled=True)  32.4 us
    ppermute x5, waiting for transfers between devices, far_swap(): lax.ppermute(value, 'feat', [(source, (source + count // FAR) % count) fo...  23.9 us
    ppermute x5, starting transfers between devices, far_swap(): lax.ppermute(value, 'feat', [(source, (source + count // FAR) % count) fo...  14.4 us
    dot_general x8, matrix products, transposed_dot(): lax.dot_general(left_side, right_side, (((0,), (0,)), ((), ())), preferre...  8.75 us
    dot_general x8, matrix products, cross_dot(): lax.dot_general(left_side, right_side, (((1,), (1,)), ((), ())), preferre...  6.95 us
  transfers between devices with their start and end apart: 19, of which 10 were waited for; matrix products, arithmetic and copies ran while one was open for 13% of the time, Pallas kernels for 0%

profile of v3, /device:TPU:1, one launch (start us, length us, event | category | flops | bytes accessed | tf_op | source)
XLA Modules:
  0.0 249.9 jit_solution(12016800607825981545)
XLA Ops:
  2.7 6.1 %all-to-all-start = ((bf16[8,128,512]{2,1,0:T(8,128)(2,1)}), bf16[8,128,512]{2,1,0:T(8,128)(2,1)S(1)}, u32[]{:S(2)}, u32[]{:S(2)}) async-start(bf16[8,128,512]{2,1,0:T(8,128)(2,1)} %broadcast_in_dim.45), calls=%async_computation | async-start | bytes 2097152 | tf_op jit(solution)/shard_map/all_to_all | solution.py:29
  8.7 6.4 %collective-permute-start = (bf16[1024,256]{1,0:T(8,128)(2,1)}, bf16[1024,256]{1,0:T(8,128)(2,1)}, u32[]{:S(2)}, u32[]{:S(2)}) collective-permute-start(bf16[1024,256]{1,0:T(8,128)(2,1)} %param.12), channel_id=1, source_target_pairs={{0,32},{32,0},{64,96},{96,64},{128,160},{160,128},{192,224},{224,1... | collective-permute-start | bytes 1572872 | tf_op jit(solution)/shard_map/ppermute | solution.py:11
  15.3 4.5 %all-to-all-done = bf16[8,128,512]{2,1,0:T(8,128)(2,1)S(1)} async-done(((bf16[8,128,512]{2,1,0:T(8,128)(2,1)}), bf16[8,128,512]{2,1,0:T(8,128)(2,1)S(1)}, u32[]{:S(2)}, u32[]{:S(2)}) %all-to-all-start) | async-done | bytes 1048608 | tf_op jit(solution)/shard_map/all_to_all | solution.py:29
  20.9 7.5 %collective-permute-start.2 = (bf16[8,64,512]{2,1,0:T(8,128)(2,1)}, bf16[8,64,512]{2,1,0:T(8,128)(2,1)}, u32[]{:S(2)}, u32[]{:S(2)}) collective-permute-start(bf16[8,64,512]{2,1,0:T(8,128)(2,1)} %get-tuple-element.24), channel_id=1, source_target_pairs={{0,32},{32,0},{64,96},{96,64},{128,160},{160,128},{192,224},{224,1... | collective-permute-start | bytes 1572872 | tf_op jit(solution)/shard_map/ppermute | solution.py:11
  31.7 4.3 %collective-permute-start.1 = (bf16[192,512]{1,0:T(8,128)(2,1)S(1)}, bf16[192,512]{1,0:T(8,128)(2,1)S(1)}, u32[]{:S(2)}, u32[]{:S(2)}) collective-permute-start(bf16[192,512]{1,0:T(8,128)(2,1)S(1)} %convolution_convert_fusion.3), channel_id=1, source_target_pairs={{0,16},{1,17},{2,18},{3,19},{4,20},{5,21},{6,22},{7,23},{8,24},{9,... | collective-permute-start | bytes 589832 | tf_op jit(solution)/shard_map/ppermute | solution.py:16
  42.1 5.3 %collective-permute-done.3 = bf16[192,512]{1,0:T(8,128)(2,1)S(1)} collective-permute-done((bf16[192,512]{1,0:T(8,128)(2,1)S(1)}, bf16[192,512]{1,0:T(8,128)(2,1)S(1)}, u32[]{:S(2)}, u32[]{:S(2)}) %collective-permute-start.3) | collective-permute-done | bytes 196640 | tf_op jit(solution)/shard_map/ppermute | solution.py:16
  47.8 32.4 %all_to_all.48 = bf16[16,24,512]{2,1,0:T(8,128)(2,1)S(1)} all-to-all(bf16[16,24,512]{2,1,0:T(8,128)(2,1)S(1)} %bitcast.115), channel_id=1, replica_groups={{0,1,2,3,4,5,6,7,8,9,10,11,12,13,14,15},{16,17,18,19,20,21,22,23,24,25,..., dimensions={0} | all-to-all | bytes 786432 | tf_op jit(solution)/shard_map/all_to_all | solution.py:29
  81.0 11.9 %all-to-all-start.2 = ((bf16[16,24,512]{2,1,0:T(8,128)(2,1)}), bf16[16,24,512]{2,1,0:T(8,128)(2,1)S(1)}, u32[]{:S(2)}, u32[]{:S(2)}) async-start(bf16[16,24,512]{2,1,0:T(8,128)(2,1)} %broadcast_in_dim.47), calls=%async_computation.2 | async-start | bytes 786432 | tf_op jit(solution)/shard_map/all_to_all | solution.py:29
  92.9 3.1 %collective-permute-start.4 = (bf16[1024,256]{1,0:T(8,128)(2,1)}, bf16[1024,256]{1,0:T(8,128)(2,1)S(1)}, u32[]{:S(2)}, u32[]{:S(2)}) collective-permute-start(bf16[1024,256]{1,0:T(8,128)(2,1)} %param.11), channel_id=1, source_target_pairs={{0,32},{32,0},{64,96},{96,64},{128,160},{160,128},{192,224},{224,1... | collective-permute-start | bytes 1572872 | tf_op jit(solution)/shard_map/ppermute | solution.py:11
  100.1 10.8 %all-to-all-done.2 = bf16[16,24,512]{2,1,0:T(8,128)(2,1)S(1)} async-done(((bf16[16,24,512]{2,1,0:T(8,128)(2,1)}), bf16[16,24,512]{2,1,0:T(8,128)(2,1)S(1)}, u32[]{:S(2)}, u32[]{:S(2)}) %all-to-all-start.2) | async-done | bytes 393248 | tf_op jit(solution)/shard_map/all_to_all | solution.py:29
  115.8 5.2 %collective-permute-done.6 = bf16[384,512]{1,0:T(8,128)(2,1)S(1)} collective-permute-done((bf16[384,512]{1,0:T(8,128)(2,1)S(1)}, bf16[384,512]{1,0:T(8,128)(2,1)S(1)}, u32[]{:S(2)}, u32[]{:S(2)}) %collective-permute-start.6) | collective-permute-done | bytes 393248 | tf_op jit(solution)/shard_map/ppermute | solution.py:16
  124.6 2.5 %collective-permute-start.7 = (bf16[384,512]{1,0:T(8,128)(2,1)S(1)}, bf16[384,512]{1,0:T(8,128)(2,1)S(1)}, u32[]{:S(2)}, u32[]{:S(2)}) collective-permute-start(bf16[384,512]{1,0:T(8,128)(2,1)S(1)} %pad_maximum_fusion.4), channel_id=1, source_target_pairs={{0,16},{1,17},{2,18},{3,19},{4,20},{5,21},{6,22},{7,23},{8,24},{9,... | collective-permute-start | bytes 1179656 | tf_op jit(solution)/shard_map/ppermute | solution.py:16
  127.1 7.5 %collective-permute-done.7 = bf16[384,512]{1,0:T(8,128)(2,1)S(1)} collective-permute-done((bf16[384,512]{1,0:T(8,128)(2,1)S(1)}, bf16[384,512]{1,0:T(8,128)(2,1)S(1)}, u32[]{:S(2)}, u32[]{:S(2)}) %collective-permute-start.7) | collective-permute-done | bytes 393248 | tf_op jit(solution)/shard_map/ppermute | solution.py:16
  136.3 16.8 %all-to-all-start.3 = ((bf16[16,24,512]{2,1,0:T(8,128)(2,1)}), bf16[16,24,512]{2,1,0:T(8,128)(2,1)S(1)}, u32[]{:S(2)}, u32[]{:S(2)}) async-start(bf16[16,24,512]{2,1,0:T(8,128)(2,1)} %bitcast.114), calls=%async_computation.3 | async-start | bytes 786432 | tf_op jit(solution)/shard_map/all_to_all | solution.py:29
  156.4 4.9 %collective-permute-start.12 = (bf16[8,64,512]{2,1,0:T(8,128)(2,1)}, bf16[8,64,512]{2,1,0:T(8,128)(2,1)}, u32[]{:S(2)}, u32[]{:S(2)}) collective-permute-start(bf16[8,64,512]{2,1,0:T(8,128)(2,1)} %fusion.24), channel_id=1, source_target_pairs={{0,32},{32,0},{64,96},{96,64},{128,160},{160,128},{192,224},{224,1... | collective-permute-start | bytes 1572872 | tf_op jit(solution)/shard_map/ppermute | solution.py:11
  163.8 4.6 %all-to-all-done.3 = bf16[16,24,512]{2,1,0:T(8,128)(2,1)S(1)} async-done(((bf16[16,24,512]{2,1,0:T(8,128)(2,1)}), bf16[16,24,512]{2,1,0:T(8,128)(2,1)S(1)}, u32[]{:S(2)}, u32[]{:S(2)}) %all-to-all-start.3) | async-done | bytes 393248 | tf_op jit(solution)/shard_map/all_to_all | solution.py:29
  169.3 13.6 %all-to-all-start.4 = ((bf16[16,24,512]{2,1,0:T(8,128)(2,1)}), bf16[16,24,512]{2,1,0:T(8,128)(2,1)}, u32[]{:S(2)}, u32[]{:S(2)}) async-start(bf16[16,24,512]{2,1,0:T(8,128)(2,1)} %broadcast_in_dim.48), calls=%async_computation.4 | async-start | bytes 786432 | tf_op jit(solution)/shard_map/all_to_all | solution.py:29
  185.6 3.8 %collective-permute-start.9 = (bf16[1024,256]{1,0:T(8,128)(2,1)}, bf16[1024,256]{1,0:T(8,128)(2,1)}, u32[]{:S(2)}, u32[]{:S(2)}) collective-permute-start(bf16[1024,256]{1,0:T(8,128)(2,1)} %slice.173), channel_id=1, source_target_pairs={{0,32},{32,0},{64,96},{96,64},{128,160},{160,128},{192,224},{224,1... | collective-permute-start | bytes 1572872 | tf_op jit(solution)/shard_map/ppermute | solution.py:11
  194.6 4.6 %all-to-all-done.4 = bf16[16,24,512]{2,1,0:T(8,128)(2,1)} async-done(((bf16[16,24,512]{2,1,0:T(8,128)(2,1)}), bf16[16,24,512]{2,1,0:T(8,128)(2,1)}, u32[]{:S(2)}, u32[]{:S(2)}) %all-to-all-start.4) | async-done | bytes 393248 | tf_op jit(solution)/shard_map/all_to_all | solution.py:29
  199.2 2.5 %collective-permute-start.8 = (bf16[384,512]{1,0:T(8,128)(2,1)}, bf16[384,512]{1,0:T(8,128)(2,1)S(1)}, u32[]{:S(2)}, u32[]{:S(2)}) collective-permute-start(bf16[384,512]{1,0:T(8,128)(2,1)} %bitcast.18), channel_id=1, source_target_pairs={{0,16},{1,17},{2,18},{3,19},{4,20},{5,21},{6,22},{7,23},{8,24},{9,... | collective-permute-start | bytes 1179656 | tf_op jit(solution)/shard_map/ppermute | solution.py:16
  204.9 4.5 %collective-permute-done.8 = bf16[384,512]{1,0:T(8,128)(2,1)S(1)} collective-permute-done((bf16[384,512]{1,0:T(8,128)(2,1)}, bf16[384,512]{1,0:T(8,128)(2,1)S(1)}, u32[]{:S(2)}, u32[]{:S(2)}) %collective-permute-start.8) | collective-permute-done | bytes 393248 | tf_op jit(solution)/shard_map/ppermute | solution.py:16
  210.2 11.4 %collective-permute-start.11 = (bf16[8,64,512]{2,1,0:T(8,128)(2,1)S(1)}, bf16[8,64,512]{2,1,0:T(8,128)(2,1)S(1)}, u32[]{:S(2)}, u32[]{:S(2)}) collective-permute-start(bf16[8,64,512]{2,1,0:T(8,128)(2,1)S(1)} %fusion.23), channel_id=1, source_target_pairs={{0,32},{32,0},{64,96},{96,64},{128,160},{160,128},{192,224},{224,1... | collective-permute-start | bytes 1572872 | tf_op jit(solution)/shard_map/ppermute | solution.py:11
  226.3 4.3 %all-to-all-start.5 = ((bf16[8,136,512]{2,1,0:T(8,128)(2,1)}), bf16[8,136,512]{2,1,0:T(8,128)(2,1)}, u32[]{:S(2)}, u32[]{:S(2)}) async-start(bf16[8,136,512]{2,1,0:T(8,128)(2,1)} %pad_maximum_fusion), calls=%async_computation.5 | async-start | bytes 2228224 | tf_op jit(solution)/shard_map/all_to_all | solution.py:29
  238.0 9.2 %all-to-all-done.5 = bf16[8,136,512]{2,1,0:T(8,128)(2,1)} async-done(((bf16[8,136,512]{2,1,0:T(8,128)(2,1)}), bf16[8,136,512]{2,1,0:T(8,128)(2,1)}, u32[]{:S(2)}, u32[]{:S(2)}) %all-to-all-start.5) | async-done | bytes 1114144 | tf_op jit(solution)/shard_map/all_to_all | solution.py:29
  (181 shorter events, 60.4 us)
Async XLA Ops:
  2.6 25.8 %copy-start.2 = (bf16[384,1024]{1,0:T(8,128)(2,1)S(1)}, bf16[384,1024]{1,0:T(8,128)(2,1)}, u32[]{:S(2)}) copy-start(bf16[384,1024]{1,0:T(8,128)(2,1)} %param.8) | copy-start | bytes 2359300
  2.6 25.8 %copy-start.11 = (bf16[384,1024]{1,0:T(8,128)(2,1)S(1)}, bf16[384,1024]{1,0:T(8,128)(2,1)}, u32[]{:S(2)}) copy-start(bf16[384,1024]{1,0:T(8,128)(2,1)} %param.9) | copy-start | bytes 2359300
  2.7 17.2 %all-to-all-start = ((bf16[8,128,512]{2,1,0:T(8,128)(2,1)}), bf16[8,128,512]{2,1,0:T(8,128)(2,1)S(1)}, u32[]{:S(2)}, u32[]{:S(2)}) async-start(bf16[8,128,512]{2,1,0:T(8,128)(2,1)} %broadcast_in_dim.45), calls=%async_computation | async-start | bytes 2097152 | tf_op jit(solution)/shard_map/all_to_all | solution.py:29
  8.7 21.5 %collective-permute-start = (bf16[1024,256]{1,0:T(8,128)(2,1)}, bf16[1024,256]{1,0:T(8,128)(2,1)}, u32[]{:S(2)}, u32[]{:S(2)}) collective-permute-start(bf16[1024,256]{1,0:T(8,128)(2,1)} %param.12), channel_id=1, source_target_pairs={{0,32},{32,0},{64,96},{96,64},{128,160},{160,128},{192,224},{224,1... | collective-permute-start | bytes 1572872 | tf_op jit(solution)/shard_map/ppermute | solution.py:11
  20.9 15.1 %collective-permute-start.2 = (bf16[8,64,512]{2,1,0:T(8,128)(2,1)}, bf16[8,64,512]{2,1,0:T(8,128)(2,1)}, u32[]{:S(2)}, u32[]{:S(2)}) collective-permute-start(bf16[8,64,512]{2,1,0:T(8,128)(2,1)} %get-tuple-element.24), channel_id=1, source_target_pairs={{0,32},{32,0},{64,96},{96,64},{128,160},{160,128},{192,224},{224,1... | collective-permute-start | bytes 1572872 | tf_op jit(solution)/shard_map/ppermute | solution.py:11
  31.7 9.9 %collective-permute-start.1 = (bf16[192,512]{1,0:T(8,128)(2,1)S(1)}, bf16[192,512]{1,0:T(8,128)(2,1)S(1)}, u32[]{:S(2)}, u32[]{:S(2)}) collective-permute-start(bf16[192,512]{1,0:T(8,128)(2,1)S(1)} %convolution_convert_fusion.3), channel_id=1, source_target_pairs={{0,16},{1,17},{2,18},{3,19},{4,20},{5,21},{6,22},{7,23},{8,24},{9,... | collective-permute-start | bytes 589832 | tf_op jit(solution)/shard_map/ppermute | solution.py:16
  37.7 9.6 %collective-permute-start.3 = (bf16[192,512]{1,0:T(8,128)(2,1)S(1)}, bf16[192,512]{1,0:T(8,128)(2,1)S(1)}, u32[]{:S(2)}, u32[]{:S(2)}) collective-permute-start(bf16[192,512]{1,0:T(8,128)(2,1)S(1)} %convolution_convert_fusion.2), channel_id=1, source_target_pairs={{0,16},{1,17},{2,18},{3,19},{4,20},{5,21},{6,22},{7,23},{8,24},{9,... | collective-permute-start | bytes 589832 | tf_op jit(solution)/shard_map/ppermute | solution.py:16
  47.4 48.6 %copy-start.27 = (bf16[8,64,512]{2,1,0:T(8,128)(2,1)S(1)}, bf16[8,64,512]{2,1,0:T(8,128)(2,1)}, u32[]{:S(2)}) copy-start(bf16[8,64,512]{2,1,0:T(8,128)(2,1)} %get-tuple-element.9) | copy-start | bytes 1572868
  81.0 30.0 %all-to-all-start.2 = ((bf16[16,24,512]{2,1,0:T(8,128)(2,1)}), bf16[16,24,512]{2,1,0:T(8,128)(2,1)S(1)}, u32[]{:S(2)}, u32[]{:S(2)}) async-start(bf16[16,24,512]{2,1,0:T(8,128)(2,1)} %broadcast_in_dim.47), calls=%async_computation.2 | async-start | bytes 786432 | tf_op jit(solution)/shard_map/all_to_all | solution.py:29
  92.9 6.9 %collective-permute-start.4 = (bf16[1024,256]{1,0:T(8,128)(2,1)}, bf16[1024,256]{1,0:T(8,128)(2,1)S(1)}, u32[]{:S(2)}, u32[]{:S(2)}) collective-permute-start(bf16[1024,256]{1,0:T(8,128)(2,1)} %param.11), channel_id=1, source_target_pairs={{0,32},{32,0},{64,96},{96,64},{128,160},{160,128},{192,224},{224,1... | collective-permute-start | bytes 1572872 | tf_op jit(solution)/shard_map/ppermute | solution.py:11
  96.0 3.9 %collective-permute-start.5 = (bf16[8,64,512]{2,1,0:T(8,128)(2,1)S(1)}, bf16[8,64,512]{2,1,0:T(8,128)(2,1)S(1)}, u32[]{:S(2)}, u32[]{:S(2)}) collective-permute-start(bf16[8,64,512]{2,1,0:T(8,128)(2,1)S(1)} %copy-done.27), channel_id=1, source_target_pairs={{0,32},{32,0},{64,96},{96,64},{128,160},{160,128},{192,224},{224,1... | collective-permute-start | bytes 1572872 | tf_op jit(solution)/shard_map/ppermute | solution.py:11
  111.0 10.0 %collective-permute-start.6 = (bf16[384,512]{1,0:T(8,128)(2,1)S(1)}, bf16[384,512]{1,0:T(8,128)(2,1)S(1)}, u32[]{:S(2)}, u32[]{:S(2)}) collective-permute-start(bf16[384,512]{1,0:T(8,128)(2,1)S(1)} %bitcast.113), channel_id=1, source_target_pairs={{0,16},{1,17},{2,18},{3,19},{4,20},{5,21},{6,22},{7,23},{8,24},{9,... | collective-permute-start | bytes 1179656 | tf_op jit(solution)/shard_map/ppermute | solution.py:16
  124.6 10.0 %collective-permute-start.7 = (bf16[384,512]{1,0:T(8,128)(2,1)S(1)}, bf16[384,512]{1,0:T(8,128)(2,1)S(1)}, u32[]{:S(2)}, u32[]{:S(2)}) collective-permute-start(bf16[384,512]{1,0:T(8,128)(2,1)S(1)} %pad_maximum_fusion.4), channel_id=1, source_target_pairs={{0,16},{1,17},{2,18},{3,19},{4,20},{5,21},{6,22},{7,23},{8,24},{9,... | collective-permute-start | bytes 1179656 | tf_op jit(solution)/shard_map/ppermute | solution.py:16
  136.3 32.1 %all-to-all-start.3 = ((bf16[16,24,512]{2,1,0:T(8,128)(2,1)}), bf16[16,24,512]{2,1,0:T(8,128)(2,1)S(1)}, u32[]{:S(2)}, u32[]{:S(2)}) async-start(bf16[16,24,512]{2,1,0:T(8,128)(2,1)} %bitcast.114), calls=%async_computation.3 | async-start | bytes 786432 | tf_op jit(solution)/shard_map/all_to_all | solution.py:29
  154.2 28.7 %copy-start.22 = (bf16[192,1024]{1,0:T(8,128)(2,1)S(1)}, bf16[192,1024]{1,0:T(8,128)(2,1)}, u32[]{:S(2)}) copy-start(bf16[192,1024]{1,0:T(8,128)(2,1)} %copy-done.21) | copy-start | bytes 1179652
  154.2 28.7 %copy-start.31 = (bf16[8,24,512]{2,1,0:T(8,128)(2,1)S(1)}, bf16[8,24,512]{2,1,0:T(8,128)(2,1)}, u32[]{:S(2)}) copy-start(bf16[8,24,512]{2,1,0:T(8,128)(2,1)} %copy-done.30) | copy-start | bytes 589828
  156.4 33.8 %collective-permute-start.12 = (bf16[8,64,512]{2,1,0:T(8,128)(2,1)}, bf16[8,64,512]{2,1,0:T(8,128)(2,1)}, u32[]{:S(2)}, u32[]{:S(2)}) collective-permute-start(bf16[8,64,512]{2,1,0:T(8,128)(2,1)} %fusion.24), channel_id=1, source_target_pairs={{0,32},{32,0},{64,96},{96,64},{128,160},{160,128},{192,224},{224,1... | collective-permute-start | bytes 1572872 | tf_op jit(solution)/shard_map/ppermute | solution.py:11
  161.9 27.5 %collective-permute-start.13 = (f32[2,1024]{1,0:T(2,128)}, f32[2,1024]{1,0:T(2,128)}, u32[]{:S(2)}, u32[]{:S(2)}) collective-permute-start(f32[2,1024]{1,0:T(2,128)} %pad_maximum_fusion.7), channel_id=1, source_target_pairs={{0,32},{32,0},{64,96},{96,64},{128,160},{160,128},{192,224},{224,1... | collective-permute-start | bytes 24584 | tf_op jit(solution)/shard_map/ppermute | solution.py:11
  169.3 29.9 %all-to-all-start.4 = ((bf16[16,24,512]{2,1,0:T(8,128)(2,1)}), bf16[16,24,512]{2,1,0:T(8,128)(2,1)}, u32[]{:S(2)}, u32[]{:S(2)}) async-start(bf16[16,24,512]{2,1,0:T(8,128)(2,1)} %broadcast_in_dim.48), calls=%async_computation.4 | async-start | bytes 786432 | tf_op jit(solution)/shard_map/all_to_all | solution.py:29
  185.6 7.0 %collective-permute-start.9 = (bf16[1024,256]{1,0:T(8,128)(2,1)}, bf16[1024,256]{1,0:T(8,128)(2,1)}, u32[]{:S(2)}, u32[]{:S(2)}) collective-permute-start(bf16[1024,256]{1,0:T(8,128)(2,1)} %slice.173), channel_id=1, source_target_pairs={{0,32},{32,0},{64,96},{96,64},{128,160},{160,128},{192,224},{224,1... | collective-permute-start | bytes 1572872 | tf_op jit(solution)/shard_map/ppermute | solution.py:11
  199.2 10.2 %collective-permute-start.8 = (bf16[384,512]{1,0:T(8,128)(2,1)}, bf16[384,512]{1,0:T(8,128)(2,1)S(1)}, u32[]{:S(2)}, u32[]{:S(2)}) collective-permute-start(bf16[384,512]{1,0:T(8,128)(2,1)} %bitcast.18), channel_id=1, source_target_pairs={{0,16},{1,17},{2,18},{3,19},{4,20},{5,21},{6,22},{7,23},{8,24},{9,... | collective-permute-start | bytes 1179656 | tf_op jit(solution)/shard_map/ppermute | solution.py:16
  210.2 14.8 %collective-permute-start.11 = (bf16[8,64,512]{2,1,0:T(8,128)(2,1)S(1)}, bf16[8,64,512]{2,1,0:T(8,128)(2,1)S(1)}, u32[]{:S(2)}, u32[]{:S(2)}) collective-permute-start(bf16[8,64,512]{2,1,0:T(8,128)(2,1)S(1)} %fusion.23), channel_id=1, source_target_pairs={{0,32},{32,0},{64,96},{96,64},{128,160},{160,128},{192,224},{224,1... | collective-permute-start | bytes 1572872 | tf_op jit(solution)/shard_map/ppermute | solution.py:11
  226.3 20.9 %all-to-all-start.5 = ((bf16[8,136,512]{2,1,0:T(8,128)(2,1)}), bf16[8,136,512]{2,1,0:T(8,128)(2,1)}, u32[]{:S(2)}, u32[]{:S(2)}) async-start(bf16[8,136,512]{2,1,0:T(8,128)(2,1)} %pad_maximum_fusion), calls=%async_computation.5 | async-start | bytes 2228224 | tf_op jit(solution)/shard_map/all_to_all | solution.py:29
  232.9 4.1 %collective-permute-start.10 = (bf16[1024,256]{1,0:T(8,128)(2,1)S(1)}, bf16[1024,256]{1,0:T(8,128)(2,1)S(1)}, u32[]{:S(2)}, u32[]{:S(2)}) collective-permute-start(bf16[1024,256]{1,0:T(8,128)(2,1)S(1)} %slice.172), channel_id=1, source_target_pairs={{0,32},{32,0},{64,96},{96,64},{128,160},{160,128},{192,224},{224,1... | collective-permute-start | bytes 1572872 | tf_op jit(solution)/shard_map/ppermute | solution.py:11
  (42 other events, 345.2 us)

commit v4 on v3

v4 whole, which is shorter than its diff:
```python
import jax
import jax.numpy as jnp
from jax import lax
from jax.sharding import PartitionSpec as P

FAR = 2


def core_swap(value):
    pairs = [(source, source ^ 1) for source in range(lax.axis_size("dom"))]
    return lax.ppermute(value, "dom", pairs)


def near_groups():
    half = lax.axis_size("feat") // FAR
    return [[far * half + 2 * pair + bit for far in range(FAR) for bit in range(2)] for pair in range(half // 2)]


def ring_groups():
    half = lax.axis_size("feat") // FAR
    return [[far * half + 2 * step + bit for step in range(half // 2)] for far in range(FAR) for bit in range(2)]


def chip_groups():
    return [list(range(core, lax.axis_size("dom"), 2)) for core in range(2)]


def exchange(value, axis, groups):
    return lax.all_to_all(value, axis, 0, 0, axis_index_groups=groups, tiled=True)


def gathered(value, axis, groups):
    members = len(groups[0])
    repeated = jnp.broadcast_to(value[None], (members, *value.shape))
    return exchange(repeated.reshape(members * value.shape[0], value.shape[1]), axis, groups)


def summed(value, axis, groups):
    pieces = exchange(value, axis, groups).reshape(len(groups[0]), -1, value.shape[1])
    return jnp.sum(pieces.astype(jnp.float32), axis=0).astype(jnp.bfloat16)


def feature_sum(value):
    near, ring = near_groups(), ring_groups()
    part = summed(summed(value, "feat", near), "feat", ring)
    return gathered(gathered(part, "feat", ring), "feat", near)


def dot(left_side, right_side):
    return jnp.dot(left_side, right_side, preferred_element_type=jnp.float32)


def transposed_dot(left_side, right_side):
    return lax.dot_general(
        left_side, right_side, (((0,), (0,)), ((), ())), preferred_element_type=jnp.float32
    )


def cross_dot(left_side, right_side):
    return lax.dot_general(
        left_side, right_side, (((1,), (1,)), ((), ())), preferred_element_type=jnp.float32
    )


def local(x0, cotangent, domain_ids, expert_u, expert_v, shared_u, shared_v, bias):
    low = jnp.bfloat16
    wide = jnp.float32
    rows, width = x0.shape
    half_rank = expert_u.shape[1]
    rank = 2 * half_rank
    chips = lax.axis_size("dom") // 2
    lines = shared_u.shape[0]
    domain = lax.axis_index("dom") // 2
    core = lax.axis_index("dom") % 2

    own_maps = gathered(jnp.concatenate([shared_u, shared_v], 0), "dom", chip_groups())
    own_maps = own_maps.reshape(chips, 2, lines, rank)
    other_v = core_swap(expert_v)
    other_u = core_swap(expert_u)
    full_v = jnp.concatenate([expert_v, other_v], 1)
    full_u = jnp.concatenate([expert_u, other_u], 1)

    def whole(own, other):
        pair = [jnp.where(core == 0, own, other), jnp.where(core == 0, other, own)]
        return jnp.stack(pair, 1).reshape(width, rank)

    masked = jnp.where((domain_ids == domain)[:, None], cotangent, jnp.zeros_like(cotangent)).astype(wide)
    inputs = x0.astype(wide)
    second_adj = (masked * inputs).astype(low)

    first_part = dot(x0, full_v).astype(low)
    whole_su = whole(own_maps[:, 0], core_swap(own_maps[:, 0]))
    back_two_part = dot(second_adj, whole_su).astype(low)
    both = jnp.concatenate([first_part, back_two_part], 0)
    own_sv, both = lax.optimization_barrier((own_maps[:, 1], both))
    whole_sv = whole(own_sv, core_swap(own_sv))
    sums = feature_sum(both)
    first_rank, back_two = sums[:rows], sums[rows:]
    first_gate = cross_dot(first_rank, full_u) + bias[0][None, :]
    layer_one = (inputs * first_gate + inputs).astype(low)
    layer_grad = masked + cross_dot(back_two, whole_sv)
    first_adj = (layer_grad * inputs).astype(low)
    second_part = dot(layer_one, whole_sv).astype(low)
    back_one_part = dot(first_adj, full_u).astype(low)
    sums = feature_sum(jnp.concatenate([second_part, back_one_part], 0))

    def with_partner(partial):
        peer = core_swap(partial[:, half_rank:].astype(low))
        return (partial[:, :half_rank] + peer.astype(wide)).astype(low)

    def chip_part(term):
        blocks = term.reshape(chips, 2, lines, rank)
        keep, give = [
            lax.dynamic_index_in_dim(blocks, place, 1, keepdims=False) for place in (core, 1 - core)
        ]
        return (keep + core_swap(give.astype(low)).astype(wide)).astype(low)

    grad_eu = with_partner(transposed_dot(first_adj, first_rank))
    part_sv = chip_part(transposed_dot(layer_one, back_two))
    bias_terms = jnp.stack([jnp.sum(a.astype(wide), axis=0) for a in (first_adj, second_adj)])
    bias_terms = bias_terms + core_swap(bias_terms)
    bias_high = bias_terms.astype(low)
    bias_rest = (bias_terms - bias_high.astype(wide)).astype(low)
    bias_lines = jnp.stack([bias_high, bias_rest]).reshape(4 * width // rank, rank)
    bias_lines = jnp.broadcast_to(bias_lines[None], (chips, *bias_lines.shape))

    second_rank, back_one = sums[:rows], sums[rows:]
    part_su = chip_part(transposed_dot(second_adj, second_rank))
    sent = jnp.concatenate([part_su, part_sv, bias_lines], 1)
    taken = exchange(sent.reshape(-1, rank), "dom", chip_groups()).reshape(sent.shape)
    taken = jnp.sum(taken.astype(wide), axis=0)
    bias_sum = taken[2 * lines :].reshape(2, 2, width)
    grad_ev = with_partner(transposed_dot(x0, back_one))
    second_gate = cross_dot(second_rank, whole_su) + bias[1][None, :]
    grad_inputs = (
        masked * second_gate + layer_grad * first_gate + layer_grad + cross_dot(back_one, full_v)
    ).astype(low)
    return (
        grad_inputs,
        grad_eu,
        grad_ev,
        taken[:lines].astype(low),
        taken[lines : 2 * lines].astype(low),
        bias_sum[0] + bias_sum[1],
    )


def solution(mesh):
    placed = (
        P("dom", "feat"),
        P("dom", "feat"),
        P("dom"),
        P("feat", "dom"),
        P("feat", "dom"),
        P(("feat", "dom"), None),
        P(("feat", "dom"), None),
        P(None, "feat"),
    )
    return jax.shard_map(
        local,
        mesh=mesh,
        in_specs=placed,
        out_specs=(
            P("dom", "feat"),
            P("feat", "dom"),
            P("feat", "dom"),
            P(("feat", "dom"), None),
            P(("feat", "dom"), None),
            P(None, "feat"),
        ),
        check_vma=False,
    )
```

time: 251 us -> 247 us (0.984)
  blocking collectives: 32.4 us -> 118 us
  starting transfers between devices: 110 us -> 56.1 us
  waiting for transfers between devices: 57.7 us -> 14.8 us
  local copies, waits for them, and re-layouts: 16.1 us -> 24.2 us
    all_to_all x1 -> x6, blocking collectives: 32.4 us -> 118 us  [exchange(): lax.all_to_all(value, axis, 0, 0, axis_index_groups=groups, tiled=True)]
    all_to_all x5 -> x4, starting transfers between devices: 52.6 us -> 18.3 us  [exchange(): lax.all_to_all(value, axis, 0, 0, axis_index_groups=groups, tiled=True)]
    ppermute x5 -> x0, waiting for transfers between devices: 23.9 us -> none  [far_swap(): lax.ppermute(value, 'feat', [(source, (source + count // FAR) % count) fo...]
    all_to_all x5 -> x4, waiting for transfers between devices: 33.8 us -> 14.6 us  [exchange(): lax.all_to_all(value, axis, 0, 0, axis_index_groups=groups, tiled=True)]
    ppermute x5 -> x0, starting transfers between devices: 14.4 us -> none  [far_swap(): lax.ppermute(value, 'feat', [(source, (source + count // FAR) % count) fo...]
    ppermute x9, starting transfers between devices: 43 us -> 37.8 us  [core_swap(): return lax.ppermute(value, 'dom', pairs)]
    dot_general x0 -> x2, local copies, waits for them, and re-layouts: none -> 4.65 us  [transposed_dot(): lax.dot_general(left_side, right_side, (((0,), (0,)), ((), ())), preferre...]
    dot_general x8 -> x4, matrix products: 8.75 us -> 5.43 us  [transposed_dot(): lax.dot_general(left_side, right_side, (((0,), (0,)), ((), ())), preferre...]
  transfers between devices with their start and end apart: 19 -> 13, of which waited for: 10 -> 3; matrix products, arithmetic and copies ran while one was open for 13% -> 14% of each run, Pallas kernels for 0% -> 0%
where the time goes in v4:
time: 247 us; the launch traced here: 245 us
  blocking collectives  118 us (48%)
  starting transfers between devices  56.1 us (23%)
  local copies, waits for them, and re-layouts  24.2 us (10%)
  matrix products  17.2 us (7%)
  waiting for transfers between devices  14.8 us (6%)
  other arithmetic  13.4 us (5%)
    all_to_all x6, blocking collectives, exchange(): lax.all_to_all(value, axis, 0, 0, axis_index_groups=groups, tiled=True)  118 us
    ppermute x9, starting transfers between devices, core_swap(): return lax.ppermute(value, 'dom', pairs)  37.8 us
    all_to_all x4, starting transfers between devices, exchange(): lax.all_to_all(value, axis, 0, 0, axis_index_groups=groups, tiled=True)  18.3 us
    all_to_all x4, waiting for transfers between devices, exchange(): lax.all_to_all(value, axis, 0, 0, axis_index_groups=groups, tiled=True)  14.6 us
    dot_general x4, matrix products, cross_dot(): lax.dot_general(left_side, right_side, (((1,), (1,)), ((), ())), preferre...  8.02 us
    unnamed x57, local copies, waits for them, and re-layouts  6.98 us
    dot_general x4, matrix products, transposed_dot(): lax.dot_general(left_side, right_side, (((0,), (0,)), ((), ())), preferre...  5.43 us
  transfers between devices with their start and end apart: 13, of which 3 were waited for; matrix products, arithmetic and copies ran while one was open for 14% of the time, Pallas kernels for 0%

profile of v4, /device:TPU:1, one launch (start us, length us, event | category | flops | bytes accessed | tf_op | source)
XLA Modules:
  0.0 245.1 jit_solution(16457321020317289034)
XLA Ops:
  2.6 5.9 %all-to-all-start = ((bf16[8,128,512]{2,1,0:T(8,128)(2,1)}), bf16[8,128,512]{2,1,0:T(8,128)(2,1)S(1)}, u32[]{:S(2)}, u32[]{:S(2)}) async-start(bf16[8,128,512]{2,1,0:T(8,128)(2,1)} %broadcast_in_dim.30), calls=%async_computation | async-start | bytes 2097152 | tf_op jit(solution)/shard_map/all_to_all | solution.py:29
  8.6 6.4 %collective-permute-start = (bf16[1024,256]{1,0:T(8,128)(2,1)}, bf16[1024,256]{1,0:T(8,128)(2,1)}, u32[]{:S(2)}, u32[]{:S(2)}) collective-permute-start(bf16[1024,256]{1,0:T(8,128)(2,1)} %param.12), channel_id=1, source_target_pairs={{0,32},{32,0},{64,96},{96,64},{128,160},{160,128},{192,224},{224,1... | collective-permute-start | bytes 1572872 | tf_op jit(solution)/shard_map/ppermute | solution.py:11
  15.4 4.2 %all-to-all-done = bf16[8,128,512]{2,1,0:T(8,128)(2,1)S(1)} async-done(((bf16[8,128,512]{2,1,0:T(8,128)(2,1)}), bf16[8,128,512]{2,1,0:T(8,128)(2,1)S(1)}, u32[]{:S(2)}, u32[]{:S(2)}) %all-to-all-start) | async-done | bytes 1048608 | tf_op jit(solution)/shard_map/all_to_all | solution.py:29
  20.6 7.5 %collective-permute-start.1 = (bf16[8,64,512]{2,1,0:T(8,128)(2,1)S(1)}, bf16[8,64,512]{2,1,0:T(8,128)(2,1)S(1)}, u32[]{:S(2)}, u32[]{:S(2)}) collective-permute-start(bf16[8,64,512]{2,1,0:T(8,128)(2,1)S(1)} %get-tuple-element.42), channel_id=1, source_target_pairs={{0,32},{32,0},{64,96},{96,64},{128,160},{160,128},{192,224},{224,1... | collective-permute-start | bytes 1572872 | tf_op jit(solution)/shard_map/ppermute | solution.py:11
  33.8 17.1 %all_to_all.72 = bf16[4,192,512]{2,1,0:T(8,128)(2,1)S(1)} all-to-all(bf16[4,192,512]{2,1,0:T(8,128)(2,1)S(1)} %bitcast.109), channel_id=1, replica_groups={{0,1,16,17},{2,3,18,19},{4,5,20,21},{6,7,22,23},{8,9,24,25},{10,11,26,2..., dimensions={0} | all-to-all | bytes 1572864 | tf_op jit(solution)/shard_map/all_to_all | solution.py:29
  51.1 28.6 %all_to_all.73 = bf16[8,24,512]{2,1,0:T(8,128)(2,1)S(1)} all-to-all(bf16[8,24,512]{2,1,0:T(8,128)(2,1)S(1)} %bitcast.114), channel_id=1, replica_groups={{0,2,4,6,8,10,12,14},{1,3,5,7,9,11,13,15},{16,18,20,22,24,26,28,30},{17..., dimensions={0} | all-to-all | bytes 393216 | tf_op jit(solution)/shard_map/all_to_all | solution.py:29
  79.7 20.0 %all_to_all.74 = bf16[8,24,512]{2,1,0:T(8,128)(2,1)S(1)} all-to-all(bf16[8,24,512]{2,1,0:T(8,128)(2,1)S(1)} %broadcast_in_dim.56), channel_id=1, replica_groups={{0,2,4,6,8,10,12,14},{1,3,5,7,9,11,13,15},{16,18,20,22,24,26,28,30},{17..., dimensions={0} | all-to-all | bytes 393216 | tf_op jit(solution)/shard_map/all_to_all | solution.py:29
  100.7 3.9 %all-to-all-start.4 = ((bf16[4,192,512]{2,1,0:T(8,128)(2,1)}), bf16[4,192,512]{2,1,0:T(8,128)(2,1)S(1)}, u32[]{:S(2)}, u32[]{:S(2)}) async-start(bf16[4,192,512]{2,1,0:T(8,128)(2,1)} %broadcast_in_dim.58), calls=%async_computation.4 | async-start | bytes 1572864 | tf_op jit(solution)/shard_map/all_to_all | solution.py:29
  104.6 6.5 %collective-permute-start.2 = (bf16[1024,256]{1,0:T(8,128)(2,1)S(1)}, bf16[1024,256]{1,0:T(8,128)(2,1)S(1)}, u32[]{:S(2)}, u32[]{:S(2)}) collective-permute-start(bf16[1024,256]{1,0:T(8,128)(2,1)S(1)} %copy-done.24), channel_id=1, source_target_pairs={{0,32},{32,0},{64,96},{96,64},{128,160},{160,128},{192,224},{224,1... | collective-permute-start | bytes 1572872 | tf_op jit(solution)/shard_map/ppermute | solution.py:11
  115.3 2.4 convolution_add_fusion
  124.3 16.8 %all_to_all.75 = bf16[4,192,512]{2,1,0:T(8,128)(2,1)} all-to-all(bf16[4,192,512]{2,1,0:T(8,128)(2,1)S(1)} %bitcast.110), channel_id=1, replica_groups={{0,1,16,17},{2,3,18,19},{4,5,20,21},{6,7,22,23},{8,9,24,25},{10,11,26,2..., dimensions={0} | all-to-all | bytes 1572864 | tf_op jit(solution)/shard_map/all_to_all | solution.py:29
  142.4 17.6 %all_to_all.76 = bf16[8,24,512]{2,1,0:T(8,128)(2,1)S(1)} all-to-all(bf16[8,24,512]{2,1,0:T(8,128)(2,1)S(1)} %bitcast.115), channel_id=1, replica_groups={{0,2,4,6,8,10,12,14},{1,3,5,7,9,11,13,15},{16,18,20,22,24,26,28,30},{17..., dimensions={0} | all-to-all | bytes 393216 | tf_op jit(solution)/shard_map/all_to_all | solution.py:29
  160.1 17.8 %all_to_all.77 = bf16[8,24,512]{2,1,0:T(8,128)(2,1)S(1)} all-to-all(bf16[8,24,512]{2,1,0:T(8,128)(2,1)S(1)} %broadcast_in_dim.59), channel_id=1, replica_groups={{0,2,4,6,8,10,12,14},{1,3,5,7,9,11,13,15},{16,18,20,22,24,26,28,30},{17..., dimensions={0} | all-to-all | bytes 393216 | tf_op jit(solution)/shard_map/all_to_all | solution.py:29
  178.9 4.2 %all-to-all-start.8 = ((bf16[4,192,512]{2,1,0:T(8,128)(2,1)}), bf16[4,192,512]{2,1,0:T(8,128)(2,1)}, u32[]{:S(2)}, u32[]{:S(2)}) async-start(bf16[4,192,512]{2,1,0:T(8,128)(2,1)} %broadcast_in_dim.61), calls=%async_computation.8 | async-start | bytes 1572864 | tf_op jit(solution)/shard_map/all_to_all | solution.py:29
  183.1 2.3 copy.35
  186.1 6.7 %collective-permute-start.8 = (f32[2,1024]{1,0:T(2,128)}, f32[2,1024]{1,0:T(2,128)}, u32[]{:S(2)}, u32[]{:S(2)}) collective-permute-start(f32[2,1024]{1,0:T(2,128)} %pad_maximum_fusion.6), channel_id=1, source_target_pairs={{0,32},{32,0},{64,96},{96,64},{128,160},{160,128},{192,224},{224,1... | collective-permute-start | bytes 24584 | tf_op jit(solution)/shard_map/ppermute | solution.py:11
  192.8 2.3 copy.36
  195.1 3.3 %fusion.25 = f32[1024,512]{1,0:T(8,128)} fusion(bf16[384,1024]{1,0:T(8,128)(2,1)} %copy-done.17, bf16[384,512]{1,0:T(8,128)(2,1)S(1)} %bitcast.106), kind=kOutput, calls=%fused_computation.68 | convolution fusion | flops 402653184 | bytes 3276800 | tf_op jit(solution)/shard_map/dot_general | solution.py:54
  205.3 2.4 collective-permute-start.7
  208.5 2.3 fusion.9
  217.9 2.4 collective-permute-start.5
  221.7 4.2 %all-to-all-start.9 = ((bf16[8,136,512]{2,1,0:T(8,128)(2,1)}), bf16[8,136,512]{2,1,0:T(8,128)(2,1)}, u32[]{:S(2)}, u32[]{:S(2)}) async-start(bf16[8,136,512]{2,1,0:T(8,128)(2,1)} %pad_maximum_fusion), calls=%async_computation.9 | async-start | bytes 2228224 | tf_op jit(solution)/shard_map/all_to_all | solution.py:29
  226.0 2.1 fusion.24
  232.0 10.4 %all-to-all-done.9 = bf16[8,136,512]{2,1,0:T(8,128)(2,1)} async-done(((bf16[8,136,512]{2,1,0:T(8,128)(2,1)}), bf16[8,136,512]{2,1,0:T(8,128)(2,1)}, u32[]{:S(2)}, u32[]{:S(2)}) %all-to-all-start.9) | async-done | bytes 1114144 | tf_op jit(solution)/shard_map/all_to_all | solution.py:29
  (125 shorter events, 46.2 us)
Async XLA Ops:
  1.5 13.5 %copy-start.26 = (s32[384]{0:T(512)S(1)}, s32[384]{0:T(512)}, u32[]{:S(2)}) copy-start(s32[384]{0:T(512)} %param.10) | copy-start | bytes 4612
  1.5 13.5 %copy-start = (bf16[384,1024]{1,0:T(8,128)(2,1)S(1)}, bf16[384,1024]{1,0:T(8,128)(2,1)}, u32[]{:S(2)}) copy-start(bf16[384,1024]{1,0:T(8,128)(2,1)} %param.8) | copy-start | bytes 2359300
  1.5 13.5 %copy-start.4 = (bf16[384,1024]{1,0:T(8,128)(2,1)S(1)}, bf16[384,1024]{1,0:T(8,128)(2,1)}, u32[]{:S(2)}) copy-start(bf16[384,1024]{1,0:T(8,128)(2,1)} %param.9) | copy-start | bytes 2359300
  2.6 17.0 %all-to-all-start = ((bf16[8,128,512]{2,1,0:T(8,128)(2,1)}), bf16[8,128,512]{2,1,0:T(8,128)(2,1)S(1)}, u32[]{:S(2)}, u32[]{:S(2)}) async-start(bf16[8,128,512]{2,1,0:T(8,128)(2,1)} %broadcast_in_dim.30), calls=%async_computation | async-start | bytes 2097152 | tf_op jit(solution)/shard_map/all_to_all | solution.py:29
  8.6 20.6 %collective-permute-start = (bf16[1024,256]{1,0:T(8,128)(2,1)}, bf16[1024,256]{1,0:T(8,128)(2,1)}, u32[]{:S(2)}, u32[]{:S(2)}) collective-permute-start(bf16[1024,256]{1,0:T(8,128)(2,1)} %param.12), channel_id=1, source_target_pairs={{0,32},{32,0},{64,96},{96,64},{128,160},{160,128},{192,224},{224,1... | collective-permute-start | bytes 1572872 | tf_op jit(solution)/shard_map/ppermute | solution.py:11
  15.4 16.8 %copy-start.18 = (bf16[384,1024]{1,0:T(8,128)(2,1)}, bf16[384,1024]{1,0:T(8,128)(2,1)S(1)}, u32[]{:S(2)}) copy-start(bf16[384,1024]{1,0:T(8,128)(2,1)S(1)} %get-tuple-element.37) | copy-start | bytes 2359300
  20.6 11.3 %collective-permute-start.1 = (bf16[8,64,512]{2,1,0:T(8,128)(2,1)S(1)}, bf16[8,64,512]{2,1,0:T(8,128)(2,1)S(1)}, u32[]{:S(2)}, u32[]{:S(2)}) collective-permute-start(bf16[8,64,512]{2,1,0:T(8,128)(2,1)S(1)} %get-tuple-element.42), channel_id=1, source_target_pairs={{0,32},{32,0},{64,96},{96,64},{128,160},{160,128},{192,224},{224,1... | collective-permute-start | bytes 1572872 | tf_op jit(solution)/shard_map/ppermute | solution.py:11
  79.7 25.0 %copy-start.24 = (bf16[1024,256]{1,0:T(8,128)(2,1)S(1)}, bf16[1024,256]{1,0:T(8,128)(2,1)}, u32[]{:S(2)}) copy-start(bf16[1024,256]{1,0:T(8,128)(2,1)} %param.11) | copy-start | bytes 1572868
  79.7 31.4 %copy-start.23 = (bf16[8,64,512]{2,1,0:T(8,128)(2,1)S(1)}, bf16[8,64,512]{2,1,0:T(8,128)(2,1)}, u32[]{:S(2)}) copy-start(bf16[8,64,512]{2,1,0:T(8,128)(2,1)} %get-tuple-element.9) | copy-start | bytes 1572868
  99.7 14.2 %copy-start.25 = (f32[2,1024]{1,0:T(2,128)S(1)}, f32[2,1024]{1,0:T(2,128)}, u32[]{:S(2)}) copy-start(f32[2,1024]{1,0:T(2,128)} %param.15) | copy-start | bytes 24580
  100.7 14.5 %all-to-all-start.4 = ((bf16[4,192,512]{2,1,0:T(8,128)(2,1)}), bf16[4,192,512]{2,1,0:T(8,128)(2,1)S(1)}, u32[]{:S(2)}, u32[]{:S(2)}) async-start(bf16[4,192,512]{2,1,0:T(8,128)(2,1)} %broadcast_in_dim.58), calls=%async_computation.4 | async-start | bytes 1572864 | tf_op jit(solution)/shard_map/all_to_all | solution.py:29
  104.6 9.3 %collective-permute-start.2 = (bf16[1024,256]{1,0:T(8,128)(2,1)S(1)}, bf16[1024,256]{1,0:T(8,128)(2,1)S(1)}, u32[]{:S(2)}, u32[]{:S(2)}) collective-permute-start(bf16[1024,256]{1,0:T(8,128)(2,1)S(1)} %copy-done.24), channel_id=1, source_target_pairs={{0,32},{32,0},{64,96},{96,64},{128,160},{160,128},{192,224},{224,1... | collective-permute-start | bytes 1572872 | tf_op jit(solution)/shard_map/ppermute | solution.py:11
  111.1 3.8 %collective-permute-start.3 = (bf16[8,64,512]{2,1,0:T(8,128)(2,1)S(1)}, bf16[8,64,512]{2,1,0:T(8,128)(2,1)S(1)}, u32[]{:S(2)}, u32[]{:S(2)}) collective-permute-start(bf16[8,64,512]{2,1,0:T(8,128)(2,1)S(1)} %copy-done.23), channel_id=1, source_target_pairs={{0,32},{32,0},{64,96},{96,64},{128,160},{160,128},{192,224},{224,1... | collective-permute-start | bytes 1572872 | tf_op jit(solution)/shard_map/ppermute | solution.py:11
  178.9 31.9 %all-to-all-start.8 = ((bf16[4,192,512]{2,1,0:T(8,128)(2,1)}), bf16[4,192,512]{2,1,0:T(8,128)(2,1)}, u32[]{:S(2)}, u32[]{:S(2)}) async-start(bf16[4,192,512]{2,1,0:T(8,128)(2,1)} %broadcast_in_dim.61), calls=%async_computation.8 | async-start | bytes 1572864 | tf_op jit(solution)/shard_map/all_to_all | solution.py:29
  183.1 12.0 %copy-start.15 = (bf16[2,192,512]{2,1,0:T(8,128)(2,1)S(1)}, bf16[2,192,512]{2,1,0:T(8,128)(2,1)}, u32[]{:S(2)}) copy-start(bf16[2,192,512]{2,1,0:T(8,128)(2,1)} %copy-done.14) | copy-start | bytes 1179652
  186.1 21.6 %collective-permute-start.8 = (f32[2,1024]{1,0:T(2,128)}, f32[2,1024]{1,0:T(2,128)}, u32[]{:S(2)}, u32[]{:S(2)}) collective-permute-start(f32[2,1024]{1,0:T(2,128)} %pad_maximum_fusion.6), channel_id=1, source_target_pairs={{0,32},{32,0},{64,96},{96,64},{128,160},{160,128},{192,224},{224,1... | collective-permute-start | bytes 24584 | tf_op jit(solution)/shard_map/ppermute | solution.py:11
  195.1 7.3 %copy-start.13 = (bf16[2,192,512]{2,1,0:T(8,128)(2,1)S(1)}, bf16[2,192,512]{2,1,0:T(8,128)(2,1)}, u32[]{:S(2)}) copy-start(bf16[2,192,512]{2,1,0:T(8,128)(2,1)} %copy-done.12) | copy-start | bytes 1179652
  195.1 7.3 %copy-start.20 = (bf16[1024,384]{1,0:T(8,128)(2,1)S(1)}, bf16[1024,384]{1,0:T(8,128)(2,1)}, u32[]{:S(2)}) copy-start(bf16[1024,384]{1,0:T(8,128)(2,1)} %copy.36) | copy-start | bytes 2359300
  200.5 8.0 %collective-permute-start.4 = (bf16[1024,256]{1,0:T(8,128)(2,1)}, bf16[1024,256]{1,0:T(8,128)(2,1)}, u32[]{:S(2)}, u32[]{:S(2)}) collective-permute-start(bf16[1024,256]{1,0:T(8,128)(2,1)} %slice.121), channel_id=1, source_target_pairs={{0,32},{32,0},{64,96},{96,64},{128,160},{160,128},{192,224},{224,1... | collective-permute-start | bytes 1572872 | tf_op jit(solution)/shard_map/ppermute | solution.py:11
  205.3 9.7 %collective-permute-start.7 = (bf16[8,64,512]{2,1,0:T(8,128)(2,1)}, bf16[8,64,512]{2,1,0:T(8,128)(2,1)}, u32[]{:S(2)}, u32[]{:S(2)}) collective-permute-start(bf16[8,64,512]{2,1,0:T(8,128)(2,1)} %fusion.13), channel_id=1, source_target_pairs={{0,32},{32,0},{64,96},{96,64},{128,160},{160,128},{192,224},{224,1... | collective-permute-start | bytes 1572872 | tf_op jit(solution)/shard_map/ppermute | solution.py:11
  213.0 7.4 %collective-permute-start.6 = (bf16[8,64,512]{2,1,0:T(8,128)(2,1)S(1)}, bf16[8,64,512]{2,1,0:T(8,128)(2,1)S(1)}, u32[]{:S(2)}, u32[]{:S(2)}) collective-permute-start(bf16[8,64,512]{2,1,0:T(8,128)(2,1)S(1)} %fusion.12), channel_id=1, source_target_pairs={{0,32},{32,0},{64,96},{96,64},{128,160},{160,128},{192,224},{224,1... | collective-permute-start | bytes 1572872 | tf_op jit(solution)/shard_map/ppermute | solution.py:11
  217.0 3.5 %copy-start.9 = (f32[1024,512]{0,1:T(8,128)}, f32[1024,512]{0,1:T(8,128)S(1)}, u32[]{:S(2)}) copy-start(f32[1024,512]{0,1:T(8,128)S(1)} %convolution_bitcast_fusion) | copy-start | bytes 6291460
  217.9 11.8 %collective-permute-start.5 = (bf16[1024,256]{0,1:T(8,128)(2,1)}, bf16[1024,256]{0,1:T(8,128)(2,1)}, u32[]{:S(2)}, u32[]{:S(2)}) collective-permute-start(bf16[1024,256]{0,1:T(8,128)(2,1)} %slice.120), channel_id=1, source_target_pairs={{0,32},{32,0},{64,96},{96,64},{128,160},{160,128},{192,224},{224,1... | collective-permute-start | bytes 1572872 | tf_op jit(solution)/shard_map/ppermute | solution.py:11
  221.7 20.7 %all-to-all-start.9 = ((bf16[8,136,512]{2,1,0:T(8,128)(2,1)}), bf16[8,136,512]{2,1,0:T(8,128)(2,1)}, u32[]{:S(2)}, u32[]{:S(2)}) async-start(bf16[8,136,512]{2,1,0:T(8,128)(2,1)} %pad_maximum_fusion), calls=%async_computation.9 | async-start | bytes 2228224 | tf_op jit(solution)/shard_map/all_to_all | solution.py:29
  (16 other events, 31.5 us)

commit v5 on v4

--- a/solution.py
+++ b/solution.py
@@ -40,10 +40,11 @@
     return jnp.sum(pieces.astype(jnp.float32), axis=0).astype(jnp.bfloat16)
 
 
-def feature_sum(value):
+def feature_sum(value, beside):
     near, ring = near_groups(), ring_groups()
     part = summed(summed(value, "feat", near), "feat", ring)
-    return gathered(gathered(part, "feat", ring), "feat", near)
+    part, beside = lax.optimization_barrier((part, beside))
+    return gathered(gathered(part, "feat", ring), "feat", near), beside
 
 
 def dot(left_side, right_side):
@@ -76,9 +77,7 @@
     own_maps = gathered(jnp.concatenate([shared_u, shared_v], 0), "dom", chip_groups())
     own_maps = own_maps.reshape(chips, 2, lines, rank)
     other_v = core_swap(expert_v)
-    other_u = core_swap(expert_u)
     full_v = jnp.concatenate([expert_v, other_v], 1)
-    full_u = jnp.concatenate([expert_u, other_u], 1)
 
     def whole(own, other):
         pair = [jnp.where(core == 0, own, other), jnp.where(core == 0, other, own)]
@@ -92,9 +91,10 @@
     whole_su = whole(own_maps[:, 0], core_swap(own_maps[:, 0]))
     back_two_part = dot(second_adj, whole_su).astype(low)
     both = jnp.concatenate([first_part, back_two_part], 0)
-    own_sv, both = lax.optimization_barrier((own_maps[:, 1], both))
+    own_sv, expert_u, both = lax.optimization_barrier((own_maps[:, 1], expert_u, both))
     whole_sv = whole(own_sv, core_swap(own_sv))
-    sums = feature_sum(both)
+    full_u = jnp.concatenate([expert_u, core_swap(expert_u)], 1)
+    sums, (whole_sv, full_u) = feature_sum(both, (whole_sv, full_u))
     first_rank, back_two = sums[:rows], sums[rows:]
     first_gate = cross_dot(first_rank, full_u) + bias[0][None, :]
     layer_one = (inputs * first_gate + inputs).astype(low)
@@ -102,7 +102,7 @@
     first_adj = (layer_grad * inputs).astype(low)
     second_part = dot(layer_one, whole_sv).astype(low)
     back_one_part = dot(first_adj, full_u).astype(low)
-    sums = feature_sum(jnp.concatenate([second_part, back_one_part], 0))
+    both = jnp.concatenate([second_part, back_one_part], 0)
 
     def with_partner(partial):
         peer = core_swap(partial[:, half_rank:].astype(low))
@@ -124,9 +124,11 @@
     bias_lines = jnp.stack([bias_high, bias_rest]).reshape(4 * width // rank, rank)
     bias_lines = jnp.broadcast_to(bias_lines[None], (chips, *bias_lines.shape))
 
+    sums, (grad_eu, part_sv, bias_lines) = feature_sum(both, (grad_eu, part_sv, bias_lines))
     second_rank, back_one = sums[:rows], sums[rows:]
     part_su = chip_part(transposed_dot(second_adj, second_rank))
     sent = jnp.concatenate([part_su, part_sv, bias_lines], 1)
+    sent, second_rank, back_one = lax.optimization_barrier((sent, second_rank, back_one))
     taken = exchange(sent.reshape(-1, rank), "dom", chip_groups()).reshape(sent.shape)
     taken = jnp.sum(taken.astype(wide), axis=0)
     bias_sum = taken[2 * lines :].reshape(2, 2, width)

time: 247 us -> 246 us (level)
  blocking collectives: 118 us -> 40.9 us
  waiting for transfers between devices: 14.8 us -> 61.5 us
  starting transfers between devices: 56.1 us -> 84.8 us
  other arithmetic: 13.4 us -> 19.5 us
  matrix products: 17.2 us -> 12.4 us
    all_to_all x6 -> x2, blocking collectives: 118 us -> 40.9 us  [exchange(): lax.all_to_all(value, axis, 0, 0, axis_index_groups=groups, tiled=True)]
    all_to_all x4 -> x8, waiting for transfers between devices: 14.6 us -> 59.5 us  [exchange(): lax.all_to_all(value, axis, 0, 0, axis_index_groups=groups, tiled=True)]
    all_to_all x4 -> x8, starting transfers between devices: 18.3 us -> 47.3 us  [exchange(): lax.all_to_all(value, axis, 0, 0, axis_index_groups=groups, tiled=True)]
    dot_general x4, matrix products: 8.02 us -> 4.84 us  [cross_dot(): lax.dot_general(left_side, right_side, (((1,), (1,)), ((), ())), preferre...]
    concatenate x1 -> x2, other arithmetic: 0.05 us -> 3.08 us  [the longest x1 2.1 us: local(): full_u = jnp.concatenate([expert_u, core_swap(expert_u)], 1)]
    unnamed x57 -> x54, local copies, waits for them, and re-layouts: 6.98 us -> 8.35 us
  transfers between devices with their start and end apart: 13 -> 17, of which waited for: 3 -> 9; matrix products, arithmetic and copies ran while one was open for 14% -> 12% of each run, Pallas kernels for 0% -> 0%
where the time goes in v5:
time: 246 us; the launch traced here: 244 us
  starting transfers between devices  84.8 us (34%)
  waiting for transfers between devices  61.5 us (25%)
  blocking collectives  40.9 us (17%)
  local copies, waits for them, and re-layouts  23.4 us (10%)
  other arithmetic  19.5 us (8%)
  matrix products  12.4 us (5%)
    all_to_all x8, waiting for transfers between devices, exchange(): lax.all_to_all(value, axis, 0, 0, axis_index_groups=groups, tiled=True)  59.5 us
    all_to_all x8, starting transfers between devices, exchange(): lax.all_to_all(value, axis, 0, 0, axis_index_groups=groups, tiled=True)  47.3 us
    all_to_all x2, blocking collectives, exchange(): lax.all_to_all(value, axis, 0, 0, axis_index_groups=groups, tiled=True)  40.9 us
    ppermute x9, starting transfers between devices, core_swap(): return lax.ppermute(value, 'dom', pairs)  37.5 us
    unnamed x54, local copies, waits for them, and re-layouts  8.35 us
    dot_general x4, matrix products, transposed_dot(): lax.dot_general(left_side, right_side, (((0,), (0,)), ((), ())), preferre...  5.33 us
  transfers between devices with their start and end apart: 17, of which 9 were waited for; matrix products, arithmetic and copies ran while one was open for 12% of the time, Pallas kernels for 0%

profile of v5, /device:TPU:1, one launch (start us, length us, event | category | flops | bytes accessed | tf_op | source)
XLA Modules:
  0.0 243.9 jit_solution(5933745841421744577)
XLA Ops:
  2.6 5.9 %all-to-all-start = ((bf16[8,128,512]{2,1,0:T(8,128)(2,1)}), bf16[8,128,512]{2,1,0:T(8,128)(2,1)S(1)}, u32[]{:S(2)}, u32[]{:S(2)}) async-start(bf16[8,128,512]{2,1,0:T(8,128)(2,1)} %broadcast_in_dim.30), calls=%async_computation | async-start | bytes 2097152 | tf_op jit(solution)/shard_map/all_to_all | solution.py:29
  8.6 6.4 %collective-permute-start = (bf16[1024,256]{1,0:T(8,128)(2,1)}, bf16[1024,256]{1,0:T(8,128)(2,1)}, u32[]{:S(2)}, u32[]{:S(2)}) collective-permute-start(bf16[1024,256]{1,0:T(8,128)(2,1)} %param.12), channel_id=1, source_target_pairs={{0,32},{32,0},{64,96},{96,64},{128,160},{160,128},{192,224},{224,1... | collective-permute-start | bytes 1572872 | tf_op jit(solution)/shard_map/ppermute | solution.py:11
  16.3 3.4 %all-to-all-done = bf16[8,128,512]{2,1,0:T(8,128)(2,1)S(1)} async-done(((bf16[8,128,512]{2,1,0:T(8,128)(2,1)}), bf16[8,128,512]{2,1,0:T(8,128)(2,1)S(1)}, u32[]{:S(2)}, u32[]{:S(2)}) %all-to-all-start) | async-done | bytes 1048608 | tf_op jit(solution)/shard_map/all_to_all | solution.py:29
  19.8 7.6 %collective-permute-start.1 = (bf16[8,64,512]{2,1,0:T(8,128)(2,1)S(1)}, bf16[8,64,512]{2,1,0:T(8,128)(2,1)S(1)}, u32[]{:S(2)}, u32[]{:S(2)}) collective-permute-start(bf16[8,64,512]{2,1,0:T(8,128)(2,1)S(1)} %get-tuple-element.64), channel_id=1, source_target_pairs={{0,32},{32,0},{64,96},{96,64},{128,160},{160,128},{192,224},{224,1... | collective-permute-start | bytes 1572872 | tf_op jit(solution)/shard_map/ppermute | solution.py:11
  34.2 5.0 %all-to-all-start.1 = ((bf16[4,192,512]{2,1,0:T(8,128)(2,1)}), bf16[4,192,512]{2,1,0:T(8,128)(2,1)S(1)}, u32[]{:S(2)}, u32[]{:S(2)}) async-start(bf16[4,192,512]{2,1,0:T(8,128)(2,1)} %bitcast.110), calls=%async_computation.1 | async-start | bytes 1572864 | tf_op jit(solution)/shard_map/all_to_all | solution.py:29
  41.4 9.9 %all-to-all-done.1 = bf16[4,192,512]{2,1,0:T(8,128)(2,1)S(1)} async-done(((bf16[4,192,512]{2,1,0:T(8,128)(2,1)}), bf16[4,192,512]{2,1,0:T(8,128)(2,1)S(1)}, u32[]{:S(2)}, u32[]{:S(2)}) %all-to-all-start.1) | async-done | bytes 786464 | tf_op jit(solution)/shard_map/all_to_all | solution.py:29
  52.2 13.9 %all-to-all-start.2 = ((bf16[8,24,512]{2,1,0:T(8,128)(2,1)}), bf16[8,24,512]{2,1,0:T(8,128)(2,1)S(1)}, u32[]{:S(2)}, u32[]{:S(2)}) async-start(bf16[8,24,512]{2,1,0:T(8,128)(2,1)} %bitcast.10), calls=%async_computation.2 | async-start | bytes 393216 | tf_op jit(solution)/shard_map/all_to_all | solution.py:29
  66.1 3.3 %collective-permute-start.3 = (bf16[1024,256]{1,0:T(8,128)(2,1)}, bf16[1024,256]{1,0:T(8,128)(2,1)S(1)}, u32[]{:S(2)}, u32[]{:S(2)}) collective-permute-start(bf16[1024,256]{1,0:T(8,128)(2,1)} %param.11), channel_id=1, source_target_pairs={{0,32},{32,0},{64,96},{96,64},{128,160},{160,128},{192,224},{224,1... | collective-permute-start | bytes 1572872 | tf_op jit(solution)/shard_map/ppermute | solution.py:11
  73.2 8.2 %all-to-all-done.2 = bf16[8,24,512]{2,1,0:T(8,128)(2,1)S(1)} async-done(((bf16[8,24,512]{2,1,0:T(8,128)(2,1)}), bf16[8,24,512]{2,1,0:T(8,128)(2,1)S(1)}, u32[]{:S(2)}, u32[]{:S(2)}) %all-to-all-start.2) | async-done | bytes 196640 | tf_op jit(solution)/shard_map/all_to_all | solution.py:29
  81.5 20.8 %all_to_all.72 = bf16[8,24,512]{2,1,0:T(8,128)(2,1)S(1)} all-to-all(bf16[8,24,512]{2,1,0:T(8,128)(2,1)S(1)} %broadcast_in_dim.56), channel_id=1, replica_groups={{0,2,4,6,8,10,12,14},{1,3,5,7,9,11,13,15},{16,18,20,22,24,26,28,30},{17..., dimensions={0} | all-to-all | bytes 393216 | tf_op jit(solution)/shard_map/all_to_all | solution.py:29
  103.2 3.5 %all-to-all-start.4 = ((bf16[4,192,512]{2,1,0:T(8,128)(2,1)}), bf16[4,192,512]{2,1,0:T(8,128)(2,1)S(1)}, u32[]{:S(2)}, u32[]{:S(2)}) async-start(bf16[4,192,512]{2,1,0:T(8,128)(2,1)} %broadcast_in_dim.58), calls=%async_computation.4 | async-start | bytes 1572864 | tf_op jit(solution)/shard_map/all_to_all | solution.py:29
  106.7 8.3 %all-to-all-done.4 = bf16[4,192,512]{2,1,0:T(8,128)(2,1)S(1)} async-done(((bf16[4,192,512]{2,1,0:T(8,128)(2,1)}), bf16[4,192,512]{2,1,0:T(8,128)(2,1)S(1)}, u32[]{:S(2)}, u32[]{:S(2)}) %all-to-all-start.4) | async-done | bytes 786464 | tf_op jit(solution)/shard_map/all_to_all | solution.py:29
  122.3 4.2 %all-to-all-start.5 = ((bf16[4,192,512]{2,1,0:T(8,128)(2,1)}), bf16[4,192,512]{2,1,0:T(8,128)(2,1)}, u32[]{:S(2)}, u32[]{:S(2)}) async-start(bf16[4,192,512]{2,1,0:T(8,128)(2,1)} %bitcast.109), calls=%async_computation.5 | async-start | bytes 1572864 | tf_op jit(solution)/shard_map/all_to_all | solution.py:29
  127.2 7.9 %collective-permute-start.6 = (f32[2,1024]{1,0:T(2,128)}, f32[2,1024]{1,0:T(2,128)}, u32[]{:S(2)}, u32[]{:S(2)}) collective-permute-start(f32[2,1024]{1,0:T(2,128)} %pad_maximum_fusion.7), channel_id=1, source_target_pairs={{0,32},{32,0},{64,96},{96,64},{128,160},{160,128},{192,224},{224,1... | collective-permute-start | bytes 24584 | tf_op jit(solution)/shard_map/ppermute | solution.py:11
  150.8 4.6 %all-to-all-start.6 = ((bf16[8,24,512]{2,1,0:T(8,128)(2,1)}), bf16[8,24,512]{2,1,0:T(8,128)(2,1)S(1)}, u32[]{:S(2)}, u32[]{:S(2)}) async-start(bf16[8,24,512]{2,1,0:T(8,128)(2,1)} %bitcast.19), calls=%async_computation.6 | async-start | bytes 393216 | tf_op jit(solution)/shard_map/all_to_all | solution.py:29
  156.1 2.5 %fusion.11 = bf16[8,64,512]{2,1,0:T(8,128)(2,1)} fusion(bf16[8,64,512]{2,1,0:T(8,128)(2,1)} %collective-permute-done.5, f32[8,2,64,512]{3,2,1,0:T(8,128)} %copy-done.6, s32[]{:T(128)S(6)} %select_n.52), kind=kLoop, calls=%fused_computation.37 | loop fusion | flops 786432 | bytes 2097156 | tf_op jit(solution)/shard_map/convert_element_type | solution.py:116
  160.6 11.9 %all-to-all-done.6 = bf16[8,24,512]{2,1,0:T(8,128)(2,1)S(1)} async-done(((bf16[8,24,512]{2,1,0:T(8,128)(2,1)}), bf16[8,24,512]{2,1,0:T(8,128)(2,1)S(1)}, u32[]{:S(2)}, u32[]{:S(2)}) %all-to-all-start.6) | async-done | bytes 196640 | tf_op jit(solution)/shard_map/all_to_all | solution.py:29
  173.2 20.1 %all_to_all.73 = bf16[8,24,512]{2,1,0:T(8,128)(2,1)S(1)} all-to-all(bf16[8,24,512]{2,1,0:T(8,128)(2,1)S(1)} %broadcast_in_dim.61), channel_id=1, replica_groups={{0,2,4,6,8,10,12,14},{1,3,5,7,9,11,13,15},{16,18,20,22,24,26,28,30},{17..., dimensions={0} | all-to-all | bytes 393216 | tf_op jit(solution)/shard_map/all_to_all | solution.py:29
  194.3 6.0 %all-to-all-start.8 = ((bf16[4,192,512]{2,1,0:T(8,128)(2,1)}), bf16[4,192,512]{2,1,0:T(8,128)(2,1)}, u32[]{:S(2)}, u32[]{:S(2)}) async-start(bf16[4,192,512]{2,1,0:T(8,128)(2,1)} %broadcast_in_dim.63), calls=%async_computation.8 | async-start | bytes 1572864 | tf_op jit(solution)/shard_map/all_to_all | solution.py:29
  202.5 9.6 %all-to-all-done.8 = bf16[4,192,512]{2,1,0:T(8,128)(2,1)} async-done(((bf16[4,192,512]{2,1,0:T(8,128)(2,1)}), bf16[4,192,512]{2,1,0:T(8,128)(2,1)}, u32[]{:S(2)}, u32[]{:S(2)}) %all-to-all-start.8) | async-done | bytes 786464 | tf_op jit(solution)/shard_map/all_to_all | solution.py:29
  214.3 3.5 %collective-permute-start.7 = (bf16[8,64,512]{2,1,0:T(8,128)(2,1)S(1)}, bf16[8,64,512]{2,1,0:T(8,128)(2,1)S(1)}, u32[]{:S(2)}, u32[]{:S(2)}) collective-permute-start(bf16[8,64,512]{2,1,0:T(8,128)(2,1)S(1)} %fusion.13), channel_id=1, source_target_pairs={{0,32},{32,0},{64,96},{96,64},{128,160},{160,128},{192,224},{224,1... | collective-permute-start | bytes 1572872 | tf_op jit(solution)/shard_map/ppermute | solution.py:11
  220.7 4.2 %all-to-all-start.9 = ((bf16[8,136,512]{2,1,0:T(8,128)(2,1)}), bf16[8,136,512]{2,1,0:T(8,128)(2,1)}, u32[]{:S(2)}, u32[]{:S(2)}) async-start(bf16[8,136,512]{2,1,0:T(8,128)(2,1)} %pad_maximum_fusion), calls=%async_computation.9 | async-start | bytes 2228224 | tf_op jit(solution)/shard_map/all_to_all | solution.py:29
  227.0 2.4 collective-permute-start.8
  232.9 8.2 %all-to-all-done.9 = bf16[8,136,512]{2,1,0:T(8,128)(2,1)} async-done(((bf16[8,136,512]{2,1,0:T(8,128)(2,1)}), bf16[8,136,512]{2,1,0:T(8,128)(2,1)}, u32[]{:S(2)}, u32[]{:S(2)}) %all-to-all-start.9) | async-done | bytes 1114144 | tf_op jit(solution)/shard_map/all_to_all | solution.py:29
  (126 shorter events, 61.3 us)
Async XLA Ops:
  1.5 13.5 %copy-start.25 = (s32[384]{0:T(512)S(1)}, s32[384]{0:T(512)}, u32[]{:S(2)}) copy-start(s32[384]{0:T(512)} %param.10) | copy-start | bytes 4612
  1.5 13.5 %copy-start = (bf16[384,1024]{1,0:T(8,128)(2,1)S(1)}, bf16[384,1024]{1,0:T(8,128)(2,1)}, u32[]{:S(2)}) copy-start(bf16[384,1024]{1,0:T(8,128)(2,1)} %param.8) | copy-start | bytes 2359300
  1.5 13.5 %copy-start.3 = (bf16[384,1024]{1,0:T(8,128)(2,1)S(1)}, bf16[384,1024]{1,0:T(8,128)(2,1)}, u32[]{:S(2)}) copy-start(bf16[384,1024]{1,0:T(8,128)(2,1)} %param.9) | copy-start | bytes 2359300
  2.6 17.0 %all-to-all-start = ((bf16[8,128,512]{2,1,0:T(8,128)(2,1)}), bf16[8,128,512]{2,1,0:T(8,128)(2,1)S(1)}, u32[]{:S(2)}, u32[]{:S(2)}) async-start(bf16[8,128,512]{2,1,0:T(8,128)(2,1)} %broadcast_in_dim.30), calls=%async_computation | async-start | bytes 2097152 | tf_op jit(solution)/shard_map/all_to_all | solution.py:29
  8.6 19.8 %collective-permute-start = (bf16[1024,256]{1,0:T(8,128)(2,1)}, bf16[1024,256]{1,0:T(8,128)(2,1)}, u32[]{:S(2)}, u32[]{:S(2)}) collective-permute-start(bf16[1024,256]{1,0:T(8,128)(2,1)} %param.12), channel_id=1, source_target_pairs={{0,32},{32,0},{64,96},{96,64},{128,160},{160,128},{192,224},{224,1... | collective-permute-start | bytes 1572872 | tf_op jit(solution)/shard_map/ppermute | solution.py:11
  19.8 11.3 %collective-permute-start.1 = (bf16[8,64,512]{2,1,0:T(8,128)(2,1)S(1)}, bf16[8,64,512]{2,1,0:T(8,128)(2,1)S(1)}, u32[]{:S(2)}, u32[]{:S(2)}) collective-permute-start(bf16[8,64,512]{2,1,0:T(8,128)(2,1)S(1)} %get-tuple-element.64), channel_id=1, source_target_pairs={{0,32},{32,0},{64,96},{96,64},{128,160},{160,128},{192,224},{224,1... | collective-permute-start | bytes 1572872 | tf_op jit(solution)/shard_map/ppermute | solution.py:11
  34.2 17.1 %all-to-all-start.1 = ((bf16[4,192,512]{2,1,0:T(8,128)(2,1)}), bf16[4,192,512]{2,1,0:T(8,128)(2,1)S(1)}, u32[]{:S(2)}, u32[]{:S(2)}) async-start(bf16[4,192,512]{2,1,0:T(8,128)(2,1)} %bitcast.110), calls=%async_computation.1 | async-start | bytes 1572864 | tf_op jit(solution)/shard_map/all_to_all | solution.py:29
  39.2 30.2 %collective-permute-start.2 = (bf16[8,64,512]{2,1,0:T(8,128)(2,1)S(1)}, bf16[8,64,512]{2,1,0:T(8,128)(2,1)S(1)}, u32[]{:S(2)}, u32[]{:S(2)}) collective-permute-start(bf16[8,64,512]{2,1,0:T(8,128)(2,1)S(1)} %get-tuple-element.20), channel_id=1, source_target_pairs={{0,32},{32,0},{64,96},{96,64},{128,160},{160,128},{192,224},{224,1... | collective-permute-start | bytes 1572872 | tf_op jit(solution)/shard_map/ppermute | solution.py:11
  52.2 29.2 %all-to-all-start.2 = ((bf16[8,24,512]{2,1,0:T(8,128)(2,1)}), bf16[8,24,512]{2,1,0:T(8,128)(2,1)S(1)}, u32[]{:S(2)}, u32[]{:S(2)}) async-start(bf16[8,24,512]{2,1,0:T(8,128)(2,1)} %bitcast.10), calls=%async_computation.2 | async-start | bytes 393216 | tf_op jit(solution)/shard_map/all_to_all | solution.py:29
  66.1 5.0 %collective-permute-start.3 = (bf16[1024,256]{1,0:T(8,128)(2,1)}, bf16[1024,256]{1,0:T(8,128)(2,1)S(1)}, u32[]{:S(2)}, u32[]{:S(2)}) collective-permute-start(bf16[1024,256]{1,0:T(8,128)(2,1)} %param.11), channel_id=1, source_target_pairs={{0,32},{32,0},{64,96},{96,64},{128,160},{160,128},{192,224},{224,1... | collective-permute-start | bytes 1572872 | tf_op jit(solution)/shard_map/ppermute | solution.py:11
  81.4 25.3 %copy-start.24 = (f32[2,1024]{1,0:T(2,128)S(1)}, f32[2,1024]{1,0:T(2,128)}, u32[]{:S(2)}) copy-start(f32[2,1024]{1,0:T(2,128)} %param.15) | copy-start | bytes 24580
  103.2 11.8 %all-to-all-start.4 = ((bf16[4,192,512]{2,1,0:T(8,128)(2,1)}), bf16[4,192,512]{2,1,0:T(8,128)(2,1)S(1)}, u32[]{:S(2)}, u32[]{:S(2)}) async-start(bf16[4,192,512]{2,1,0:T(8,128)(2,1)} %broadcast_in_dim.58), calls=%async_computation.4 | async-start | bytes 1572864 | tf_op jit(solution)/shard_map/all_to_all | solution.py:29
  122.3 26.4 %all-to-all-start.5 = ((bf16[4,192,512]{2,1,0:T(8,128)(2,1)}), bf16[4,192,512]{2,1,0:T(8,128)(2,1)}, u32[]{:S(2)}, u32[]{:S(2)}) async-start(bf16[4,192,512]{2,1,0:T(8,128)(2,1)} %bitcast.109), calls=%async_computation.5 | async-start | bytes 1572864 | tf_op jit(solution)/shard_map/all_to_all | solution.py:29
  127.2 28.2 %collective-permute-start.6 = (f32[2,1024]{1,0:T(2,128)}, f32[2,1024]{1,0:T(2,128)}, u32[]{:S(2)}, u32[]{:S(2)}) collective-permute-start(f32[2,1024]{1,0:T(2,128)} %pad_maximum_fusion.7), channel_id=1, source_target_pairs={{0,32},{32,0},{64,96},{96,64},{128,160},{160,128},{192,224},{224,1... | collective-permute-start | bytes 24584 | tf_op jit(solution)/shard_map/ppermute | solution.py:11
  137.3 6.1 %copy-start.13 = (bf16[2,192,512]{2,1,0:T(8,128)(2,1)S(1)}, bf16[2,192,512]{2,1,0:T(8,128)(2,1)}, u32[]{:S(2)}) copy-start(bf16[2,192,512]{2,1,0:T(8,128)(2,1)} %copy-done.12) | copy-start | bytes 1179652
  137.3 6.1 %copy-start.17 = (bf16[384,1024]{1,0:T(8,128)(2,1)S(1)}, bf16[384,1024]{1,0:T(8,128)(2,1)}, u32[]{:S(2)}) copy-start(bf16[384,1024]{1,0:T(8,128)(2,1)} %copy-done.16) | copy-start | bytes 2359300
  141.5 14.6 %collective-permute-start.5 = (bf16[8,64,512]{2,1,0:T(8,128)(2,1)}, bf16[8,64,512]{2,1,0:T(8,128)(2,1)}, u32[]{:S(2)}, u32[]{:S(2)}) collective-permute-start(bf16[8,64,512]{2,1,0:T(8,128)(2,1)} %fusion.12), channel_id=1, source_target_pairs={{0,32},{32,0},{64,96},{96,64},{128,160},{160,128},{192,224},{224,1... | collective-permute-start | bytes 1572872 | tf_op jit(solution)/shard_map/ppermute | solution.py:11
  146.4 12.2 %collective-permute-start.4 = (bf16[1024,256]{1,0:T(8,128)(2,1)}, bf16[1024,256]{1,0:T(8,128)(2,1)}, u32[]{:S(2)}, u32[]{:S(2)}) collective-permute-start(bf16[1024,256]{1,0:T(8,128)(2,1)} %slice.121), channel_id=1, source_target_pairs={{0,32},{32,0},{64,96},{96,64},{128,160},{160,128},{192,224},{224,1... | collective-permute-start | bytes 1572872 | tf_op jit(solution)/shard_map/ppermute | solution.py:11
  150.8 21.8 %all-to-all-start.6 = ((bf16[8,24,512]{2,1,0:T(8,128)(2,1)}), bf16[8,24,512]{2,1,0:T(8,128)(2,1)S(1)}, u32[]{:S(2)}, u32[]{:S(2)}) async-start(bf16[8,24,512]{2,1,0:T(8,128)(2,1)} %bitcast.19), calls=%async_computation.6 | async-start | bytes 393216 | tf_op jit(solution)/shard_map/all_to_all | solution.py:29
  194.3 17.9 %all-to-all-start.8 = ((bf16[4,192,512]{2,1,0:T(8,128)(2,1)}), bf16[4,192,512]{2,1,0:T(8,128)(2,1)}, u32[]{:S(2)}, u32[]{:S(2)}) async-start(bf16[4,192,512]{2,1,0:T(8,128)(2,1)} %broadcast_in_dim.63), calls=%async_computation.8 | async-start | bytes 1572864 | tf_op jit(solution)/shard_map/all_to_all | solution.py:29
  214.2 5.3 %copy-start.22 = (bf16[8,64,512]{2,1,0:T(8,128)(2,1)S(1)}, bf16[8,64,512]{2,1,0:T(8,128)(2,1)}, u32[]{:S(2)}) copy-start(bf16[8,64,512]{2,1,0:T(8,128)(2,1)} %fusion.11) | copy-start | bytes 1572868
  214.3 5.0 %collective-permute-start.7 = (bf16[8,64,512]{2,1,0:T(8,128)(2,1)S(1)}, bf16[8,64,512]{2,1,0:T(8,128)(2,1)S(1)}, u32[]{:S(2)}, u32[]{:S(2)}) collective-permute-start(bf16[8,64,512]{2,1,0:T(8,128)(2,1)S(1)} %fusion.13), channel_id=1, source_target_pairs={{0,32},{32,0},{64,96},{96,64},{128,160},{160,128},{192,224},{224,1... | collective-permute-start | bytes 1572872 | tf_op jit(solution)/shard_map/ppermute | solution.py:11
  220.7 20.5 %all-to-all-start.9 = ((bf16[8,136,512]{2,1,0:T(8,128)(2,1)}), bf16[8,136,512]{2,1,0:T(8,128)(2,1)}, u32[]{:S(2)}, u32[]{:S(2)}) async-start(bf16[8,136,512]{2,1,0:T(8,128)(2,1)} %pad_maximum_fusion), calls=%async_computation.9 | async-start | bytes 2228224 | tf_op jit(solution)/shard_map/all_to_all | solution.py:29
  227.0 4.7 %collective-permute-start.8 = (bf16[1024,256]{0,1:T(8,128)(2,1)S(1)}, bf16[1024,256]{0,1:T(8,128)(2,1)S(1)}, u32[]{:S(2)}, u32[]{:S(2)}) collective-permute-start(bf16[1024,256]{0,1:T(8,128)(2,1)S(1)} %slice.120), channel_id=1, source_target_pairs={{0,32},{32,0},{64,96},{96,64},{128,160},{160,128},{192,224},{224,1... | collective-permute-start | bytes 1572872 | tf_op jit(solution)/shard_map/ppermute | solution.py:11
  (19 other events, 43.1 us)

commit v6 on v5

v6 whole, which is shorter than its diff:
```python
import functools

import jax
import jax.numpy as jnp
from jax import lax
from jax.experimental import pallas as pl
from jax.experimental.pallas import tpu as pltpu
from jax.sharding import PartitionSpec as P

FAR = 2
CHUNK = 256
PARAMS = pltpu.CompilerParams(vmem_limit_bytes=32 * 1024 * 1024)


def core_swap(value):
    pairs = [(source, source ^ 1) for source in range(lax.axis_size("dom"))]
    return lax.ppermute(value, "dom", pairs)


def near_groups():
    half = lax.axis_size("feat") // FAR
    return [[far * half + 2 * pair + bit for far in range(FAR) for bit in range(2)] for pair in range(half // 2)]


def ring_groups():
    half = lax.axis_size("feat") // FAR
    return [[far * half + 2 * step + bit for step in range(half // 2)] for far in range(FAR) for bit in range(2)]


def chip_groups():
    return [list(range(core, lax.axis_size("dom"), 2)) for core in range(2)]


def exchange(value, axis, groups):
    return lax.all_to_all(value, axis, 0, 0, axis_index_groups=groups, tiled=True)


def gathered(value, axis, groups):
    members = len(groups[0])
    repeated = jnp.broadcast_to(value[None], (members, *value.shape))
    return exchange(repeated.reshape(members * value.shape[0], value.shape[1]), axis, groups)


def summed(value, axis, groups):
    pieces = exchange(value, axis, groups).reshape(len(groups[0]), -1, value.shape[1])
    return jnp.sum(pieces.astype(jnp.float32), axis=0).astype(jnp.bfloat16)


def dot(left_side, right_side):
    return jnp.dot(left_side, right_side, preferred_element_type=jnp.float32)


def transposed_dot(left_side, right_side):
    return lax.dot_general(
        left_side, right_side, (((0,), (0,)), ((), ())), preferred_element_type=jnp.float32
    )


def cross_dot(left_side, right_side):
    return lax.dot_general(
        left_side, right_side, (((1,), (1,)), ((), ())), preferred_element_type=jnp.float32
    )


def middle_kernel(sums, x0, masked, own_u, other_u, map_v, bias, both, layer_one, first_adj, kept, bias_sum, total):
    low, wide = jnp.bfloat16, jnp.float32
    rows, half_rank = x0.shape[0], own_u.shape[1]
    step = pl.program_id(0)

    @pl.when(step == 0)
    def _():
        total[...] = jnp.zeros_like(total)

    inputs = x0[...].astype(wide)
    first_gate = (
        cross_dot(sums[:rows, :half_rank], own_u[...])
        + cross_dot(sums[:rows, half_rank:], other_u[...])
        + bias[:1, :]
    )
    layer = (inputs * first_gate + inputs).astype(low)
    layer_grad = masked[...].astype(wide) + cross_dot(sums[rows:, :], map_v[...])
    adj = (layer_grad * inputs).astype(low)
    layer_one[...] = layer
    first_adj[...] = adj
    kept[...] = layer_grad * (first_gate + 1.0)
    bias_sum[...] = jnp.sum(adj.astype(wide), axis=0, keepdims=True)
    total[:rows, :] += dot(layer, map_v[...])
    total[rows:, :half_rank] += dot(adj, own_u[...])
    total[rows:, half_rank:] += dot(adj, other_u[...])

    @pl.when(step == pl.num_programs(0) - 1)
    def _():
        both[...] = total[...].astype(low)


def middle(sums, x0, masked, own_u, other_u, map_v, bias):
    low, wide = jnp.bfloat16, jnp.float32
    rows, width = x0.shape
    rank = sums.shape[1]
    across = pl.BlockSpec((rows, CHUNK), lambda i: (0, i))
    half = pl.BlockSpec((CHUNK, rank // 2), lambda i: (i, 0))
    fixed = pl.BlockSpec((2 * rows, rank), lambda i: (0, 0))
    return pl.pallas_call(
        middle_kernel,
        grid=(width // CHUNK,),
        in_specs=[
            fixed,
            across,
            across,
            half,
            half,
            pl.BlockSpec((CHUNK, rank), lambda i: (i, 0)),
            pl.BlockSpec((2, CHUNK), lambda i: (0, i)),
        ],
        out_specs=[fixed, across, across, across, pl.BlockSpec((1, CHUNK), lambda i: (0, i))],
        out_shape=[
            jax.ShapeDtypeStruct((2 * rows, rank), low),
            jax.ShapeDtypeStruct((rows, width), low),
            jax.ShapeDtypeStruct((rows, width), low),
            jax.ShapeDtypeStruct((rows, width), wide),
            jax.ShapeDtypeStruct((1, width), wide),
        ],
        scratch_shapes=[pltpu.VMEM((2 * rows, rank), wide)],
        compiler_params=PARAMS,
    )(sums, x0, masked, own_u, other_u, map_v, bias)


def split_rows(core, term, keep, give):
    lines = keep.shape[1]
    for pair in range(keep.shape[0]):
        first = term[2 * pair * lines : (2 * pair + 1) * lines]
        second = term[(2 * pair + 1) * lines : (2 * pair + 2) * lines]
        keep[pair] = jnp.where(core == 0, first, second)
        give[pair] = jnp.where(core == 0, second, first).astype(give.dtype)


def early_kernel(place, first_adj, layer_one, sums, keep_u, give_u, keep_v, give_v):
    rows, half_rank = first_adj.shape[0], keep_u.shape[1]
    keep_u[...] = transposed_dot(first_adj[...], sums[:rows, :half_rank])
    give_u[...] = transposed_dot(first_adj[...], sums[:rows, half_rank:]).astype(give_u.dtype)
    split_rows(place[0], transposed_dot(layer_one[...], sums[rows:, :]), keep_v, give_v)


def late_kernel(place, second_adj, sums, keep, give):
    rows = second_adj.shape[0]
    split_rows(place[0], transposed_dot(second_adj[...], sums[:rows, :]), keep, give)


def terms(kernel, core, acts, sums, lines, with_expert):
    low, wide = jnp.bfloat16, jnp.float32
    rows, width = acts[0].shape
    rank = sums.shape[1]
    pairs = CHUNK // (2 * lines)
    expert = pl.BlockSpec((CHUNK, rank // 2), lambda i, place: (i, 0))
    shared = pl.BlockSpec((pairs, lines, rank), lambda i, place: (i, 0, 0))
    whole_expert, whole_shared = (width, rank // 2), (width // (2 * lines), lines, rank)
    specs = ([expert] * 2 if with_expert else []) + [shared] * 2
    shapes = ([whole_expert] * 2 if with_expert else []) + [whole_shared] * 2
    return pl.pallas_call(
        kernel,
        grid_spec=pltpu.PrefetchScalarGridSpec(
            num_scalar_prefetch=1,
            grid=(width // CHUNK,),
            in_specs=[pl.BlockSpec((rows, CHUNK), lambda i, place: (0, i))] * len(acts)
            + [pl.BlockSpec(sums.shape, lambda i, place: (0, 0))],
            out_specs=specs,
        ),
        out_shape=[jax.ShapeDtypeStruct(shape, (wide, low)[i % 2]) for i, shape in enumerate(shapes)],
        compiler_params=PARAMS,
    )(core[None], *acts, sums)


def last_kernel(lines, taken, grad_su, grad_sv, grad_bias):
    low, wide = jnp.bfloat16, jnp.float32
    total = jnp.sum(taken[...].astype(wide), axis=0)
    grad_su[...] = total[:lines].astype(low)
    grad_sv[...] = total[lines : 2 * lines].astype(low)
    sums = total[2 * lines :]
    half = sums.shape[0] // 2
    sums = sums[:half] + sums[half:]
    rank = sums.shape[1]
    per_row = half // 2
    for i in range(half):
        column = (i % per_row) * rank
        grad_bias[i // per_row : i // per_row + 1, column : column + rank] = sums[i : i + 1]


def last_sum(taken, lines, width):
    rank = taken.shape[2]
    return pl.pallas_call(
        functools.partial(last_kernel, lines),
        out_shape=[
            jax.ShapeDtypeStruct((lines, rank), jnp.bfloat16),
            jax.ShapeDtypeStruct((lines, rank), jnp.bfloat16),
            jax.ShapeDtypeStruct((2, width), jnp.float32),
        ],
        compiler_params=PARAMS,
    )(taken)


def local(x0, cotangent, domain_ids, expert_u, expert_v, shared_u, shared_v, bias):
    low = jnp.bfloat16
    wide = jnp.float32
    rows, width = x0.shape
    half_rank = expert_u.shape[1]
    rank = 2 * half_rank
    chips = lax.axis_size("dom") // 2
    lines = shared_u.shape[0]
    domain = lax.axis_index("dom") // 2
    core = lax.axis_index("dom") % 2

    own_maps = gathered(jnp.concatenate([shared_u, shared_v], 0), "dom", chip_groups())
    own_maps = own_maps.reshape(chips, 2, lines, rank)
    other_v = core_swap(expert_v)
    full_v = jnp.concatenate([expert_v, other_v], 1)

    def whole(own, other):
        pair = [jnp.where(core == 0, own, other), jnp.where(core == 0, other, own)]
        return jnp.stack(pair, 1).reshape(width, rank)

    masked = jnp.where((domain_ids == domain)[:, None], cotangent, jnp.zeros_like(cotangent))
    second_adj = (masked.astype(wide) * x0.astype(wide)).astype(low)
    bias_two = jnp.sum(second_adj.astype(wide), axis=0, keepdims=True)

    first_part = dot(x0, full_v).astype(low)
    whole_su = whole(own_maps[:, 0], core_swap(own_maps[:, 0]))
    back_two_part = dot(second_adj, whole_su).astype(low)
    both = jnp.concatenate([first_part, back_two_part], 0)
    own_sv, expert_u, both = lax.optimization_barrier((own_maps[:, 1], expert_u, both))
    near, ring = near_groups(), ring_groups()
    part = summed(summed(both, "feat", near), "feat", ring)
    whole_sv = whole(own_sv, core_swap(own_sv))
    other_u = core_swap(expert_u)
    part, whole_sv, other_u, masked = lax.optimization_barrier((part, whole_sv, other_u, masked))
    sums = gathered(gathered(part, "feat", ring), "feat", near)

    both, layer_one, first_adj, kept, bias_one = middle(sums, x0, masked, expert_u, other_u, whole_sv, bias)
    part = summed(both, "feat", near)
    part, sums, first_adj, layer_one = lax.optimization_barrier((part, sums, first_adj, layer_one))
    keep_eu, give_eu, keep_sv, give_sv = terms(early_kernel, core, [first_adj, layer_one], sums, lines, True)
    part = summed(part, "feat", ring)
    peer_eu, peer_sv = core_swap(give_eu), core_swap(give_sv)
    bias_terms = jnp.concatenate([bias_one, bias_two], 0)
    bias_terms = bias_terms + core_swap(bias_terms)
    part, peer_eu, peer_sv, bias_terms = lax.optimization_barrier((part, peer_eu, peer_sv, bias_terms))
    part = gathered(part, "feat", ring)
    bias_high = bias_terms.astype(low)
    bias_rest = (bias_terms - bias_high.astype(wide)).astype(low)
    bias_lines = jnp.stack([bias_high, bias_rest]).reshape(4 * width // rank, rank)
    bias_lines = jnp.broadcast_to(bias_lines[None], (chips, *bias_lines.shape))
    grad_eu = (keep_eu + peer_eu.astype(wide)).astype(low)
    part_sv = (keep_sv + peer_sv.astype(wide)).astype(low)
    sent = jnp.concatenate([jnp.zeros_like(part_sv), part_sv, bias_lines], 1)
    part, sent, grad_eu = lax.optimization_barrier((part, sent, grad_eu))
    sums = gathered(part, "feat", near)

    keep_su, give_su = terms(late_kernel, core, [second_adj], sums, lines, False)
    part_su = (keep_su + core_swap(give_su).astype(wide)).astype(low)
    sent = lax.dynamic_update_slice(sent, part_su, (0, 0, 0))
    sent, sums = lax.optimization_barrier((sent, sums))
    taken = exchange(sent.reshape(-1, rank), "dom", chip_groups()).reshape(sent.shape)
    second_rank, back_one = sums[:rows], sums[rows:]
    partial_ev = transposed_dot(x0, back_one)
    peer_ev = core_swap(partial_ev[:, half_rank:].astype(low))
    grad_ev = (partial_ev[:, :half_rank] + peer_ev.astype(wide)).astype(low)
    second_gate = cross_dot(second_rank, whole_su) + bias[1][None, :]
    grad_inputs = (masked.astype(wide) * second_gate + kept + cross_dot(back_one, full_v)).astype(low)
    grad_su, grad_sv, grad_bias = last_sum(taken, lines, width)
    return (grad_inputs, grad_eu, grad_ev, grad_su, grad_sv, grad_bias)


def solution(mesh):
    placed = (
        P("dom", "feat"),
        P("dom", "feat"),
        P("dom"),
        P("feat", "dom"),
        P("feat", "dom"),
        P(("feat", "dom"), None),
        P(("feat", "dom"), None),
        P(None, "feat"),
    )
    return jax.shard_map(
        local,
        mesh=mesh,
        in_specs=placed,
        out_specs=(
            P("dom", "feat"),
            P("feat", "dom"),
            P("feat", "dom"),
            P(("feat", "dom"), None),
            P(("feat", "dom"), None),
            P(None, "feat"),
        ),
        check_vma=False,
    )
```

time: 246 us -> 233 us (0.947)
  blocking collectives: 40.9 us -> 55.5 us
  waiting for transfers between devices: 61.5 us -> 47.6 us
  local copies, waits for them, and re-layouts: 23.4 us -> 13.5 us
  Pallas kernels: 0 us -> 9.72 us
  matrix products: 12.4 us -> 3.99 us
  other arithmetic: 19.5 us -> 12.5 us
  starting transfers between devices: 84.8 us -> 87.8 us
    all_to_all x2 -> x4, blocking collectives: 40.9 us -> 55.5 us  [exchange(): lax.all_to_all(value, axis, 0, 0, axis_index_groups=groups, tiled=True)]
    all_to_all x8 -> x6, waiting for transfers between devices: 59.5 us -> 45.3 us  [exchange(): lax.all_to_all(value, axis, 0, 0, axis_index_groups=groups, tiled=True)]
    pallas_call x0 -> x4, Pallas kernels: none -> 9.72 us  [the longest x1 4.53 us: middle(): pl.pallas_call(middle_kernel, grid=(width // CHUNK,), in_specs=[fixed, ac...]
    dot_general x4 -> x1, matrix products: 5.33 us -> 0.73 us  [transposed_dot(): lax.dot_general(left_side, right_side, (((0,), (0,)), ((), ())), preferre...]
    dot_general x2 -> x0, local copies, waits for them, and re-layouts: 4.59 us -> none  [transposed_dot(): lax.dot_general(left_side, right_side, (((0,), (0,)), ((), ())), preferre...]
    concatenate x3 -> x2, other arithmetic: 4.22 us -> 1.27 us  [the longest x1 1.25 us: local(): sent = jnp.concatenate([jnp.zeros_like(part_sv), part_sv, bias_lines], 1)]
    slice x5 -> x1, local copies, waits for them, and re-layouts: 2.9 us -> 0.07 us  [local(): peer_ev = core_swap(partial_ev[:, half_rank:].astype(low))]
    dot_general x4 -> x2, matrix products: 4.84 us -> 2.13 us  [cross_dot(): lax.dot_general(left_side, right_side, (((1,), (1,)), ((), ())), preferre...]
  transfers between devices with their start and end apart: 17 -> 15, of which waited for: 9 -> 7; matrix products, arithmetic and copies ran while one was open for 12% -> 7% of each run, Pallas kernels for 0% -> 1%
where the time goes in v6:
time: 233 us; the launch traced here: 232 us
  starting transfers between devices  87.8 us (38%)
  blocking collectives  55.5 us (24%)
  waiting for transfers between devices  47.6 us (20%)
  local copies, waits for them, and re-layouts  13.5 us (6%)
  other arithmetic  12.5 us (5%)
  Pallas kernels  9.72 us (4%)
  matrix products  3.99 us (2%)
    all_to_all x4, blocking collectives, exchange(): lax.all_to_all(value, axis, 0, 0, axis_index_groups=groups, tiled=True)  55.5 us
    all_to_all x6, starting transfers between devices, exchange(): lax.all_to_all(value, axis, 0, 0, axis_index_groups=groups, tiled=True)  49.1 us
    all_to_all x6, waiting for transfers between devices, exchange(): lax.all_to_all(value, axis, 0, 0, axis_index_groups=groups, tiled=True)  45.3 us
    ppermute x9, starting transfers between devices, core_swap(): return lax.ppermute(value, 'dom', pairs)  38.7 us
    unnamed x42, local copies, waits for them, and re-layouts  9.33 us
  transfers between devices with their start and end apart: 15, of which 7 were waited for; matrix products, arithmetic and copies ran while one was open for 7% of the time, Pallas kernels for 1%

profile of v6, /device:TPU:1, one launch (start us, length us, event | category | flops | bytes accessed | tf_op | source)
XLA Modules:
  0.0 231.9 jit_solution(12854509086427590351)
XLA Ops:
  2.6 5.9 %all-to-all-start = ((bf16[8,128,512]{2,1,0:T(8,128)(2,1)}), bf16[8,128,512]{2,1,0:T(8,128)(2,1)S(1)}, u32[]{:S(2)}, u32[]{:S(2)}) async-start(bf16[8,128,512]{2,1,0:T(8,128)(2,1)} %broadcast_in_dim.32), calls=%async_computation | async-start | bytes 2097152 | tf_op jit(solution)/shard_map/all_to_all | solution.py:35
  8.6 6.4 %collective-permute-start = (bf16[1024,256]{1,0:T(8,128)(2,1)}, bf16[1024,256]{1,0:T(8,128)(2,1)}, u32[]{:S(2)}, u32[]{:S(2)}) collective-permute-start(bf16[1024,256]{1,0:T(8,128)(2,1)} %param.12), channel_id=1, source_target_pairs={{0,32},{32,0},{64,96},{96,64},{128,160},{160,128},{192,224},{224,1... | collective-permute-start | bytes 1572872 | tf_op jit(solution)/shard_map/ppermute | solution.py:17
  16.6 3.1 %all-to-all-done = bf16[8,128,512]{2,1,0:T(8,128)(2,1)S(1)} async-done(((bf16[8,128,512]{2,1,0:T(8,128)(2,1)}), bf16[8,128,512]{2,1,0:T(8,128)(2,1)S(1)}, u32[]{:S(2)}, u32[]{:S(2)}) %all-to-all-start) | async-done | bytes 1048608 | tf_op jit(solution)/shard_map/all_to_all | solution.py:35
  20.5 7.5 %collective-permute-start.1 = (bf16[8,64,512]{2,1,0:T(8,128)(2,1)S(1)}, bf16[8,64,512]{2,1,0:T(8,128)(2,1)S(1)}, u32[]{:S(2)}, u32[]{:S(2)}) collective-permute-start(bf16[8,64,512]{2,1,0:T(8,128)(2,1)S(1)} %get-tuple-element.99), channel_id=1, source_target_pairs={{0,32},{32,0},{64,96},{96,64},{128,160},{160,128},{192,224},{224,1... | collective-permute-start | bytes 1572872 | tf_op jit(solution)/shard_map/ppermute | solution.py:17
  33.7 5.1 %all-to-all-start.1 = ((bf16[4,192,512]{2,1,0:T(8,128)(2,1)}), bf16[4,192,512]{2,1,0:T(8,128)(2,1)S(1)}, u32[]{:S(2)}, u32[]{:S(2)}) async-start(bf16[4,192,512]{2,1,0:T(8,128)(2,1)} %bitcast.59), calls=%async_computation.1 | async-start | bytes 1572864 | tf_op jit(solution)/shard_map/all_to_all | solution.py:35
  41.0 9.9 %all-to-all-done.1 = bf16[4,192,512]{2,1,0:T(8,128)(2,1)S(1)} async-done(((bf16[4,192,512]{2,1,0:T(8,128)(2,1)}), bf16[4,192,512]{2,1,0:T(8,128)(2,1)S(1)}, u32[]{:S(2)}, u32[]{:S(2)}) %all-to-all-start.1) | async-done | bytes 786464 | tf_op jit(solution)/shard_map/all_to_all | solution.py:35
  51.7 13.9 %all-to-all-start.2 = ((bf16[8,24,512]{2,1,0:T(8,128)(2,1)}), bf16[8,24,512]{2,1,0:T(8,128)(2,1)S(1)}, u32[]{:S(2)}, u32[]{:S(2)}) async-start(bf16[8,24,512]{2,1,0:T(8,128)(2,1)} %bitcast.8), calls=%async_computation.2 | async-start | bytes 393216 | tf_op jit(solution)/shard_map/all_to_all | solution.py:35
  65.6 3.3 %collective-permute-start.3 = (bf16[1024,256]{1,0:T(8,128)(2,1)S(1)}, bf16[1024,256]{1,0:T(8,128)(2,1)}, u32[]{:S(2)}, u32[]{:S(2)}) collective-permute-start(bf16[1024,256]{1,0:T(8,128)(2,1)S(1)} %copy-done.10), channel_id=1, source_target_pairs={{0,32},{32,0},{64,96},{96,64},{128,160},{160,128},{192,224},{224,1... | collective-permute-start | bytes 1572872 | tf_op jit(solution)/shard_map/ppermute | solution.py:17
  70.4 10.5 %all-to-all-done.2 = bf16[8,24,512]{2,1,0:T(8,128)(2,1)S(1)} async-done(((bf16[8,24,512]{2,1,0:T(8,128)(2,1)}), bf16[8,24,512]{2,1,0:T(8,128)(2,1)S(1)}, u32[]{:S(2)}, u32[]{:S(2)}) %all-to-all-start.2) | async-done | bytes 196640 | tf_op jit(solution)/shard_map/all_to_all | solution.py:35
  81.1 20.9 %all_to_all.79 = bf16[8,24,512]{2,1,0:T(8,128)(2,1)S(1)} all-to-all(bf16[8,24,512]{2,1,0:T(8,128)(2,1)S(1)} %broadcast_in_dim.64), channel_id=1, replica_groups={{0,2,4,6,8,10,12,14},{1,3,5,7,9,11,13,15},{16,18,20,22,24,26,28,30},{17..., dimensions={0} | all-to-all | bytes 393216 | tf_op jit(solution)/shard_map/all_to_all | solution.py:35
  102.0 12.1 %all_to_all.80 = bf16[4,192,512]{2,1,0:T(8,128)(2,1)S(1)} all-to-all(bf16[4,192,512]{2,1,0:T(8,128)(2,1)S(1)} %broadcast_in_dim.66), channel_id=1, replica_groups={{0,1,16,17},{2,3,18,19},{4,5,20,21},{6,7,22,23},{8,9,24,25},{10,11,26,2..., dimensions={0} | all-to-all | bytes 1572864 | tf_op jit(solution)/shard_map/all_to_all | solution.py:35
  114.1 4.5 %shard_map.127 = (bf16[768,512]{1,0:T(8,128)(2,1)S(1)}, bf16[384,1024]{1,0:T(8,128)(2,1)S(1)}, bf16[384,1024]{1,0:T(8,128)(2,1)S(1)}, f32[384,1024]{1,0:T(8,128)S(1)}, f32[1,1024]{1,0:T(1,128)S(1)}) custom-call(bf16[768,512]{1,0:T(8,128)(2,1)S(1)} %bitcast.51, bf16[384,1024]{1,0:T(8,128)(2,1)S(1)} %copy-done, ...), custom_call_target="tpu_custom_call" | custom-call | tf_op jit(solution)/shard_map/pallas_call | solution.py:103
  121.6 11.3 %all_to_all.81 = bf16[4,192,512]{2,1,0:T(8,128)(2,1)S(1)} all-to-all(bf16[4,192,512]{2,1,0:T(8,128)(2,1)S(1)} %bitcast.54), channel_id=1, replica_groups={{0,1,16,17},{2,3,18,19},{4,5,20,21},{6,7,22,23},{8,9,24,25},{10,11,26,2..., dimensions={0} | all-to-all | bytes 1572864 | tf_op jit(solution)/shard_map/all_to_all | solution.py:35
  133.7 8.8 %all-to-all-start.6 = ((bf16[8,24,512]{2,1,0:T(8,128)(2,1)}), bf16[8,24,512]{2,1,0:T(8,128)(2,1)}, u32[]{:S(2)}, u32[]{:S(2)}) async-start(bf16[8,24,512]{2,1,0:T(8,128)(2,1)} %bitcast.15), calls=%async_computation.6 | async-start | bytes 393216 | tf_op jit(solution)/shard_map/all_to_all | solution.py:35
  144.8 3.0 %shard_map.128 = (f32[1024,256]{1,0:T(8,128)S(1)}, bf16[1024,256]{1,0:T(8,128)(2,1)}, f32[8,64,512]{2,1,0:T(8,128)S(1)}, bf16[8,64,512]{2,1,0:T(8,128)(2,1)}) custom-call(s32[1]{0:T(128)} %bitcast.16.place, bf16[384,1024]{1,0:T(8,128)(2,1)S(1)} %copy-done.9, bf16[384,1024]{1,0:T(8,128)(2,1)S(1)} %copy-done.7, bf16[768,512]{1,0:T(8,128)(2,1)S(1)} %bitcast.52), custom_call_target="tpu_custom_call" | custom-call | tf_op jit(solution)/shard_map/pallas_call | solution.py:159
  148.7 5.7 %collective-permute-start.4 = (bf16[1024,256]{1,0:T(8,128)(2,1)}, bf16[1024,256]{1,0:T(8,128)(2,1)S(1)}, u32[]{:S(2)}, u32[]{:S(2)}) collective-permute-start(bf16[1024,256]{1,0:T(8,128)(2,1)} %get-tuple-element.54), channel_id=1, source_target_pairs={{0,32},{32,0},{64,96},{96,64},{128,160},{160,128},{192,224},{224,1... | collective-permute-start | bytes 1572872 | tf_op jit(solution)/shard_map/ppermute | solution.py:17
  156.4 2.4 %collective-permute-start.6 = (f32[2,1024]{1,0:T(2,128)S(1)}, f32[2,1024]{1,0:T(2,128)S(1)}, u32[]{:S(2)}, u32[]{:S(2)}) collective-permute-start(f32[2,1024]{1,0:T(2,128)S(1)} %pad_maximum_fusion.5), channel_id=1, source_target_pairs={{0,32},{32,0},{64,96},{96,64},{128,160},{160,128},{192,224},{224,1... | collective-permute-start | bytes 24584 | tf_op jit(solution)/shard_map/ppermute | solution.py:17
  161.4 11.7 %all-to-all-start.7 = ((bf16[8,24,512]{2,1,0:T(8,128)(2,1)}), bf16[8,24,512]{2,1,0:T(8,128)(2,1)S(1)}, u32[]{:S(2)}, u32[]{:S(2)}) async-start(bf16[8,24,512]{2,1,0:T(8,128)(2,1)} %broadcast_in_dim.69), calls=%async_computation.7 | async-start | bytes 393216 | tf_op jit(solution)/shard_map/all_to_all | solution.py:35
  177.0 12.2 %all-to-all-done.7 = bf16[8,24,512]{2,1,0:T(8,128)(2,1)S(1)} async-done(((bf16[8,24,512]{2,1,0:T(8,128)(2,1)}), bf16[8,24,512]{2,1,0:T(8,128)(2,1)S(1)}, u32[]{:S(2)}, u32[]{:S(2)}) %all-to-all-start.7) | async-done | bytes 196640 | tf_op jit(solution)/shard_map/all_to_all | solution.py:35
  189.3 11.3 %all_to_all.82 = bf16[4,192,512]{2,1,0:T(8,128)(2,1)S(1)} all-to-all(bf16[4,192,512]{2,1,0:T(8,128)(2,1)S(1)} %broadcast_in_dim.73), channel_id=1, replica_groups={{0,1,16,17},{2,3,18,19},{4,5,20,21},{6,7,22,23},{8,9,24,25},{10,11,26,2..., dimensions={0} | all-to-all | bytes 1572864 | tf_op jit(solution)/shard_map/all_to_all | solution.py:35
  202.1 6.8 %collective-permute-start.7 = (bf16[8,64,512]{2,1,0:T(8,128)(2,1)S(1)}, bf16[8,64,512]{2,1,0:T(8,128)(2,1)S(1)}, u32[]{:S(2)}, u32[]{:S(2)}) collective-permute-start(bf16[8,64,512]{2,1,0:T(8,128)(2,1)S(1)} %get-tuple-element.66), channel_id=1, source_target_pairs={{0,32},{32,0},{64,96},{96,64},{128,160},{160,128},{192,224},{224,1... | collective-permute-start | bytes 1572872 | tf_op jit(solution)/shard_map/ppermute | solution.py:17
  211.4 3.6 %all-to-all-start.9 = ((bf16[8,136,512]{2,1,0:T(8,128)(2,1)}), bf16[8,136,512]{2,1,0:T(8,128)(2,1)S(1)}, u32[]{:S(2)}, u32[]{:S(2)}) async-start(bf16[8,136,512]{2,1,0:T(8,128)(2,1)} %fusion.2), calls=%async_computation.9 | async-start | bytes 2228224 | tf_op jit(solution)/shard_map/all_to_all | solution.py:35
  215.8 2.4 %collective-permute-start.8 = (bf16[1024,256]{0,1:T(8,128)(2,1)S(1)}, bf16[1024,256]{0,1:T(8,128)(2,1)S(1)}, u32[]{:S(2)}, u32[]{:S(2)}) collective-permute-start(bf16[1024,256]{0,1:T(8,128)(2,1)S(1)} %slice.50), channel_id=1, source_target_pairs={{0,32},{32,0},{64,96},{96,64},{128,160},{160,128},{192,224},{224,1... | collective-permute-start | bytes 1572872 | tf_op jit(solution)/shard_map/ppermute | solution.py:17
  221.6 9.5 %all-to-all-done.9.taken = bf16[8,136,512]{2,1,0:T(8,128)(2,1)S(1)} async-done(((bf16[8,136,512]{2,1,0:T(8,128)(2,1)}), bf16[8,136,512]{2,1,0:T(8,128)(2,1)S(1)}, u32[]{:S(2)}, u32[]{:S(2)}) %all-to-all-start.9) | async-done | bytes 1114144 | tf_op jit(solution)/shard_map/all_to_all | solution.py:35
  (97 shorter events, 38.6 us)
Async XLA Ops:
  1.5 13.5 %copy-start.19 = (s32[384]{0:T(512)S(1)}, s32[384]{0:T(512)}, u32[]{:S(2)}) copy-start(s32[384]{0:T(512)} %param.10) | copy-start | bytes 4612
  1.5 13.5 %copy-start = (bf16[384,1024]{1,0:T(8,128)(2,1)S(1)}, bf16[384,1024]{1,0:T(8,128)(2,1)}, u32[]{:S(2)}) copy-start(bf16[384,1024]{1,0:T(8,128)(2,1)} %x0.1) | copy-start | bytes 2359300
  2.6 17.0 %all-to-all-start = ((bf16[8,128,512]{2,1,0:T(8,128)(2,1)}), bf16[8,128,512]{2,1,0:T(8,128)(2,1)S(1)}, u32[]{:S(2)}, u32[]{:S(2)}) async-start(bf16[8,128,512]{2,1,0:T(8,128)(2,1)} %broadcast_in_dim.32), calls=%async_computation | async-start | bytes 2097152 | tf_op jit(solution)/shard_map/all_to_all | solution.py:35
  8.6 20.6 %collective-permute-start = (bf16[1024,256]{1,0:T(8,128)(2,1)}, bf16[1024,256]{1,0:T(8,128)(2,1)}, u32[]{:S(2)}, u32[]{:S(2)}) collective-permute-start(bf16[1024,256]{1,0:T(8,128)(2,1)} %param.12), channel_id=1, source_target_pairs={{0,32},{32,0},{64,96},{96,64},{128,160},{160,128},{192,224},{224,1... | collective-permute-start | bytes 1572872 | tf_op jit(solution)/shard_map/ppermute | solution.py:17
  16.6 15.6 %copy-start.1 = (bf16[384,1024]{1,0:T(8,128)(2,1)}, bf16[384,1024]{1,0:T(8,128)(2,1)S(1)}, u32[]{:S(2)}) copy-start(bf16[384,1024]{1,0:T(8,128)(2,1)S(1)} %get-tuple-element.93.second_adj) | copy-start | bytes 2359300
  20.5 11.3 %collective-permute-start.1 = (bf16[8,64,512]{2,1,0:T(8,128)(2,1)S(1)}, bf16[8,64,512]{2,1,0:T(8,128)(2,1)S(1)}, u32[]{:S(2)}, u32[]{:S(2)}) collective-permute-start(bf16[8,64,512]{2,1,0:T(8,128)(2,1)S(1)} %get-tuple-element.99), channel_id=1, source_target_pairs={{0,32},{32,0},{64,96},{96,64},{128,160},{160,128},{192,224},{224,1... | collective-permute-start | bytes 1572872 | tf_op jit(solution)/shard_map/ppermute | solution.py:17
  33.7 32.0 %copy-start.10 = (bf16[1024,256]{1,0:T(8,128)(2,1)S(1)}, bf16[1024,256]{1,0:T(8,128)(2,1)}, u32[]{:S(2)}) copy-start(bf16[1024,256]{1,0:T(8,128)(2,1)} %own_u) | copy-start | bytes 1572868
  33.7 17.2 %all-to-all-start.1 = ((bf16[4,192,512]{2,1,0:T(8,128)(2,1)}), bf16[4,192,512]{2,1,0:T(8,128)(2,1)S(1)}, u32[]{:S(2)}, u32[]{:S(2)}) async-start(bf16[4,192,512]{2,1,0:T(8,128)(2,1)} %bitcast.59), calls=%async_computation.1 | async-start | bytes 1572864 | tf_op jit(solution)/shard_map/all_to_all | solution.py:35
  38.8 30.2 %collective-permute-start.2 = (bf16[8,64,512]{2,1,0:T(8,128)(2,1)}, bf16[8,64,512]{2,1,0:T(8,128)(2,1)}, u32[]{:S(2)}, u32[]{:S(2)}) collective-permute-start(bf16[8,64,512]{2,1,0:T(8,128)(2,1)} %get-tuple-element.41), channel_id=1, source_target_pairs={{0,32},{32,0},{64,96},{96,64},{128,160},{160,128},{192,224},{224,1... | collective-permute-start | bytes 1572872 | tf_op jit(solution)/shard_map/ppermute | solution.py:17
  51.7 29.2 %all-to-all-start.2 = ((bf16[8,24,512]{2,1,0:T(8,128)(2,1)}), bf16[8,24,512]{2,1,0:T(8,128)(2,1)S(1)}, u32[]{:S(2)}, u32[]{:S(2)}) async-start(bf16[8,24,512]{2,1,0:T(8,128)(2,1)} %bitcast.8), calls=%async_computation.2 | async-start | bytes 393216 | tf_op jit(solution)/shard_map/all_to_all | solution.py:35
  65.6 15.4 %collective-permute-start.3 = (bf16[1024,256]{1,0:T(8,128)(2,1)S(1)}, bf16[1024,256]{1,0:T(8,128)(2,1)}, u32[]{:S(2)}, u32[]{:S(2)}) collective-permute-start(bf16[1024,256]{1,0:T(8,128)(2,1)S(1)} %copy-done.10), channel_id=1, source_target_pairs={{0,32},{32,0},{64,96},{96,64},{128,160},{160,128},{192,224},{224,1... | collective-permute-start | bytes 1572872 | tf_op jit(solution)/shard_map/ppermute | solution.py:17
  81.0 33.1 %copy-start.11 = (bf16[1024,256]{1,0:T(8,128)(2,1)S(1)}, bf16[1024,256]{1,0:T(8,128)(2,1)}, u32[]{:S(2)}) copy-start(bf16[1024,256]{1,0:T(8,128)(2,1)} %own_u) | copy-start | bytes 1572868
  81.0 33.1 %copy-start.12 = (f32[2,1024]{1,0:T(2,128)S(1)}, f32[2,1024]{1,0:T(2,128)}, u32[]{:S(2)}) copy-start(f32[2,1024]{1,0:T(2,128)} %bias.1) | copy-start | bytes 24580
  133.7 26.0 %all-to-all-start.6 = ((bf16[8,24,512]{2,1,0:T(8,128)(2,1)}), bf16[8,24,512]{2,1,0:T(8,128)(2,1)}, u32[]{:S(2)}, u32[]{:S(2)}) async-start(bf16[8,24,512]{2,1,0:T(8,128)(2,1)} %bitcast.15), calls=%async_computation.6 | async-start | bytes 393216 | tf_op jit(solution)/shard_map/all_to_all | solution.py:35
  148.7 11.9 %collective-permute-start.4 = (bf16[1024,256]{1,0:T(8,128)(2,1)}, bf16[1024,256]{1,0:T(8,128)(2,1)S(1)}, u32[]{:S(2)}, u32[]{:S(2)}) collective-permute-start(bf16[1024,256]{1,0:T(8,128)(2,1)} %get-tuple-element.54), channel_id=1, source_target_pairs={{0,32},{32,0},{64,96},{96,64},{128,160},{160,128},{192,224},{224,1... | collective-permute-start | bytes 1572872 | tf_op jit(solution)/shard_map/ppermute | solution.py:17
  154.5 6.2 %collective-permute-start.5 = (bf16[8,64,512]{2,1,0:T(8,128)(2,1)}, bf16[8,64,512]{2,1,0:T(8,128)(2,1)}, u32[]{:S(2)}, u32[]{:S(2)}) collective-permute-start(bf16[8,64,512]{2,1,0:T(8,128)(2,1)} %get-tuple-element.55), channel_id=1, source_target_pairs={{0,32},{32,0},{64,96},{96,64},{128,160},{160,128},{192,224},{224,1... | collective-permute-start | bytes 1572872 | tf_op jit(solution)/shard_map/ppermute | solution.py:17
  156.4 3.2 %collective-permute-start.6 = (f32[2,1024]{1,0:T(2,128)S(1)}, f32[2,1024]{1,0:T(2,128)S(1)}, u32[]{:S(2)}, u32[]{:S(2)}) collective-permute-start(f32[2,1024]{1,0:T(2,128)S(1)} %pad_maximum_fusion.5), channel_id=1, source_target_pairs={{0,32},{32,0},{64,96},{96,64},{128,160},{160,128},{192,224},{224,1... | collective-permute-start | bytes 24584 | tf_op jit(solution)/shard_map/ppermute | solution.py:17
  160.7 12.5 %copy-start.17 = (bf16[1024,256]{1,0:T(8,128)(2,1)}, bf16[1024,256]{1,0:T(8,128)(2,1)S(1)}, u32[]{:S(2)}) copy-start(bf16[1024,256]{1,0:T(8,128)(2,1)S(1)} %collective-permute-done.4) | copy-start | bytes 1572868
  161.4 27.8 %all-to-all-start.7 = ((bf16[8,24,512]{2,1,0:T(8,128)(2,1)}), bf16[8,24,512]{2,1,0:T(8,128)(2,1)S(1)}, u32[]{:S(2)}, u32[]{:S(2)}) async-start(bf16[8,24,512]{2,1,0:T(8,128)(2,1)} %broadcast_in_dim.69), calls=%async_computation.7 | async-start | bytes 393216 | tf_op jit(solution)/shard_map/all_to_all | solution.py:35
  177.0 23.6 %copy-start.2 = (bf16[384,1024]{1,0:T(8,128)(2,1)S(1)}, bf16[384,1024]{1,0:T(8,128)(2,1)}, u32[]{:S(2)}) copy-start(bf16[384,1024]{1,0:T(8,128)(2,1)} %copy-done.1) | copy-start | bytes 2359300
  202.1 8.3 %collective-permute-start.7 = (bf16[8,64,512]{2,1,0:T(8,128)(2,1)S(1)}, bf16[8,64,512]{2,1,0:T(8,128)(2,1)S(1)}, u32[]{:S(2)}, u32[]{:S(2)}) collective-permute-start(bf16[8,64,512]{2,1,0:T(8,128)(2,1)S(1)} %get-tuple-element.66), channel_id=1, source_target_pairs={{0,32},{32,0},{64,96},{96,64},{128,160},{160,128},{192,224},{224,1... | collective-permute-start | bytes 1572872 | tf_op jit(solution)/shard_map/ppermute | solution.py:17
  211.4 19.7 %all-to-all-start.9 = ((bf16[8,136,512]{2,1,0:T(8,128)(2,1)}), bf16[8,136,512]{2,1,0:T(8,128)(2,1)S(1)}, u32[]{:S(2)}, u32[]{:S(2)}) async-start(bf16[8,136,512]{2,1,0:T(8,128)(2,1)} %fusion.2), calls=%async_computation.9 | async-start | bytes 2228224 | tf_op jit(solution)/shard_map/all_to_all | solution.py:35
  215.0 3.3 %copy-start.14 = (bf16[8,2,64,512]{3,2,1,0:T(8,128)(2,1)S(1)}, bf16[8,2,64,512]{3,2,1,0:T(8,128)(2,1)}, u32[]{:S(2)}) copy-start(bf16[8,2,64,512]{3,2,1,0:T(8,128)(2,1)} %copy-done.13) | copy-start | bytes 3145732
  215.8 4.6 %collective-permute-start.8 = (bf16[1024,256]{0,1:T(8,128)(2,1)S(1)}, bf16[1024,256]{0,1:T(8,128)(2,1)S(1)}, u32[]{:S(2)}, u32[]{:S(2)}) collective-permute-start(bf16[1024,256]{0,1:T(8,128)(2,1)S(1)} %slice.50), channel_id=1, source_target_pairs={{0,32},{32,0},{64,96},{96,64},{128,160},{160,128},{192,224},{224,1... | collective-permute-start | bytes 1572872 | tf_op jit(solution)/shard_map/ppermute | solution.py:17
  (11 other events, 17.7 us)

commit v7 on v6

--- a/solution.py
+++ b/solution.py
@@ -9,12 +9,23 @@
 
 FAR = 2
 CHUNK = 256
+SPARE = 16
 PARAMS = pltpu.CompilerParams(vmem_limit_bytes=32 * 1024 * 1024)
 
 
+def dom_swap(value, bit):
+    pairs = [(source, source ^ 2**bit) for source in range(lax.axis_size("dom"))]
+    return lax.ppermute(value, "dom", pairs)
+
+
 def core_swap(value):
-    pairs = [(source, source ^ 1) for source in range(lax.axis_size("dom"))]
-    return lax.ppermute(value, "dom", pairs)
+    return dom_swap(value, 0)
+
+
+def joined(value, bit):
+    other = dom_swap(value, bit)
+    low_side = (lax.axis_index("dom") // 2**bit) % 2 == 0
+    return jnp.where(low_side, jnp.concatenate([value, other], 0), jnp.concatenate([other, value], 0))
 
 
 def near_groups():
@@ -60,6 +71,10 @@
     return lax.dot_general(
         left_side, right_side, (((1,), (1,)), ((), ())), preferred_element_type=jnp.float32
     )
+
+
+def in_hbm(value):
+    return pltpu.with_memory_space_constraint(value, pltpu.HBM)
 
 
 def middle_kernel(sums, x0, masked, own_u, other_u, map_v, bias, both, layer_one, first_adj, kept, bias_sum, total):
@@ -115,9 +130,9 @@
         out_specs=[fixed, across, across, across, pl.BlockSpec((1, CHUNK), lambda i: (0, i))],
         out_shape=[
             jax.ShapeDtypeStruct((2 * rows, rank), low),
-            jax.ShapeDtypeStruct((rows, width), low),
-            jax.ShapeDtypeStruct((rows, width), low),
-            jax.ShapeDtypeStruct((rows, width), wide),
+            pltpu.HBM((rows, width), low),
+            pltpu.HBM((rows, width), low),
+            pltpu.HBM((rows, width), wide),
             jax.ShapeDtypeStruct((1, width), wide),
         ],
         scratch_shapes=[pltpu.VMEM((2 * rows, rank), wide)],
@@ -125,49 +140,134 @@
     )(sums, x0, masked, own_u, other_u, map_v, bias)
 
 
-def split_rows(core, term, keep, give):
-    lines = keep.shape[1]
-    for pair in range(keep.shape[0]):
-        first = term[2 * pair * lines : (2 * pair + 1) * lines]
-        second = term[(2 * pair + 1) * lines : (2 * pair + 2) * lines]
-        keep[pair] = jnp.where(core == 0, first, second)
-        give[pair] = jnp.where(core == 0, second, first).astype(give.dtype)
-
-
-def early_kernel(place, first_adj, layer_one, sums, keep_u, give_u, keep_v, give_v):
+def halves_of(term, core, pair, lines):
+    first = term[2 * pair * lines : (2 * pair + 1) * lines]
+    second = term[(2 * pair + 1) * lines : (2 * pair + 2) * lines]
+    return jnp.where(core == 0, first, second), jnp.where(core == 0, second, first)
+
+
+def in_two(line):
+    high = line.astype(jnp.bfloat16).astype(jnp.float32)
+    return high, (line - high).astype(jnp.bfloat16).astype(jnp.float32)
+
+
+def early_kernel(place, first_adj, layer_one, sums, bias_one, bias_two, keep_u, keep_v, give):
+    low = give.dtype
     rows, half_rank = first_adj.shape[0], keep_u.shape[1]
+    pairs, lines, _ = keep_v.shape
     keep_u[...] = transposed_dot(first_adj[...], sums[:rows, :half_rank])
-    give_u[...] = transposed_dot(first_adj[...], sums[:rows, half_rank:]).astype(give_u.dtype)
-    split_rows(place[0], transposed_dot(layer_one[...], sums[rows:, :]), keep_v, give_v)
+    give[0, :CHUNK, :half_rank] = transposed_dot(first_adj[...], sums[:rows, half_rank:]).astype(low)
+    term = transposed_dot(layer_one[...], sums[rows:, :])
+    for pair in range(pairs):
+        keep_v[pair], away = halves_of(term, place[0], pair, lines)
+        top = 2 * pair * lines
+        give[0, top : top + lines, half_rank:] = away[:, :half_rank].astype(low)
+        give[0, top + lines : top + 2 * lines, half_rank:] = away[:, half_rank:].astype(low)
+    one = jnp.concatenate(in_two(bias_one[...]), 1)
+    two = jnp.concatenate(in_two(bias_two[...]), 1)
+    row = lax.broadcasted_iota(jnp.int32, (SPARE, one.shape[1]), 0)
+    give[0, CHUNK:, :] = jnp.where(row == 0, one, jnp.where(row == 1, two, 0.0)).astype(low)
+
+
+def early_terms(core, first_adj, layer_one, sums, bias_one, bias_two, lines):
+    low, wide = jnp.bfloat16, jnp.float32
+    rows, width = first_adj.shape
+    rank = sums.shape[1]
+    pairs = CHUNK // (2 * lines)
+    chunks = width // CHUNK
+    across = pl.BlockSpec((rows, CHUNK), lambda i, place: (0, i))
+    line = pl.BlockSpec((1, CHUNK), lambda i, place: (0, i))
+    return pl.pallas_call(
+        early_kernel,
+        grid_spec=pltpu.PrefetchScalarGridSpec(
+            num_scalar_prefetch=1,
+            grid=(chunks,),
+            in_specs=[across, across, pl.BlockSpec(sums.shape, lambda i, place: (0, 0)), line, line],
+            out_specs=[
+                pl.BlockSpec((CHUNK, rank // 2), lambda i, place: (i, 0)),
+                pl.BlockSpec((pairs, lines, rank), lambda i, place: (i, 0, 0)),
+                pl.BlockSpec((1, CHUNK + SPARE, rank), lambda i, place: (i, 0, 0)),
+            ],
+        ),
+        out_shape=[
+            pltpu.HBM((width, rank // 2), wide),
+            pltpu.HBM((width // (2 * lines), lines, rank), wide),
+            pltpu.HBM((chunks, CHUNK + SPARE, rank), low),
+        ],
+        compiler_params=PARAMS,
+    )(core[None], in_hbm(first_adj), in_hbm(layer_one), sums, bias_one, bias_two)
+
+
+def finish_kernel(keep_u, keep_v, peer, bias_one, bias_two, grad_eu, sent):
+    low, wide = sent.dtype, jnp.float32
+    half_rank = grad_eu.shape[1]
+    chips, lines, _ = keep_v.shape
+    chunks = peer.shape[0]
+    pairs = chips // chunks
+    tail = jnp.zeros((SPARE, 2 * half_rank), wide)
+    row = lax.broadcasted_iota(jnp.int32, tail.shape, 0)
+    for i in range(chunks):
+        spot = slice(i * CHUNK, (i + 1) * CHUNK)
+        grad_eu[spot, :] = (keep_u[spot, :] + peer[i, :CHUNK, :half_rank].astype(wide)).astype(low)
+        for pair in range(pairs):
+            top = 2 * pair * lines
+            left = peer[i, top : top + lines, half_rank:].astype(wide)
+            right = peer[i, top + lines : top + 2 * lines, half_rank:].astype(wide)
+            chip = i * pairs + pair
+            sent[chip, :lines, :] = jnp.zeros((lines, 2 * half_rank), low)
+            sent[chip, lines : 2 * lines, :half_rank] = (keep_v[chip, :, :half_rank] + left).astype(low)
+            sent[chip, lines : 2 * lines, half_rank:] = (keep_v[chip, :, half_rank:] + right).astype(low)
+        theirs = peer[i, CHUNK:, :].astype(wide)
+        theirs = theirs[:, :half_rank] + theirs[:, half_rank:]
+        for t, bias in enumerate((bias_one, bias_two)):
+            high, rest = in_two(bias[:, spot])
+            line = jnp.concatenate(in_two((high + rest) + theirs[t : t + 1]), 1)
+            tail = jnp.where(row == 2 * i + t, line, tail)
+    for chip in range(chips):
+        sent[chip, 2 * lines :, :] = tail.astype(low)
+
+
+def finished(keep_u, keep_v, peer, bias_one, bias_two):
+    low = jnp.bfloat16
+    chips, lines, rank = keep_v.shape
+    return pl.pallas_call(
+        finish_kernel,
+        out_shape=[
+            jax.ShapeDtypeStruct(keep_u.shape, low),
+            jax.ShapeDtypeStruct((chips, 2 * lines + SPARE, rank), low),
+        ],
+        compiler_params=PARAMS,
+    )(keep_u, keep_v, peer, bias_one, bias_two)
 
 
 def late_kernel(place, second_adj, sums, keep, give):
     rows = second_adj.shape[0]
-    split_rows(place[0], transposed_dot(second_adj[...], sums[:rows, :]), keep, give)
-
-
-def terms(kernel, core, acts, sums, lines, with_expert):
-    low, wide = jnp.bfloat16, jnp.float32
-    rows, width = acts[0].shape
+    pairs, lines, _ = keep.shape
+    term = transposed_dot(second_adj[...], sums[:rows, :])
+    for pair in range(pairs):
+        keep[pair], away = halves_of(term, place[0], pair, lines)
+        give[pair] = away.astype(give.dtype)
+
+
+def late_terms(core, second_adj, sums, lines):
+    rows, width = second_adj.shape
     rank = sums.shape[1]
-    pairs = CHUNK // (2 * lines)
-    expert = pl.BlockSpec((CHUNK, rank // 2), lambda i, place: (i, 0))
-    shared = pl.BlockSpec((pairs, lines, rank), lambda i, place: (i, 0, 0))
-    whole_expert, whole_shared = (width, rank // 2), (width // (2 * lines), lines, rank)
-    specs = ([expert] * 2 if with_expert else []) + [shared] * 2
-    shapes = ([whole_expert] * 2 if with_expert else []) + [whole_shared] * 2
-    return pl.pallas_call(
-        kernel,
+    shared = pl.BlockSpec((CHUNK // (2 * lines), lines, rank), lambda i, place: (i, 0, 0))
+    shape = (width // (2 * lines), lines, rank)
+    return pl.pallas_call(
+        late_kernel,
         grid_spec=pltpu.PrefetchScalarGridSpec(
             num_scalar_prefetch=1,
             grid=(width // CHUNK,),
-            in_specs=[pl.BlockSpec((rows, CHUNK), lambda i, place: (0, i))] * len(acts)
-            + [pl.BlockSpec(sums.shape, lambda i, place: (0, 0))],
-            out_specs=specs,
+            in_specs=[
+                pl.BlockSpec((rows, CHUNK), lambda i, place: (0, i)),
+                pl.BlockSpec(sums.shape, lambda i, place: (0, 0)),
+            ],
+            out_specs=[shared, shared],
         ),
-        out_shape=[jax.ShapeDtypeStruct(shape, (wide, low)[i % 2]) for i, shape in enumerate(shapes)],
-        compiler_params=PARAMS,
-    )(core[None], *acts, sums)
+        out_shape=[jax.ShapeDtypeStruct(shape, jnp.float32), jax.ShapeDtypeStruct(shape, jnp.bfloat16)],
+        compiler_params=PARAMS,
+    )(core[None], second_adj, sums)
 
 
 def last_kernel(lines, taken, grad_su, grad_sv, grad_bias):
@@ -176,13 +276,9 @@
     grad_su[...] = total[:lines].astype(low)
     grad_sv[...] = total[lines : 2 * lines].astype(low)
     sums = total[2 * lines :]
-    half = sums.shape[0] // 2
-    sums = sums[:half] + sums[half:]
-    rank = sums.shape[1]
-    per_row = half // 2
-    for i in range(half):
-        column = (i % per_row) * rank
-        grad_bias[i // per_row : i // per_row + 1, column : column + rank] = sums[i : i + 1]
+    sums = sums[:, : sums.shape[1] // 2] + sums[:, sums.shape[1] // 2 :]
+    for i in range(grad_bias.shape[1] // CHUNK):
+        grad_bias[:, i * CHUNK : (i + 1) * CHUNK] = sums[2 * i : 2 * i + 2]
 
 
 def last_sum(taken, lines, width):
@@ -209,8 +305,7 @@
     domain = lax.axis_index("dom") // 2
     core = lax.axis_index("dom") % 2
 
-    own_maps = gathered(jnp.concatenate([shared_u, shared_v], 0), "dom", chip_groups())
-    own_maps = own_maps.reshape(chips, 2, lines, rank)
+    own_su = gathered(shared_u, "dom", chip_groups()).reshape(chips, lines, rank)
     other_v = core_swap(expert_v)
     full_v = jnp.concatenate([expert_v, other_v], 1)
 
@@ -223,38 +318,35 @@
     bias_two = jnp.sum(second_adj.astype(wide), axis=0, keepdims=True)
 
     first_part = dot(x0, full_v).astype(low)
-    whole_su = whole(own_maps[:, 0], core_swap(own_maps[:, 0]))
+    whole_su = whole(own_su, core_swap(own_su))
     back_two_part = dot(second_adj, whole_su).astype(low)
     both = jnp.concatenate([first_part, back_two_part], 0)
-    own_sv, expert_u, both = lax.optimization_barrier((own_maps[:, 1], expert_u, both))
     near, ring = near_groups(), ring_groups()
-    part = summed(summed(both, "feat", near), "feat", ring)
-    whole_sv = whole(own_sv, core_swap(own_sv))
+    shared_v, both = lax.optimization_barrier((shared_v, both))
+    whole_sv = joined(shared_v, 0)
+    part = summed(both, "feat", near)
+    part, whole_sv = lax.optimization_barrier((part, whole_sv))
+    whole_sv = joined(joined(whole_sv, 1), 2)
+    part = summed(part, "feat", ring)
+    part, whole_sv, expert_u = lax.optimization_barrier((part, whole_sv, expert_u))
+    whole_sv = joined(whole_sv, 3)
     other_u = core_swap(expert_u)
+    part = gathered(part, "feat", ring)
     part, whole_sv, other_u, masked = lax.optimization_barrier((part, whole_sv, other_u, masked))
-    sums = gathered(gathered(part, "feat", ring), "feat", near)
+    sums = gathered(part, "feat", near)
 
     both, layer_one, first_adj, kept, bias_one = middle(sums, x0, masked, expert_u, other_u, whole_sv, bias)
+    keep_eu, keep_sv, give = early_terms(core, first_adj, layer_one, sums, bias_one, bias_two, lines)
     part = summed(both, "feat", near)
-    part, sums, first_adj, layer_one = lax.optimization_barrier((part, sums, first_adj, layer_one))
-    keep_eu, give_eu, keep_sv, give_sv = terms(early_kernel, core, [first_adj, layer_one], sums, lines, True)
+    part, give = lax.optimization_barrier((part, give))
     part = summed(part, "feat", ring)
-    peer_eu, peer_sv = core_swap(give_eu), core_swap(give_sv)
-    bias_terms = jnp.concatenate([bias_one, bias_two], 0)
-    bias_terms = bias_terms + core_swap(bias_terms)
-    part, peer_eu, peer_sv, bias_terms = lax.optimization_barrier((part, peer_eu, peer_sv, bias_terms))
+    part, peer = lax.optimization_barrier((part, core_swap(give)))
+    grad_eu, sent = finished(keep_eu, keep_sv, peer, bias_one, bias_two)
     part = gathered(part, "feat", ring)
-    bias_high = bias_terms.astype(low)
-    bias_rest = (bias_terms - bias_high.astype(wide)).astype(low)
-    bias_lines = jnp.stack([bias_high, bias_rest]).reshape(4 * width // rank, rank)
-    bias_lines = jnp.broadcast_to(bias_lines[None], (chips, *bias_lines.shape))
-    grad_eu = (keep_eu + peer_eu.astype(wide)).astype(low)
-    part_sv = (keep_sv + peer_sv.astype(wide)).astype(low)
-    sent = jnp.concatenate([jnp.zeros_like(part_sv), part_sv, bias_lines], 1)
     part, sent, grad_eu = lax.optimization_barrier((part, sent, grad_eu))
     sums = gathered(part, "feat", near)
 
-    keep_su, give_su = terms(late_kernel, core, [second_adj], sums, lines, False)
+    keep_su, give_su = late_terms(core, second_adj, sums, lines)
     part_su = (keep_su + core_swap(give_su).astype(wide)).astype(low)
     sent = lax.dynamic_update_slice(sent, part_su, (0, 0, 0))
     sent, sums = lax.optimization_barrier((sent, sums))

time: 233 us -> 235 us (level)
  waiting for transfers between devices: 47.6 us -> 54.1 us
  other arithmetic: 12.5 us -> 6.87 us
  blocking collectives: 55.5 us -> 51.2 us
  Pallas kernels: 9.72 us -> 13.7 us
  starting transfers between devices: 87.8 us -> 90.6 us
    ppermute x9 -> x10, waiting for transfers between devices: 2.3 us -> 16.5 us  [dom_swap(): return lax.ppermute(value, 'dom', pairs)]
    ppermute x9 -> x10, starting transfers between devices: 38.7 us -> 48 us  [dom_swap(): return lax.ppermute(value, 'dom', pairs)]
    all_to_all x6 -> x7, waiting for transfers between devices: 45.3 us -> 37.6 us  [exchange(): lax.all_to_all(value, axis, 0, 0, axis_index_groups=groups, tiled=True)]
    all_to_all x6 -> x7, starting transfers between devices: 49.1 us -> 42.6 us  [exchange(): lax.all_to_all(value, axis, 0, 0, axis_index_groups=groups, tiled=True)]
    all_to_all x4 -> x3, blocking collectives: 55.5 us -> 51.2 us  [exchange(): lax.all_to_all(value, axis, 0, 0, axis_index_groups=groups, tiled=True)]
    pallas_call x2 -> x3, Pallas kernels: 4.42 us -> 7.55 us  [the longest x1 4.7 us: early_terms(): pl.pallas_call(early_kernel, grid_spec=pltpu.PrefetchScalarGridSpec(num_s...]
    unnamed x42 -> x38, local copies, waits for them, and re-layouts: 9.33 us -> 6.56 us
    convert_element_type x2 -> x0, other arithmetic: 2.52 us -> none  [the longest x1 1.58 us: local(): part_sv = (keep_sv + peer_sv.astype(wide)).astype(low)]
  transfers between devices with their start and end apart: 15 -> 17, of which waited for: 7 -> 12; matrix products, arithmetic and copies ran while one was open for 7% -> 4% of each run, Pallas kernels for 1% -> 3%
where the time goes in v7:
time: 235 us; the launch traced here: 234 us
  starting transfers between devices  90.6 us (39%)
  waiting for transfers between devices  54.1 us (23%)
  blocking collectives  51.2 us (22%)
  Pallas kernels  13.7 us (6%)
  local copies, waits for them, and re-layouts  11.9 us (5%)
  other arithmetic  6.87 us (3%)
  matrix products  4 us (2%)
    all_to_all x3, blocking collectives, exchange(): lax.all_to_all(value, axis, 0, 0, axis_index_groups=groups, tiled=True)  51.2 us
    ppermute x10, starting transfers between devices, dom_swap(): return lax.ppermute(value, 'dom', pairs)  48 us
    all_to_all x7, starting transfers between devices, exchange(): lax.all_to_all(value, axis, 0, 0, axis_index_groups=groups, tiled=True)  42.6 us
    all_to_all x7, waiting for transfers between devices, exchange(): lax.all_to_all(value, axis, 0, 0, axis_index_groups=groups, tiled=True)  37.6 us
    ppermute x10, waiting for transfers between devices, dom_swap(): return lax.ppermute(value, 'dom', pairs)  16.5 us
    unnamed x38, local copies, waits for them, and re-layouts  6.56 us
    pallas_call x1, Pallas kernels, middle(): pl.pallas_call(middle_kernel, grid=(width // CHUNK,), in_specs=[fixed, ac...  5.42 us
    pallas_call x1, Pallas kernels, early_terms(): pl.pallas_call(early_kernel, grid_spec=pltpu.PrefetchScalarGridSpec(num_s...  4.7 us
  transfers between devices with their start and end apart: 17, of which 12 were waited for; matrix products, arithmetic and copies ran while one was open for 4% of the time, Pallas kernels for 3%

profile of v7, /device:TPU:1, one launch (start us, length us, event | category | flops | bytes accessed | tf_op | source)
XLA Modules:
  0.0 233.6 jit_solution(17209811795694371023)
XLA Ops:
  2.5 5.9 %all-to-all-start = ((bf16[8,64,512]{2,1,0:T(8,128)(2,1)}), bf16[8,64,512]{2,1,0:T(8,128)(2,1)}, u32[]{:S(2)}, u32[]{:S(2)}) async-start(bf16[8,64,512]{2,1,0:T(8,128)(2,1)} %broadcast_in_dim.26), calls=%async_computation | async-start | bytes 1048576 | tf_op jit(solution)/shard_map/all_to_all | solution.py:46
  8.4 7.0 %collective-permute-start = (bf16[1024,256]{1,0:T(8,128)(2,1)}, bf16[1024,256]{1,0:T(8,128)(2,1)}, u32[]{:S(2)}, u32[]{:S(2)}) collective-permute-start(bf16[1024,256]{1,0:T(8,128)(2,1)} %param.12), channel_id=1, source_target_pairs={{0,32},{32,0},{64,96},{96,64},{128,160},{160,128},{192,224},{224,1... | collective-permute-start | bytes 1572872 | tf_op jit(solution)/shard_map/ppermute | solution.py:18
  16.0 8.0 %collective-permute-start.1 = (bf16[8,64,512]{2,1,0:T(8,128)(2,1)}, bf16[8,64,512]{2,1,0:T(8,128)(2,1)S(1)}, u32[]{:S(2)}, u32[]{:S(2)}) collective-permute-start(bf16[8,64,512]{2,1,0:T(8,128)(2,1)} %all-to-all-done), channel_id=1, source_target_pairs={{0,32},{32,0},{64,96},{96,64},{128,160},{160,128},{192,224},{224,1... | collective-permute-start | bytes 1572872 | tf_op jit(solution)/shard_map/ppermute | solution.py:18
  29.7 3.5 %all-to-all-start.1 = ((bf16[4,192,512]{2,1,0:T(8,128)(2,1)}), bf16[4,192,512]{2,1,0:T(8,128)(2,1)S(1)}, u32[]{:S(2)}, u32[]{:S(2)}) async-start(bf16[4,192,512]{2,1,0:T(8,128)(2,1)} %bitcast.40), calls=%async_computation.1 | async-start | bytes 1572864 | tf_op jit(solution)/shard_map/all_to_all | solution.py:46
  36.3 9.2 %all-to-all-done.1 = bf16[4,192,512]{2,1,0:T(8,128)(2,1)S(1)} async-done(((bf16[4,192,512]{2,1,0:T(8,128)(2,1)}), bf16[4,192,512]{2,1,0:T(8,128)(2,1)S(1)}, u32[]{:S(2)}, u32[]{:S(2)}) %all-to-all-start.1) | async-done | bytes 786464 | tf_op jit(solution)/shard_map/all_to_all | solution.py:46
  46.4 12.7 %all-to-all-start.2 = ((bf16[8,24,512]{2,1,0:T(8,128)(2,1)}), bf16[8,24,512]{2,1,0:T(8,128)(2,1)S(1)}, u32[]{:S(2)}, u32[]{:S(2)}) async-start(bf16[8,24,512]{2,1,0:T(8,128)(2,1)} %bitcast.6), calls=%async_computation.2 | async-start | bytes 393216 | tf_op jit(solution)/shard_map/all_to_all | solution.py:46
  61.0 4.1 %collective-permute-done.3 = bf16[128,512]{1,0:T(8,128)(2,1)S(1)} collective-permute-done((bf16[128,512]{1,0:T(8,128)(2,1)S(1)}, bf16[128,512]{1,0:T(8,128)(2,1)S(1)}, u32[]{:S(2)}, u32[]{:S(2)}) %collective-permute-start.3) | collective-permute-done | bytes 131104 | tf_op jit(solution)/shard_map/ppermute | solution.py:18
  67.1 5.5 %collective-permute-done.4 = bf16[256,512]{1,0:T(8,128)(2,1)S(1)} collective-permute-done((bf16[256,512]{1,0:T(8,128)(2,1)S(1)}, bf16[256,512]{1,0:T(8,128)(2,1)S(1)}, u32[]{:S(2)}, u32[]{:S(2)}) %collective-permute-start.4) | collective-permute-done | bytes 262176 | tf_op jit(solution)/shard_map/ppermute | solution.py:18
  75.1 9.6 %all-to-all-start.3 = ((bf16[8,24,512]{2,1,0:T(8,128)(2,1)}), bf16[8,24,512]{2,1,0:T(8,128)(2,1)}, u32[]{:S(2)}, u32[]{:S(2)}) async-start(bf16[8,24,512]{2,1,0:T(8,128)(2,1)} %broadcast_in_dim.27), calls=%async_computation.3 | async-start | bytes 393216 | tf_op jit(solution)/shard_map/all_to_all | solution.py:46
  87.3 6.1 %collective-permute-start.6 = (bf16[1024,256]{1,0:T(8,128)(2,1)S(1)}, bf16[1024,256]{1,0:T(8,128)(2,1)}, u32[]{:S(2)}, u32[]{:S(2)}) collective-permute-start(bf16[1024,256]{1,0:T(8,128)(2,1)S(1)} %copy-done.6), channel_id=1, source_target_pairs={{0,32},{32,0},{64,96},{96,64},{128,160},{160,128},{192,224},{224,1... | collective-permute-start | bytes 1572872 | tf_op jit(solution)/shard_map/ppermute | solution.py:18
  93.5 4.3 %collective-permute-done.5 = bf16[512,512]{1,0:T(8,128)(2,1)} collective-permute-done((bf16[512,512]{1,0:T(8,128)(2,1)S(1)}, bf16[512,512]{1,0:T(8,128)(2,1)}, u32[]{:S(2)}, u32[]{:S(2)}) %collective-permute-start.5) | collective-permute-done | bytes 524320 | tf_op jit(solution)/shard_map/ppermute | solution.py:18
  101.1 11.3 %all_to_all.82 = bf16[4,192,512]{2,1,0:T(8,128)(2,1)S(1)} all-to-all(bf16[4,192,512]{2,1,0:T(8,128)(2,1)S(1)} %broadcast_in_dim.28), channel_id=1, replica_groups={{0,1,16,17},{2,3,18,19},{4,5,20,21},{6,7,22,23},{8,9,24,25},{10,11,26,2..., dimensions={0} | all-to-all | bytes 1572864 | tf_op jit(solution)/shard_map/all_to_all | solution.py:46
  113.4 5.4 %shard_map.127 = (bf16[768,512]{1,0:T(8,128)(2,1)S(1)}, bf16[384,1024]{1,0:T(8,128)(2,1)}, bf16[384,1024]{1,0:T(8,128)(2,1)}, f32[384,1024]{1,0:T(8,128)}, f32[1,1024]{1,0:T(1,128)S(1)}) custom-call(bf16[768,512]{1,0:T(8,128)(2,1)S(1)} %bitcast.33, bf16[384,1024]{1,0:T(8,128)(2,1)S(1)} %copy-done, bf16[384,1024]{1,0:T(8,128)(2,1)S(1)} %get-tuple-element.48.masked, ...), custom_call_target="tpu_custom_call" | custom-call | tf_op jit(solution)/shard_map/pallas_call | solution.py:118
  119.8 3.5 %all-to-all-start.5 = ((bf16[4,192,512]{2,1,0:T(8,128)(2,1)}), bf16[4,192,512]{2,1,0:T(8,128)(2,1)S(1)}, u32[]{:S(2)}, u32[]{:S(2)}) async-start(bf16[4,192,512]{2,1,0:T(8,128)(2,1)} %bitcast.35), calls=%async_computation.5 | async-start | bytes 1572864 | tf_op jit(solution)/shard_map/all_to_all | solution.py:46
  123.3 4.7 %shard_map.128 = (f32[1024,256]{1,0:T(8,128)}, f32[8,64,512]{2,1,0:T(8,128)}, bf16[4,272,512]{2,1,0:T(8,128)(2,1)}) custom-call(s32[1]{0:T(128)} %bitcast.10.place, bf16[384,1024]{1,0:T(8,128)(2,1)} %get-tuple-element.53.first_adj, bf16[384,1024]{1,0:T(8,128)(2,1)} %get-tuple-element.54.layer_one, bf16[768,512]{1,0:T(8,128)(2,1)S(1)} %bitcast.34, ...), custom_call_target="tpu_custom_call" | custom-call | tf_op jit(solution)/shard_map/pallas_call | solution.py:180
  128.0 3.6 %all-to-all-done.5 = bf16[4,192,512]{2,1,0:T(8,128)(2,1)S(1)} async-done(((bf16[4,192,512]{2,1,0:T(8,128)(2,1)}), bf16[4,192,512]{2,1,0:T(8,128)(2,1)S(1)}, u32[]{:S(2)}, u32[]{:S(2)}) %all-to-all-start.5) | async-done | bytes 786464 | tf_op jit(solution)/shard_map/all_to_all | solution.py:46
  131.7 9.3 %collective-permute-start.7 = (bf16[4,272,512]{2,1,0:T(8,128)(2,1)}, bf16[4,272,512]{2,1,0:T(8,128)(2,1)S(1)}, u32[]{:S(2)}, u32[]{:S(2)}) collective-permute-start(bf16[4,272,512]{2,1,0:T(8,128)(2,1)} %get-tuple-element.58), channel_id=1, source_target_pairs={{0,32},{32,0},{64,96},{96,64},{128,160},{160,128},{192,224},{224,1... | collective-permute-start | bytes 3342344 | tf_op jit(solution)/shard_map/ppermute | solution.py:18
  141.1 28.3 %all_to_all.83 = bf16[8,24,512]{2,1,0:T(8,128)(2,1)S(1)} all-to-all(bf16[8,24,512]{2,1,0:T(8,128)(2,1)S(1)} %bitcast.41), channel_id=1, replica_groups={{0,2,4,6,8,10,12,14},{1,3,5,7,9,11,13,15},{16,18,20,22,24,26,28,30},{17..., dimensions={0} | all-to-all | bytes 393216 | tf_op jit(solution)/shard_map/all_to_all | solution.py:46
  170.1 3.8 %all-to-all-start.7 = ((bf16[8,24,512]{2,1,0:T(8,128)(2,1)}), bf16[8,24,512]{2,1,0:T(8,128)(2,1)S(1)}, u32[]{:S(2)}, u32[]{:S(2)}) async-start(bf16[8,24,512]{2,1,0:T(8,128)(2,1)} %broadcast_in_dim.56), calls=%async_computation.7 | async-start | bytes 393216 | tf_op jit(solution)/shard_map/all_to_all | solution.py:46
  177.8 12.2 %all-to-all-done.7 = bf16[8,24,512]{2,1,0:T(8,128)(2,1)S(1)} async-done(((bf16[8,24,512]{2,1,0:T(8,128)(2,1)}), bf16[8,24,512]{2,1,0:T(8,128)(2,1)S(1)}, u32[]{:S(2)}, u32[]{:S(2)}) %all-to-all-start.7) | async-done | bytes 196640 | tf_op jit(solution)/shard_map/all_to_all | solution.py:46
  190.1 11.6 %all_to_all.84 = bf16[4,192,512]{2,1,0:T(8,128)(2,1)S(1)} all-to-all(bf16[4,192,512]{2,1,0:T(8,128)(2,1)S(1)} %broadcast_in_dim.57), channel_id=1, replica_groups={{0,1,16,17},{2,3,18,19},{4,5,20,21},{6,7,22,23},{8,9,24,25},{10,11,26,2..., dimensions={0} | all-to-all | bytes 1572864 | tf_op jit(solution)/shard_map/all_to_all | solution.py:46
  203.1 6.8 %collective-permute-start.8 = (bf16[8,64,512]{2,1,0:T(8,128)(2,1)S(1)}, bf16[8,64,512]{2,1,0:T(8,128)(2,1)S(1)}, u32[]{:S(2)}, u32[]{:S(2)}) collective-permute-start(bf16[8,64,512]{2,1,0:T(8,128)(2,1)S(1)} %get-tuple-element.68), channel_id=1, source_target_pairs={{0,32},{32,0},{64,96},{96,64},{128,160},{160,128},{192,224},{224,1... | collective-permute-start | bytes 1572872 | tf_op jit(solution)/shard_map/ppermute | solution.py:18
  212.4 3.6 %all-to-all-start.9 = ((bf16[8,144,512]{2,1,0:T(8,128)(2,1)}), bf16[8,144,512]{2,1,0:T(8,128)(2,1)S(1)}, u32[]{:S(2)}, u32[]{:S(2)}) async-start(bf16[8,144,512]{2,1,0:T(8,128)(2,1)} %fusion.2), calls=%async_computation.9 | async-start | bytes 2359296 | tf_op jit(solution)/shard_map/all_to_all | solution.py:46
  222.6 10.2 %all-to-all-done.9.taken = bf16[8,144,512]{2,1,0:T(8,128)(2,1)S(1)} async-done(((bf16[8,144,512]{2,1,0:T(8,128)(2,1)}), bf16[8,144,512]{2,1,0:T(8,128)(2,1)S(1)}, u32[]{:S(2)}, u32[]{:S(2)}) %all-to-all-start.9) | async-done | bytes 1179680 | tf_op jit(solution)/shard_map/all_to_all | solution.py:46
  (84 shorter events, 42.0 us)
Async XLA Ops:
  0.6 14.8 %copy-start.17 = (s32[384]{0:T(512)S(1)}, s32[384]{0:T(512)}, u32[]{:S(2)}) copy-start(s32[384]{0:T(512)} %param.10) | copy-start | bytes 4612
  0.6 14.8 %copy-start = (bf16[384,1024]{1,0:T(8,128)(2,1)S(1)}, bf16[384,1024]{1,0:T(8,128)(2,1)}, u32[]{:S(2)}) copy-start(bf16[384,1024]{1,0:T(8,128)(2,1)} %x0.1) | copy-start | bytes 2359300
  0.7 14.8 %copy-start.15 = (bf16[384,1024]{1,0:T(8,128)(2,1)S(1)}, bf16[384,1024]{1,0:T(8,128)(2,1)}, u32[]{:S(2)}) copy-start(bf16[384,1024]{1,0:T(8,128)(2,1)} %param.9) | copy-start | bytes 2359300
  2.5 13.6 %all-to-all-start = ((bf16[8,64,512]{2,1,0:T(8,128)(2,1)}), bf16[8,64,512]{2,1,0:T(8,128)(2,1)}, u32[]{:S(2)}, u32[]{:S(2)}) async-start(bf16[8,64,512]{2,1,0:T(8,128)(2,1)} %broadcast_in_dim.26), calls=%async_computation | async-start | bytes 1048576 | tf_op jit(solution)/shard_map/all_to_all | solution.py:46
  8.4 16.8 %collective-permute-start = (bf16[1024,256]{1,0:T(8,128)(2,1)}, bf16[1024,256]{1,0:T(8,128)(2,1)}, u32[]{:S(2)}, u32[]{:S(2)}) collective-permute-start(bf16[1024,256]{1,0:T(8,128)(2,1)} %param.12), channel_id=1, source_target_pairs={{0,32},{32,0},{64,96},{96,64},{128,160},{160,128},{192,224},{224,1... | collective-permute-start | bytes 1572872 | tf_op jit(solution)/shard_map/ppermute | solution.py:18
  16.0 10.8 %collective-permute-start.1 = (bf16[8,64,512]{2,1,0:T(8,128)(2,1)}, bf16[8,64,512]{2,1,0:T(8,128)(2,1)S(1)}, u32[]{:S(2)}, u32[]{:S(2)}) collective-permute-start(bf16[8,64,512]{2,1,0:T(8,128)(2,1)} %all-to-all-done), channel_id=1, source_target_pairs={{0,32},{32,0},{64,96},{96,64},{128,160},{160,128},{192,224},{224,1... | collective-permute-start | bytes 1572872 | tf_op jit(solution)/shard_map/ppermute | solution.py:18
  29.7 15.9 %all-to-all-start.1 = ((bf16[4,192,512]{2,1,0:T(8,128)(2,1)}), bf16[4,192,512]{2,1,0:T(8,128)(2,1)S(1)}, u32[]{:S(2)}, u32[]{:S(2)}) async-start(bf16[4,192,512]{2,1,0:T(8,128)(2,1)} %bitcast.40), calls=%async_computation.1 | async-start | bytes 1572864 | tf_op jit(solution)/shard_map/all_to_all | solution.py:46
  33.2 3.1 %collective-permute-start.2 = (bf16[64,512]{1,0:T(8,128)(2,1)S(1)}, bf16[64,512]{1,0:T(8,128)(2,1)S(1)}, u32[]{:S(2)}, u32[]{:S(2)}) collective-permute-start(bf16[64,512]{1,0:T(8,128)(2,1)S(1)} %copy-done.16), channel_id=1, source_target_pairs={{0,32},{32,0},{64,96},{96,64},{128,160},{160,128},{192,224},{224,1... | collective-permute-start | bytes 196616 | tf_op jit(solution)/shard_map/ppermute | solution.py:18
  46.4 40.9 %copy-start.6 = (bf16[1024,256]{1,0:T(8,128)(2,1)S(1)}, bf16[1024,256]{1,0:T(8,128)(2,1)}, u32[]{:S(2)}) copy-start(bf16[1024,256]{1,0:T(8,128)(2,1)} %own_u) | copy-start | bytes 1572868
  46.4 28.0 %all-to-all-start.2 = ((bf16[8,24,512]{2,1,0:T(8,128)(2,1)}), bf16[8,24,512]{2,1,0:T(8,128)(2,1)S(1)}, u32[]{:S(2)}, u32[]{:S(2)}) async-start(bf16[8,24,512]{2,1,0:T(8,128)(2,1)} %bitcast.6), calls=%async_computation.2 | async-start | bytes 393216 | tf_op jit(solution)/shard_map/all_to_all | solution.py:46
  59.1 6.0 %collective-permute-start.3 = (bf16[128,512]{1,0:T(8,128)(2,1)S(1)}, bf16[128,512]{1,0:T(8,128)(2,1)S(1)}, u32[]{:S(2)}, u32[]{:S(2)}) collective-permute-start(bf16[128,512]{1,0:T(8,128)(2,1)S(1)} %maximum_select_fusion.3), channel_id=1, source_target_pairs={{0,64},{32,96},{64,0},{96,32},{128,192},{160,224},{192,128},{224,1... | collective-permute-start | bytes 393224 | tf_op jit(solution)/shard_map/ppermute | solution.py:18
  65.1 7.4 %collective-permute-start.4 = (bf16[256,512]{1,0:T(8,128)(2,1)S(1)}, bf16[256,512]{1,0:T(8,128)(2,1)S(1)}, u32[]{:S(2)}, u32[]{:S(2)}) collective-permute-start(bf16[256,512]{1,0:T(8,128)(2,1)S(1)} %maximum_select_fusion.2), channel_id=1, source_target_pairs={{0,128},{32,160},{64,192},{96,224},{128,0},{160,32},{192,64},{224,... | collective-permute-start | bytes 786440 | tf_op jit(solution)/shard_map/ppermute | solution.py:18
  72.8 20.7 %copy-start.13 = (bf16[512,512]{1,0:T(8,128)(2,1)}, bf16[512,512]{1,0:T(8,128)(2,1)S(1)}, u32[]{:S(2)}) copy-start(bf16[512,512]{1,0:T(8,128)(2,1)S(1)} %maximum_select_fusion.1) | copy-start | bytes 1572868
  75.1 25.0 %all-to-all-start.3 = ((bf16[8,24,512]{2,1,0:T(8,128)(2,1)}), bf16[8,24,512]{2,1,0:T(8,128)(2,1)}, u32[]{:S(2)}, u32[]{:S(2)}) async-start(bf16[8,24,512]{2,1,0:T(8,128)(2,1)} %broadcast_in_dim.27), calls=%async_computation.3 | async-start | bytes 393216 | tf_op jit(solution)/shard_map/all_to_all | solution.py:46
  84.8 12.9 %collective-permute-start.5 = (bf16[512,512]{1,0:T(8,128)(2,1)S(1)}, bf16[512,512]{1,0:T(8,128)(2,1)}, u32[]{:S(2)}, u32[]{:S(2)}) collective-permute-start(bf16[512,512]{1,0:T(8,128)(2,1)S(1)} %maximum_select_fusion.1), channel_id=1, source_target_pairs={{0,256},{32,288},{64,320},{96,352},{128,384},{160,416},{192,448},{... | collective-permute-start | bytes 1572872 | tf_op jit(solution)/shard_map/ppermute | solution.py:18
  87.3 12.3 %collective-permute-start.6 = (bf16[1024,256]{1,0:T(8,128)(2,1)S(1)}, bf16[1024,256]{1,0:T(8,128)(2,1)}, u32[]{:S(2)}, u32[]{:S(2)}) collective-permute-start(bf16[1024,256]{1,0:T(8,128)(2,1)S(1)} %copy-done.6), channel_id=1, source_target_pairs={{0,32},{32,0},{64,96},{96,64},{128,160},{160,128},{192,224},{224,1... | collective-permute-start | bytes 1572872 | tf_op jit(solution)/shard_map/ppermute | solution.py:18
  99.6 12.8 %copy-start.8 = (f32[2,1024]{1,0:T(2,128)S(1)}, f32[2,1024]{1,0:T(2,128)}, u32[]{:S(2)}) copy-start(f32[2,1024]{1,0:T(2,128)} %bias.1) | copy-start | bytes 24580
  119.8 11.8 %all-to-all-start.5 = ((bf16[4,192,512]{2,1,0:T(8,128)(2,1)}), bf16[4,192,512]{2,1,0:T(8,128)(2,1)S(1)}, u32[]{:S(2)}, u32[]{:S(2)}) async-start(bf16[4,192,512]{2,1,0:T(8,128)(2,1)} %bitcast.35), calls=%async_computation.5 | async-start | bytes 1572864 | tf_op jit(solution)/shard_map/all_to_all | solution.py:46
  131.7 37.7 %collective-permute-start.7 = (bf16[4,272,512]{2,1,0:T(8,128)(2,1)}, bf16[4,272,512]{2,1,0:T(8,128)(2,1)S(1)}, u32[]{:S(2)}, u32[]{:S(2)}) collective-permute-start(bf16[4,272,512]{2,1,0:T(8,128)(2,1)} %get-tuple-element.58), channel_id=1, source_target_pairs={{0,32},{32,0},{64,96},{96,64},{128,160},{160,128},{192,224},{224,1... | collective-permute-start | bytes 3342344 | tf_op jit(solution)/shard_map/ppermute | solution.py:18
  170.1 19.9 %all-to-all-start.7 = ((bf16[8,24,512]{2,1,0:T(8,128)(2,1)}), bf16[8,24,512]{2,1,0:T(8,128)(2,1)S(1)}, u32[]{:S(2)}, u32[]{:S(2)}) async-start(bf16[8,24,512]{2,1,0:T(8,128)(2,1)} %broadcast_in_dim.56), calls=%async_computation.7 | async-start | bytes 393216 | tf_op jit(solution)/shard_map/all_to_all | solution.py:46
  177.8 23.9 %copy-start.2 = (bf16[384,1024]{1,0:T(8,128)(2,1)S(1)}, bf16[384,1024]{1,0:T(8,128)(2,1)}, u32[]{:S(2)}) copy-start(bf16[384,1024]{1,0:T(8,128)(2,1)} %copy-done.1) | copy-start | bytes 2359300
  203.1 8.3 %collective-permute-start.8 = (bf16[8,64,512]{2,1,0:T(8,128)(2,1)S(1)}, bf16[8,64,512]{2,1,0:T(8,128)(2,1)S(1)}, u32[]{:S(2)}, u32[]{:S(2)}) collective-permute-start(bf16[8,64,512]{2,1,0:T(8,128)(2,1)S(1)} %get-tuple-element.68), channel_id=1, source_target_pairs={{0,32},{32,0},{64,96},{96,64},{128,160},{160,128},{192,224},{224,1... | collective-permute-start | bytes 1572872 | tf_op jit(solution)/shard_map/ppermute | solution.py:18
  212.4 20.4 %all-to-all-start.9 = ((bf16[8,144,512]{2,1,0:T(8,128)(2,1)}), bf16[8,144,512]{2,1,0:T(8,128)(2,1)S(1)}, u32[]{:S(2)}, u32[]{:S(2)}) async-start(bf16[8,144,512]{2,1,0:T(8,128)(2,1)} %fusion.2), calls=%async_computation.9 | async-start | bytes 2359296 | tf_op jit(solution)/shard_map/all_to_all | solution.py:46
  216.8 4.6 %collective-permute-start.9 = (bf16[1024,256]{0,1:T(8,128)(2,1)S(1)}, bf16[1024,256]{0,1:T(8,128)(2,1)S(1)}, u32[]{:S(2)}, u32[]{:S(2)}) collective-permute-start(bf16[1024,256]{0,1:T(8,128)(2,1)S(1)} %slice.33), channel_id=1, source_target_pairs={{0,32},{32,0},{64,96},{96,64},{128,160},{160,128},{192,224},{224,1... | collective-permute-start | bytes 1572872 | tf_op jit(solution)/shard_map/ppermute | solution.py:18
  (11 other events, 33.8 us)

commit v8 on v7

--- a/solution.py
+++ b/solution.py
@@ -22,10 +22,11 @@
     return dom_swap(value, 0)
 
 
-def joined(value, bit):
+def joined(value, bit, axis):
     other = dom_swap(value, bit)
     low_side = (lax.axis_index("dom") // 2**bit) % 2 == 0
-    return jnp.where(low_side, jnp.concatenate([value, other], 0), jnp.concatenate([other, value], 0))
+    pair = [jnp.where(low_side, value, other), jnp.where(low_side, other, value)]
+    return jnp.stack(pair, axis)
 
 
 def near_groups():
@@ -129,7 +130,7 @@
         ],
         out_specs=[fixed, across, across, across, pl.BlockSpec((1, CHUNK), lambda i: (0, i))],
         out_shape=[
-            jax.ShapeDtypeStruct((2 * rows, rank), low),
+            pltpu.HBM((2 * rows, rank), low),
             pltpu.HBM((rows, width), low),
             pltpu.HBM((rows, width), low),
             pltpu.HBM((rows, width), wide),
@@ -137,7 +138,7 @@
         ],
         scratch_shapes=[pltpu.VMEM((2 * rows, rank), wide)],
         compiler_params=PARAMS,
-    )(sums, x0, masked, own_u, other_u, map_v, bias)
+    )(sums, *map(in_hbm, (x0, masked, own_u, other_u, map_v)), bias)
 
 
 def halves_of(term, core, pair, lines):
@@ -198,27 +199,26 @@
     )(core[None], in_hbm(first_adj), in_hbm(layer_one), sums, bias_one, bias_two)
 
 
-def finish_kernel(keep_u, keep_v, peer, bias_one, bias_two, grad_eu, sent):
+def finish_kernel(keep_u, give_u, keep_v, peer, bias_one, bias_two, sent):
     low, wide = sent.dtype, jnp.float32
-    half_rank = grad_eu.shape[1]
-    chips, lines, _ = keep_v.shape
+    chips, lines, rank = keep_v.shape
+    half_rank = rank // 2
     chunks = peer.shape[0]
     pairs = chips // chunks
-    tail = jnp.zeros((SPARE, 2 * half_rank), wide)
+    tail = jnp.zeros((SPARE, rank), wide)
     row = lax.broadcasted_iota(jnp.int32, tail.shape, 0)
     for i in range(chunks):
-        spot = slice(i * CHUNK, (i + 1) * CHUNK)
-        grad_eu[spot, :] = (keep_u[spot, :] + peer[i, :CHUNK, :half_rank].astype(wide)).astype(low)
         for pair in range(pairs):
             top = 2 * pair * lines
             left = peer[i, top : top + lines, half_rank:].astype(wide)
             right = peer[i, top + lines : top + 2 * lines, half_rank:].astype(wide)
             chip = i * pairs + pair
-            sent[chip, :lines, :] = jnp.zeros((lines, 2 * half_rank), low)
+            sent[chip, :lines, :] = (keep_u[chip] + give_u[chip].astype(wide)).astype(low)
             sent[chip, lines : 2 * lines, :half_rank] = (keep_v[chip, :, :half_rank] + left).astype(low)
             sent[chip, lines : 2 * lines, half_rank:] = (keep_v[chip, :, half_rank:] + right).astype(low)
         theirs = peer[i, CHUNK:, :].astype(wide)
         theirs = theirs[:, :half_rank] + theirs[:, half_rank:]
+        spot = slice(i * CHUNK, (i + 1) * CHUNK)
         for t, bias in enumerate((bias_one, bias_two)):
             high, rest = in_two(bias[:, spot])
             line = jnp.concatenate(in_two((high + rest) + theirs[t : t + 1]), 1)
@@ -227,17 +227,13 @@
         sent[chip, 2 * lines :, :] = tail.astype(low)
 
 
-def finished(keep_u, keep_v, peer, bias_one, bias_two):
-    low = jnp.bfloat16
+def finished(keep_u, peer_u, keep_v, peer, bias_one, bias_two):
     chips, lines, rank = keep_v.shape
     return pl.pallas_call(
         finish_kernel,
-        out_shape=[
-            jax.ShapeDtypeStruct(keep_u.shape, low),
-            jax.ShapeDtypeStruct((chips, 2 * lines + SPARE, rank), low),
-        ],
-        compiler_params=PARAMS,
-    )(keep_u, keep_v, peer, bias_one, bias_two)
+        out_shape=jax.ShapeDtypeStruct((chips, 2 * lines + SPARE, rank), jnp.bfloat16),
+        compiler_params=PARAMS,
+    )(keep_u, peer_u, keep_v, peer, bias_one, bias_two)
 
 
 def late_kernel(place, second_adj, sums, keep, give):
@@ -307,32 +303,28 @@
 
     own_su = gathered(shared_u, "dom", chip_groups()).reshape(chips, lines, rank)
     other_v = core_swap(expert_v)
+    other_u = core_swap(expert_u)
     full_v = jnp.concatenate([expert_v, other_v], 1)
-
-    def whole(own, other):
-        pair = [jnp.where(core == 0, own, other), jnp.where(core == 0, other, own)]
-        return jnp.stack(pair, 1).reshape(width, rank)
 
     masked = jnp.where((domain_ids == domain)[:, None], cotangent, jnp.zeros_like(cotangent))
     second_adj = (masked.astype(wide) * x0.astype(wide)).astype(low)
     bias_two = jnp.sum(second_adj.astype(wide), axis=0, keepdims=True)
 
     first_part = dot(x0, full_v).astype(low)
-    whole_su = whole(own_su, core_swap(own_su))
+    whole_su = joined(own_su, 0, 1).reshape(width, rank)
     back_two_part = dot(second_adj, whole_su).astype(low)
     both = jnp.concatenate([first_part, back_two_part], 0)
     near, ring = near_groups(), ring_groups()
-    shared_v, both = lax.optimization_barrier((shared_v, both))
-    whole_sv = joined(shared_v, 0)
+    other_u, shared_v, both = lax.optimization_barrier((other_u, shared_v, both))
+    maps = joined(shared_v, 2, 0)
     part = summed(both, "feat", near)
-    part, whole_sv = lax.optimization_barrier((part, whole_sv))
-    whole_sv = joined(joined(whole_sv, 1), 2)
+    part, maps = lax.optimization_barrier((part, maps))
+    maps = joined(joined(maps, 3, 0), 1, 2)
     part = summed(part, "feat", ring)
-    part, whole_sv, expert_u = lax.optimization_barrier((part, whole_sv, expert_u))
-    whole_sv = joined(whole_sv, 3)
-    other_u = core_swap(expert_u)
+    part, maps = lax.optimization_barrier((part, maps))
+    whole_sv = joined(maps, 0, 3).reshape(width, rank)
     part = gathered(part, "feat", ring)
-    part, whole_sv, other_u, masked = lax.optimization_barrier((part, whole_sv, other_u, masked))
+    part, whole_sv, masked = lax.optimization_barrier((part, whole_sv, masked))
     sums = gathered(part, "feat", near)
 
     both, layer_one, first_adj, kept, bias_one = middle(sums, x0, masked, expert_u, other_u, whole_sv, bias)
@@ -340,17 +332,16 @@
     part = summed(both, "feat", near)
     part, give = lax.optimization_barrier((part, give))
     part = summed(part, "feat", ring)
-    part, peer = lax.optimization_barrier((part, core_swap(give)))
-    grad_eu, sent = finished(keep_eu, keep_sv, peer, bias_one, bias_two)
-    part = gathered(part, "feat", ring)
-    part, sent, grad_eu = lax.optimization_barrier((part, sent, grad_eu))
+    part, give = lax.optimization_barrier((gathered(part, "feat", ring), give))
+    peer = core_swap(give)
     sums = gathered(part, "feat", near)
 
     keep_su, give_su = late_terms(core, second_adj, sums, lines)
-    part_su = (keep_su + core_swap(give_su).astype(wide)).astype(low)
-    sent = lax.dynamic_update_slice(sent, part_su, (0, 0, 0))
+    sent = finished(keep_su, core_swap(give_su), keep_sv, peer, bias_one, bias_two)
     sent, sums = lax.optimization_barrier((sent, sums))
     taken = exchange(sent.reshape(-1, rank), "dom", chip_groups()).reshape(sent.shape)
+    peer_eu = peer[:, :CHUNK, :half_rank].reshape(width, half_rank)
+    grad_eu = (keep_eu + peer_eu.astype(wide)).astype(low)
     second_rank, back_one = sums[:rows], sums[rows:]
     partial_ev = transposed_dot(x0, back_one)
     peer_ev = core_swap(partial_ev[:, half_rank:].astype(low))

time: 235 us -> 226 us (0.962)
  starting transfers between devices: 90.6 us -> 76 us
  waiting for transfers between devices: 54.1 us -> 66.3 us
  local copies, waits for them, and re-layouts: 11.9 us -> 8.1 us
    all_to_all x7, waiting for transfers between devices: 37.6 us -> 56.1 us  [exchange(): lax.all_to_all(value, axis, 0, 0, axis_index_groups=groups, tiled=True)]
    all_to_all x7, starting transfers between devices: 42.6 us -> 32.7 us  [exchange(): lax.all_to_all(value, axis, 0, 0, axis_index_groups=groups, tiled=True)]
    ppermute x10, waiting for transfers between devices: 16.5 us -> 10.2 us  [dom_swap(): return lax.ppermute(value, 'dom', pairs)]
    ppermute x10, starting transfers between devices: 48 us -> 43.3 us  [dom_swap(): return lax.ppermute(value, 'dom', pairs)]
    unnamed x38 -> x32, local copies, waits for them, and re-layouts: 6.56 us -> 2.45 us
  transfers between devices with their start and end apart: 17 -> 17, of which waited for: 12 -> 10; matrix products, arithmetic and copies ran while one was open for 4% -> 6% of each run, Pallas kernels for 3% -> 3%
where the time goes in v8:
time: 226 us; the launch traced here: 225 us
  starting transfers between devices  76 us (34%)
  waiting for transfers between devices  66.3 us (29%)
  blocking collectives  49.5 us (22%)
  Pallas kernels  14.5 us (6%)
  local copies, waits for them, and re-layouts  8.1 us (4%)
  other arithmetic  4.89 us (2%)
  matrix products  4.03 us (2%)
    all_to_all x7, waiting for transfers between devices, exchange(): lax.all_to_all(value, axis, 0, 0, axis_index_groups=groups, tiled=True)  56.1 us
    all_to_all x3, blocking collectives, exchange(): lax.all_to_all(value, axis, 0, 0, axis_index_groups=groups, tiled=True)  49.5 us
    ppermute x10, starting transfers between devices, dom_swap(): return lax.ppermute(value, 'dom', pairs)  43.3 us
    all_to_all x7, starting transfers between devices, exchange(): lax.all_to_all(value, axis, 0, 0, axis_index_groups=groups, tiled=True)  32.7 us
    ppermute x10, waiting for transfers between devices, dom_swap(): return lax.ppermute(value, 'dom', pairs)  10.2 us
    pallas_call x1, Pallas kernels, middle(): pl.pallas_call(middle_kernel, grid=(width // CHUNK,), in_specs=[fixed, ac...  6.31 us
    pallas_call x1, Pallas kernels, early_terms(): pl.pallas_call(early_kernel, grid_spec=pltpu.PrefetchScalarGridSpec(num_s...  4.68 us
  transfers between devices with their start and end apart: 17, of which 10 were waited for; matrix products, arithmetic and copies ran while one was open for 6% of the time, Pallas kernels for 3%

profile of v8, /device:TPU:1, one launch (start us, length us, event | category | flops | bytes accessed | tf_op | source)
XLA Modules:
  0.0 224.6 jit_solution(15083835018478427997)
XLA Ops:
  0.7 8.9 %collective-permute-start = (bf16[1024,256]{1,0:T(8,128)(2,1)}, bf16[1024,256]{1,0:T(8,128)(2,1)S(1)}, u32[]{:S(2)}, u32[]{:S(2)}) collective-permute-start(bf16[1024,256]{1,0:T(8,128)(2,1)} %own_u.1), channel_id=1, source_target_pairs={{0,32},{32,0},{64,96},{96,64},{128,160},{160,128},{192,224},{224,1... | collective-permute-start | bytes 1572872 | tf_op jit(solution)/shard_map/ppermute | solution.py:18
  11.3 3.5 %all-to-all-start = ((bf16[8,64,512]{2,1,0:T(8,128)(2,1)}), bf16[8,64,512]{2,1,0:T(8,128)(2,1)S(1)}, u32[]{:S(2)}, u32[]{:S(2)}) async-start(bf16[8,64,512]{2,1,0:T(8,128)(2,1)} %broadcast_in_dim.26), calls=%async_computation | async-start | bytes 1048576 | tf_op jit(solution)/shard_map/all_to_all | solution.py:47
  18.0 7.0 %all-to-all-done = bf16[8,64,512]{2,1,0:T(8,128)(2,1)S(1)} async-done(((bf16[8,64,512]{2,1,0:T(8,128)(2,1)}), bf16[8,64,512]{2,1,0:T(8,128)(2,1)S(1)}, u32[]{:S(2)}, u32[]{:S(2)}) %all-to-all-start) | async-done | bytes 524320 | tf_op jit(solution)/shard_map/all_to_all | solution.py:47
  32.5 3.5 %all-to-all-start.1 = ((bf16[4,192,512]{2,1,0:T(8,128)(2,1)}), bf16[4,192,512]{2,1,0:T(8,128)(2,1)S(1)}, u32[]{:S(2)}, u32[]{:S(2)}) async-start(bf16[4,192,512]{2,1,0:T(8,128)(2,1)} %bitcast.5), calls=%async_computation.1 | async-start | bytes 1572864 | tf_op jit(solution)/shard_map/all_to_all | solution.py:47
  38.0 3.7 %collective-permute-done.3 = bf16[64,512]{1,0:T(8,128)(2,1)S(1)} collective-permute-done((bf16[64,512]{1,0:T(8,128)(2,1)S(1)}, bf16[64,512]{1,0:T(8,128)(2,1)S(1)}, u32[]{:S(2)}, u32[]{:S(2)}) %collective-permute-start.3) | collective-permute-done | bytes 65568 | tf_op jit(solution)/shard_map/ppermute | solution.py:18
  41.7 6.8 %all-to-all-done.1 = bf16[4,192,512]{2,1,0:T(8,128)(2,1)S(1)} async-done(((bf16[4,192,512]{2,1,0:T(8,128)(2,1)}), bf16[4,192,512]{2,1,0:T(8,128)(2,1)S(1)}, u32[]{:S(2)}, u32[]{:S(2)}) %all-to-all-start.1) | async-done | bytes 786464 | tf_op jit(solution)/shard_map/all_to_all | solution.py:47
  51.7 11.5 %all-to-all-start.2 = ((bf16[8,24,512]{2,1,0:T(8,128)(2,1)}), bf16[8,24,512]{2,1,0:T(8,128)(2,1)S(1)}, u32[]{:S(2)}, u32[]{:S(2)}) async-start(bf16[8,24,512]{2,1,0:T(8,128)(2,1)} %bitcast.8), calls=%async_computation.2 | async-start | bytes 393216 | tf_op jit(solution)/shard_map/all_to_all | solution.py:47
  65.3 6.1 %collective-permute-done.5 = bf16[2,2,64,512]{3,2,1,0:T(8,128)(2,1)S(1)} collective-permute-done((bf16[2,2,64,512]{3,2,1,0:T(8,128)(2,1)S(1)}, bf16[2,2,64,512]{3,2,1,0:T(8,128)(2,1)S(1)}, u32[]{:S(2)}, u32[]{:S(2)}) %collective-permute-start.5) | collective-permute-done | bytes 262176 | tf_op jit(solution)/shard_map/ppermute | solution.py:18
  71.4 6.7 %all-to-all-done.2 = bf16[8,24,512]{2,1,0:T(8,128)(2,1)S(1)} async-done(((bf16[8,24,512]{2,1,0:T(8,128)(2,1)}), bf16[8,24,512]{2,1,0:T(8,128)(2,1)S(1)}, u32[]{:S(2)}, u32[]{:S(2)}) %all-to-all-start.2) | async-done | bytes 196640 | tf_op jit(solution)/shard_map/all_to_all | solution.py:47
  78.2 7.1 %collective-permute-start.6 = (bf16[2,2,2,64,512]{4,3,1,0,2:T(8,128)(2,1)S(1)}, bf16[2,2,2,64,512]{4,3,1,0,2:T(8,128)(2,1)S(1)}, u32[]{:S(2)}, u32[]{:S(2)}) collective-permute-start(bf16[2,2,2,64,512]{4,3,1,0,2:T(8,128)(2,1)S(1)} %pad_maximum_fusion.3), channel_id=1, source_target_pairs={{0,32},{32,0},{64,96},{96,64},{128,160},{160,128},{192,224},{224,1... | collective-permute-start | bytes 1572872 | tf_op jit(solution)/shard_map/ppermute | solution.py:18
  86.0 3.4 %all-to-all-start.3 = ((bf16[8,24,512]{2,1,0:T(8,128)(2,1)}), bf16[8,24,512]{2,1,0:T(8,128)(2,1)S(1)}, u32[]{:S(2)}, u32[]{:S(2)}) async-start(bf16[8,24,512]{2,1,0:T(8,128)(2,1)} %broadcast_in_dim.27), calls=%async_computation.3 | async-start | bytes 393216 | tf_op jit(solution)/shard_map/all_to_all | solution.py:47
  90.7 17.1 %all-to-all-done.3 = bf16[8,24,512]{2,1,0:T(8,128)(2,1)S(1)} async-done(((bf16[8,24,512]{2,1,0:T(8,128)(2,1)}), bf16[8,24,512]{2,1,0:T(8,128)(2,1)S(1)}, u32[]{:S(2)}, u32[]{:S(2)}) %all-to-all-start.3) | async-done | bytes 196640 | tf_op jit(solution)/shard_map/all_to_all | solution.py:47
  107.8 14.6 %all_to_all.82 = bf16[4,192,512]{2,1,0:T(8,128)(2,1)S(1)} all-to-all(bf16[4,192,512]{2,1,0:T(8,128)(2,1)S(1)} %broadcast_in_dim.29), channel_id=1, replica_groups={{0,1,16,17},{2,3,18,19},{4,5,20,21},{6,7,22,23},{8,9,24,25},{10,11,26,2..., dimensions={0} | all-to-all | bytes 1572864 | tf_op jit(solution)/shard_map/all_to_all | solution.py:47
  122.4 6.3 %shard_map.127 = (bf16[768,512]{1,0:T(8,128)(2,1)}, bf16[384,1024]{1,0:T(8,128)(2,1)}, bf16[384,1024]{1,0:T(8,128)(2,1)}, f32[384,1024]{1,0:T(8,128)}, f32[1,1024]{1,0:T(1,128)S(1)}) custom-call(bf16[768,512]{1,0:T(8,128)(2,1)S(1)} %bitcast.53, bf16[384,1024]{1,0:T(8,128)(2,1)} %x0.1, bf16[384,1024]{1,0:T(8,128)(2,1)} %get-tuple-element.41.masked, ...), custom_call_target="tpu_custom_call" | custom-call | tf_op jit(solution)/shard_map/pallas_call | solution.py:119
  128.7 3.5 %all-to-all-start.5 = ((bf16[4,192,512]{2,1,0:T(8,128)(2,1)}), bf16[4,192,512]{2,1,0:T(8,128)(2,1)S(1)}, u32[]{:S(2)}, u32[]{:S(2)}) async-start(bf16[4,192,512]{2,1,0:T(8,128)(2,1)} %bitcast.61), calls=%async_computation.5 | async-start | bytes 1572864 | tf_op jit(solution)/shard_map/all_to_all | solution.py:47
  132.2 4.7 %shard_map.128 = (f32[1024,256]{1,0:T(8,128)}, f32[8,64,512]{2,1,0:T(8,128)}, bf16[4,272,512]{2,1,0:T(8,128)(2,1)}) custom-call(s32[1]{0:T(128)} %bitcast.17.place, bf16[384,1024]{1,0:T(8,128)(2,1)} %get-tuple-element.46.first_adj, bf16[384,1024]{1,0:T(8,128)(2,1)} %get-tuple-element.47.layer_one, bf16[768,512]{1,0:T(8,128)(2,1)S(1)} %bitcast.54, ...), custom_call_target="tpu_custom_call" | custom-call | tf_op jit(solution)/shard_map/pallas_call | solution.py:181
  136.9 7.1 %all-to-all-done.5 = bf16[4,192,512]{2,1,0:T(8,128)(2,1)S(1)} async-done(((bf16[4,192,512]{2,1,0:T(8,128)(2,1)}), bf16[4,192,512]{2,1,0:T(8,128)(2,1)S(1)}, u32[]{:S(2)}, u32[]{:S(2)}) %all-to-all-start.5) | async-done | bytes 786464 | tf_op jit(solution)/shard_map/all_to_all | solution.py:47
  144.1 16.2 %all_to_all.83 = bf16[8,24,512]{2,1,0:T(8,128)(2,1)S(1)} all-to-all(bf16[8,24,512]{2,1,0:T(8,128)(2,1)S(1)} %bitcast.60), channel_id=1, replica_groups={{0,2,4,6,8,10,12,14},{1,3,5,7,9,11,13,15},{16,18,20,22,24,26,28,30},{17..., dimensions={0} | all-to-all | bytes 393216 | tf_op jit(solution)/shard_map/all_to_all | solution.py:47
  160.3 18.7 %all_to_all.84 = bf16[8,24,512]{2,1,0:T(8,128)(2,1)S(1)} all-to-all(bf16[8,24,512]{2,1,0:T(8,128)(2,1)S(1)} %broadcast_in_dim.56), channel_id=1, replica_groups={{0,2,4,6,8,10,12,14},{1,3,5,7,9,11,13,15},{16,18,20,22,24,26,28,30},{17..., dimensions={0} | all-to-all | bytes 393216 | tf_op jit(solution)/shard_map/all_to_all | solution.py:47
  180.0 3.5 %all-to-all-start.8 = ((bf16[4,192,512]{2,1,0:T(8,128)(2,1)}), bf16[4,192,512]{2,1,0:T(8,128)(2,1)S(1)}, u32[]{:S(2)}, u32[]{:S(2)}) async-start(bf16[4,192,512]{2,1,0:T(8,128)(2,1)} %broadcast_in_dim.57), calls=%async_computation.8 | async-start | bytes 1572864 | tf_op jit(solution)/shard_map/all_to_all | solution.py:47
  183.5 6.2 %collective-permute-start.8 = (bf16[4,272,512]{2,1,0:T(8,128)(2,1)}, bf16[4,272,512]{2,1,0:T(8,128)(2,1)S(1)}, u32[]{:S(2)}, u32[]{:S(2)}) collective-permute-start(bf16[4,272,512]{2,1,0:T(8,128)(2,1)} %get-tuple-element.56), channel_id=1, source_target_pairs={{0,32},{32,0},{64,96},{96,64},{128,160},{160,128},{192,224},{224,1... | collective-permute-start | bytes 3342344 | tf_op jit(solution)/shard_map/ppermute | solution.py:18
  193.3 7.4 %collective-permute-start.7 = (bf16[8,64,512]{2,1,0:T(8,128)(2,1)S(1)}, bf16[8,64,512]{2,1,0:T(8,128)(2,1)S(1)}, u32[]{:S(2)}, u32[]{:S(2)}) collective-permute-start(bf16[8,64,512]{2,1,0:T(8,128)(2,1)S(1)} %get-tuple-element.54), channel_id=1, source_target_pairs={{0,32},{32,0},{64,96},{96,64},{128,160},{160,128},{192,224},{224,1... | collective-permute-start | bytes 1572872 | tf_op jit(solution)/shard_map/ppermute | solution.py:18
  203.5 3.8 %all-to-all-start.9 = ((bf16[8,144,512]{2,1,0:T(8,128)(2,1)}), bf16[8,144,512]{2,1,0:T(8,128)(2,1)S(1)}, u32[]{:S(2)}, u32[]{:S(2)}) async-start(bf16[8,144,512]{2,1,0:T(8,128)(2,1)} %shard_map.130), calls=%async_computation.9 | async-start | bytes 2359296 | tf_op jit(solution)/shard_map/all_to_all | solution.py:47
  214.3 9.5 %all-to-all-done.9.taken = bf16[8,144,512]{2,1,0:T(8,128)(2,1)S(1)} async-done(((bf16[8,144,512]{2,1,0:T(8,128)(2,1)}), bf16[8,144,512]{2,1,0:T(8,128)(2,1)S(1)}, u32[]{:S(2)}, u32[]{:S(2)}) %all-to-all-start.9) | async-done | bytes 1179680 | tf_op jit(solution)/shard_map/all_to_all | solution.py:47
  (84 shorter events, 36.8 us)
Async XLA Ops:
  0.6 16.1 %copy-start.14 = (s32[384]{0:T(512)S(1)}, s32[384]{0:T(512)}, u32[]{:S(2)}) copy-start(s32[384]{0:T(512)} %param.10) | copy-start | bytes 4612
  0.6 16.1 %copy-start.2 = (bf16[384,1024]{1,0:T(8,128)(2,1)S(1)}, bf16[384,1024]{1,0:T(8,128)(2,1)}, u32[]{:S(2)}) copy-start(bf16[384,1024]{1,0:T(8,128)(2,1)} %x0.1) | copy-start | bytes 2359300
  0.7 16.1 %copy-start.11 = (bf16[384,1024]{1,0:T(8,128)(2,1)S(1)}, bf16[384,1024]{1,0:T(8,128)(2,1)}, u32[]{:S(2)}) copy-start(bf16[384,1024]{1,0:T(8,128)(2,1)} %param.9) | copy-start | bytes 2359300
  0.7 31.8 %collective-permute-start = (bf16[1024,256]{1,0:T(8,128)(2,1)}, bf16[1024,256]{1,0:T(8,128)(2,1)S(1)}, u32[]{:S(2)}, u32[]{:S(2)}) collective-permute-start(bf16[1024,256]{1,0:T(8,128)(2,1)} %own_u.1), channel_id=1, source_target_pairs={{0,32},{32,0},{64,96},{96,64},{128,160},{160,128},{192,224},{224,1... | collective-permute-start | bytes 1572872 | tf_op jit(solution)/shard_map/ppermute | solution.py:18
  11.3 13.7 %all-to-all-start = ((bf16[8,64,512]{2,1,0:T(8,128)(2,1)}), bf16[8,64,512]{2,1,0:T(8,128)(2,1)S(1)}, u32[]{:S(2)}, u32[]{:S(2)}) async-start(bf16[8,64,512]{2,1,0:T(8,128)(2,1)} %broadcast_in_dim.26), calls=%async_computation | async-start | bytes 1048576 | tf_op jit(solution)/shard_map/all_to_all | solution.py:47
  14.8 14.0 %collective-permute-start.1 = (bf16[1024,256]{1,0:T(8,128)(2,1)}, bf16[1024,256]{1,0:T(8,128)(2,1)}, u32[]{:S(2)}, u32[]{:S(2)}) collective-permute-start(bf16[1024,256]{1,0:T(8,128)(2,1)} %param.12), channel_id=1, source_target_pairs={{0,32},{32,0},{64,96},{96,64},{128,160},{160,128},{192,224},{224,1... | collective-permute-start | bytes 1572872 | tf_op jit(solution)/shard_map/ppermute | solution.py:18
  25.0 5.5 %collective-permute-start.2 = (bf16[8,64,512]{2,1,0:T(8,128)(2,1)S(1)}, bf16[8,64,512]{2,1,0:T(8,128)(2,1)S(1)}, u32[]{:S(2)}, u32[]{:S(2)}) collective-permute-start(bf16[8,64,512]{2,1,0:T(8,128)(2,1)S(1)} %all-to-all-done), channel_id=1, source_target_pairs={{0,32},{32,0},{64,96},{96,64},{128,160},{160,128},{192,224},{224,1... | collective-permute-start | bytes 1572872 | tf_op jit(solution)/shard_map/ppermute | solution.py:18
  31.5 4.5 %copy-start.13 = (bf16[64,512]{1,0:T(8,128)(2,1)S(1)}, bf16[64,512]{1,0:T(8,128)(2,1)}, u32[]{:S(2)}) copy-start(bf16[64,512]{1,0:T(8,128)(2,1)} %param.14) | copy-start | bytes 196612
  32.5 19.2 %copy-start.12 = (bf16[1024,256]{1,0:T(8,128)(2,1)}, bf16[1024,256]{1,0:T(8,128)(2,1)S(1)}, u32[]{:S(2)}) copy-start(bf16[1024,256]{1,0:T(8,128)(2,1)S(1)} %collective-permute-done.other_u) | copy-start | bytes 1572868
  32.5 15.9 %all-to-all-start.1 = ((bf16[4,192,512]{2,1,0:T(8,128)(2,1)}), bf16[4,192,512]{2,1,0:T(8,128)(2,1)S(1)}, u32[]{:S(2)}, u32[]{:S(2)}) async-start(bf16[4,192,512]{2,1,0:T(8,128)(2,1)} %bitcast.5), calls=%async_computation.1 | async-start | bytes 1572864 | tf_op jit(solution)/shard_map/all_to_all | solution.py:47
  36.0 5.6 %collective-permute-start.3 = (bf16[64,512]{1,0:T(8,128)(2,1)S(1)}, bf16[64,512]{1,0:T(8,128)(2,1)S(1)}, u32[]{:S(2)}, u32[]{:S(2)}) collective-permute-start(bf16[64,512]{1,0:T(8,128)(2,1)S(1)} %copy-done.13), channel_id=1, source_target_pairs={{0,128},{32,160},{64,192},{96,224},{128,0},{160,32},{192,64},{224,... | collective-permute-start | bytes 196616 | tf_op jit(solution)/shard_map/ppermute | solution.py:18
  49.2 14.0 %collective-permute-start.4 = (bf16[2,64,512]{2,1,0:T(8,128)(2,1)S(1)}, bf16[2,64,512]{2,1,0:T(8,128)(2,1)S(1)}, u32[]{:S(2)}, u32[]{:S(2)}) collective-permute-start(bf16[2,64,512]{2,1,0:T(8,128)(2,1)S(1)} %pad_maximum_fusion.5), channel_id=1, source_target_pairs={{0,256},{32,288},{64,320},{96,352},{128,384},{160,416},{192,448},{... | collective-permute-start | bytes 393224 | tf_op jit(solution)/shard_map/ppermute | solution.py:18
  51.7 26.4 %all-to-all-start.2 = ((bf16[8,24,512]{2,1,0:T(8,128)(2,1)}), bf16[8,24,512]{2,1,0:T(8,128)(2,1)S(1)}, u32[]{:S(2)}, u32[]{:S(2)}) async-start(bf16[8,24,512]{2,1,0:T(8,128)(2,1)} %bitcast.8), calls=%async_computation.2 | async-start | bytes 393216 | tf_op jit(solution)/shard_map/all_to_all | solution.py:47
  63.3 8.0 %collective-permute-start.5 = (bf16[2,2,64,512]{3,2,1,0:T(8,128)(2,1)S(1)}, bf16[2,2,64,512]{3,2,1,0:T(8,128)(2,1)S(1)}, u32[]{:S(2)}, u32[]{:S(2)}) collective-permute-start(bf16[2,2,64,512]{3,2,1,0:T(8,128)(2,1)S(1)} %pad_maximum_fusion.4), channel_id=1, source_target_pairs={{0,64},{32,96},{64,0},{96,32},{128,192},{160,224},{192,128},{224,1... | collective-permute-start | bytes 786440 | tf_op jit(solution)/shard_map/ppermute | solution.py:18
  78.2 11.2 %collective-permute-start.6 = (bf16[2,2,2,64,512]{4,3,1,0,2:T(8,128)(2,1)S(1)}, bf16[2,2,2,64,512]{4,3,1,0,2:T(8,128)(2,1)S(1)}, u32[]{:S(2)}, u32[]{:S(2)}) collective-permute-start(bf16[2,2,2,64,512]{4,3,1,0,2:T(8,128)(2,1)S(1)} %pad_maximum_fusion.3), channel_id=1, source_target_pairs={{0,32},{32,0},{64,96},{96,64},{128,160},{160,128},{192,224},{224,1... | collective-permute-start | bytes 1572872 | tf_op jit(solution)/shard_map/ppermute | solution.py:18
  86.0 21.7 %all-to-all-start.3 = ((bf16[8,24,512]{2,1,0:T(8,128)(2,1)}), bf16[8,24,512]{2,1,0:T(8,128)(2,1)S(1)}, u32[]{:S(2)}, u32[]{:S(2)}) async-start(bf16[8,24,512]{2,1,0:T(8,128)(2,1)} %broadcast_in_dim.27), calls=%async_computation.3 | async-start | bytes 393216 | tf_op jit(solution)/shard_map/all_to_all | solution.py:47
  90.7 31.7 %copy-start.1 = (f32[2,1024]{1,0:T(2,128)S(1)}, f32[2,1024]{1,0:T(2,128)}, u32[]{:S(2)}) copy-start(f32[2,1024]{1,0:T(2,128)} %bias.1) | copy-start | bytes 24580
  128.7 15.2 %all-to-all-start.5 = ((bf16[4,192,512]{2,1,0:T(8,128)(2,1)}), bf16[4,192,512]{2,1,0:T(8,128)(2,1)S(1)}, u32[]{:S(2)}, u32[]{:S(2)}) async-start(bf16[4,192,512]{2,1,0:T(8,128)(2,1)} %bitcast.61), calls=%async_computation.5 | async-start | bytes 1572864 | tf_op jit(solution)/shard_map/all_to_all | solution.py:47
  180.0 11.8 %all-to-all-start.8 = ((bf16[4,192,512]{2,1,0:T(8,128)(2,1)}), bf16[4,192,512]{2,1,0:T(8,128)(2,1)S(1)}, u32[]{:S(2)}, u32[]{:S(2)}) async-start(bf16[4,192,512]{2,1,0:T(8,128)(2,1)} %broadcast_in_dim.57), calls=%async_computation.8 | async-start | bytes 1572864 | tf_op jit(solution)/shard_map/all_to_all | solution.py:47
  183.5 17.2 %collective-permute-start.8 = (bf16[4,272,512]{2,1,0:T(8,128)(2,1)}, bf16[4,272,512]{2,1,0:T(8,128)(2,1)S(1)}, u32[]{:S(2)}, u32[]{:S(2)}) collective-permute-start(bf16[4,272,512]{2,1,0:T(8,128)(2,1)} %get-tuple-element.56), channel_id=1, source_target_pairs={{0,32},{32,0},{64,96},{96,64},{128,160},{160,128},{192,224},{224,1... | collective-permute-start | bytes 3342344 | tf_op jit(solution)/shard_map/ppermute | solution.py:18
  191.8 8.9 %copy-start.10 = (f32[1024,256]{1,0:T(8,128)S(1)}, f32[1024,256]{1,0:T(8,128)}, u32[]{:S(2)}) copy-start(f32[1024,256]{1,0:T(8,128)} %get-tuple-element.59) | copy-start | bytes 3145732
  193.3 8.9 %collective-permute-start.7 = (bf16[8,64,512]{2,1,0:T(8,128)(2,1)S(1)}, bf16[8,64,512]{2,1,0:T(8,128)(2,1)S(1)}, u32[]{:S(2)}, u32[]{:S(2)}) collective-permute-start(bf16[8,64,512]{2,1,0:T(8,128)(2,1)S(1)} %get-tuple-element.54), channel_id=1, source_target_pairs={{0,32},{32,0},{64,96},{96,64},{128,160},{160,128},{192,224},{224,1... | collective-permute-start | bytes 1572872 | tf_op jit(solution)/shard_map/ppermute | solution.py:18
  203.5 20.4 %all-to-all-start.9 = ((bf16[8,144,512]{2,1,0:T(8,128)(2,1)}), bf16[8,144,512]{2,1,0:T(8,128)(2,1)S(1)}, u32[]{:S(2)}, u32[]{:S(2)}) async-start(bf16[8,144,512]{2,1,0:T(8,128)(2,1)} %shard_map.130), calls=%async_computation.9 | async-start | bytes 2359296 | tf_op jit(solution)/shard_map/all_to_all | solution.py:47
  208.1 5.1 %collective-permute-start.9 = (bf16[1024,256]{0,1:T(8,128)(2,1)S(1)}, bf16[1024,256]{0,1:T(8,128)(2,1)S(1)}, u32[]{:S(2)}, u32[]{:S(2)}) collective-permute-start(bf16[1024,256]{0,1:T(8,128)(2,1)S(1)} %slice.38), channel_id=1, source_target_pairs={{0,32},{32,0},{64,96},{96,64},{128,160},{160,128},{192,224},{224,1... | collective-permute-start | bytes 1572872 | tf_op jit(solution)/shard_map/ppermute | solution.py:18
  (8 other events, 22.1 us)

commit v9 on v8

--- a/solution.py
+++ b/solution.py
@@ -13,20 +13,9 @@
 PARAMS = pltpu.CompilerParams(vmem_limit_bytes=32 * 1024 * 1024)
 
 
-def dom_swap(value, bit):
-    pairs = [(source, source ^ 2**bit) for source in range(lax.axis_size("dom"))]
+def core_swap(value):
+    pairs = [(source, source ^ 1) for source in range(lax.axis_size("dom"))]
     return lax.ppermute(value, "dom", pairs)
-
-
-def core_swap(value):
-    return dom_swap(value, 0)
-
-
-def joined(value, bit, axis):
-    other = dom_swap(value, bit)
-    low_side = (lax.axis_index("dom") // 2**bit) % 2 == 0
-    pair = [jnp.where(low_side, value, other), jnp.where(low_side, other, value)]
-    return jnp.stack(pair, axis)
 
 
 def near_groups():
@@ -78,10 +67,27 @@
     return pltpu.with_memory_space_constraint(value, pltpu.HBM)
 
 
-def middle_kernel(sums, x0, masked, own_u, other_u, map_v, bias, both, layer_one, first_adj, kept, bias_sum, total):
+def middle_kernel(
+    place, sums, x0, masked, own_u, other_u, own_v, other_v, bias, both, layer_one, first_adj, kept, bias_sum, total, map_v
+):
     low, wide = jnp.bfloat16, jnp.float32
     rows, half_rank = x0.shape[0], own_u.shape[1]
+    chips, lines, _ = own_v.shape
     step = pl.program_id(0)
+
+    def fill(pair):
+        for chip in range(chips):
+            for i, part in enumerate(pair):
+                top = (2 * chip + i) * lines
+                map_v[top : top + lines, :] = part[chip]
+
+    @pl.when(place[0] == 0)
+    def _():
+        fill((own_v, other_v))
+
+    @pl.when(place[0] != 0)
+    def _():
+        fill((other_v, own_v))
 
     @pl.when(step == 0)
     def _():
@@ -109,26 +115,33 @@
         both[...] = total[...].astype(low)
 
 
-def middle(sums, x0, masked, own_u, other_u, map_v, bias):
+def middle(core, sums, x0, masked, own_u, other_u, own_maps, other_maps, bias):
     low, wide = jnp.bfloat16, jnp.float32
     rows, width = x0.shape
     rank = sums.shape[1]
-    across = pl.BlockSpec((rows, CHUNK), lambda i: (0, i))
-    half = pl.BlockSpec((CHUNK, rank // 2), lambda i: (i, 0))
-    fixed = pl.BlockSpec((2 * rows, rank), lambda i: (0, 0))
+    lines = own_maps.shape[1] // 2
+    across = pl.BlockSpec((rows, CHUNK), lambda i, place: (0, i))
+    half = pl.BlockSpec((CHUNK, rank // 2), lambda i, place: (i, 0))
+    fixed = pl.BlockSpec((2 * rows, rank), lambda i, place: (0, 0))
+    map_rows = pl.BlockSpec((CHUNK // (2 * lines), lines, rank), lambda i, place: (i, 1, 0))
     return pl.pallas_call(
         middle_kernel,
-        grid=(width // CHUNK,),
-        in_specs=[
-            fixed,
-            across,
-            across,
-            half,
-            half,
-            pl.BlockSpec((CHUNK, rank), lambda i: (i, 0)),
-            pl.BlockSpec((2, CHUNK), lambda i: (0, i)),
-        ],
-        out_specs=[fixed, across, across, across, pl.BlockSpec((1, CHUNK), lambda i: (0, i))],
+        grid_spec=pltpu.PrefetchScalarGridSpec(
+            num_scalar_prefetch=1,
+            grid=(width // CHUNK,),
+            in_specs=[
+                fixed,
+                across,
+                across,
+                half,
+                half,
+                map_rows,
+                map_rows,
+                pl.BlockSpec((2, CHUNK), lambda i, place: (0, i)),
+            ],
+            out_specs=[fixed, across, across, across, pl.BlockSpec((1, CHUNK), lambda i, place: (0, i))],
+            scratch_shapes=[pltpu.VMEM((2 * rows, rank), wide), pltpu.VMEM((CHUNK, rank), low)],
+        ),
         out_shape=[
             pltpu.HBM((2 * rows, rank), low),
             pltpu.HBM((rows, width), low),
@@ -136,9 +149,28 @@
             pltpu.HBM((rows, width), wide),
             jax.ShapeDtypeStruct((1, width), wide),
         ],
-        scratch_shapes=[pltpu.VMEM((2 * rows, rank), wide)],
-        compiler_params=PARAMS,
-    )(sums, *map(in_hbm, (x0, masked, own_u, other_u, map_v)), bias)
+        compiler_params=PARAMS,
+    )(core[None], sums, *map(in_hbm, (x0, masked, own_u, other_u, own_maps, other_maps)), bias)
+
+
+def spread_kernel(map_u, map_v, out):
+    lines = map_u.shape[0]
+    for chip in range(out.shape[0]):
+        out[chip, :lines, :] = map_u[...]
+        out[chip, lines:, :] = map_v[...]
+
+
+def spread(map_u, map_v, chips):
+    lines, rank = map_u.shape
+    rows = pl.BlockSpec((lines, rank), lambda i: (0, 0))
+    return pl.pallas_call(
+        spread_kernel,
+        grid=(2,),
+        in_specs=[rows, rows],
+        out_specs=pl.BlockSpec((chips // 2, 2 * lines, rank), lambda i: (i, 0, 0)),
+        out_shape=jax.ShapeDtypeStruct((chips, 2 * lines, rank), map_u.dtype),
+        compiler_params=PARAMS,
+    )(map_u, map_v)
 
 
 def halves_of(term, core, pair, lines):
@@ -301,7 +333,10 @@
     domain = lax.axis_index("dom") // 2
     core = lax.axis_index("dom") % 2
 
-    own_su = gathered(shared_u, "dom", chip_groups()).reshape(chips, lines, rank)
+    maps = spread(shared_u, shared_v, chips)
+    maps, expert_u, expert_v = lax.optimization_barrier((maps, expert_u, expert_v))
+    own_maps = exchange(maps.reshape(-1, rank), "dom", chip_groups()).reshape(maps.shape)
+    other_maps = core_swap(own_maps)
     other_v = core_swap(expert_v)
     other_u = core_swap(expert_u)
     full_v = jnp.concatenate([expert_v, other_v], 1)
@@ -311,23 +346,19 @@
     bias_two = jnp.sum(second_adj.astype(wide), axis=0, keepdims=True)
 
     first_part = dot(x0, full_v).astype(low)
-    whole_su = joined(own_su, 0, 1).reshape(width, rank)
+    own_su, other_su = own_maps[:, :lines], other_maps[:, :lines]
+    pair = [jnp.where(core == 0, own_su, other_su), jnp.where(core == 0, other_su, own_su)]
+    whole_su = jnp.stack(pair, 1).reshape(width, rank)
     back_two_part = dot(second_adj, whole_su).astype(low)
     both = jnp.concatenate([first_part, back_two_part], 0)
     near, ring = near_groups(), ring_groups()
-    other_u, shared_v, both = lax.optimization_barrier((other_u, shared_v, both))
-    maps = joined(shared_v, 2, 0)
-    part = summed(both, "feat", near)
-    part, maps = lax.optimization_barrier((part, maps))
-    maps = joined(joined(maps, 3, 0), 1, 2)
-    part = summed(part, "feat", ring)
-    part, maps = lax.optimization_barrier((part, maps))
-    whole_sv = joined(maps, 0, 3).reshape(width, rank)
-    part = gathered(part, "feat", ring)
-    part, whole_sv, masked = lax.optimization_barrier((part, whole_sv, masked))
-    sums = gathered(part, "feat", near)
-
-    both, layer_one, first_adj, kept, bias_one = middle(sums, x0, masked, expert_u, other_u, whole_sv, bias)
+    other_u, both = lax.optimization_barrier((other_u, both))
+    part = summed(summed(both, "feat", near), "feat", ring)
+    sums = gathered(gathered(part, "feat", ring), "feat", near)
+
+    both, layer_one, first_adj, kept, bias_one = middle(
+        core, sums, x0, masked, expert_u, other_u, own_maps, other_maps, bias
+    )
     keep_eu, keep_sv, give = early_terms(core, first_adj, layer_one, sums, bias_one, bias_two, lines)
     part = summed(both, "feat", near)
     part, give = lax.optimization_barrier((part, give))

time: 226 us -> 220 us (0.973)
  blocking collectives: 49.5 us -> 118 us
  waiting for transfers between devices: 66.3 us -> 16.9 us
  starting transfers between devices: 76 us -> 52.9 us
    all_to_all x3 -> x6, blocking collectives: 49.5 us -> 118 us  [exchange(): lax.all_to_all(value, axis, 0, 0, axis_index_groups=groups, tiled=True)]
    all_to_all x7 -> x4, waiting for transfers between devices: 56.1 us -> 16.4 us  [exchange(): lax.all_to_all(value, axis, 0, 0, axis_index_groups=groups, tiled=True)]
    all_to_all x7 -> x4, starting transfers between devices: 32.7 us -> 16.8 us  [exchange(): lax.all_to_all(value, axis, 0, 0, axis_index_groups=groups, tiled=True)]
    ppermute x10 -> x6, waiting for transfers between devices: 10.2 us -> 0.45 us  [core_swap(): return lax.ppermute(value, 'dom', pairs)]
    ppermute x10 -> x6, starting transfers between devices: 43.3 us -> 36.1 us  [core_swap(): return lax.ppermute(value, 'dom', pairs)]
    unnamed x32 -> x36, local copies, waits for them, and re-layouts: 2.45 us -> 4.96 us
    broadcast_in_dim x5 -> x4, local copies, waits for them, and re-layouts: 3.38 us -> 1.03 us  [gathered(): repeated = jnp.broadcast_to(value[None], (members, *value.shape))]
    pallas_call x1 -> x2, Pallas kernels: 6.31 us -> 7.38 us  [the longest x1 6.34 us: middle(): pl.pallas_call(middle_kernel, grid_spec=pltpu.PrefetchScalarGridSpec(num_...]
  transfers between devices with their start and end apart: 17 -> 10, of which waited for: 10 -> 4; matrix products, arithmetic and copies ran while one was open for 6% -> 5% of each run, Pallas kernels for 3% -> 3%
where the time goes in v9:
time: 220 us; the launch traced here: 218 us
  blocking collectives  118 us (54%)
  starting transfers between devices  52.9 us (24%)
  waiting for transfers between devices  16.9 us (8%)
  Pallas kernels  15.6 us (7%)
  local copies, waits for them, and re-layouts  7.25 us (3%)
  matrix products  4.03 us (2%)
  other arithmetic  2.99 us (1%)
    all_to_all x6, blocking collectives, exchange(): lax.all_to_all(value, axis, 0, 0, axis_index_groups=groups, tiled=True)  118 us
    ppermute x6, starting transfers between devices, core_swap(): return lax.ppermute(value, 'dom', pairs)  36.1 us
    all_to_all x4, starting transfers between devices, exchange(): lax.all_to_all(value, axis, 0, 0, axis_index_groups=groups, tiled=True)  16.8 us
    all_to_all x4, waiting for transfers between devices, exchange(): lax.all_to_all(value, axis, 0, 0, axis_index_groups=groups, tiled=True)  16.4 us
    pallas_call x1, Pallas kernels, middle(): pl.pallas_call(middle_kernel, grid_spec=pltpu.PrefetchScalarGridSpec(num_...  6.34 us
    unnamed x36, local copies, waits for them, and re-layouts  4.96 us
    pallas_call x1, Pallas kernels, early_terms(): pl.pallas_call(early_kernel, grid_spec=pltpu.PrefetchScalarGridSpec(num_s...  4.66 us
  transfers between devices with their start and end apart: 10, of which 4 were waited for; matrix products, arithmetic and copies ran while one was open for 5% of the time, Pallas kernels for 3%

profile of v9, /device:TPU:1, one launch (start us, length us, event | category | flops | bytes accessed | tf_op | source)
XLA Modules:
  0.0 218.5 jit_solution(604619163699443119)
XLA Ops:
  3.4 6.1 %all-to-all-start = ((bf16[8,128,512]{2,1,0:T(8,128)(2,1)}), bf16[8,128,512]{2,1,0:T(8,128)(2,1)S(1)}, u32[]{:S(2)}, u32[]{:S(2)}) async-start(bf16[8,128,512]{2,1,0:T(8,128)(2,1)} %shard_map.127), calls=%async_computation | async-start | bytes 2097152 | tf_op jit(solution)/shard_map/all_to_all | solution.py:36
  9.4 6.4 %collective-permute-start = (bf16[1024,256]{1,0:T(8,128)(2,1)}, bf16[1024,256]{1,0:T(8,128)(2,1)}, u32[]{:S(2)}, u32[]{:S(2)}) collective-permute-start(bf16[1024,256]{1,0:T(8,128)(2,1)} %own_u), channel_id=1, source_target_pairs={{0,32},{32,0},{64,96},{96,64},{128,160},{160,128},{192,224},{224,1... | collective-permute-start | bytes 1572872 | tf_op jit(solution)/shard_map/ppermute | solution.py:18
  15.8 1.9 collective-permute-start.1
  17.8 2.7 %all-to-all-done.own_v = bf16[8,128,512]{2,1,0:T(8,128)(2,1)S(1)} async-done(((bf16[8,128,512]{2,1,0:T(8,128)(2,1)}), bf16[8,128,512]{2,1,0:T(8,128)(2,1)S(1)}, u32[]{:S(2)}, u32[]{:S(2)}) %all-to-all-start) | async-done | bytes 1048608 | tf_op jit(solution)/shard_map/all_to_all | solution.py:36
  20.5 7.5 %collective-permute-start.2 = (bf16[8,128,512]{2,1,0:T(8,128)(2,1)S(1)}, bf16[8,128,512]{2,1,0:T(8,128)(2,1)S(1)}, u32[]{:S(2)}, u32[]{:S(2)}) collective-permute-start(bf16[8,128,512]{2,1,0:T(8,128)(2,1)S(1)} %all-to-all-done.own_v), channel_id=1, source_target_pairs={{0,32},{32,0},{64,96},{96,64},{128,160},{160,128},{192,224},{224,1... | collective-permute-start | bytes 3145736 | tf_op jit(solution)/shard_map/ppermute | solution.py:18
  34.3 17.1 %all_to_all.79 = bf16[4,192,512]{2,1,0:T(8,128)(2,1)S(1)} all-to-all(bf16[4,192,512]{2,1,0:T(8,128)(2,1)S(1)} %bitcast.40), channel_id=1, replica_groups={{0,1,16,17},{2,3,18,19},{4,5,20,21},{6,7,22,23},{8,9,24,25},{10,11,26,2..., dimensions={0} | all-to-all | bytes 1572864 | tf_op jit(solution)/shard_map/all_to_all | solution.py:36
  51.5 28.6 %all_to_all.80 = bf16[8,24,512]{2,1,0:T(8,128)(2,1)S(1)} all-to-all(bf16[8,24,512]{2,1,0:T(8,128)(2,1)S(1)} %bitcast.41), channel_id=1, replica_groups={{0,2,4,6,8,10,12,14},{1,3,5,7,9,11,13,15},{16,18,20,22,24,26,28,30},{17..., dimensions={0} | all-to-all | bytes 393216 | tf_op jit(solution)/shard_map/all_to_all | solution.py:36
  80.1 19.9 %all_to_all.81 = bf16[8,24,512]{2,1,0:T(8,128)(2,1)S(1)} all-to-all(bf16[8,24,512]{2,1,0:T(8,128)(2,1)S(1)} %broadcast_in_dim.27), channel_id=1, replica_groups={{0,2,4,6,8,10,12,14},{1,3,5,7,9,11,13,15},{16,18,20,22,24,26,28,30},{17..., dimensions={0} | all-to-all | bytes 393216 | tf_op jit(solution)/shard_map/all_to_all | solution.py:36
  100.1 12.6 %all_to_all.82 = bf16[4,192,512]{2,1,0:T(8,128)(2,1)S(1)} all-to-all(bf16[4,192,512]{2,1,0:T(8,128)(2,1)S(1)} %broadcast_in_dim.51), channel_id=1, replica_groups={{0,1,16,17},{2,3,18,19},{4,5,20,21},{6,7,22,23},{8,9,24,25},{10,11,26,2..., dimensions={0} | all-to-all | bytes 1572864 | tf_op jit(solution)/shard_map/all_to_all | solution.py:36
  112.7 6.3 %shard_map.128 = (bf16[768,512]{1,0:T(8,128)(2,1)}, bf16[384,1024]{1,0:T(8,128)(2,1)}, bf16[384,1024]{1,0:T(8,128)(2,1)}, f32[384,1024]{1,0:T(8,128)}, f32[1,1024]{1,0:T(1,128)S(1)}) custom-call(s32[1]{0:T(128)} %bitcast.place, bf16[768,512]{1,0:T(8,128)(2,1)S(1)} %bitcast.34, bf16[384,1024]{1,0:T(8,128)(2,1)} %x0.1, ...), custom_call_target="tpu_custom_call" | custom-call | tf_op jit(solution)/shard_map/pallas_call | solution.py:127
  119.1 3.5 %all-to-all-start.5 = ((bf16[4,192,512]{2,1,0:T(8,128)(2,1)}), bf16[4,192,512]{2,1,0:T(8,128)(2,1)S(1)}, u32[]{:S(2)}, u32[]{:S(2)}) async-start(bf16[4,192,512]{2,1,0:T(8,128)(2,1)} %bitcast.43), calls=%async_computation.5 | async-start | bytes 1572864 | tf_op jit(solution)/shard_map/all_to_all | solution.py:36
  122.6 4.7 %shard_map.129 = (f32[1024,256]{1,0:T(8,128)}, f32[8,64,512]{2,1,0:T(8,128)}, bf16[4,272,512]{2,1,0:T(8,128)(2,1)}) custom-call(s32[1]{0:T(128)} %bitcast.place, bf16[384,1024]{1,0:T(8,128)(2,1)} %get-tuple-element.36.first_adj, bf16[384,1024]{1,0:T(8,128)(2,1)} %get-tuple-element.37.layer_one, bf16[768,512]{1,0:T(8,128)(2,1)S(1)} %bitcast.35, ...), custom_call_target="tpu_custom_call" | custom-call | tf_op jit(solution)/shard_map/pallas_call | solution.py:213
  127.2 3.6 %all-to-all-done.5 = bf16[4,192,512]{2,1,0:T(8,128)(2,1)S(1)} async-done(((bf16[4,192,512]{2,1,0:T(8,128)(2,1)}), bf16[4,192,512]{2,1,0:T(8,128)(2,1)S(1)}, u32[]{:S(2)}, u32[]{:S(2)}) %all-to-all-start.5) | async-done | bytes 786464 | tf_op jit(solution)/shard_map/all_to_all | solution.py:36
  131.0 22.2 %all_to_all.83 = bf16[8,24,512]{2,1,0:T(8,128)(2,1)S(1)} all-to-all(bf16[8,24,512]{2,1,0:T(8,128)(2,1)S(1)} %bitcast.42), channel_id=1, replica_groups={{0,2,4,6,8,10,12,14},{1,3,5,7,9,11,13,15},{16,18,20,22,24,26,28,30},{17..., dimensions={0} | all-to-all | bytes 393216 | tf_op jit(solution)/shard_map/all_to_all | solution.py:36
  153.3 17.3 %all_to_all.84 = bf16[8,24,512]{2,1,0:T(8,128)(2,1)S(1)} all-to-all(bf16[8,24,512]{2,1,0:T(8,128)(2,1)S(1)} %broadcast_in_dim.53), channel_id=1, replica_groups={{0,2,4,6,8,10,12,14},{1,3,5,7,9,11,13,15},{16,18,20,22,24,26,28,30},{17..., dimensions={0} | all-to-all | bytes 393216 | tf_op jit(solution)/shard_map/all_to_all | solution.py:36
  171.6 3.5 %all-to-all-start.8 = ((bf16[4,192,512]{2,1,0:T(8,128)(2,1)}), bf16[4,192,512]{2,1,0:T(8,128)(2,1)S(1)}, u32[]{:S(2)}, u32[]{:S(2)}) async-start(bf16[4,192,512]{2,1,0:T(8,128)(2,1)} %broadcast_in_dim.54), calls=%async_computation.8 | async-start | bytes 1572864 | tf_op jit(solution)/shard_map/all_to_all | solution.py:36
  175.1 8.3 %collective-permute-start.4 = (bf16[4,272,512]{2,1,0:T(8,128)(2,1)}, bf16[4,272,512]{2,1,0:T(8,128)(2,1)S(1)}, u32[]{:S(2)}, u32[]{:S(2)}) collective-permute-start(bf16[4,272,512]{2,1,0:T(8,128)(2,1)} %get-tuple-element.46), channel_id=1, source_target_pairs={{0,32},{32,0},{64,96},{96,64},{128,160},{160,128},{192,224},{224,1... | collective-permute-start | bytes 3342344 | tf_op jit(solution)/shard_map/ppermute | solution.py:18
  183.4 1.5 shard_map.130
  184.9 9.4 %collective-permute-start.3 = (bf16[8,64,512]{2,1,0:T(8,128)(2,1)S(1)}, bf16[8,64,512]{2,1,0:T(8,128)(2,1)S(1)}, u32[]{:S(2)}, u32[]{:S(2)}) collective-permute-start(bf16[8,64,512]{2,1,0:T(8,128)(2,1)S(1)} %get-tuple-element.44), channel_id=1, source_target_pairs={{0,32},{32,0},{64,96},{96,64},{128,160},{160,128},{192,224},{224,1... | collective-permute-start | bytes 1572872 | tf_op jit(solution)/shard_map/ppermute | solution.py:18
  195.8 1.3 shard_map.131
  197.1 3.7 %all-to-all-start.9 = ((bf16[8,144,512]{2,1,0:T(8,128)(2,1)}), bf16[8,144,512]{2,1,0:T(8,128)(2,1)S(1)}, u32[]{:S(2)}, u32[]{:S(2)}) async-start(bf16[8,144,512]{2,1,0:T(8,128)(2,1)} %shard_map.131), calls=%async_computation.9 | async-start | bytes 2359296 | tf_op jit(solution)/shard_map/all_to_all | solution.py:36
  201.7 2.5 %collective-permute-start.5 = (bf16[1024,256]{0,1:T(8,128)(2,1)S(1)}, bf16[1024,256]{0,1:T(8,128)(2,1)S(1)}, u32[]{:S(2)}, u32[]{:S(2)}) collective-permute-start(bf16[1024,256]{0,1:T(8,128)(2,1)S(1)} %slice.54), channel_id=1, source_target_pairs={{0,32},{32,0},{64,96},{96,64},{128,160},{160,128},{192,224},{224,1... | collective-permute-start | bytes 1572872 | tf_op jit(solution)/shard_map/ppermute | solution.py:18
  204.9 1.6 fusion.3
  207.6 10.1 %all-to-all-done.9.taken = bf16[8,144,512]{2,1,0:T(8,128)(2,1)S(1)} async-done(((bf16[8,144,512]{2,1,0:T(8,128)(2,1)}), bf16[8,144,512]{2,1,0:T(8,128)(2,1)S(1)}, u32[]{:S(2)}, u32[]{:S(2)}) %all-to-all-start.9) | async-done | bytes 1179680 | tf_op jit(solution)/shard_map/all_to_all | solution.py:36
  (69 shorter events, 15.0 us)
Async XLA Ops:
  3.3 25.8 %copy-start.16 = (s32[384]{0:T(512)S(1)}, s32[384]{0:T(512)}, u32[]{:S(2)}) copy-start(s32[384]{0:T(512)} %param.10) | copy-start | bytes 4612
  3.4 25.8 %copy-start.4 = (bf16[384,1024]{1,0:T(8,128)(2,1)S(1)}, bf16[384,1024]{1,0:T(8,128)(2,1)}, u32[]{:S(2)}) copy-start(bf16[384,1024]{1,0:T(8,128)(2,1)} %x0.1) | copy-start | bytes 2359300
  3.4 25.9 %copy-start.15 = (bf16[384,1024]{1,0:T(8,128)(2,1)S(1)}, bf16[384,1024]{1,0:T(8,128)(2,1)}, u32[]{:S(2)}) copy-start(bf16[384,1024]{1,0:T(8,128)(2,1)} %param.9) | copy-start | bytes 2359300
  3.4 17.2 %all-to-all-start = ((bf16[8,128,512]{2,1,0:T(8,128)(2,1)}), bf16[8,128,512]{2,1,0:T(8,128)(2,1)S(1)}, u32[]{:S(2)}, u32[]{:S(2)}) async-start(bf16[8,128,512]{2,1,0:T(8,128)(2,1)} %shard_map.127), calls=%async_computation | async-start | bytes 2097152 | tf_op jit(solution)/shard_map/all_to_all | solution.py:36
  9.4 24.8 %collective-permute-start = (bf16[1024,256]{1,0:T(8,128)(2,1)}, bf16[1024,256]{1,0:T(8,128)(2,1)}, u32[]{:S(2)}, u32[]{:S(2)}) collective-permute-start(bf16[1024,256]{1,0:T(8,128)(2,1)} %own_u), channel_id=1, source_target_pairs={{0,32},{32,0},{64,96},{96,64},{128,160},{160,128},{192,224},{224,1... | collective-permute-start | bytes 1572872 | tf_op jit(solution)/shard_map/ppermute | solution.py:18
  15.8 14.6 %collective-permute-start.1 = (bf16[1024,256]{1,0:T(8,128)(2,1)}, bf16[1024,256]{1,0:T(8,128)(2,1)}, u32[]{:S(2)}, u32[]{:S(2)}) collective-permute-start(bf16[1024,256]{1,0:T(8,128)(2,1)} %param.12), channel_id=1, source_target_pairs={{0,32},{32,0},{64,96},{96,64},{128,160},{160,128},{192,224},{224,1... | collective-permute-start | bytes 1572872 | tf_op jit(solution)/shard_map/ppermute | solution.py:18
  20.5 11.6 %copy-start.7 = (bf16[8,128,512]{2,1,0:T(8,128)(2,1)}, bf16[8,128,512]{2,1,0:T(8,128)(2,1)S(1)}, u32[]{:S(2)}) copy-start(bf16[8,128,512]{2,1,0:T(8,128)(2,1)S(1)} %all-to-all-done.own_v) | copy-start | bytes 3145732
  20.5 11.6 %collective-permute-start.2 = (bf16[8,128,512]{2,1,0:T(8,128)(2,1)S(1)}, bf16[8,128,512]{2,1,0:T(8,128)(2,1)S(1)}, u32[]{:S(2)}, u32[]{:S(2)}) collective-permute-start(bf16[8,128,512]{2,1,0:T(8,128)(2,1)S(1)} %all-to-all-done.own_v), channel_id=1, source_target_pairs={{0,32},{32,0},{64,96},{96,64},{128,160},{160,128},{192,224},{224,1... | collective-permute-start | bytes 3145736 | tf_op jit(solution)/shard_map/ppermute | solution.py:18
  32.2 1.0 copy-start.10
  33.3 1.0 copy-start.8
  80.1 32.6 %copy-start.3 = (f32[2,1024]{1,0:T(2,128)S(1)}, f32[2,1024]{1,0:T(2,128)}, u32[]{:S(2)}) copy-start(f32[2,1024]{1,0:T(2,128)} %bias.1) | copy-start | bytes 24580
  119.1 11.8 %all-to-all-start.5 = ((bf16[4,192,512]{2,1,0:T(8,128)(2,1)}), bf16[4,192,512]{2,1,0:T(8,128)(2,1)S(1)}, u32[]{:S(2)}, u32[]{:S(2)}) async-start(bf16[4,192,512]{2,1,0:T(8,128)(2,1)} %bitcast.43), calls=%async_computation.5 | async-start | bytes 1572864 | tf_op jit(solution)/shard_map/all_to_all | solution.py:36
  171.6 11.8 %all-to-all-start.8 = ((bf16[4,192,512]{2,1,0:T(8,128)(2,1)}), bf16[4,192,512]{2,1,0:T(8,128)(2,1)S(1)}, u32[]{:S(2)}, u32[]{:S(2)}) async-start(bf16[4,192,512]{2,1,0:T(8,128)(2,1)} %broadcast_in_dim.54), calls=%async_computation.8 | async-start | bytes 1572864 | tf_op jit(solution)/shard_map/all_to_all | solution.py:36
  175.1 19.3 %collective-permute-start.4 = (bf16[4,272,512]{2,1,0:T(8,128)(2,1)}, bf16[4,272,512]{2,1,0:T(8,128)(2,1)S(1)}, u32[]{:S(2)}, u32[]{:S(2)}) collective-permute-start(bf16[4,272,512]{2,1,0:T(8,128)(2,1)} %get-tuple-element.46), channel_id=1, source_target_pairs={{0,32},{32,0},{64,96},{96,64},{128,160},{160,128},{192,224},{224,1... | collective-permute-start | bytes 3342344 | tf_op jit(solution)/shard_map/ppermute | solution.py:18
  183.4 11.0 %copy-start.14 = (f32[1024,256]{1,0:T(8,128)S(1)}, f32[1024,256]{1,0:T(8,128)}, u32[]{:S(2)}) copy-start(f32[1024,256]{1,0:T(8,128)} %get-tuple-element.49) | copy-start | bytes 3145732
  184.9 10.9 %collective-permute-start.3 = (bf16[8,64,512]{2,1,0:T(8,128)(2,1)S(1)}, bf16[8,64,512]{2,1,0:T(8,128)(2,1)S(1)}, u32[]{:S(2)}, u32[]{:S(2)}) collective-permute-start(bf16[8,64,512]{2,1,0:T(8,128)(2,1)S(1)} %get-tuple-element.44), channel_id=1, source_target_pairs={{0,32},{32,0},{64,96},{96,64},{128,160},{160,128},{192,224},{224,1... | collective-permute-start | bytes 1572872 | tf_op jit(solution)/shard_map/ppermute | solution.py:18
  194.3 1.5 copy-start
  197.1 3.7 %copy-start.5 = (bf16[384,1024]{1,0:T(8,128)(2,1)S(1)}, bf16[384,1024]{1,0:T(8,128)(2,1)}, u32[]{:S(2)}) copy-start(bf16[384,1024]{1,0:T(8,128)(2,1)} %x0.1) | copy-start | bytes 2359300
  197.1 20.5 %all-to-all-start.9 = ((bf16[8,144,512]{2,1,0:T(8,128)(2,1)}), bf16[8,144,512]{2,1,0:T(8,128)(2,1)S(1)}, u32[]{:S(2)}, u32[]{:S(2)}) async-start(bf16[8,144,512]{2,1,0:T(8,128)(2,1)} %shard_map.131), calls=%async_computation.9 | async-start | bytes 2359296 | tf_op jit(solution)/shard_map/all_to_all | solution.py:36
  200.9 3.4 %copy-start.9 = (bf16[8,2,64,512]{3,2,1,0:T(8,128)(2,1)S(1)}, bf16[8,2,64,512]{3,2,1,0:T(8,128)(2,1)}, u32[]{:S(2)}) copy-start(bf16[8,2,64,512]{3,2,1,0:T(8,128)(2,1)} %copy-done.8) | copy-start | bytes 3145732
  201.6 3.3 %copy-start.13 = (f32[384,1024]{1,0:T(8,128)S(1)}, f32[384,1024]{1,0:T(8,128)}, u32[]{:S(2)}) copy-start(f32[384,1024]{1,0:T(8,128)} %get-tuple-element.48) | copy-start | bytes 4718596
  201.7 3.2 %copy-start.6 = (bf16[384,1024]{1,0:T(8,128)(2,1)S(1)}, bf16[384,1024]{1,0:T(8,128)(2,1)}, u32[]{:S(2)}) copy-start(bf16[384,1024]{1,0:T(8,128)(2,1)} %get-tuple-element.74.masked) | copy-start | bytes 2359300
  201.7 3.2 %copy-start.12 = (bf16[1024,512]{1,0:T(8,128)(2,1)S(1)}, bf16[1024,512]{1,0:T(8,128)(2,1)}, u32[]{:S(2)}) copy-start(bf16[1024,512]{1,0:T(8,128)(2,1)} %copy-done.11) | copy-start | bytes 3145732
  201.7 4.8 %collective-permute-start.5 = (bf16[1024,256]{0,1:T(8,128)(2,1)S(1)}, bf16[1024,256]{0,1:T(8,128)(2,1)S(1)}, u32[]{:S(2)}, u32[]{:S(2)}) collective-permute-start(bf16[1024,256]{0,1:T(8,128)(2,1)S(1)} %slice.54), channel_id=1, source_target_pairs={{0,32},{32,0},{64,96},{96,64},{128,160},{160,128},{192,224},{224,1... | collective-permute-start | bytes 1572872 | tf_op jit(solution)/shard_map/ppermute | solution.py:18
  (3 other events, 2.7 us)

commit v10 on v9

--- a/solution.py
+++ b/solution.py
@@ -170,7 +170,7 @@
         out_specs=pl.BlockSpec((chips // 2, 2 * lines, rank), lambda i: (i, 0, 0)),
         out_shape=jax.ShapeDtypeStruct((chips, 2 * lines, rank), map_u.dtype),
         compiler_params=PARAMS,
-    )(map_u, map_v)
+    )(in_hbm(map_u), in_hbm(map_v))
 
 
 def halves_of(term, core, pair, lines):
@@ -336,7 +336,6 @@
     maps = spread(shared_u, shared_v, chips)
     maps, expert_u, expert_v = lax.optimization_barrier((maps, expert_u, expert_v))
     own_maps = exchange(maps.reshape(-1, rank), "dom", chip_groups()).reshape(maps.shape)
-    other_maps = core_swap(own_maps)
     other_v = core_swap(expert_v)
     other_u = core_swap(expert_u)
     full_v = jnp.concatenate([expert_v, other_v], 1)
@@ -346,6 +345,8 @@
     bias_two = jnp.sum(second_adj.astype(wide), axis=0, keepdims=True)
 
     first_part = dot(x0, full_v).astype(low)
+    own_maps, first_part, second_adj, bias_two = lax.optimization_barrier((own_maps, first_part, second_adj, bias_two))
+    other_maps = core_swap(own_maps)
     own_su, other_su = own_maps[:, :lines], other_maps[:, :lines]
     pair = [jnp.where(core == 0, own_su, other_su), jnp.where(core == 0, other_su, own_su)]
     whole_su = jnp.stack(pair, 1).reshape(width, rank)

time: 220 us -> 217 us (0.986)
  blocking collectives: 118 us -> 115 us
  waiting for transfers between devices: 16.9 us -> 14.6 us
    all_to_all x4, waiting for transfers between devices: 16.4 us -> 13.7 us  [exchange(): lax.all_to_all(value, axis, 0, 0, axis_index_groups=groups, tiled=True)]
    all_to_all x6, blocking collectives: 118 us -> 115 us  [exchange(): lax.all_to_all(value, axis, 0, 0, axis_index_groups=groups, tiled=True)]
    unnamed x36 -> x34, local copies, waits for them, and re-layouts: 4.96 us -> 4.04 us
  transfers between devices with their start and end apart: 10 -> 10, of which waited for: 4 -> 4; matrix products, arithmetic and copies ran while one was open for 5% -> 6% of each run, Pallas kernels for 3% -> 3%
where the time goes in v10:
time: 217 us; the launch traced here: 215 us
  blocking collectives  115 us (53%)
  starting transfers between devices  53 us (24%)
  Pallas kernels  16.5 us (8%)
  waiting for transfers between devices  14.6 us (7%)
  local copies, waits for them, and re-layouts  6.68 us (3%)
  matrix products  4.41 us (2%)
  other arithmetic  4.04 us (2%)
    all_to_all x6, blocking collectives, exchange(): lax.all_to_all(value, axis, 0, 0, axis_index_groups=groups, tiled=True)  115 us
    ppermute x6, starting transfers between devices, core_swap(): return lax.ppermute(value, 'dom', pairs)  36.3 us
    all_to_all x4, starting transfers between devices, exchange(): lax.all_to_all(value, axis, 0, 0, axis_index_groups=groups, tiled=True)  16.8 us
    all_to_all x4, waiting for transfers between devices, exchange(): lax.all_to_all(value, axis, 0, 0, axis_index_groups=groups, tiled=True)  13.7 us
    pallas_call x1, Pallas kernels, middle(): pl.pallas_call(middle_kernel, grid_spec=pltpu.PrefetchScalarGridSpec(num_...  6.33 us
    pallas_call x1, Pallas kernels, early_terms(): pl.pallas_call(early_kernel, grid_spec=pltpu.PrefetchScalarGridSpec(num_s...  4.7 us
  transfers between devices with their start and end apart: 10, of which 4 were waited for; matrix products, arithmetic and copies ran while one was open for 6% of the time, Pallas kernels for 3%

profile of v10, /device:TPU:1, one launch (start us, length us, event | category | flops | bytes accessed | tf_op | source)
XLA Modules:
  0.0 215.5 jit_solution(9721451391558156392)
XLA Ops:
  0.6 1.9 shard_map.127
  2.5 6.1 %all-to-all-start = ((bf16[8,128,512]{2,1,0:T(8,128)(2,1)}), bf16[8,128,512]{2,1,0:T(8,128)(2,1)S(1)}, u32[]{:S(2)}, u32[]{:S(2)}) async-start(bf16[8,128,512]{2,1,0:T(8,128)(2,1)} %shard_map.127), calls=%async_computation | async-start | bytes 2097152 | tf_op jit(solution)/shard_map/all_to_all | solution.py:36
  8.6 6.4 %collective-permute-start = (bf16[1024,256]{1,0:T(8,128)(2,1)}, bf16[1024,256]{1,0:T(8,128)(2,1)}, u32[]{:S(2)}, u32[]{:S(2)}) collective-permute-start(bf16[1024,256]{1,0:T(8,128)(2,1)} %param.12), channel_id=1, source_target_pairs={{0,32},{32,0},{64,96},{96,64},{128,160},{160,128},{192,224},{224,1... | collective-permute-start | bytes 1572872 | tf_op jit(solution)/shard_map/ppermute | solution.py:18
  15.1 1.9 constant_dynamic-update-slice_fusion.1
  21.2 6.1 %collective-permute-start.2 = (bf16[8,128,512]{2,1,0:T(8,128)(2,1)S(1)}, bf16[8,128,512]{2,1,0:T(8,128)(2,1)}, u32[]{:S(2)}, u32[]{:S(2)}) collective-permute-start(bf16[8,128,512]{2,1,0:T(8,128)(2,1)S(1)} %all-to-all-done.own_v), channel_id=1, source_target_pairs={{0,32},{32,0},{64,96},{96,64},{128,160},{160,128},{192,224},{224,1... | collective-permute-start | bytes 3145736 | tf_op jit(solution)/shard_map/ppermute | solution.py:18
  27.3 1.9 collective-permute-start.1
  32.3 16.4 %all_to_all.79 = bf16[4,192,512]{2,1,0:T(8,128)(2,1)S(1)} all-to-all(bf16[4,192,512]{2,1,0:T(8,128)(2,1)S(1)} %bitcast.40), channel_id=1, replica_groups={{0,1,16,17},{2,3,18,19},{4,5,20,21},{6,7,22,23},{8,9,24,25},{10,11,26,2..., dimensions={0} | all-to-all | bytes 1572864 | tf_op jit(solution)/shard_map/all_to_all | solution.py:36
  48.8 28.0 %all_to_all.80 = bf16[8,24,512]{2,1,0:T(8,128)(2,1)S(1)} all-to-all(bf16[8,24,512]{2,1,0:T(8,128)(2,1)S(1)} %bitcast.41), channel_id=1, replica_groups={{0,2,4,6,8,10,12,14},{1,3,5,7,9,11,13,15},{16,18,20,22,24,26,28,30},{17..., dimensions={0} | all-to-all | bytes 393216 | tf_op jit(solution)/shard_map/all_to_all | solution.py:36
  76.8 20.1 %all_to_all.81 = bf16[8,24,512]{2,1,0:T(8,128)(2,1)S(1)} all-to-all(bf16[8,24,512]{2,1,0:T(8,128)(2,1)S(1)} %broadcast_in_dim.50), channel_id=1, replica_groups={{0,2,4,6,8,10,12,14},{1,3,5,7,9,11,13,15},{16,18,20,22,24,26,28,30},{17..., dimensions={0} | all-to-all | bytes 393216 | tf_op jit(solution)/shard_map/all_to_all | solution.py:36
  97.0 11.7 %all_to_all.82 = bf16[4,192,512]{2,1,0:T(8,128)(2,1)S(1)} all-to-all(bf16[4,192,512]{2,1,0:T(8,128)(2,1)S(1)} %broadcast_in_dim.52), channel_id=1, replica_groups={{0,1,16,17},{2,3,18,19},{4,5,20,21},{6,7,22,23},{8,9,24,25},{10,11,26,2..., dimensions={0} | all-to-all | bytes 1572864 | tf_op jit(solution)/shard_map/all_to_all | solution.py:36
  108.7 6.3 %shard_map.128 = (bf16[768,512]{1,0:T(8,128)(2,1)}, bf16[384,1024]{1,0:T(8,128)(2,1)}, bf16[384,1024]{1,0:T(8,128)(2,1)}, f32[384,1024]{1,0:T(8,128)}, f32[1,1024]{1,0:T(1,128)S(1)}) custom-call(s32[1]{0:T(128)} %bitcast.place, bf16[768,512]{1,0:T(8,128)(2,1)S(1)} %bitcast.34, bf16[384,1024]{1,0:T(8,128)(2,1)} %x0.1, ...), custom_call_target="tpu_custom_call" | custom-call | tf_op jit(solution)/shard_map/pallas_call | solution.py:127
  115.0 3.5 %all-to-all-start.5 = ((bf16[4,192,512]{2,1,0:T(8,128)(2,1)}), bf16[4,192,512]{2,1,0:T(8,128)(2,1)S(1)}, u32[]{:S(2)}, u32[]{:S(2)}) async-start(bf16[4,192,512]{2,1,0:T(8,128)(2,1)} %bitcast.43), calls=%async_computation.5 | async-start | bytes 1572864 | tf_op jit(solution)/shard_map/all_to_all | solution.py:36
  118.5 4.7 %shard_map.129 = (f32[1024,256]{1,0:T(8,128)}, f32[8,64,512]{2,1,0:T(8,128)}, bf16[4,272,512]{2,1,0:T(8,128)(2,1)}) custom-call(s32[1]{0:T(128)} %bitcast.place, bf16[384,1024]{1,0:T(8,128)(2,1)} %get-tuple-element.43.first_adj, bf16[384,1024]{1,0:T(8,128)(2,1)} %get-tuple-element.44.layer_one, bf16[768,512]{1,0:T(8,128)(2,1)S(1)} %bitcast.35, ...), custom_call_target="tpu_custom_call" | custom-call | tf_op jit(solution)/shard_map/pallas_call | solution.py:213
  123.2 3.6 %all-to-all-done.5 = bf16[4,192,512]{2,1,0:T(8,128)(2,1)S(1)} async-done(((bf16[4,192,512]{2,1,0:T(8,128)(2,1)}), bf16[4,192,512]{2,1,0:T(8,128)(2,1)S(1)}, u32[]{:S(2)}, u32[]{:S(2)}) %all-to-all-start.5) | async-done | bytes 786464 | tf_op jit(solution)/shard_map/all_to_all | solution.py:36
  126.9 21.9 %all_to_all.83 = bf16[8,24,512]{2,1,0:T(8,128)(2,1)S(1)} all-to-all(bf16[8,24,512]{2,1,0:T(8,128)(2,1)S(1)} %bitcast.42), channel_id=1, replica_groups={{0,2,4,6,8,10,12,14},{1,3,5,7,9,11,13,15},{16,18,20,22,24,26,28,30},{17..., dimensions={0} | all-to-all | bytes 393216 | tf_op jit(solution)/shard_map/all_to_all | solution.py:36
  148.9 17.2 %all_to_all.84 = bf16[8,24,512]{2,1,0:T(8,128)(2,1)S(1)} all-to-all(bf16[8,24,512]{2,1,0:T(8,128)(2,1)S(1)} %broadcast_in_dim.53), channel_id=1, replica_groups={{0,2,4,6,8,10,12,14},{1,3,5,7,9,11,13,15},{16,18,20,22,24,26,28,30},{17..., dimensions={0} | all-to-all | bytes 393216 | tf_op jit(solution)/shard_map/all_to_all | solution.py:36
  167.0 3.5 %all-to-all-start.8 = ((bf16[4,192,512]{2,1,0:T(8,128)(2,1)}), bf16[4,192,512]{2,1,0:T(8,128)(2,1)S(1)}, u32[]{:S(2)}, u32[]{:S(2)}) async-start(bf16[4,192,512]{2,1,0:T(8,128)(2,1)} %broadcast_in_dim.54), calls=%async_computation.8 | async-start | bytes 1572864 | tf_op jit(solution)/shard_map/all_to_all | solution.py:36
  170.5 9.9 %collective-permute-start.4 = (bf16[4,272,512]{2,1,0:T(8,128)(2,1)}, bf16[4,272,512]{2,1,0:T(8,128)(2,1)S(1)}, u32[]{:S(2)}, u32[]{:S(2)}) collective-permute-start(bf16[4,272,512]{2,1,0:T(8,128)(2,1)} %get-tuple-element.54), channel_id=1, source_target_pairs={{0,32},{32,0},{64,96},{96,64},{128,160},{160,128},{192,224},{224,1... | collective-permute-start | bytes 3342344 | tf_op jit(solution)/shard_map/ppermute | solution.py:18
  180.4 1.5 shard_map.130
  181.9 9.4 %collective-permute-start.3 = (bf16[8,64,512]{2,1,0:T(8,128)(2,1)S(1)}, bf16[8,64,512]{2,1,0:T(8,128)(2,1)S(1)}, u32[]{:S(2)}, u32[]{:S(2)}) collective-permute-start(bf16[8,64,512]{2,1,0:T(8,128)(2,1)S(1)} %get-tuple-element.52), channel_id=1, source_target_pairs={{0,32},{32,0},{64,96},{96,64},{128,160},{160,128},{192,224},{224,1... | collective-permute-start | bytes 1572872 | tf_op jit(solution)/shard_map/ppermute | solution.py:18
  194.2 3.7 %all-to-all-start.9 = ((bf16[8,144,512]{2,1,0:T(8,128)(2,1)}), bf16[8,144,512]{2,1,0:T(8,128)(2,1)S(1)}, u32[]{:S(2)}, u32[]{:S(2)}) async-start(bf16[8,144,512]{2,1,0:T(8,128)(2,1)} %shard_map.131), calls=%async_computation.9 | async-start | bytes 2359296 | tf_op jit(solution)/shard_map/all_to_all | solution.py:36
  198.7 2.5 %collective-permute-start.5 = (bf16[1024,256]{0,1:T(8,128)(2,1)S(1)}, bf16[1024,256]{0,1:T(8,128)(2,1)S(1)}, u32[]{:S(2)}, u32[]{:S(2)}) collective-permute-start(bf16[1024,256]{0,1:T(8,128)(2,1)S(1)} %slice.53), channel_id=1, source_target_pairs={{0,32},{32,0},{64,96},{96,64},{128,160},{160,128},{192,224},{224,1... | collective-permute-start | bytes 1572872 | tf_op jit(solution)/shard_map/ppermute | solution.py:18
  201.9 1.6 fusion.3
  204.7 10.1 %all-to-all-done.9.taken = bf16[8,144,512]{2,1,0:T(8,128)(2,1)S(1)} async-done(((bf16[8,144,512]{2,1,0:T(8,128)(2,1)}), bf16[8,144,512]{2,1,0:T(8,128)(2,1)S(1)}, u32[]{:S(2)}, u32[]{:S(2)}) %all-to-all-start.9) | async-done | bytes 1179680 | tf_op jit(solution)/shard_map/all_to_all | solution.py:36
  (68 shorter events, 14.7 us)
Async XLA Ops:
  2.5 14.4 %copy-start.15 = (s32[384]{0:T(512)S(1)}, s32[384]{0:T(512)}, u32[]{:S(2)}) copy-start(s32[384]{0:T(512)} %param.10) | copy-start | bytes 4612
  2.5 14.4 %copy-start.2 = (bf16[384,1024]{1,0:T(8,128)(2,1)S(1)}, bf16[384,1024]{1,0:T(8,128)(2,1)}, u32[]{:S(2)}) copy-start(bf16[384,1024]{1,0:T(8,128)(2,1)} %x0.1) | copy-start | bytes 2359300
  2.5 14.4 %copy-start.13 = (bf16[384,1024]{1,0:T(8,128)(2,1)S(1)}, bf16[384,1024]{1,0:T(8,128)(2,1)}, u32[]{:S(2)}) copy-start(bf16[384,1024]{1,0:T(8,128)(2,1)} %param.9) | copy-start | bytes 2359300
  2.5 18.6 %all-to-all-start = ((bf16[8,128,512]{2,1,0:T(8,128)(2,1)}), bf16[8,128,512]{2,1,0:T(8,128)(2,1)S(1)}, u32[]{:S(2)}, u32[]{:S(2)}) async-start(bf16[8,128,512]{2,1,0:T(8,128)(2,1)} %shard_map.127), calls=%async_computation | async-start | bytes 2097152 | tf_op jit(solution)/shard_map/all_to_all | solution.py:36
  8.6 9.6 %collective-permute-start = (bf16[1024,256]{1,0:T(8,128)(2,1)}, bf16[1024,256]{1,0:T(8,128)(2,1)}, u32[]{:S(2)}, u32[]{:S(2)}) collective-permute-start(bf16[1024,256]{1,0:T(8,128)(2,1)} %param.12), channel_id=1, source_target_pairs={{0,32},{32,0},{64,96},{96,64},{128,160},{160,128},{192,224},{224,1... | collective-permute-start | bytes 1572872 | tf_op jit(solution)/shard_map/ppermute | solution.py:18
  17.0 1.3 copy-start.8
  18.2 9.1 %copy-start.14 = (bf16[1024,256]{1,0:T(8,128)(2,1)S(1)}, bf16[1024,256]{1,0:T(8,128)(2,1)}, u32[]{:S(2)}) copy-start(bf16[1024,256]{1,0:T(8,128)(2,1)} %own_u) | copy-start | bytes 1572868
  21.1 9.8 %copy-start.5 = (bf16[8,128,512]{2,1,0:T(8,128)(2,1)}, bf16[8,128,512]{2,1,0:T(8,128)(2,1)S(1)}, u32[]{:S(2)}) copy-start(bf16[8,128,512]{2,1,0:T(8,128)(2,1)S(1)} %all-to-all-done.own_v) | copy-start | bytes 3145732
  21.2 8.5 %collective-permute-start.2 = (bf16[8,128,512]{2,1,0:T(8,128)(2,1)S(1)}, bf16[8,128,512]{2,1,0:T(8,128)(2,1)}, u32[]{:S(2)}, u32[]{:S(2)}) collective-permute-start(bf16[8,128,512]{2,1,0:T(8,128)(2,1)S(1)} %all-to-all-done.own_v), channel_id=1, source_target_pairs={{0,32},{32,0},{64,96},{96,64},{128,160},{160,128},{192,224},{224,1... | collective-permute-start | bytes 3145736 | tf_op jit(solution)/shard_map/ppermute | solution.py:18
  27.3 4.7 %collective-permute-start.1 = (bf16[1024,256]{1,0:T(8,128)(2,1)S(1)}, bf16[1024,256]{1,0:T(8,128)(2,1)}, u32[]{:S(2)}, u32[]{:S(2)}) collective-permute-start(bf16[1024,256]{1,0:T(8,128)(2,1)S(1)} %copy-done.14), channel_id=1, source_target_pairs={{0,32},{32,0},{64,96},{96,64},{128,160},{160,128},{192,224},{224,1... | collective-permute-start | bytes 1572872 | tf_op jit(solution)/shard_map/ppermute | solution.py:18
  76.8 31.9 %copy-start.1 = (f32[2,1024]{1,0:T(2,128)S(1)}, f32[2,1024]{1,0:T(2,128)}, u32[]{:S(2)}) copy-start(f32[2,1024]{1,0:T(2,128)} %bias.1) | copy-start | bytes 24580
  115.0 11.8 %all-to-all-start.5 = ((bf16[4,192,512]{2,1,0:T(8,128)(2,1)}), bf16[4,192,512]{2,1,0:T(8,128)(2,1)S(1)}, u32[]{:S(2)}, u32[]{:S(2)}) async-start(bf16[4,192,512]{2,1,0:T(8,128)(2,1)} %bitcast.43), calls=%async_computation.5 | async-start | bytes 1572864 | tf_op jit(solution)/shard_map/all_to_all | solution.py:36
  167.0 13.4 %all-to-all-start.8 = ((bf16[4,192,512]{2,1,0:T(8,128)(2,1)}), bf16[4,192,512]{2,1,0:T(8,128)(2,1)S(1)}, u32[]{:S(2)}, u32[]{:S(2)}) async-start(bf16[4,192,512]{2,1,0:T(8,128)(2,1)} %broadcast_in_dim.54), calls=%async_computation.8 | async-start | bytes 1572864 | tf_op jit(solution)/shard_map/all_to_all | solution.py:36
  170.5 20.8 %collective-permute-start.4 = (bf16[4,272,512]{2,1,0:T(8,128)(2,1)}, bf16[4,272,512]{2,1,0:T(8,128)(2,1)S(1)}, u32[]{:S(2)}, u32[]{:S(2)}) collective-permute-start(bf16[4,272,512]{2,1,0:T(8,128)(2,1)} %get-tuple-element.54), channel_id=1, source_target_pairs={{0,32},{32,0},{64,96},{96,64},{128,160},{160,128},{192,224},{224,1... | collective-permute-start | bytes 3342344 | tf_op jit(solution)/shard_map/ppermute | solution.py:18
  180.4 11.0 %copy-start.12 = (f32[1024,256]{1,0:T(8,128)S(1)}, f32[1024,256]{1,0:T(8,128)}, u32[]{:S(2)}) copy-start(f32[1024,256]{1,0:T(8,128)} %get-tuple-element.57) | copy-start | bytes 3145732
  181.9 10.9 %collective-permute-start.3 = (bf16[8,64,512]{2,1,0:T(8,128)(2,1)S(1)}, bf16[8,64,512]{2,1,0:T(8,128)(2,1)S(1)}, u32[]{:S(2)}, u32[]{:S(2)}) collective-permute-start(bf16[8,64,512]{2,1,0:T(8,128)(2,1)S(1)} %get-tuple-element.52), channel_id=1, source_target_pairs={{0,32},{32,0},{64,96},{96,64},{128,160},{160,128},{192,224},{224,1... | collective-permute-start | bytes 1572872 | tf_op jit(solution)/shard_map/ppermute | solution.py:18
  191.3 1.5 copy-start
  194.2 3.7 %copy-start.3 = (bf16[384,1024]{1,0:T(8,128)(2,1)S(1)}, bf16[384,1024]{1,0:T(8,128)(2,1)}, u32[]{:S(2)}) copy-start(bf16[384,1024]{1,0:T(8,128)(2,1)} %x0.1) | copy-start | bytes 2359300
  194.2 20.5 %all-to-all-start.9 = ((bf16[8,144,512]{2,1,0:T(8,128)(2,1)}), bf16[8,144,512]{2,1,0:T(8,128)(2,1)S(1)}, u32[]{:S(2)}, u32[]{:S(2)}) async-start(bf16[8,144,512]{2,1,0:T(8,128)(2,1)} %shard_map.131), calls=%async_computation.9 | async-start | bytes 2359296 | tf_op jit(solution)/shard_map/all_to_all | solution.py:36
  197.9 3.4 %copy-start.7 = (bf16[8,2,64,512]{3,2,1,0:T(8,128)(2,1)S(1)}, bf16[8,2,64,512]{3,2,1,0:T(8,128)(2,1)}, u32[]{:S(2)}) copy-start(bf16[8,2,64,512]{3,2,1,0:T(8,128)(2,1)} %copy-done.6) | copy-start | bytes 3145732
  198.6 3.3 %copy-start.11 = (f32[384,1024]{1,0:T(8,128)S(1)}, f32[384,1024]{1,0:T(8,128)}, u32[]{:S(2)}) copy-start(f32[384,1024]{1,0:T(8,128)} %get-tuple-element.56) | copy-start | bytes 4718596
  198.7 3.2 %copy-start.4 = (bf16[384,1024]{1,0:T(8,128)(2,1)S(1)}, bf16[384,1024]{1,0:T(8,128)(2,1)}, u32[]{:S(2)}) copy-start(bf16[384,1024]{1,0:T(8,128)(2,1)} %get-tuple-element.82.masked) | copy-start | bytes 2359300
  198.7 3.2 %copy-start.10 = (bf16[1024,512]{1,0:T(8,128)(2,1)S(1)}, bf16[1024,512]{1,0:T(8,128)(2,1)}, u32[]{:S(2)}) copy-start(bf16[1024,512]{1,0:T(8,128)(2,1)} %copy-done.9) | copy-start | bytes 3145732
  198.7 4.8 %collective-permute-start.5 = (bf16[1024,256]{0,1:T(8,128)(2,1)S(1)}, bf16[1024,256]{0,1:T(8,128)(2,1)S(1)}, u32[]{:S(2)}, u32[]{:S(2)}) collective-permute-start(bf16[1024,256]{0,1:T(8,128)(2,1)S(1)} %slice.53), channel_id=1, source_target_pairs={{0,32},{32,0},{64,96},{96,64},{128,160},{160,128},{192,224},{224,1... | collective-permute-start | bytes 1572872 | tf_op jit(solution)/shard_map/ppermute | solution.py:18
  (2 other events, 2.0 us)

commit v11 on v10

--- a/solution.py
+++ b/solution.py
@@ -9,6 +9,7 @@
 
 FAR = 2
 CHUNK = 256
+MIDDLE_CHUNK = 512
 SPARE = 16
 PARAMS = pltpu.CompilerParams(vmem_limit_bytes=32 * 1024 * 1024)
 
@@ -89,10 +90,6 @@
     def _():
         fill((other_v, own_v))
 
-    @pl.when(step == 0)
-    def _():
-        total[...] = jnp.zeros_like(total)
-
     inputs = x0[...].astype(wide)
     first_gate = (
         cross_dot(sums[:rows, :half_rank], own_u[...])
@@ -106,13 +103,27 @@
     first_adj[...] = adj
     kept[...] = layer_grad * (first_gate + 1.0)
     bias_sum[...] = jnp.sum(adj.astype(wide), axis=0, keepdims=True)
-    total[:rows, :] += dot(layer, map_v[...])
-    total[rows:, :half_rank] += dot(adj, own_u[...])
-    total[rows:, half_rank:] += dot(adj, other_u[...])
-
-    @pl.when(step == pl.num_programs(0) - 1)
+    parts = (
+        (slice(0, rows), slice(None), dot(layer, map_v[...])),
+        (slice(rows, None), slice(0, half_rank), dot(adj, own_u[...])),
+        (slice(rows, None), slice(half_rank, None), dot(adj, other_u[...])),
+    )
+    last = pl.num_programs(0) - 1
+
+    @pl.when(step == 0)
     def _():
-        both[...] = total[...].astype(low)
+        for across, along, part in parts:
+            total[across, along] = part
+
+    @pl.when(jnp.logical_and(step > 0, step < last))
+    def _():
+        for across, along, part in parts:
+            total[across, along] += part
+
+    @pl.when(step == last)
+    def _():
+        for across, along, part in parts:
+            both[across, along] = (total[across, along] + part).astype(low)
 
 
 def middle(core, sums, x0, masked, own_u, other_u, own_maps, other_maps, bias):
@@ -120,15 +131,15 @@
     rows, width = x0.shape
     rank = sums.shape[1]
     lines = own_maps.shape[1] // 2
-    across = pl.BlockSpec((rows, CHUNK), lambda i, place: (0, i))
-    half = pl.BlockSpec((CHUNK, rank // 2), lambda i, place: (i, 0))
+    across = pl.BlockSpec((rows, MIDDLE_CHUNK), lambda i, place: (0, i))
+    half = pl.BlockSpec((MIDDLE_CHUNK, rank // 2), lambda i, place: (i, 0))
     fixed = pl.BlockSpec((2 * rows, rank), lambda i, place: (0, 0))
-    map_rows = pl.BlockSpec((CHUNK // (2 * lines), lines, rank), lambda i, place: (i, 1, 0))
+    map_rows = pl.BlockSpec((MIDDLE_CHUNK // (2 * lines), lines, rank), lambda i, place: (i, 1, 0))
     return pl.pallas_call(
         middle_kernel,
         grid_spec=pltpu.PrefetchScalarGridSpec(
             num_scalar_prefetch=1,
-            grid=(width // CHUNK,),
+            grid=(width // MIDDLE_CHUNK,),
             in_specs=[
                 fixed,
                 across,
@@ -137,10 +148,10 @@
                 half,
                 map_rows,
                 map_rows,
-                pl.BlockSpec((2, CHUNK), lambda i, place: (0, i)),
+                pl.BlockSpec((2, MIDDLE_CHUNK), lambda i, place: (0, i)),
             ],
-            out_specs=[fixed, across, across, across, pl.BlockSpec((1, CHUNK), lambda i, place: (0, i))],
-            scratch_shapes=[pltpu.VMEM((2 * rows, rank), wide), pltpu.VMEM((CHUNK, rank), low)],
+            out_specs=[fixed, across, across, across, pl.BlockSpec((1, MIDDLE_CHUNK), lambda i, place: (0, i))],
+            scratch_shapes=[pltpu.VMEM((2 * rows, rank), wide), pltpu.VMEM((MIDDLE_CHUNK, rank), low)],
         ),
         out_shape=[
             pltpu.HBM((2 * rows, rank), low),

time: 217 us -> 216 us (level)
  no operation moved by 1% of the time
where the time goes in v11:
time: 216 us; the launch traced here: 215 us
  blocking collectives  115 us (53%)
  starting transfers between devices  53 us (25%)
  Pallas kernels  15.7 us (7%)
  waiting for transfers between devices  14.6 us (7%)
  local copies, waits for them, and re-layouts  6.68 us (3%)
  matrix products  4.42 us (2%)
  other arithmetic  4.04 us (2%)
    all_to_all x6, blocking collectives, exchange(): lax.all_to_all(value, axis, 0, 0, axis_index_groups=groups, tiled=True)  115 us
    ppermute x6, starting transfers between devices, core_swap(): return lax.ppermute(value, 'dom', pairs)  36.2 us
    all_to_all x4, starting transfers between devices, exchange(): lax.all_to_all(value, axis, 0, 0, axis_index_groups=groups, tiled=True)  16.8 us
    all_to_all x4, waiting for transfers between devices, exchange(): lax.all_to_all(value, axis, 0, 0, axis_index_groups=groups, tiled=True)  13.7 us
    pallas_call x1, Pallas kernels, middle(): pl.pallas_call(middle_kernel, grid_spec=pltpu.PrefetchScalarGridSpec(num_...  5.48 us
    pallas_call x1, Pallas kernels, early_terms(): pl.pallas_call(early_kernel, grid_spec=pltpu.PrefetchScalarGridSpec(num_s...  4.7 us
  transfers between devices with their start and end apart: 10, of which 4 were waited for; matrix products, arithmetic and copies ran while one was open for 6% of the time, Pallas kernels for 3%

profile of v11, /device:TPU:1, one launch (start us, length us, event | category | flops | bytes accessed | tf_op | source)
XLA Modules:
  0.0 214.6 jit_solution(1597449596659582591)
XLA Ops:
  0.6 1.9 shard_map.127
  2.5 6.1 %all-to-all-start = ((bf16[8,128,512]{2,1,0:T(8,128)(2,1)}), bf16[8,128,512]{2,1,0:T(8,128)(2,1)S(1)}, u32[]{:S(2)}, u32[]{:S(2)}) async-start(bf16[8,128,512]{2,1,0:T(8,128)(2,1)} %shard_map.127), calls=%async_computation | async-start | bytes 2097152 | tf_op jit(solution)/shard_map/all_to_all | solution.py:37
  8.6 6.4 %collective-permute-start = (bf16[1024,256]{1,0:T(8,128)(2,1)}, bf16[1024,256]{1,0:T(8,128)(2,1)}, u32[]{:S(2)}, u32[]{:S(2)}) collective-permute-start(bf16[1024,256]{1,0:T(8,128)(2,1)} %param.12), channel_id=1, source_target_pairs={{0,32},{32,0},{64,96},{96,64},{128,160},{160,128},{192,224},{224,1... | collective-permute-start | bytes 1572872 | tf_op jit(solution)/shard_map/ppermute | solution.py:19
  15.1 1.9 constant_dynamic-update-slice_fusion.1
  21.2 6.1 %collective-permute-start.2 = (bf16[8,128,512]{2,1,0:T(8,128)(2,1)S(1)}, bf16[8,128,512]{2,1,0:T(8,128)(2,1)}, u32[]{:S(2)}, u32[]{:S(2)}) collective-permute-start(bf16[8,128,512]{2,1,0:T(8,128)(2,1)S(1)} %all-to-all-done.own_v), channel_id=1, source_target_pairs={{0,32},{32,0},{64,96},{96,64},{128,160},{160,128},{192,224},{224,1... | collective-permute-start | bytes 3145736 | tf_op jit(solution)/shard_map/ppermute | solution.py:19
  27.3 1.9 collective-permute-start.1
  32.3 16.4 %all_to_all.79 = bf16[4,192,512]{2,1,0:T(8,128)(2,1)S(1)} all-to-all(bf16[4,192,512]{2,1,0:T(8,128)(2,1)S(1)} %bitcast.40), channel_id=1, replica_groups={{0,1,16,17},{2,3,18,19},{4,5,20,21},{6,7,22,23},{8,9,24,25},{10,11,26,2..., dimensions={0} | all-to-all | bytes 1572864 | tf_op jit(solution)/shard_map/all_to_all | solution.py:37
  48.8 28.0 %all_to_all.80 = bf16[8,24,512]{2,1,0:T(8,128)(2,1)S(1)} all-to-all(bf16[8,24,512]{2,1,0:T(8,128)(2,1)S(1)} %bitcast.41), channel_id=1, replica_groups={{0,2,4,6,8,10,12,14},{1,3,5,7,9,11,13,15},{16,18,20,22,24,26,28,30},{17..., dimensions={0} | all-to-all | bytes 393216 | tf_op jit(solution)/shard_map/all_to_all | solution.py:37
  76.8 20.1 %all_to_all.81 = bf16[8,24,512]{2,1,0:T(8,128)(2,1)S(1)} all-to-all(bf16[8,24,512]{2,1,0:T(8,128)(2,1)S(1)} %broadcast_in_dim.50), channel_id=1, replica_groups={{0,2,4,6,8,10,12,14},{1,3,5,7,9,11,13,15},{16,18,20,22,24,26,28,30},{17..., dimensions={0} | all-to-all | bytes 393216 | tf_op jit(solution)/shard_map/all_to_all | solution.py:37
  97.0 11.7 %all_to_all.82 = bf16[4,192,512]{2,1,0:T(8,128)(2,1)S(1)} all-to-all(bf16[4,192,512]{2,1,0:T(8,128)(2,1)S(1)} %broadcast_in_dim.52), channel_id=1, replica_groups={{0,1,16,17},{2,3,18,19},{4,5,20,21},{6,7,22,23},{8,9,24,25},{10,11,26,2..., dimensions={0} | all-to-all | bytes 1572864 | tf_op jit(solution)/shard_map/all_to_all | solution.py:37
  108.7 5.5 %shard_map.128 = (bf16[768,512]{1,0:T(8,128)(2,1)}, bf16[384,1024]{1,0:T(8,128)(2,1)}, bf16[384,1024]{1,0:T(8,128)(2,1)}, f32[384,1024]{1,0:T(8,128)}, f32[1,1024]{1,0:T(1,128)S(1)}) custom-call(s32[1]{0:T(128)} %bitcast.place, bf16[768,512]{1,0:T(8,128)(2,1)S(1)} %bitcast.34, bf16[384,1024]{1,0:T(8,128)(2,1)} %x0.1, ...), custom_call_target="tpu_custom_call" | custom-call | tf_op jit(solution)/shard_map/pallas_call | solution.py:138
  114.1 3.5 %all-to-all-start.5 = ((bf16[4,192,512]{2,1,0:T(8,128)(2,1)}), bf16[4,192,512]{2,1,0:T(8,128)(2,1)S(1)}, u32[]{:S(2)}, u32[]{:S(2)}) async-start(bf16[4,192,512]{2,1,0:T(8,128)(2,1)} %bitcast.43), calls=%async_computation.5 | async-start | bytes 1572864 | tf_op jit(solution)/shard_map/all_to_all | solution.py:37
  117.6 4.7 %shard_map.129 = (f32[1024,256]{1,0:T(8,128)}, f32[8,64,512]{2,1,0:T(8,128)}, bf16[4,272,512]{2,1,0:T(8,128)(2,1)}) custom-call(s32[1]{0:T(128)} %bitcast.place, bf16[384,1024]{1,0:T(8,128)(2,1)} %get-tuple-element.43.first_adj, bf16[384,1024]{1,0:T(8,128)(2,1)} %get-tuple-element.44.layer_one, bf16[768,512]{1,0:T(8,128)(2,1)S(1)} %bitcast.35, ...), custom_call_target="tpu_custom_call" | custom-call | tf_op jit(solution)/shard_map/pallas_call | solution.py:224
  122.3 3.6 %all-to-all-done.5 = bf16[4,192,512]{2,1,0:T(8,128)(2,1)S(1)} async-done(((bf16[4,192,512]{2,1,0:T(8,128)(2,1)}), bf16[4,192,512]{2,1,0:T(8,128)(2,1)S(1)}, u32[]{:S(2)}, u32[]{:S(2)}) %all-to-all-start.5) | async-done | bytes 786464 | tf_op jit(solution)/shard_map/all_to_all | solution.py:37
  126.1 21.9 %all_to_all.83 = bf16[8,24,512]{2,1,0:T(8,128)(2,1)S(1)} all-to-all(bf16[8,24,512]{2,1,0:T(8,128)(2,1)S(1)} %bitcast.42), channel_id=1, replica_groups={{0,2,4,6,8,10,12,14},{1,3,5,7,9,11,13,15},{16,18,20,22,24,26,28,30},{17..., dimensions={0} | all-to-all | bytes 393216 | tf_op jit(solution)/shard_map/all_to_all | solution.py:37
  148.1 17.2 %all_to_all.84 = bf16[8,24,512]{2,1,0:T(8,128)(2,1)S(1)} all-to-all(bf16[8,24,512]{2,1,0:T(8,128)(2,1)S(1)} %broadcast_in_dim.53), channel_id=1, replica_groups={{0,2,4,6,8,10,12,14},{1,3,5,7,9,11,13,15},{16,18,20,22,24,26,28,30},{17..., dimensions={0} | all-to-all | bytes 393216 | tf_op jit(solution)/shard_map/all_to_all | solution.py:37
  166.2 3.5 %all-to-all-start.8 = ((bf16[4,192,512]{2,1,0:T(8,128)(2,1)}), bf16[4,192,512]{2,1,0:T(8,128)(2,1)S(1)}, u32[]{:S(2)}, u32[]{:S(2)}) async-start(bf16[4,192,512]{2,1,0:T(8,128)(2,1)} %broadcast_in_dim.54), calls=%async_computation.8 | async-start | bytes 1572864 | tf_op jit(solution)/shard_map/all_to_all | solution.py:37
  169.7 9.8 %collective-permute-start.4 = (bf16[4,272,512]{2,1,0:T(8,128)(2,1)}, bf16[4,272,512]{2,1,0:T(8,128)(2,1)S(1)}, u32[]{:S(2)}, u32[]{:S(2)}) collective-permute-start(bf16[4,272,512]{2,1,0:T(8,128)(2,1)} %get-tuple-element.54), channel_id=1, source_target_pairs={{0,32},{32,0},{64,96},{96,64},{128,160},{160,128},{192,224},{224,1... | collective-permute-start | bytes 3342344 | tf_op jit(solution)/shard_map/ppermute | solution.py:19
  179.6 1.5 shard_map.130
  181.0 9.4 %collective-permute-start.3 = (bf16[8,64,512]{2,1,0:T(8,128)(2,1)S(1)}, bf16[8,64,512]{2,1,0:T(8,128)(2,1)S(1)}, u32[]{:S(2)}, u32[]{:S(2)}) collective-permute-start(bf16[8,64,512]{2,1,0:T(8,128)(2,1)S(1)} %get-tuple-element.52), channel_id=1, source_target_pairs={{0,32},{32,0},{64,96},{96,64},{128,160},{160,128},{192,224},{224,1... | collective-permute-start | bytes 1572872 | tf_op jit(solution)/shard_map/ppermute | solution.py:19
  193.3 3.7 %all-to-all-start.9 = ((bf16[8,144,512]{2,1,0:T(8,128)(2,1)}), bf16[8,144,512]{2,1,0:T(8,128)(2,1)S(1)}, u32[]{:S(2)}, u32[]{:S(2)}) async-start(bf16[8,144,512]{2,1,0:T(8,128)(2,1)} %shard_map.131), calls=%async_computation.9 | async-start | bytes 2359296 | tf_op jit(solution)/shard_map/all_to_all | solution.py:37
  197.9 2.5 %collective-permute-start.5 = (bf16[1024,256]{0,1:T(8,128)(2,1)S(1)}, bf16[1024,256]{0,1:T(8,128)(2,1)S(1)}, u32[]{:S(2)}, u32[]{:S(2)}) collective-permute-start(bf16[1024,256]{0,1:T(8,128)(2,1)S(1)} %slice.53), channel_id=1, source_target_pairs={{0,32},{32,0},{64,96},{96,64},{128,160},{160,128},{192,224},{224,1... | collective-permute-start | bytes 1572872 | tf_op jit(solution)/shard_map/ppermute | solution.py:19
  201.1 1.6 fusion.3
  203.8 10.0 %all-to-all-done.9.taken = bf16[8,144,512]{2,1,0:T(8,128)(2,1)S(1)} async-done(((bf16[8,144,512]{2,1,0:T(8,128)(2,1)}), bf16[8,144,512]{2,1,0:T(8,128)(2,1)S(1)}, u32[]{:S(2)}, u32[]{:S(2)}) %all-to-all-start.9) | async-done | bytes 1179680 | tf_op jit(solution)/shard_map/all_to_all | solution.py:37
  (68 shorter events, 14.7 us)
Async XLA Ops:
  2.5 14.4 %copy-start.15 = (s32[384]{0:T(512)S(1)}, s32[384]{0:T(512)}, u32[]{:S(2)}) copy-start(s32[384]{0:T(512)} %param.10) | copy-start | bytes 4612
  2.5 14.4 %copy-start.2 = (bf16[384,1024]{1,0:T(8,128)(2,1)S(1)}, bf16[384,1024]{1,0:T(8,128)(2,1)}, u32[]{:S(2)}) copy-start(bf16[384,1024]{1,0:T(8,128)(2,1)} %x0.1) | copy-start | bytes 2359300
  2.5 14.4 %copy-start.13 = (bf16[384,1024]{1,0:T(8,128)(2,1)S(1)}, bf16[384,1024]{1,0:T(8,128)(2,1)}, u32[]{:S(2)}) copy-start(bf16[384,1024]{1,0:T(8,128)(2,1)} %param.9) | copy-start | bytes 2359300
  2.5 18.6 %all-to-all-start = ((bf16[8,128,512]{2,1,0:T(8,128)(2,1)}), bf16[8,128,512]{2,1,0:T(8,128)(2,1)S(1)}, u32[]{:S(2)}, u32[]{:S(2)}) async-start(bf16[8,128,512]{2,1,0:T(8,128)(2,1)} %shard_map.127), calls=%async_computation | async-start | bytes 2097152 | tf_op jit(solution)/shard_map/all_to_all | solution.py:37
  8.6 9.6 %collective-permute-start = (bf16[1024,256]{1,0:T(8,128)(2,1)}, bf16[1024,256]{1,0:T(8,128)(2,1)}, u32[]{:S(2)}, u32[]{:S(2)}) collective-permute-start(bf16[1024,256]{1,0:T(8,128)(2,1)} %param.12), channel_id=1, source_target_pairs={{0,32},{32,0},{64,96},{96,64},{128,160},{160,128},{192,224},{224,1... | collective-permute-start | bytes 1572872 | tf_op jit(solution)/shard_map/ppermute | solution.py:19
  17.0 1.3 copy-start.8
  18.2 9.1 %copy-start.14 = (bf16[1024,256]{1,0:T(8,128)(2,1)S(1)}, bf16[1024,256]{1,0:T(8,128)(2,1)}, u32[]{:S(2)}) copy-start(bf16[1024,256]{1,0:T(8,128)(2,1)} %own_u) | copy-start | bytes 1572868
  21.1 9.8 %copy-start.5 = (bf16[8,128,512]{2,1,0:T(8,128)(2,1)}, bf16[8,128,512]{2,1,0:T(8,128)(2,1)S(1)}, u32[]{:S(2)}) copy-start(bf16[8,128,512]{2,1,0:T(8,128)(2,1)S(1)} %all-to-all-done.own_v) | copy-start | bytes 3145732
  21.2 8.5 %collective-permute-start.2 = (bf16[8,128,512]{2,1,0:T(8,128)(2,1)S(1)}, bf16[8,128,512]{2,1,0:T(8,128)(2,1)}, u32[]{:S(2)}, u32[]{:S(2)}) collective-permute-start(bf16[8,128,512]{2,1,0:T(8,128)(2,1)S(1)} %all-to-all-done.own_v), channel_id=1, source_target_pairs={{0,32},{32,0},{64,96},{96,64},{128,160},{160,128},{192,224},{224,1... | collective-permute-start | bytes 3145736 | tf_op jit(solution)/shard_map/ppermute | solution.py:19
  27.3 4.7 %collective-permute-start.1 = (bf16[1024,256]{1,0:T(8,128)(2,1)S(1)}, bf16[1024,256]{1,0:T(8,128)(2,1)}, u32[]{:S(2)}, u32[]{:S(2)}) collective-permute-start(bf16[1024,256]{1,0:T(8,128)(2,1)S(1)} %copy-done.14), channel_id=1, source_target_pairs={{0,32},{32,0},{64,96},{96,64},{128,160},{160,128},{192,224},{224,1... | collective-permute-start | bytes 1572872 | tf_op jit(solution)/shard_map/ppermute | solution.py:19
  76.8 31.9 %copy-start.1 = (f32[2,1024]{1,0:T(2,128)S(1)}, f32[2,1024]{1,0:T(2,128)}, u32[]{:S(2)}) copy-start(f32[2,1024]{1,0:T(2,128)} %bias.1) | copy-start | bytes 24580
  114.1 11.8 %all-to-all-start.5 = ((bf16[4,192,512]{2,1,0:T(8,128)(2,1)}), bf16[4,192,512]{2,1,0:T(8,128)(2,1)S(1)}, u32[]{:S(2)}, u32[]{:S(2)}) async-start(bf16[4,192,512]{2,1,0:T(8,128)(2,1)} %bitcast.43), calls=%async_computation.5 | async-start | bytes 1572864 | tf_op jit(solution)/shard_map/all_to_all | solution.py:37
  166.2 13.3 %all-to-all-start.8 = ((bf16[4,192,512]{2,1,0:T(8,128)(2,1)}), bf16[4,192,512]{2,1,0:T(8,128)(2,1)S(1)}, u32[]{:S(2)}, u32[]{:S(2)}) async-start(bf16[4,192,512]{2,1,0:T(8,128)(2,1)} %broadcast_in_dim.54), calls=%async_computation.8 | async-start | bytes 1572864 | tf_op jit(solution)/shard_map/all_to_all | solution.py:37
  169.7 20.8 %collective-permute-start.4 = (bf16[4,272,512]{2,1,0:T(8,128)(2,1)}, bf16[4,272,512]{2,1,0:T(8,128)(2,1)S(1)}, u32[]{:S(2)}, u32[]{:S(2)}) collective-permute-start(bf16[4,272,512]{2,1,0:T(8,128)(2,1)} %get-tuple-element.54), channel_id=1, source_target_pairs={{0,32},{32,0},{64,96},{96,64},{128,160},{160,128},{192,224},{224,1... | collective-permute-start | bytes 3342344 | tf_op jit(solution)/shard_map/ppermute | solution.py:19
  179.5 11.0 %copy-start.12 = (f32[1024,256]{1,0:T(8,128)S(1)}, f32[1024,256]{1,0:T(8,128)}, u32[]{:S(2)}) copy-start(f32[1024,256]{1,0:T(8,128)} %get-tuple-element.57) | copy-start | bytes 3145732
  181.0 10.9 %collective-permute-start.3 = (bf16[8,64,512]{2,1,0:T(8,128)(2,1)S(1)}, bf16[8,64,512]{2,1,0:T(8,128)(2,1)S(1)}, u32[]{:S(2)}, u32[]{:S(2)}) collective-permute-start(bf16[8,64,512]{2,1,0:T(8,128)(2,1)S(1)} %get-tuple-element.52), channel_id=1, source_target_pairs={{0,32},{32,0},{64,96},{96,64},{128,160},{160,128},{192,224},{224,1... | collective-permute-start | bytes 1572872 | tf_op jit(solution)/shard_map/ppermute | solution.py:19
  190.5 1.5 copy-start
  193.3 3.7 %copy-start.3 = (bf16[384,1024]{1,0:T(8,128)(2,1)S(1)}, bf16[384,1024]{1,0:T(8,128)(2,1)}, u32[]{:S(2)}) copy-start(bf16[384,1024]{1,0:T(8,128)(2,1)} %x0.1) | copy-start | bytes 2359300
  193.3 20.5 %all-to-all-start.9 = ((bf16[8,144,512]{2,1,0:T(8,128)(2,1)}), bf16[8,144,512]{2,1,0:T(8,128)(2,1)S(1)}, u32[]{:S(2)}, u32[]{:S(2)}) async-start(bf16[8,144,512]{2,1,0:T(8,128)(2,1)} %shard_map.131), calls=%async_computation.9 | async-start | bytes 2359296 | tf_op jit(solution)/shard_map/all_to_all | solution.py:37
  197.0 3.4 %copy-start.7 = (bf16[8,2,64,512]{3,2,1,0:T(8,128)(2,1)S(1)}, bf16[8,2,64,512]{3,2,1,0:T(8,128)(2,1)}, u32[]{:S(2)}) copy-start(bf16[8,2,64,512]{3,2,1,0:T(8,128)(2,1)} %copy-done.6) | copy-start | bytes 3145732
  197.8 3.3 %copy-start.11 = (f32[384,1024]{1,0:T(8,128)S(1)}, f32[384,1024]{1,0:T(8,128)}, u32[]{:S(2)}) copy-start(f32[384,1024]{1,0:T(8,128)} %get-tuple-element.56) | copy-start | bytes 4718596
  197.9 3.2 %copy-start.4 = (bf16[384,1024]{1,0:T(8,128)(2,1)S(1)}, bf16[384,1024]{1,0:T(8,128)(2,1)}, u32[]{:S(2)}) copy-start(bf16[384,1024]{1,0:T(8,128)(2,1)} %get-tuple-element.82.masked) | copy-start | bytes 2359300
  197.9 3.2 %copy-start.10 = (bf16[1024,512]{1,0:T(8,128)(2,1)S(1)}, bf16[1024,512]{1,0:T(8,128)(2,1)}, u32[]{:S(2)}) copy-start(bf16[1024,512]{1,0:T(8,128)(2,1)} %copy-done.9) | copy-start | bytes 3145732
  197.9 4.8 %collective-permute-start.5 = (bf16[1024,256]{0,1:T(8,128)(2,1)S(1)}, bf16[1024,256]{0,1:T(8,128)(2,1)S(1)}, u32[]{:S(2)}, u32[]{:S(2)}) collective-permute-start(bf16[1024,256]{0,1:T(8,128)(2,1)S(1)} %slice.53), channel_id=1, source_target_pairs={{0,32},{32,0},{64,96},{96,64},{128,160},{160,128},{192,224},{224,1... | collective-permute-start | bytes 1572872 | tf_op jit(solution)/shard_map/ppermute | solution.py:19
  (2 other events, 2.0 us)

commit v12 on v11

--- a/solution.py
+++ b/solution.py
@@ -161,7 +161,7 @@
             jax.ShapeDtypeStruct((1, width), wide),
         ],
         compiler_params=PARAMS,
-    )(core[None], sums, *map(in_hbm, (x0, masked, own_u, other_u, own_maps, other_maps)), bias)
+    )(core[None], sums, x0, masked, own_u, other_u, own_maps, other_maps, bias)
 
 
 def spread_kernel(map_u, map_v, out):

time: 216 us -> 220 us (1.019)
  local copies, waits for them, and re-layouts: 6.68 us -> 11.4 us
    unnamed x34 -> x36, local copies, waits for them, and re-layouts: 4.04 us -> 6.51 us
  transfers between devices with their start and end apart: 10 -> 10, of which waited for: 4 -> 3; matrix products, arithmetic and copies ran while one was open for 6% -> 7% of each run, Pallas kernels for 3% -> 3%
where the time goes in v12:
time: 220 us; the launch traced here: 219 us
  blocking collectives  116 us (53%)
  starting transfers between devices  51 us (23%)
  waiting for transfers between devices  15 us (7%)
  Pallas kernels  14.6 us (7%)
  local copies, waits for them, and re-layouts  11.4 us (5%)
  matrix products  5.17 us (2%)
  other arithmetic  5.06 us (2%)
    all_to_all x6, blocking collectives, exchange(): lax.all_to_all(value, axis, 0, 0, axis_index_groups=groups, tiled=True)  116 us
    ppermute x6, starting transfers between devices, core_swap(): return lax.ppermute(value, 'dom', pairs)  34.4 us
    all_to_all x4, starting transfers between devices, exchange(): lax.all_to_all(value, axis, 0, 0, axis_index_groups=groups, tiled=True)  16.6 us
    all_to_all x4, waiting for transfers between devices, exchange(): lax.all_to_all(value, axis, 0, 0, axis_index_groups=groups, tiled=True)  14.5 us
    unnamed x36, local copies, waits for them, and re-layouts  6.51 us
    pallas_call x1, Pallas kernels, middle(): pl.pallas_call(middle_kernel, grid_spec=pltpu.PrefetchScalarGridSpec(num_...  5.14 us
    pallas_call x1, Pallas kernels, early_terms(): pl.pallas_call(early_kernel, grid_spec=pltpu.PrefetchScalarGridSpec(num_s...  4.73 us
  transfers between devices with their start and end apart: 10, of which 3 were waited for; matrix products, arithmetic and copies ran while one was open for 7% of the time, Pallas kernels for 3%

profile of v12, /device:TPU:1, one launch (start us, length us, event | category | flops | bytes accessed | tf_op | source)
XLA Modules:
  0.0 219.2 jit_solution(8155292831306058331)
XLA Ops:
  2.6 6.1 %all-to-all-start = ((bf16[8,128,512]{2,1,0:T(8,128)(2,1)}), bf16[8,128,512]{2,1,0:T(8,128)(2,1)S(1)}, u32[]{:S(2)}, u32[]{:S(2)}) async-start(bf16[8,128,512]{2,1,0:T(8,128)(2,1)} %copy-done.2), calls=%async_computation | async-start | bytes 2097152 | tf_op jit(solution)/shard_map/all_to_all | solution.py:37
  8.7 6.4 %collective-permute-start = (bf16[1024,256]{1,0:T(8,128)(2,1)}, bf16[1024,256]{1,0:T(8,128)(2,1)}, u32[]{:S(2)}, u32[]{:S(2)}) collective-permute-start(bf16[1024,256]{1,0:T(8,128)(2,1)} %param.12), channel_id=1, source_target_pairs={{0,32},{32,0},{64,96},{96,64},{128,160},{160,128},{192,224},{224,1... | collective-permute-start | bytes 1572872 | tf_op jit(solution)/shard_map/ppermute | solution.py:19
  15.1 1.9 constant_dynamic-update-slice_fusion.1
  17.1 1.6 convert_reduce_fusion
  21.1 1.5 fusion.4
  22.6 4.8 %collective-permute-start.2 = (bf16[8,128,512]{2,1,0:T(8,128)(2,1)S(1)}, bf16[8,128,512]{2,1,0:T(8,128)(2,1)}, u32[]{:S(2)}, u32[]{:S(2)}) collective-permute-start(bf16[8,128,512]{2,1,0:T(8,128)(2,1)S(1)} %all-to-all-done.own_v), channel_id=1, source_target_pairs={{0,32},{32,0},{64,96},{96,64},{128,160},{160,128},{192,224},{224,1... | collective-permute-start | bytes 3145736 | tf_op jit(solution)/shard_map/ppermute | solution.py:19
  27.4 1.9 collective-permute-start.1
  33.6 16.6 %all_to_all.79 = bf16[4,192,512]{2,1,0:T(8,128)(2,1)S(1)} all-to-all(bf16[4,192,512]{2,1,0:T(8,128)(2,1)} %bitcast.40), channel_id=1, replica_groups={{0,1,16,17},{2,3,18,19},{4,5,20,21},{6,7,22,23},{8,9,24,25},{10,11,26,2..., dimensions={0} | all-to-all | bytes 1572864 | tf_op jit(solution)/shard_map/all_to_all | solution.py:37
  51.0 28.2 %all_to_all.80 = bf16[8,24,512]{2,1,0:T(8,128)(2,1)S(1)} all-to-all(bf16[8,24,512]{2,1,0:T(8,128)(2,1)} %bitcast.41), channel_id=1, replica_groups={{0,2,4,6,8,10,12,14},{1,3,5,7,9,11,13,15},{16,18,20,22,24,26,28,30},{17..., dimensions={0} | all-to-all | bytes 393216 | tf_op jit(solution)/shard_map/all_to_all | solution.py:37
  79.3 20.2 %all_to_all.81 = bf16[8,24,512]{2,1,0:T(8,128)(2,1)S(1)} all-to-all(bf16[8,24,512]{2,1,0:T(8,128)(2,1)S(1)} %broadcast_in_dim.50), channel_id=1, replica_groups={{0,2,4,6,8,10,12,14},{1,3,5,7,9,11,13,15},{16,18,20,22,24,26,28,30},{17..., dimensions={0} | all-to-all | bytes 393216 | tf_op jit(solution)/shard_map/all_to_all | solution.py:37
  99.5 11.7 %all_to_all.82 = bf16[4,192,512]{2,1,0:T(8,128)(2,1)S(1)} all-to-all(bf16[4,192,512]{2,1,0:T(8,128)(2,1)S(1)} %broadcast_in_dim.52), channel_id=1, replica_groups={{0,1,16,17},{2,3,18,19},{4,5,20,21},{6,7,22,23},{8,9,24,25},{10,11,26,2..., dimensions={0} | all-to-all | bytes 1572864 | tf_op jit(solution)/shard_map/all_to_all | solution.py:37
  111.2 5.1 %shard_map.128 = (bf16[768,512]{1,0:T(8,128)(2,1)}, bf16[384,1024]{1,0:T(8,128)(2,1)}, bf16[384,1024]{1,0:T(8,128)(2,1)}, f32[384,1024]{1,0:T(8,128)}, f32[1,1024]{1,0:T(1,128)S(1)}) custom-call(s32[1]{0:T(128)} %bitcast.place, bf16[768,512]{1,0:T(8,128)(2,1)S(1)} %bitcast.34, bf16[384,1024]{1,0:T(8,128)(2,1)S(1)} %copy-done, ...), custom_call_target="tpu_custom_call" | custom-call | tf_op jit(solution)/shard_map/pallas_call | solution.py:138
  116.4 3.5 %all-to-all-start.5 = ((bf16[4,192,512]{2,1,0:T(8,128)(2,1)}), bf16[4,192,512]{2,1,0:T(8,128)(2,1)S(1)}, u32[]{:S(2)}, u32[]{:S(2)}) async-start(bf16[4,192,512]{2,1,0:T(8,128)(2,1)} %bitcast.43), calls=%async_computation.5 | async-start | bytes 1572864 | tf_op jit(solution)/shard_map/all_to_all | solution.py:37
  119.9 4.7 %shard_map.129 = (f32[1024,256]{1,0:T(8,128)}, f32[8,64,512]{2,1,0:T(8,128)}, bf16[4,272,512]{2,1,0:T(8,128)(2,1)}) custom-call(s32[1]{0:T(128)} %bitcast.place, bf16[384,1024]{1,0:T(8,128)(2,1)} %get-tuple-element.43.first_adj, bf16[384,1024]{1,0:T(8,128)(2,1)} %get-tuple-element.44.layer_one, bf16[768,512]{1,0:T(8,128)(2,1)S(1)} %bitcast.35, ...), custom_call_target="tpu_custom_call" | custom-call | tf_op jit(solution)/shard_map/pallas_call | solution.py:224
  124.6 3.6 %all-to-all-done.5 = bf16[4,192,512]{2,1,0:T(8,128)(2,1)S(1)} async-done(((bf16[4,192,512]{2,1,0:T(8,128)(2,1)}), bf16[4,192,512]{2,1,0:T(8,128)(2,1)S(1)}, u32[]{:S(2)}, u32[]{:S(2)}) %all-to-all-start.5) | async-done | bytes 786464 | tf_op jit(solution)/shard_map/all_to_all | solution.py:37
  128.3 21.9 %all_to_all.83 = bf16[8,24,512]{2,1,0:T(8,128)(2,1)S(1)} all-to-all(bf16[8,24,512]{2,1,0:T(8,128)(2,1)S(1)} %bitcast.42), channel_id=1, replica_groups={{0,2,4,6,8,10,12,14},{1,3,5,7,9,11,13,15},{16,18,20,22,24,26,28,30},{17..., dimensions={0} | all-to-all | bytes 393216 | tf_op jit(solution)/shard_map/all_to_all | solution.py:37
  150.3 17.3 %all_to_all.84 = bf16[8,24,512]{2,1,0:T(8,128)(2,1)S(1)} all-to-all(bf16[8,24,512]{2,1,0:T(8,128)(2,1)S(1)} %broadcast_in_dim.53), channel_id=1, replica_groups={{0,2,4,6,8,10,12,14},{1,3,5,7,9,11,13,15},{16,18,20,22,24,26,28,30},{17..., dimensions={0} | all-to-all | bytes 393216 | tf_op jit(solution)/shard_map/all_to_all | solution.py:37
  168.6 3.5 %all-to-all-start.8 = ((bf16[4,192,512]{2,1,0:T(8,128)(2,1)}), bf16[4,192,512]{2,1,0:T(8,128)(2,1)S(1)}, u32[]{:S(2)}, u32[]{:S(2)}) async-start(bf16[4,192,512]{2,1,0:T(8,128)(2,1)} %broadcast_in_dim.54), calls=%async_computation.8 | async-start | bytes 1572864 | tf_op jit(solution)/shard_map/all_to_all | solution.py:37
  172.1 9.8 %collective-permute-start.4 = (bf16[4,272,512]{2,1,0:T(8,128)(2,1)}, bf16[4,272,512]{2,1,0:T(8,128)(2,1)}, u32[]{:S(2)}, u32[]{:S(2)}) collective-permute-start(bf16[4,272,512]{2,1,0:T(8,128)(2,1)} %get-tuple-element.54), channel_id=1, source_target_pairs={{0,32},{32,0},{64,96},{96,64},{128,160},{160,128},{192,224},{224,1... | collective-permute-start | bytes 3342344 | tf_op jit(solution)/shard_map/ppermute | solution.py:19
  183.4 9.4 %collective-permute-start.3 = (bf16[8,64,512]{2,1,0:T(8,128)(2,1)S(1)}, bf16[8,64,512]{2,1,0:T(8,128)(2,1)S(1)}, u32[]{:S(2)}, u32[]{:S(2)}) collective-permute-start(bf16[8,64,512]{2,1,0:T(8,128)(2,1)S(1)} %get-tuple-element.52), channel_id=1, source_target_pairs={{0,32},{32,0},{64,96},{96,64},{128,160},{160,128},{192,224},{224,1... | collective-permute-start | bytes 1572872 | tf_op jit(solution)/shard_map/ppermute | solution.py:19
  197.6 3.6 %all-to-all-start.9 = ((bf16[8,144,512]{2,1,0:T(8,128)(2,1)}), bf16[8,144,512]{2,1,0:T(8,128)(2,1)S(1)}, u32[]{:S(2)}, u32[]{:S(2)}) async-start(bf16[8,144,512]{2,1,0:T(8,128)(2,1)} %copy-done.1), calls=%async_computation.9 | async-start | bytes 2359296 | tf_op jit(solution)/shard_map/all_to_all | solution.py:37
  202.0 2.1 collective-permute-start.5
  204.7 1.6 fusion.3
  207.5 11.0 %all-to-all-done.9.taken = bf16[8,144,512]{2,1,0:T(8,128)(2,1)S(1)} async-done(((bf16[8,144,512]{2,1,0:T(8,128)(2,1)}), bf16[8,144,512]{2,1,0:T(8,128)(2,1)S(1)}, u32[]{:S(2)}, u32[]{:S(2)}) %all-to-all-start.9) | async-done | bytes 1179680 | tf_op jit(solution)/shard_map/all_to_all | solution.py:37
  (70 shorter events, 20.2 us)
Async XLA Ops:
  2.6 14.4 %copy-start.16 = (s32[384]{0:T(512)S(1)}, s32[384]{0:T(512)}, u32[]{:S(2)}) copy-start(s32[384]{0:T(512)} %param.10) | copy-start | bytes 4612
  2.6 14.4 %copy-start = (bf16[384,1024]{1,0:T(8,128)(2,1)S(1)}, bf16[384,1024]{1,0:T(8,128)(2,1)}, u32[]{:S(2)}) copy-start(bf16[384,1024]{1,0:T(8,128)(2,1)} %x0.1) | copy-start | bytes 2359300
  2.6 19.9 %all-to-all-start = ((bf16[8,128,512]{2,1,0:T(8,128)(2,1)}), bf16[8,128,512]{2,1,0:T(8,128)(2,1)S(1)}, u32[]{:S(2)}, u32[]{:S(2)}) async-start(bf16[8,128,512]{2,1,0:T(8,128)(2,1)} %copy-done.2), calls=%async_computation | async-start | bytes 2097152 | tf_op jit(solution)/shard_map/all_to_all | solution.py:37
  8.7 10.0 %collective-permute-start = (bf16[1024,256]{1,0:T(8,128)(2,1)}, bf16[1024,256]{1,0:T(8,128)(2,1)}, u32[]{:S(2)}, u32[]{:S(2)}) collective-permute-start(bf16[1024,256]{1,0:T(8,128)(2,1)} %param.12), channel_id=1, source_target_pairs={{0,32},{32,0},{64,96},{96,64},{128,160},{160,128},{192,224},{224,1... | collective-permute-start | bytes 1572872 | tf_op jit(solution)/shard_map/ppermute | solution.py:19
  17.1 1.6 copy-start.10
  18.7 12.4 %copy-start.3 = (bf16[384,1024]{1,0:T(8,128)(2,1)}, bf16[384,1024]{1,0:T(8,128)(2,1)S(1)}, u32[]{:S(2)}) copy-start(bf16[384,1024]{1,0:T(8,128)(2,1)S(1)} %get-tuple-element.36.second_adj) | copy-start | bytes 2359300
  22.6 7.2 %collective-permute-start.2 = (bf16[8,128,512]{2,1,0:T(8,128)(2,1)S(1)}, bf16[8,128,512]{2,1,0:T(8,128)(2,1)}, u32[]{:S(2)}, u32[]{:S(2)}) collective-permute-start(bf16[8,128,512]{2,1,0:T(8,128)(2,1)S(1)} %all-to-all-done.own_v), channel_id=1, source_target_pairs={{0,32},{32,0},{64,96},{96,64},{128,160},{160,128},{192,224},{224,1... | collective-permute-start | bytes 3145736 | tf_op jit(solution)/shard_map/ppermute | solution.py:19
  27.4 5.1 %collective-permute-start.1 = (bf16[1024,256]{1,0:T(8,128)(2,1)}, bf16[1024,256]{1,0:T(8,128)(2,1)}, u32[]{:S(2)}, u32[]{:S(2)}) collective-permute-start(bf16[1024,256]{1,0:T(8,128)(2,1)} %own_u), channel_id=1, source_target_pairs={{0,32},{32,0},{64,96},{96,64},{128,160},{160,128},{192,224},{224,1... | collective-permute-start | bytes 1572872 | tf_op jit(solution)/shard_map/ppermute | solution.py:19
  31.1 1.4 copy-start.8
  31.1 1.3 copy-start.15
  79.2 32.0 %copy-start.6 = (bf16[1024,256]{1,0:T(8,128)(2,1)S(1)}, bf16[1024,256]{1,0:T(8,128)(2,1)}, u32[]{:S(2)}) copy-start(bf16[1024,256]{1,0:T(8,128)(2,1)} %own_u) | copy-start | bytes 1572868
  79.2 32.0 %copy-start.7 = (f32[2,1024]{1,0:T(2,128)S(1)}, f32[2,1024]{1,0:T(2,128)}, u32[]{:S(2)}) copy-start(f32[2,1024]{1,0:T(2,128)} %bias.1) | copy-start | bytes 24580
  116.4 11.8 %all-to-all-start.5 = ((bf16[4,192,512]{2,1,0:T(8,128)(2,1)}), bf16[4,192,512]{2,1,0:T(8,128)(2,1)S(1)}, u32[]{:S(2)}, u32[]{:S(2)}) async-start(bf16[4,192,512]{2,1,0:T(8,128)(2,1)} %bitcast.43), calls=%async_computation.5 | async-start | bytes 1572864 | tf_op jit(solution)/shard_map/all_to_all | solution.py:37
  150.3 31.6 %copy-start.4 = (bf16[384,1024]{1,0:T(8,128)(2,1)S(1)}, bf16[384,1024]{1,0:T(8,128)(2,1)}, u32[]{:S(2)}) copy-start(bf16[384,1024]{1,0:T(8,128)(2,1)} %copy-done.3) | copy-start | bytes 2359300
  168.6 13.3 %all-to-all-start.8 = ((bf16[4,192,512]{2,1,0:T(8,128)(2,1)}), bf16[4,192,512]{2,1,0:T(8,128)(2,1)S(1)}, u32[]{:S(2)}, u32[]{:S(2)}) async-start(bf16[4,192,512]{2,1,0:T(8,128)(2,1)} %broadcast_in_dim.54), calls=%async_computation.8 | async-start | bytes 1572864 | tf_op jit(solution)/shard_map/all_to_all | solution.py:37
  172.1 20.8 %collective-permute-start.4 = (bf16[4,272,512]{2,1,0:T(8,128)(2,1)}, bf16[4,272,512]{2,1,0:T(8,128)(2,1)}, u32[]{:S(2)}, u32[]{:S(2)}) collective-permute-start(bf16[4,272,512]{2,1,0:T(8,128)(2,1)} %get-tuple-element.54), channel_id=1, source_target_pairs={{0,32},{32,0},{64,96},{96,64},{128,160},{160,128},{192,224},{224,1... | collective-permute-start | bytes 3342344 | tf_op jit(solution)/shard_map/ppermute | solution.py:19
  181.9 12.1 %copy-start.14 = (f32[1024,256]{1,0:T(8,128)S(1)}, f32[1024,256]{1,0:T(8,128)}, u32[]{:S(2)}) copy-start(f32[1024,256]{1,0:T(8,128)} %get-tuple-element.57) | copy-start | bytes 3145732
  183.4 11.6 %collective-permute-start.3 = (bf16[8,64,512]{2,1,0:T(8,128)(2,1)S(1)}, bf16[8,64,512]{2,1,0:T(8,128)(2,1)S(1)}, u32[]{:S(2)}, u32[]{:S(2)}) collective-permute-start(bf16[8,64,512]{2,1,0:T(8,128)(2,1)S(1)} %get-tuple-element.52), channel_id=1, source_target_pairs={{0,32},{32,0},{64,96},{96,64},{128,160},{160,128},{192,224},{224,1... | collective-permute-start | bytes 1572872 | tf_op jit(solution)/shard_map/ppermute | solution.py:19
  192.8 2.2 %copy-start.5 = (f32[8,64,512]{2,1,0:T(8,128)S(1)}, f32[8,64,512]{2,1,0:T(8,128)}, u32[]{:S(2)}) copy-start(f32[8,64,512]{2,1,0:T(8,128)} %get-tuple-element.53.keep_v) | copy-start | bytes 3145732
  197.6 20.8 %all-to-all-start.9 = ((bf16[8,144,512]{2,1,0:T(8,128)(2,1)}), bf16[8,144,512]{2,1,0:T(8,128)(2,1)S(1)}, u32[]{:S(2)}, u32[]{:S(2)}) async-start(bf16[8,144,512]{2,1,0:T(8,128)(2,1)} %copy-done.1), calls=%async_computation.9 | async-start | bytes 2359296 | tf_op jit(solution)/shard_map/all_to_all | solution.py:37
  201.2 2.9 %copy-start.9 = (bf16[8,2,64,512]{3,2,1,0:T(8,128)(2,1)S(1)}, bf16[8,2,64,512]{3,2,1,0:T(8,128)(2,1)}, u32[]{:S(2)}) copy-start(bf16[8,2,64,512]{3,2,1,0:T(8,128)(2,1)} %copy-done.8) | copy-start | bytes 3145732
  202.0 2.7 %copy-start.12 = (bf16[1024,512]{1,0:T(8,128)(2,1)S(1)}, bf16[1024,512]{1,0:T(8,128)(2,1)}, u32[]{:S(2)}) copy-start(bf16[1024,512]{1,0:T(8,128)(2,1)} %copy-done.11) | copy-start | bytes 3145732
  202.0 2.7 %copy-start.13 = (f32[384,1024]{1,0:T(8,128)S(1)}, f32[384,1024]{1,0:T(8,128)}, u32[]{:S(2)}) copy-start(f32[384,1024]{1,0:T(8,128)} %get-tuple-element.56) | copy-start | bytes 4718596
  202.0 4.3 %collective-permute-start.5 = (bf16[1024,256]{0,1:T(8,128)(2,1)S(1)}, bf16[1024,256]{0,1:T(8,128)(2,1)S(1)}, u32[]{:S(2)}, u32[]{:S(2)}) collective-permute-start(bf16[1024,256]{0,1:T(8,128)(2,1)S(1)} %slice.53), channel_id=1, source_target_pairs={{0,32},{32,0},{64,96},{96,64},{128,160},{160,128},{192,224},{224,1... | collective-permute-start | bytes 1572872 | tf_op jit(solution)/shard_map/ppermute | solution.py:19
  (3 other events, 3.1 us)

commit v13 on v11

--- a/solution.py
+++ b/solution.py
@@ -356,7 +356,9 @@
     bias_two = jnp.sum(second_adj.astype(wide), axis=0, keepdims=True)
 
     first_part = dot(x0, full_v).astype(low)
-    own_maps, first_part, second_adj, bias_two = lax.optimization_barrier((own_maps, first_part, second_adj, bias_two))
+    own_maps, other_u, first_part, second_adj, bias_two = lax.optimization_barrier(
+        (own_maps, other_u, first_part, second_adj, bias_two)
+    )
     other_maps = core_swap(own_maps)
     own_su, other_su = own_maps[:, :lines], other_maps[:, :lines]
     pair = [jnp.where(core == 0, own_su, other_su), jnp.where(core == 0, other_su, own_su)]

time: 216 us -> 215 us (level)
  transfers between devices with their start and end apart: 10 -> 10, of which waited for: 4 -> 4; matrix products, arithmetic and copies ran while one was open for 6% -> 4% of each run, Pallas kernels for 3% -> 3%
where the time goes in v13:
time: 215 us; the launch traced here: 214 us
  blocking collectives  114 us (53%)
  starting transfers between devices  53.2 us (25%)
  waiting for transfers between devices  16.5 us (8%)
  Pallas kernels  15.7 us (7%)
  local copies, waits for them, and re-layouts  5.85 us (3%)
  matrix products  4.41 us (2%)
  other arithmetic  4.05 us (2%)
    all_to_all x6, blocking collectives, exchange(): lax.all_to_all(value, axis, 0, 0, axis_index_groups=groups, tiled=True)  114 us
    ppermute x6, starting transfers between devices, core_swap(): return lax.ppermute(value, 'dom', pairs)  36.6 us
    all_to_all x4, starting transfers between devices, exchange(): lax.all_to_all(value, axis, 0, 0, axis_index_groups=groups, tiled=True)  16.6 us
    all_to_all x4, waiting for transfers between devices, exchange(): lax.all_to_all(value, axis, 0, 0, axis_index_groups=groups, tiled=True)  13.7 us
    pallas_call x1, Pallas kernels, middle(): pl.pallas_call(middle_kernel, grid_spec=pltpu.PrefetchScalarGridSpec(num_...  5.43 us
    pallas_call x1, Pallas kernels, early_terms(): pl.pallas_call(early_kernel, grid_spec=pltpu.PrefetchScalarGridSpec(num_s...  4.67 us
  transfers between devices with their start and end apart: 10, of which 4 were waited for; matrix products, arithmetic and copies ran while one was open for 4% of the time, Pallas kernels for 3%

profile of v13, /device:TPU:1, one launch (start us, length us, event | category | flops | bytes accessed | tf_op | source)
XLA Modules:
  0.0 214.5 jit_solution(11965058792257879629)
XLA Ops:
  0.7 2.0 shard_map.127
  2.7 5.9 %all-to-all-start = ((bf16[8,128,512]{2,1,0:T(8,128)(2,1)}), bf16[8,128,512]{2,1,0:T(8,128)(2,1)S(1)}, u32[]{:S(2)}, u32[]{:S(2)}) async-start(bf16[8,128,512]{2,1,0:T(8,128)(2,1)} %shard_map.127), calls=%async_computation | async-start | bytes 2097152 | tf_op jit(solution)/shard_map/all_to_all | solution.py:37
  8.6 6.4 %collective-permute-start = (bf16[1024,256]{1,0:T(8,128)(2,1)}, bf16[1024,256]{1,0:T(8,128)(2,1)}, u32[]{:S(2)}, u32[]{:S(2)}) collective-permute-start(bf16[1024,256]{1,0:T(8,128)(2,1)} %own_u), channel_id=1, source_target_pairs={{0,32},{32,0},{64,96},{96,64},{128,160},{160,128},{192,224},{224,1... | collective-permute-start | bytes 1572872 | tf_op jit(solution)/shard_map/ppermute | solution.py:19
  15.1 1.9 collective-permute-start.1
  21.5 5.8 %collective-permute-start.2 = (bf16[8,128,512]{2,1,0:T(8,128)(2,1)S(1)}, bf16[8,128,512]{2,1,0:T(8,128)(2,1)}, u32[]{:S(2)}, u32[]{:S(2)}) collective-permute-start(bf16[8,128,512]{2,1,0:T(8,128)(2,1)S(1)} %all-to-all-done.own_v), channel_id=1, source_target_pairs={{0,32},{32,0},{64,96},{96,64},{128,160},{160,128},{192,224},{224,1... | collective-permute-start | bytes 3145736 | tf_op jit(solution)/shard_map/ppermute | solution.py:19
  27.3 2.4 %collective-permute-done.2.other_v = bf16[8,128,512]{2,1,0:T(8,128)(2,1)} collective-permute-done((bf16[8,128,512]{2,1,0:T(8,128)(2,1)S(1)}, bf16[8,128,512]{2,1,0:T(8,128)(2,1)}, u32[]{:S(2)}, u32[]{:S(2)}) %collective-permute-start.2) | collective-permute-done | bytes 1048608 | tf_op jit(solution)/shard_map/ppermute | solution.py:19
  33.1 16.4 %all_to_all.79 = bf16[4,192,512]{2,1,0:T(8,128)(2,1)S(1)} all-to-all(bf16[4,192,512]{2,1,0:T(8,128)(2,1)S(1)} %bitcast.40), channel_id=1, replica_groups={{0,1,16,17},{2,3,18,19},{4,5,20,21},{6,7,22,23},{8,9,24,25},{10,11,26,2..., dimensions={0} | all-to-all | bytes 1572864 | tf_op jit(solution)/shard_map/all_to_all | solution.py:37
  49.6 28.0 %all_to_all.80 = bf16[8,24,512]{2,1,0:T(8,128)(2,1)S(1)} all-to-all(bf16[8,24,512]{2,1,0:T(8,128)(2,1)S(1)} %bitcast.41), channel_id=1, replica_groups={{0,2,4,6,8,10,12,14},{1,3,5,7,9,11,13,15},{16,18,20,22,24,26,28,30},{17..., dimensions={0} | all-to-all | bytes 393216 | tf_op jit(solution)/shard_map/all_to_all | solution.py:37
  77.7 20.0 %all_to_all.81 = bf16[8,24,512]{2,1,0:T(8,128)(2,1)S(1)} all-to-all(bf16[8,24,512]{2,1,0:T(8,128)(2,1)S(1)} %broadcast_in_dim.50), channel_id=1, replica_groups={{0,2,4,6,8,10,12,14},{1,3,5,7,9,11,13,15},{16,18,20,22,24,26,28,30},{17..., dimensions={0} | all-to-all | bytes 393216 | tf_op jit(solution)/shard_map/all_to_all | solution.py:37
  97.7 12.1 %all_to_all.82 = bf16[4,192,512]{2,1,0:T(8,128)(2,1)S(1)} all-to-all(bf16[4,192,512]{2,1,0:T(8,128)(2,1)S(1)} %broadcast_in_dim.52), channel_id=1, replica_groups={{0,1,16,17},{2,3,18,19},{4,5,20,21},{6,7,22,23},{8,9,24,25},{10,11,26,2..., dimensions={0} | all-to-all | bytes 1572864 | tf_op jit(solution)/shard_map/all_to_all | solution.py:37
  109.8 5.4 %shard_map.128 = (bf16[768,512]{1,0:T(8,128)(2,1)}, bf16[384,1024]{1,0:T(8,128)(2,1)}, bf16[384,1024]{1,0:T(8,128)(2,1)}, f32[384,1024]{1,0:T(8,128)}, f32[1,1024]{1,0:T(1,128)S(1)}) custom-call(s32[1]{0:T(128)} %bitcast.place, bf16[768,512]{1,0:T(8,128)(2,1)S(1)} %bitcast.34, bf16[384,1024]{1,0:T(8,128)(2,1)} %x0.1, ...), custom_call_target="tpu_custom_call" | custom-call | tf_op jit(solution)/shard_map/pallas_call | solution.py:138
  115.2 3.5 %all-to-all-start.5 = ((bf16[4,192,512]{2,1,0:T(8,128)(2,1)}), bf16[4,192,512]{2,1,0:T(8,128)(2,1)S(1)}, u32[]{:S(2)}, u32[]{:S(2)}) async-start(bf16[4,192,512]{2,1,0:T(8,128)(2,1)} %bitcast.43), calls=%async_computation.5 | async-start | bytes 1572864 | tf_op jit(solution)/shard_map/all_to_all | solution.py:37
  118.7 4.7 %shard_map.129 = (f32[1024,256]{1,0:T(8,128)}, f32[8,64,512]{2,1,0:T(8,128)}, bf16[4,272,512]{2,1,0:T(8,128)(2,1)}) custom-call(s32[1]{0:T(128)} %bitcast.place, bf16[384,1024]{1,0:T(8,128)(2,1)} %get-tuple-element.45.first_adj, bf16[384,1024]{1,0:T(8,128)(2,1)} %get-tuple-element.46.layer_one, bf16[768,512]{1,0:T(8,128)(2,1)S(1)} %bitcast.35, ...), custom_call_target="tpu_custom_call" | custom-call | tf_op jit(solution)/shard_map/pallas_call | solution.py:224
  123.4 3.6 %all-to-all-done.5 = bf16[4,192,512]{2,1,0:T(8,128)(2,1)S(1)} async-done(((bf16[4,192,512]{2,1,0:T(8,128)(2,1)}), bf16[4,192,512]{2,1,0:T(8,128)(2,1)S(1)}, u32[]{:S(2)}, u32[]{:S(2)}) %all-to-all-start.5) | async-done | bytes 786464 | tf_op jit(solution)/shard_map/all_to_all | solution.py:37
  127.2 20.1 %all_to_all.83 = bf16[8,24,512]{2,1,0:T(8,128)(2,1)S(1)} all-to-all(bf16[8,24,512]{2,1,0:T(8,128)(2,1)S(1)} %bitcast.42), channel_id=1, replica_groups={{0,2,4,6,8,10,12,14},{1,3,5,7,9,11,13,15},{16,18,20,22,24,26,28,30},{17..., dimensions={0} | all-to-all | bytes 393216 | tf_op jit(solution)/shard_map/all_to_all | solution.py:37
  147.3 17.1 %all_to_all.84 = bf16[8,24,512]{2,1,0:T(8,128)(2,1)S(1)} all-to-all(bf16[8,24,512]{2,1,0:T(8,128)(2,1)S(1)} %broadcast_in_dim.53), channel_id=1, replica_groups={{0,2,4,6,8,10,12,14},{1,3,5,7,9,11,13,15},{16,18,20,22,24,26,28,30},{17..., dimensions={0} | all-to-all | bytes 393216 | tf_op jit(solution)/shard_map/all_to_all | solution.py:37
  165.4 3.5 %all-to-all-start.8 = ((bf16[4,192,512]{2,1,0:T(8,128)(2,1)}), bf16[4,192,512]{2,1,0:T(8,128)(2,1)S(1)}, u32[]{:S(2)}, u32[]{:S(2)}) async-start(bf16[4,192,512]{2,1,0:T(8,128)(2,1)} %broadcast_in_dim.54), calls=%async_computation.8 | async-start | bytes 1572864 | tf_op jit(solution)/shard_map/all_to_all | solution.py:37
  168.9 10.5 %collective-permute-start.4 = (bf16[4,272,512]{2,1,0:T(8,128)(2,1)}, bf16[4,272,512]{2,1,0:T(8,128)(2,1)S(1)}, u32[]{:S(2)}, u32[]{:S(2)}) collective-permute-start(bf16[4,272,512]{2,1,0:T(8,128)(2,1)} %get-tuple-element.56), channel_id=1, source_target_pairs={{0,32},{32,0},{64,96},{96,64},{128,160},{160,128},{192,224},{224,1... | collective-permute-start | bytes 3342344 | tf_op jit(solution)/shard_map/ppermute | solution.py:19
  179.4 1.5 shard_map.130
  180.9 9.4 %collective-permute-start.3 = (bf16[8,64,512]{2,1,0:T(8,128)(2,1)S(1)}, bf16[8,64,512]{2,1,0:T(8,128)(2,1)S(1)}, u32[]{:S(2)}, u32[]{:S(2)}) collective-permute-start(bf16[8,64,512]{2,1,0:T(8,128)(2,1)S(1)} %get-tuple-element.54), channel_id=1, source_target_pairs={{0,32},{32,0},{64,96},{96,64},{128,160},{160,128},{192,224},{224,1... | collective-permute-start | bytes 1572872 | tf_op jit(solution)/shard_map/ppermute | solution.py:19
  193.2 3.7 %all-to-all-start.9 = ((bf16[8,144,512]{2,1,0:T(8,128)(2,1)}), bf16[8,144,512]{2,1,0:T(8,128)(2,1)S(1)}, u32[]{:S(2)}, u32[]{:S(2)}) async-start(bf16[8,144,512]{2,1,0:T(8,128)(2,1)} %shard_map.131), calls=%async_computation.9 | async-start | bytes 2359296 | tf_op jit(solution)/shard_map/all_to_all | solution.py:37
  197.7 2.5 %collective-permute-start.5 = (bf16[1024,256]{0,1:T(8,128)(2,1)S(1)}, bf16[1024,256]{0,1:T(8,128)(2,1)S(1)}, u32[]{:S(2)}, u32[]{:S(2)}) collective-permute-start(bf16[1024,256]{0,1:T(8,128)(2,1)S(1)} %slice.53), channel_id=1, source_target_pairs={{0,32},{32,0},{64,96},{96,64},{128,160},{160,128},{192,224},{224,1... | collective-permute-start | bytes 1572872 | tf_op jit(solution)/shard_map/ppermute | solution.py:19
  200.9 1.6 fusion.3
  203.7 10.1 %all-to-all-done.9.taken = bf16[8,144,512]{2,1,0:T(8,128)(2,1)S(1)} async-done(((bf16[8,144,512]{2,1,0:T(8,128)(2,1)}), bf16[8,144,512]{2,1,0:T(8,128)(2,1)S(1)}, u32[]{:S(2)}, u32[]{:S(2)}) %all-to-all-start.9) | async-done | bytes 1179680 | tf_op jit(solution)/shard_map/all_to_all | solution.py:37
  (64 shorter events, 15.3 us)
Async XLA Ops:
  0.6 16.4 %copy-start.13 = (s32[384]{0:T(512)S(1)}, s32[384]{0:T(512)}, u32[]{:S(2)}) copy-start(s32[384]{0:T(512)} %param.10) | copy-start | bytes 4612
  0.6 16.4 %copy-start.2 = (bf16[384,1024]{1,0:T(8,128)(2,1)S(1)}, bf16[384,1024]{1,0:T(8,128)(2,1)}, u32[]{:S(2)}) copy-start(bf16[384,1024]{1,0:T(8,128)(2,1)} %x0.1) | copy-start | bytes 2359300
  0.7 16.4 %copy-start.12 = (bf16[384,1024]{1,0:T(8,128)(2,1)S(1)}, bf16[384,1024]{1,0:T(8,128)(2,1)}, u32[]{:S(2)}) copy-start(bf16[384,1024]{1,0:T(8,128)(2,1)} %param.9) | copy-start | bytes 2359300
  2.7 18.8 %all-to-all-start = ((bf16[8,128,512]{2,1,0:T(8,128)(2,1)}), bf16[8,128,512]{2,1,0:T(8,128)(2,1)S(1)}, u32[]{:S(2)}, u32[]{:S(2)}) async-start(bf16[8,128,512]{2,1,0:T(8,128)(2,1)} %shard_map.127), calls=%async_computation | async-start | bytes 2097152 | tf_op jit(solution)/shard_map/all_to_all | solution.py:37
  8.6 12.8 %collective-permute-start = (bf16[1024,256]{1,0:T(8,128)(2,1)}, bf16[1024,256]{1,0:T(8,128)(2,1)}, u32[]{:S(2)}, u32[]{:S(2)}) collective-permute-start(bf16[1024,256]{1,0:T(8,128)(2,1)} %own_u), channel_id=1, source_target_pairs={{0,32},{32,0},{64,96},{96,64},{128,160},{160,128},{192,224},{224,1... | collective-permute-start | bytes 1572872 | tf_op jit(solution)/shard_map/ppermute | solution.py:19
  15.1 4.3 %collective-permute-start.1 = (bf16[1024,256]{1,0:T(8,128)(2,1)}, bf16[1024,256]{1,0:T(8,128)(2,1)}, u32[]{:S(2)}, u32[]{:S(2)}) collective-permute-start(bf16[1024,256]{1,0:T(8,128)(2,1)} %param.12), channel_id=1, source_target_pairs={{0,32},{32,0},{64,96},{96,64},{128,160},{160,128},{192,224},{224,1... | collective-permute-start | bytes 1572872 | tf_op jit(solution)/shard_map/ppermute | solution.py:19
  20.5 1.0 copy-start.8
  21.5 9.5 %copy-start.5 = (bf16[8,128,512]{2,1,0:T(8,128)(2,1)}, bf16[8,128,512]{2,1,0:T(8,128)(2,1)S(1)}, u32[]{:S(2)}) copy-start(bf16[8,128,512]{2,1,0:T(8,128)(2,1)S(1)} %all-to-all-done.own_v) | copy-start | bytes 3145732
  21.5 8.2 %collective-permute-start.2 = (bf16[8,128,512]{2,1,0:T(8,128)(2,1)S(1)}, bf16[8,128,512]{2,1,0:T(8,128)(2,1)}, u32[]{:S(2)}, u32[]{:S(2)}) collective-permute-start(bf16[8,128,512]{2,1,0:T(8,128)(2,1)S(1)} %all-to-all-done.own_v), channel_id=1, source_target_pairs={{0,32},{32,0},{64,96},{96,64},{128,160},{160,128},{192,224},{224,1... | collective-permute-start | bytes 3145736 | tf_op jit(solution)/shard_map/ppermute | solution.py:19
  31.0 1.0 copy-start.6
  77.6 32.1 %copy-start.1 = (f32[2,1024]{1,0:T(2,128)S(1)}, f32[2,1024]{1,0:T(2,128)}, u32[]{:S(2)}) copy-start(f32[2,1024]{1,0:T(2,128)} %bias.1) | copy-start | bytes 24580
  115.2 11.8 %all-to-all-start.5 = ((bf16[4,192,512]{2,1,0:T(8,128)(2,1)}), bf16[4,192,512]{2,1,0:T(8,128)(2,1)S(1)}, u32[]{:S(2)}, u32[]{:S(2)}) async-start(bf16[4,192,512]{2,1,0:T(8,128)(2,1)} %bitcast.43), calls=%async_computation.5 | async-start | bytes 1572864 | tf_op jit(solution)/shard_map/all_to_all | solution.py:37
  165.4 14.0 %all-to-all-start.8 = ((bf16[4,192,512]{2,1,0:T(8,128)(2,1)}), bf16[4,192,512]{2,1,0:T(8,128)(2,1)S(1)}, u32[]{:S(2)}, u32[]{:S(2)}) async-start(bf16[4,192,512]{2,1,0:T(8,128)(2,1)} %broadcast_in_dim.54), calls=%async_computation.8 | async-start | bytes 1572864 | tf_op jit(solution)/shard_map/all_to_all | solution.py:37
  168.9 21.5 %collective-permute-start.4 = (bf16[4,272,512]{2,1,0:T(8,128)(2,1)}, bf16[4,272,512]{2,1,0:T(8,128)(2,1)S(1)}, u32[]{:S(2)}, u32[]{:S(2)}) collective-permute-start(bf16[4,272,512]{2,1,0:T(8,128)(2,1)} %get-tuple-element.56), channel_id=1, source_target_pairs={{0,32},{32,0},{64,96},{96,64},{128,160},{160,128},{192,224},{224,1... | collective-permute-start | bytes 3342344 | tf_op jit(solution)/shard_map/ppermute | solution.py:19
  179.4 11.0 %copy-start.11 = (f32[1024,256]{1,0:T(8,128)S(1)}, f32[1024,256]{1,0:T(8,128)}, u32[]{:S(2)}) copy-start(f32[1024,256]{1,0:T(8,128)} %get-tuple-element.59) | copy-start | bytes 3145732
  180.9 10.9 %collective-permute-start.3 = (bf16[8,64,512]{2,1,0:T(8,128)(2,1)S(1)}, bf16[8,64,512]{2,1,0:T(8,128)(2,1)S(1)}, u32[]{:S(2)}, u32[]{:S(2)}) collective-permute-start(bf16[8,64,512]{2,1,0:T(8,128)(2,1)S(1)} %get-tuple-element.54), channel_id=1, source_target_pairs={{0,32},{32,0},{64,96},{96,64},{128,160},{160,128},{192,224},{224,1... | collective-permute-start | bytes 1572872 | tf_op jit(solution)/shard_map/ppermute | solution.py:19
  190.3 1.5 copy-start
  193.2 3.7 %copy-start.3 = (bf16[384,1024]{1,0:T(8,128)(2,1)S(1)}, bf16[384,1024]{1,0:T(8,128)(2,1)}, u32[]{:S(2)}) copy-start(bf16[384,1024]{1,0:T(8,128)(2,1)} %x0.1) | copy-start | bytes 2359300
  193.2 20.5 %all-to-all-start.9 = ((bf16[8,144,512]{2,1,0:T(8,128)(2,1)}), bf16[8,144,512]{2,1,0:T(8,128)(2,1)S(1)}, u32[]{:S(2)}, u32[]{:S(2)}) async-start(bf16[8,144,512]{2,1,0:T(8,128)(2,1)} %shard_map.131), calls=%async_computation.9 | async-start | bytes 2359296 | tf_op jit(solution)/shard_map/all_to_all | solution.py:37
  196.9 3.4 %copy-start.7 = (bf16[8,2,64,512]{3,2,1,0:T(8,128)(2,1)S(1)}, bf16[8,2,64,512]{3,2,1,0:T(8,128)(2,1)}, u32[]{:S(2)}) copy-start(bf16[8,2,64,512]{3,2,1,0:T(8,128)(2,1)} %copy-done.6) | copy-start | bytes 3145732
  197.6 3.3 %copy-start.10 = (f32[384,1024]{1,0:T(8,128)S(1)}, f32[384,1024]{1,0:T(8,128)}, u32[]{:S(2)}) copy-start(f32[384,1024]{1,0:T(8,128)} %get-tuple-element.58) | copy-start | bytes 4718596
  197.7 3.2 %copy-start.4 = (bf16[384,1024]{1,0:T(8,128)(2,1)S(1)}, bf16[384,1024]{1,0:T(8,128)(2,1)}, u32[]{:S(2)}) copy-start(bf16[384,1024]{1,0:T(8,128)(2,1)} %get-tuple-element.84.masked) | copy-start | bytes 2359300
  197.7 3.2 %copy-start.9 = (bf16[1024,512]{1,0:T(8,128)(2,1)S(1)}, bf16[1024,512]{1,0:T(8,128)(2,1)}, u32[]{:S(2)}) copy-start(bf16[1024,512]{1,0:T(8,128)(2,1)} %copy-done.8) | copy-start | bytes 3145732
  197.7 4.8 %collective-permute-start.5 = (bf16[1024,256]{0,1:T(8,128)(2,1)S(1)}, bf16[1024,256]{0,1:T(8,128)(2,1)S(1)}, u32[]{:S(2)}, u32[]{:S(2)}) collective-permute-start(bf16[1024,256]{0,1:T(8,128)(2,1)S(1)} %slice.53), channel_id=1, source_target_pairs={{0,32},{32,0},{64,96},{96,64},{128,160},{160,128},{192,224},{224,1... | collective-permute-start | bytes 1572872 | tf_op jit(solution)/shard_map/ppermute | solution.py:19
